TPU v7x, 32 devices: a whole 2x2x4 slice. The times are simulated.
32 devices in a mesh: grp: 2 (over y), pol: 16 (over z, x, core).
Axes of the slice: x: 2, y: 2, z: 4, core: 2. Of those that a mesh axis runs over, the one named last changes fastest.
Arguments:
- shocks: float32 [6, 128, 1024], P('grp'), parts along dimension 0, may hold values from -6 to 6
- loadings: float32 [1024, 128], P('pol'), may hold values from -0.5 to 0.5
- sec_drift: float32 [1024], P('pol'), may hold values from -0.02 to 0.08
- holdings: float32 [1024, 128], P('pol'), may hold values from -0.1875 to 0.1875
- fund_of: int32 [8192, 1], P('pol'), may hold values from 0 to 127
- product_type: int32 [8192], P('pol'), may hold values from 0 to 7
- term_years: int32 [8192], P('pol'), may hold values from 1 to 3
- asset_start: float32 [8192], P('pol'), may hold values from 0.35 to 3
- liab_start: float32 [8192], P('pol'), may hold values from 0.3 to 3
- base_lapse: float32 [8], replicated, may hold values from 0.02 to 0.2
- guarantee: float32 [8], replicated, may hold values from 0 to 0.08
- lapse_draw: bfloat16 [8192, 6, 1024], P('pol', 'grp'), parts along dimension 1, may hold values from 0 to 1
Outputs:
- assets: float32 [8192, 2048], P('pol', 'grp'), parts along dimension 1
- liability: float32 [8192, 2048], P('pol', 'grp'), parts along dimension 1
- credit_rates: float32 [6, 128, 1024], P('grp', None, 'pol'), parts along dimension 0
There are 2 independent parts, one for each index of `grp`. A program takes and returns all parts, laid end to end along the dimension named above; an argument that names none is the same for every part. Nothing has to cross between parts.
Inputs may be any that keep to these rules, and one draw needn't show every extreme that they name: `fund_of`: every fund backs at least one policy.
All inputs are finite; a program needn't handle non-finite values.
Results may differ from a plain program's by a relative error of at most 0.0003.
Values sent between devices are 32-bit elements; how exact they have to be, the bound alone decides.
No kernel may reach another device: no remote copies, remote signals or barrier semaphores. Data moves between devices by JAX's collectives and lax.ppermute only.
A program may use at most 64 MiB of HBM per device.

v0:
```python
import jax
import jax.numpy as jnp
from jax import lax
from jax.sharding import PartitionSpec as P


def crediting(totals):
    return 0.01 + jax.nn.softplus(20.0 * (totals[0] / totals[1] - 1.05)) / 20.0


def local(
    shocks,
    loadings,
    sec_drift,
    holdings,
    fund_of,
    product_type,
    term_years,
    asset_start,
    liab_start,
    base_lapse,
    guarantee,
    lapse_draw,
):
    highest = lax.Precision.HIGHEST
    num_years = shocks.shape[0]
    num_paths = shocks.shape[2]
    num_funds = holdings.shape[1]
    sec_ret = (
        0.25 * jnp.tanh(jnp.einsum("sk,ykp->ysp", loadings, shocks, precision=highest))
        + sec_drift[None, :, None]
    )
    partial_funds = jnp.einsum("sf,ysp->yfp", holdings, sec_ret, precision=highest)
    fund_ret = lax.psum(partial_funds, "pol")
    member = (fund_of[:, 0][:, None] == jnp.arange(num_funds, dtype=jnp.int32)[None, :]).astype(
        jnp.float32
    )
    type_hot = (
        product_type[:, None] == jnp.arange(base_lapse.shape[0], dtype=jnp.int32)[None, :]
    ).astype(jnp.float32)
    guaranteed = jnp.sum(type_hot * guarantee[None, :], axis=1)
    base_rate = jnp.sum(type_hot * base_lapse[None, :], axis=1)
    count = asset_start.shape[0]
    assets = jnp.broadcast_to(asset_start[:, None], (count, num_paths))
    liability = jnp.broadcast_to(liab_start[:, None], (count, num_paths))
    owned_paths = num_paths // lax.axis_size("pol")
    first_path = lax.axis_index("pol") * owned_paths
    collected = []
    for year in range(num_years):
        year_ret = fund_ret[year]
        in_force = (term_years > year).astype(jnp.float32)[:, None]
        growth = jnp.dot(member, year_ret, precision=highest)
        assets = assets * (1.0 + in_force * growth)
        fund_sums = jnp.stack(
            [
                jnp.dot(member.T, in_force * assets, precision=highest),
                jnp.dot(member.T, liability, precision=highest),
            ]
        )
        totals = lax.psum(fund_sums, "pol")
        declared = crediting(totals)
        own_rates = lax.dynamic_slice_in_dim(declared, first_path, owned_paths, 1)
        collected.append(own_rates)
        credit = jnp.maximum(jnp.dot(member, declared, precision=highest), guaranteed[:, None])
        lapse_rate = jnp.minimum(
            base_rate[:, None]
            * (0.5 + lapse_draw[:, year, :].astype(jnp.float32))
            * jnp.exp(5.0 * (growth - credit)),
            0.5,
        )
        liability = liability * (1.0 + in_force * credit) * (1.0 - in_force * lapse_rate)
        assets = assets * (1.0 - in_force * lapse_rate)
    return (assets, liability, jnp.stack(collected))


def solution(mesh):
    in_specs = (
        P("grp", None, None),
        P("pol", None),
        P("pol"),
        P("pol", None),
        P("pol", None),
        P("pol"),
        P("pol"),
        P("pol"),
        P("pol"),
        P(),
        P(),
        P("pol", "grp", None),
    )
    out_specs = (P("pol", "grp"), P("pol", "grp"), P("grp", None, "pol"))
    return jax.shard_map(local, mesh=mesh, in_specs=in_specs, out_specs=out_specs, check_vma=False)
```

profile of v0, /device:TPU:0, one launch (start us, length us, event | category | flops | bytes accessed | tf_op | source)
XLA Modules:
  0.0 431.9 jit_solution(17481085283756002193)
XLA Ops:
  7.2 0.0 copy-start
  7.2 0.0 copy-start.12
  7.2 0.0 all-reduce.5.cloned.1.call-start
  7.2 1.3 copy-done
  8.6 1.8 fusion.20
  10.4 0.0 copy-done.12
  10.4 0.0 copy-start.11
  10.4 0.0 copy-start.17
  10.4 0.0 copy-start.14
  10.4 3.8 convolution_bitcast_fusion
  14.2 0.0 all-reduce.5.cloned.1.call-update
  14.2 0.0 all-reduce.7.cloned.1.call-start
  14.3 0.0 copy-done.11
  14.3 0.0 copy-done.17
  14.3 1.6 convolution_bitcast_fusion.3
  15.9 0.0 copy-done.14
  15.9 96.4 %all-reduce.5.cloned.1.call-done = f32[3,128,1024]{1,2,0:T(8,128)} async-done(((f32[3,128,1024]{1,2,0:T(8,128)}), f32[3,128,1024]{1,2,0:T(8,128)}) %all-reduce.5.cloned.1.call-update) | async-done | bytes 1572880 | tf_op jit(solution)/shard_map/psum | solution.py:34
  112.4 2.1 fusion.53
  114.4 0.0 copy-start.7
  114.4 0.0 copy-start.10
  114.5 1.3 copy-done.7
  115.8 0.0 copy-done.18
  115.8 1.3 fusion.27
  117.0 0.0 copy-done.10
  117.0 0.0 copy-start.13
  117.1 0.0 copy-start.15
  117.1 0.0 copy-start.16
  117.1 0.0 copy-start.8
  117.1 1.0 pad_maximum_fusion
  118.1 0.0 all-reduce.7.cloned.1.call-update
  118.1 0.0 all-reduce.9.cloned.1.call-start
  118.2 0.1 select_reduce_fusion.1
  118.3 0.6 copy-done.8
  118.9 2.3 fusion.49
  121.2 89.1 %all-reduce.7.cloned.1.call-done = f32[2,128,1024]{2,1,0:T(8,128)} async-done(((f32[2,128,1024]{2,1,0:T(8,128)}), f32[2,128,1024]{2,1,0:T(8,128)}) %all-reduce.7.cloned.1.call-update) | async-done | bytes 1048592 | tf_op jit(solution)/shard_map/psum | solution.py:60
  210.3 1.6 fusion.37
  211.9 4.7 %multiply_multiply_fusion.2 = (f32[512,1024]{1,0:T(8,128)S(1)}, f32[512,1024]{1,0:T(8,128)S(1)}) fusion(f32[512,1024]{1,0:T(8,128)} %copy-done.7, f32[512]{0:T(512)S(1)} %get-tuple-element.4, f32[512]{0:T(512)S(1)} %get-tuple-element.3, f32[512]{0:T(512)S(1)} %get-tuple-element.11, f32[512]{0:T(512)S(1)} %copy-done.17, bf16[512,3,1024]{2,0,1:T(8,128)(2,1)} %param.23, ...), kind=kOutput, calls=%fused_computation.20 | convolution fusion | flops 816381952 | bytes 9975808 | tf_op jit(solution)/shard_map/dot_general | solution.py:64
  216.7 0.0 copy-start.6
  216.7 1.1 fusion.21
  217.8 1.0 convolution_bitcast_fusion.2
  218.8 1.1 pad_maximum_fusion.1
  219.8 0.0 all-reduce.9.cloned.1.call-update
  219.9 0.2 all-reduce.11.cloned.1.call-start
  220.1 2.3 fusion.45
  222.4 90.1 %all-reduce.9.cloned.1.call-done = f32[2,128,1024]{2,1,0:T(8,128)} async-done(((f32[2,128,1024]{2,1,0:T(8,128)}), f32[2,128,1024]{2,1,0:T(8,128)}) %all-reduce.9.cloned.1.call-update) | async-done | bytes 1048592 | tf_op jit(solution)/shard_map/psum | solution.py:60
  312.5 1.6 fusion.39
  314.1 0.0 copy-start.3
  314.1 4.2 multiply_multiply_fusion.1
  318.3 0.0 copy-start.4
  318.3 0.0 copy-start.5
  318.3 1.0 convolution_bitcast_fusion.1
  319.3 2.1 copy-done.2
  321.4 1.3 fusion.24
  322.8 1.1 pad_maximum_fusion.2
  323.9 0.0 all-reduce.11.cloned.1.call-update
  323.9 0.9 constant_dynamic-slice_fusion.2
  324.8 0.1 copy.18
  324.9 91.6 %all-reduce.11.cloned.1.call-done = f32[2,128,1024]{2,1,0:T(8,128)} async-done(((f32[2,128,1024]{2,1,0:T(8,128)}), f32[2,128,1024]{2,1,0:T(8,128)}) %all-reduce.11.cloned.1.call-update) | async-done | bytes 1048592 | tf_op jit(solution)/shard_map/psum | solution.py:60
  416.5 1.6 fusion.41
  418.1 0.1 constant_dynamic-slice_fusion
  418.2 6.3 %multiply_multiply_fusion = (f32[512,1024]{1,0:T(8,128)}, f32[512,1024]{1,0:T(8,128)}) fusion(f32[512,1024]{1,0:T(8,128)} %copy-done.5, f32[512]{0:T(512)S(1)} %get-tuple-element.12, f32[512]{0:T(512)S(1)} %get-tuple-element.4, f32[512,1024]{1,0:T(8,128)} %fusion.45, bf16[512,3,1024]{2,0,1:T(8,128)(2,1)} %param.23, f32[512]{0:T(512)S(1)} %get-tuple-element.3, ...), kind=kOutput, calls=%fused_computation.15 | convolution fusion | flops 815333376 | bytes 14163968 | tf_op jit(solution)/shard_map/dot_general | solution.py:64
  424.6 0.1 copy.19
  424.7 0.1 copy.20
  424.7 0.7 pad_maximum_fusion.3
  (14 shorter events, 0.0 us)
Async XLA Ops:
  7.2 1.4 copy-start
  7.2 3.2 copy-start.12
  7.2 105.2 %all-reduce.5.cloned.1.call-start = ((), (), s32[]{:S(2)}) async-start(), calls=%async_computation | async-start | bytes 3145728 | tf_op jit(solution)/shard_map/psum | solution.py:34
  10.4 3.9 copy-start.11
  10.4 3.9 copy-start.17
  10.4 5.5 %copy-start.14 = (s32[512]{0:T(512)S(1)}, s32[512]{0:T(512)}, u32[]{:S(2)}) copy-start(s32[512]{0:T(512)} %param.18) | copy-start | bytes 6148
  14.2 101.5 %copy-start.18 = (f32[512]{0:T(512)S(1)}, f32[512]{0:T(512)}, u32[]{:S(2)}) copy-start(f32[512]{0:T(512)} %param.19) | copy-start | bytes 6148
  14.2 196.1 %all-reduce.7.cloned.1.call-start = ((), (), s32[]{:S(2)}) async-start(), calls=%async_computation.1 | async-start | bytes 2097152 | tf_op jit(solution)/shard_map/psum | solution.py:60
  114.4 1.3 copy-start.7
  114.4 2.6 copy-start.10
  117.0 1.2 copy-start.13
  117.1 1.2 copy-start.15
  117.1 1.1 copy-start.16
  117.1 1.8 copy-start.8
  118.1 194.4 %all-reduce.9.cloned.1.call-start = ((), (), s32[]{:S(2)}) async-start(), calls=%async_computation.2 | async-start | bytes 2097152 | tf_op jit(solution)/shard_map/psum | solution.py:60
  211.9 4.8 %copy-start.9 = (f32[128,1024]{1,0:T(8,128)}, f32[128,1024]{1,0:T(8,128)S(1)}, u32[]{:S(2)}) copy-start(f32[128,1024]{1,0:T(8,128)S(1)} %fusion.37) | copy-start | bytes 1572868
  216.7 2.1 copy-start.1
  216.7 2.1 copy-start.6
  219.9 196.7 %all-reduce.11.cloned.1.call-start = ((), (), s32[]{:S(2)}) async-start(), calls=%async_computation.3 | async-start | bytes 2097152 | tf_op jit(solution)/shard_map/psum | solution.py:60
  314.1 5.2 %copy-start.3 = (f32[512,1024]{1,0:T(8,128)S(1)}, f32[512,1024]{1,0:T(8,128)}, u32[]{:S(2)}) copy-start(f32[512,1024]{1,0:T(8,128)} %fusion.45) | copy-start | bytes 6291460
  318.3 4.5 %copy-start.4 = (f32[512,1024]{1,0:T(8,128)}, f32[512,1024]{1,0:T(8,128)S(1)}, u32[]{:S(2)}) copy-start(f32[512,1024]{1,0:T(8,128)S(1)} %get-tuple-element.6) | copy-start | bytes 6291460
  318.3 4.5 %copy-start.5 = (f32[512,1024]{1,0:T(8,128)}, f32[512,1024]{1,0:T(8,128)S(1)}, u32[]{:S(2)}) copy-start(f32[512,1024]{1,0:T(8,128)S(1)} %get-tuple-element.5) | copy-start | bytes 6291460
  318.3 3.1 copy-start.2
Sparse Core Ops, SparseCore 0:
  14.4 97.9 all-reduce.4
  118.3 92.0 all-reduce.6
  220.0 92.4 all-reduce.8
  324.0 92.4 all-reduce.10
where the time goes:
time: 432 us
  waiting for transfers between devices  367 us (85%)
  matrix products  34.8 us (8%)
  between operations  14.1 us (3%)
  other arithmetic  8.72 us (2%)
  local copies, waits for them, and re-layouts  6.66 us (2%)
    psum x3, waiting for transfers between devices, local(): totals = lax.psum(fund_sums, 'pol')  271 us
    psum x1, waiting for transfers between devices, local(): fund_ret = lax.psum(partial_funds, 'pol')  96.4 us
    dot_general x3, matrix products, local(): jnp.dot(member, declared, precision=highest)  15.3 us
  transfers between devices with their start and end apart: 4, of which 4 were waited for; matrix products, arithmetic and copies ran while one was open for 2% of the time, Pallas kernels for 0%

commit v1 on v0

v1 whole, which is shorter than its diff:
```python
import jax
import jax.numpy as jnp
from jax import lax
from jax.sharding import PartitionSpec as P

HIGHEST = lax.Precision.HIGHEST
HIGH = lax.Precision.HIGH
SQUARE = (2, 4, 6)


def swap(x, offset):
    n = lax.axis_size("pol")
    return lax.ppermute(x, "pol", [(i, i ^ offset) for i in range(n)])


def far_offsets():
    n = lax.axis_size("pol")
    return [1 << b for b in range(3, n.bit_length() - 1)]


def reduce_slices(sums):
    held = sums[0] + swap(sums[1], 1)
    arrived = [swap(held[i + 1], o) for i, o in enumerate(SQUARE)]
    total = held[0] + arrived[0] + arrived[1] + arrived[2]
    for o in far_offsets():
        total = total + swap(total, o)
    return total


def gather_slices(own):
    near = jnp.stack([own] + [swap(own, o) for o in SQUARE])
    return jnp.concatenate([near, swap(near, 1)])


def rate(ratio):
    return 0.01 + jax.nn.softplus(20.0 * (ratio - 1.05)) / 20.0


def local(
    shocks,
    loadings,
    sec_drift,
    holdings,
    fund_of,
    product_type,
    term_years,
    asset_start,
    liab_start,
    base_lapse,
    guarantee,
    lapse_draw,
):
    num_years, _, num_paths = shocks.shape
    num_funds = holdings.shape[1]
    n = lax.axis_size("pol")
    me = lax.axis_index("pol")
    slice_funds = num_funds // 8
    count = asset_start.shape[0]
    funds = jnp.arange(num_funds, dtype=jnp.int32)
    member = (fund_of == funds[None, :]).astype(jnp.float32)
    offset = (fund_of // slice_funds) ^ (me & 7)
    place = ((offset & 1) * 4 + (offset >> 1)) * slice_funds + fund_of % slice_funds
    placed = (place == funds[None, :]).astype(jnp.float32)
    type_hot = (
        product_type[:, None] == jnp.arange(base_lapse.shape[0], dtype=jnp.int32)[None, :]
    ).astype(jnp.float32)
    guaranteed = jnp.sum(type_hot * guarantee[None, :], axis=1)
    base_rate = jnp.sum(type_hot * base_lapse[None, :], axis=1)
    in_force = [(term_years > year).astype(jnp.float32) for year in range(num_years)]

    start = jnp.stack([in_force[0] * asset_start, liab_start])
    start_sums = jnp.dot(start, member, precision=HIGHEST)
    secs = loadings.shape[0]
    drift_row = jnp.pad(sec_drift, (0, num_funds - secs))[None, :]
    extra = jnp.concatenate([start_sums, drift_row, jnp.zeros((5, num_funds), jnp.float32)])
    block = jnp.concatenate([loadings, holdings, extra])[None]
    for o in reversed(far_offsets()):
        block = jnp.concatenate([block, swap(block, o)])
    block = jnp.concatenate([block] + [swap(block, o) for o in SQUARE])
    all_load = block[:, :secs].reshape(-1, loadings.shape[1])
    all_hold = block[:, secs : 2 * secs].reshape(-1, num_funds)
    all_drift = block[:, 2 * secs + 2, :secs].reshape(-1)
    start_sums = jnp.sum(block[:, 2 * secs : 2 * secs + 2], axis=0)
    start_sums = start_sums + swap(start_sums, 1)

    def returns(year):
        sec = jnp.dot(all_load, shocks[year], precision=HIGH)
        sec = 0.25 * jnp.tanh(sec) + all_drift[:, None]
        part = lax.dot_general(all_hold, sec, (((0,), (0,)), ((), ())), precision=HIGH)
        return part + swap(part, 1)

    fund_ret = [returns(year) for year in range(num_years)]

    owned_paths = num_paths // n
    collected = []
    order = jnp.arange(8, dtype=jnp.int32) ^ (me & 7)
    order = (order & 1) * 4 + (order >> 1)
    assets, liability = asset_start[:, None], liab_start[:, None]
    for year in range(num_years):
        if year == 0:
            declared = rate(
                start_sums[0][:, None] * (1.0 + fund_ret[0]) / start_sums[1][:, None]
            )
            canonical, credit = declared, jnp.dot(member, declared, precision=HIGH)
        else:
            here = lax.dynamic_slice_in_dim(
                fund_ret[year], (me & 7) * slice_funds, slice_funds, 0
            )
            own = rate(totals[0] * (1.0 + here) / totals[1])
            declared = gather_slices(own)
            canonical = declared[order].reshape(num_funds, num_paths)
            credit = jnp.dot(placed, declared.reshape(num_funds, num_paths), precision=HIGH)
        collected.append(
            lax.dynamic_slice_in_dim(canonical, me * owned_paths, owned_paths, 1)
        )
        alive = in_force[year][:, None]
        growth = jnp.dot(member, fund_ret[year], precision=HIGH)
        credit = jnp.maximum(credit, guaranteed[:, None])
        lapse_rate = jnp.minimum(
            base_rate[:, None]
            * (0.5 + lapse_draw[:, year, :].astype(jnp.float32))
            * jnp.exp(5.0 * (growth - credit)),
            0.5,
        )
        stay = 1.0 - alive * lapse_rate
        assets = assets * (1.0 + alive * growth) * stay
        liability = liability * (1.0 + alive * credit) * stay
        if year + 1 < num_years:
            sums = jnp.stack(
                [
                    jnp.dot(placed.T, in_force[year + 1][:, None] * assets, precision=HIGH),
                    jnp.dot(placed.T, liability, precision=HIGH),
                ]
            ).reshape(2, 2, 4, slice_funds, num_paths)
            totals = reduce_slices(sums.transpose(1, 2, 0, 3, 4))
    return (assets, liability, jnp.stack(collected))


def solution(mesh):
    in_specs = (
        P("grp", None, None),
        P("pol", None),
        P("pol"),
        P("pol", None),
        P("pol", None),
        P("pol"),
        P("pol"),
        P("pol"),
        P("pol"),
        P(),
        P(),
        P("pol", "grp", None),
    )
    out_specs = (P("pol", "grp"), P("pol", "grp"), P("grp", None, "pol"))
    return jax.shard_map(local, mesh=mesh, in_specs=in_specs, out_specs=out_specs, check_vma=False)
```

time: 432 us -> 109 us (0.25)
  waiting for transfers between devices: 367 us -> 35.9 us
  starting transfers between devices: 0.34 us -> 29.2 us
  between operations: 14.1 us -> 1.23 us
  matrix products: 34.8 us -> 27.5 us
    psum x4 -> x0, waiting for transfers between devices: 367 us -> none  [the longest x3 271 us: local(): totals = lax.psum(fund_sums, 'pol')]
    ppermute x0 -> x26, waiting for transfers between devices: none -> 35.9 us  [swap(): return lax.ppermute(x, 'pol', [(i, i ^ offset) for i in range(n)])]
    ppermute x0 -> x26, starting transfers between devices: none -> 29.2 us  [swap(): return lax.ppermute(x, 'pol', [(i, i ^ offset) for i in range(n)])]
    dot_general x14 -> x17, matrix products: 34.8 us -> 27.5 us  [the longest x2 8.94 us: local(): jnp.dot(placed, declared.reshape(num_funds, num_paths), precision=HIGH)]
    unnamed x38 -> x40, local copies, waits for them, and re-layouts: 5.43 us -> 0.72 us
  transfers between devices with their start and end apart: 4 -> 26, of which waited for: 4 -> 16; matrix products, arithmetic and copies ran while one was open for 2% -> 14% of each run, Pallas kernels for 0% -> 0%
where the time goes in v1:
time: 109 us; the launch traced here: 108 us
  waiting for transfers between devices  35.9 us (33%)
  starting transfers between devices  29.2 us (27%)
  matrix products  27.5 us (25%)
  local copies, waits for them, and re-layouts  8.28 us (8%)
  other arithmetic  6.35 us (6%)
  between operations  1.23 us (1%)
    ppermute x26, waiting for transfers between devices, swap(): return lax.ppermute(x, 'pol', [(i, i ^ offset) for i in range(n)])  35.9 us
    ppermute x26, starting transfers between devices, swap(): return lax.ppermute(x, 'pol', [(i, i ^ offset) for i in range(n)])  29.2 us
    dot_general x2, matrix products, local(): jnp.dot(placed, declared.reshape(num_funds, num_paths), precision=HIGH)  8.94 us
    dot_general x3, matrix products, returns(): sec = jnp.dot(all_load, shocks[year], precision=HIGH)  3.95 us
    dot_general x3, matrix products, returns(): lax.dot_general(all_hold, sec, (((0,), (0,)), ((), ())), precision=HIGH)  3.68 us
    dot_general x1, matrix products, local(): canonical, credit = (declared, jnp.dot(member, declared, precision=HIGH))  3.58 us
    dot_general x3, matrix products, local(): growth = jnp.dot(member, fund_ret[year], precision=HIGH)  3.56 us
    gather x2, local copies, waits for them, and re-layouts, local(): canonical = declared[order].reshape(num_funds, num_paths)  2.22 us
  transfers between devices with their start and end apart: 26, of which 16 were waited for; matrix products, arithmetic and copies ran while one was open for 14% of the time, Pallas kernels for 0%

profile of v1, /device:TPU:0, one launch (start us, length us, event | category | flops | bytes accessed | tf_op | source)
XLA Modules:
  0.0 108.5 jit_solution(6265274154775396219)
XLA Ops:
  0.6 0.8 fusion.99
  1.4 0.7 pad_bitcast_fusion
  2.1 0.7 broadcast_select_fusion
  2.8 1.0 fusion.57
  3.8 1.5 %concatenate.20 = f32[136,128]{1,0:T(8,128)S(1)} concatenate(f32[64,128]{1,0:T(8,128)} %param.13, f32[64,128]{1,0:T(8,128)} %param.15, f32[2,128]{1,0:T(2,128)S(1)} %fusion.57, f32[1,128]{1,0:T(1,128)S(1)} %pad_bitcast_fusion, f32[5,128]{1,0:T(8,128)S(1)} %broadcast_in_dim.7), dimensions={0} | concatenate | bytes 139264 | tf_op jit(solution)/shard_map/concatenate | solution.py:76
  5.3 4.1 %collective-permute-start = (f32[1,136,128]{2,1,0:T(8,128)S(1)}, f32[1,136,128]{2,1,0:T(8,128)S(1)}, u32[]{:S(2)}, u32[]{:S(2)}) collective-permute-start(f32[1,136,128]{2,1,0:T(8,128)S(1)} %bitcast.205), channel_id=1, source_target_pairs={{0,8},{1,9},{2,10},{3,11},{4,12},{5,13},{6,14},{7,15},{8,0},{9,1},... | collective-permute-start | bytes 208904 | tf_op jit(solution)/shard_map/ppermute | solution.py:13
  9.4 3.8 %collective-permute-done = f32[1,136,128]{2,1,0:T(8,128)S(1)} collective-permute-done((f32[1,136,128]{2,1,0:T(8,128)S(1)}, f32[1,136,128]{2,1,0:T(8,128)S(1)}, u32[]{:S(2)}, u32[]{:S(2)}) %collective-permute-start) | collective-permute-done | bytes 69664 | tf_op jit(solution)/shard_map/ppermute | solution.py:13
  13.2 1.8 %collective-permute-start.1 = (f32[2,136,128]{2,1,0:T(8,128)S(1)}, f32[2,136,128]{2,1,0:T(8,128)S(1)}, u32[]{:S(2)}, u32[]{:S(2)}) collective-permute-start(f32[2,136,128]{2,1,0:T(8,128)S(1)} %pad_maximum_fusion.2), channel_id=1, source_target_pairs={{0,2},{1,3},{2,0},{3,1},{4,6},{5,7},{6,4},{7,5},{8,10},{9,11},{10,... | collective-permute-start | bytes 417800 | tf_op jit(solution)/shard_map/ppermute | solution.py:13
  15.4 1.4 %collective-permute-start.3 = (f32[2,136,128]{2,1,0:T(8,128)S(1)}, f32[2,136,128]{2,1,0:T(8,128)S(1)}, u32[]{:S(2)}, u32[]{:S(2)}) collective-permute-start(f32[2,136,128]{2,1,0:T(8,128)S(1)} %pad_maximum_fusion.2), channel_id=1, source_target_pairs={{0,6},{1,7},{2,4},{3,5},{4,2},{5,3},{6,0},{7,1},{8,14},{9,15},{10,... | collective-permute-start | bytes 417800 | tf_op jit(solution)/shard_map/ppermute | solution.py:13
  16.8 2.3 %collective-permute-done.1 = f32[2,136,128]{2,1,0:T(8,128)S(1)} collective-permute-done((f32[2,136,128]{2,1,0:T(8,128)S(1)}, f32[2,136,128]{2,1,0:T(8,128)S(1)}, u32[]{:S(2)}, u32[]{:S(2)}) %collective-permute-start.1) | collective-permute-done | bytes 139296 | tf_op jit(solution)/shard_map/ppermute | solution.py:13
  19.1 0.9 collective-permute-done.2
  20.0 2.3 %collective-permute-done.3 = f32[2,136,128]{2,1,0:T(8,128)S(1)} collective-permute-done((f32[2,136,128]{2,1,0:T(8,128)S(1)}, f32[2,136,128]{2,1,0:T(8,128)S(1)}, u32[]{:S(2)}, u32[]{:S(2)}) %collective-permute-start.3) | collective-permute-done | bytes 139296 | tf_op jit(solution)/shard_map/ppermute | solution.py:13
  22.5 1.0 fusion.44
  23.6 1.0 fusion.24
  24.7 0.5 collective-permute-start.5
  25.3 1.2 %collective-permute-done.5 = f32[2,128]{1,0:T(2,128)S(1)} collective-permute-done((f32[2,128]{1,0:T(2,128)S(1)}, f32[2,128]{1,0:T(2,128)S(1)}, u32[]{:S(2)}, u32[]{:S(2)}) %collective-permute-start.5) | collective-permute-done | bytes 1056 | tf_op jit(solution)/shard_map/ppermute | solution.py:13
  26.5 0.7 fusion.56
  27.3 0.5 fusion.37
  27.8 3.6 %multiply_multiply_fusion.3 = (f32[512,1024]{1,0:T(8,128)S(1)}, f32[512,1024]{1,0:T(8,128)S(1)}) fusion(f32[512,1024]{1,0:T(8,128)S(1)} %fusion.56, f32[512]{0:T(512)S(1)} %copy-done.14, f32[512]{0:T(512)S(1)} %get-tuple-element.4, f32[512]{0:T(512)S(1)} %get-tuple-element.3, f32[512]{0:T(512)S(1)} %get-tuple-element.9, bf16[512,3,1024]{2,0,1:T(8,128)(2,1)} %param.23, ...), kind=kOutput, calls=%fused_computation.26 | convolution fusion | flops 412155904 | bytes 7876608 | tf_op jit(solution)/shard_map/dot_general | solution.py:104
  31.4 0.7 fusion.52
  32.1 0.8 fusion.18
  32.9 0.5 copy-done.3
  33.8 1.0 fusion.42
  34.8 1.0 fusion.20
  36.3 1.8 %collective-permute-start.10 = (f32[2,16,1024]{2,1,0:T(8,128)S(1)}, f32[2,16,1024]{2,1,0:T(8,128)S(1)}, u32[]{:S(2)}, u32[]{:S(2)}) collective-permute-start(f32[2,16,1024]{2,1,0:T(8,128)S(1)} %get-tuple-element.23), channel_id=1, source_target_pairs={{0,6},{1,7},{2,4},{3,5},{4,2},{5,3},{6,0},{7,1},{8,14},{9,15},{10,... | collective-permute-start | bytes 393224 | tf_op jit(solution)/shard_map/ppermute | solution.py:13
  38.1 0.5 collective-permute-start.8
  38.7 1.2 %collective-permute-start.9 = (f32[2,16,1024]{2,1,0:T(8,128)S(1)}, f32[2,16,1024]{2,1,0:T(8,128)S(1)}, u32[]{:S(2)}, u32[]{:S(2)}) collective-permute-start(f32[2,16,1024]{2,1,0:T(8,128)S(1)} %get-tuple-element.24), channel_id=1, source_target_pairs={{0,4},{1,5},{2,6},{3,7},{4,0},{5,1},{6,2},{7,3},{8,12},{9,13},{10,... | collective-permute-start | bytes 393224 | tf_op jit(solution)/shard_map/ppermute | solution.py:13
  39.8 3.8 %collective-permute-done.10 = f32[2,16,1024]{2,1,0:T(8,128)S(1)} collective-permute-done((f32[2,16,1024]{2,1,0:T(8,128)S(1)}, f32[2,16,1024]{2,1,0:T(8,128)S(1)}, u32[]{:S(2)}, u32[]{:S(2)}) %collective-permute-start.10) | collective-permute-done | bytes 131104 | tf_op jit(solution)/shard_map/ppermute | solution.py:13
  43.6 2.0 %collective-permute-done.8 = f32[2,16,1024]{2,1,0:T(8,128)S(1)} collective-permute-done((f32[2,16,1024]{2,1,0:T(8,128)S(1)}, f32[2,16,1024]{2,1,0:T(8,128)S(1)}, u32[]{:S(2)}, u32[]{:S(2)}) %collective-permute-start.8) | collective-permute-done | bytes 131104 | tf_op jit(solution)/shard_map/ppermute | solution.py:13
  45.6 2.7 %collective-permute-start.11 = (f32[2,16,1024]{2,1,0:T(8,128)S(1)}, f32[2,16,1024]{2,1,0:T(8,128)S(1)}, u32[]{:S(2)}, u32[]{:S(2)}) collective-permute-start(f32[2,16,1024]{2,1,0:T(8,128)S(1)} %fusion.64), channel_id=1, source_target_pairs={{0,8},{1,9},{2,10},{3,11},{4,12},{5,13},{6,14},{7,15},{8,0},{9,1},... | collective-permute-start | bytes 393224 | tf_op jit(solution)/shard_map/ppermute | solution.py:13
  48.4 6.4 %collective-permute-done.11 = f32[2,16,1024]{2,1,0:T(8,128)S(1)} collective-permute-done((f32[2,16,1024]{2,1,0:T(8,128)S(1)}, f32[2,16,1024]{2,1,0:T(8,128)S(1)}, u32[]{:S(2)}, u32[]{:S(2)}) %collective-permute-start.11) | collective-permute-done | bytes 131104 | tf_op jit(solution)/shard_map/ppermute | solution.py:13
  55.0 1.5 %collective-permute-start.12 = (f32[16,1024]{1,0:T(8,128)S(1)}, f32[16,1024]{1,0:T(8,128)S(1)}, u32[]{:S(2)}, u32[]{:S(2)}) collective-permute-start(f32[16,1024]{1,0:T(8,128)S(1)} %get-tuple-element.8), channel_id=1, source_target_pairs={{0,2},{1,3},{2,0},{3,1},{4,6},{5,7},{6,4},{7,5},{8,10},{9,11},{10,... | collective-permute-start | bytes 196616 | tf_op jit(solution)/shard_map/ppermute | solution.py:13
  56.5 2.0 %collective-permute-start.14 = (f32[16,1024]{1,0:T(8,128)S(1)}, f32[16,1024]{1,0:T(8,128)S(1)}, u32[]{:S(2)}, u32[]{:S(2)}) collective-permute-start(f32[16,1024]{1,0:T(8,128)S(1)} %get-tuple-element.8), channel_id=1, source_target_pairs={{0,6},{1,7},{2,4},{3,5},{4,2},{5,3},{6,0},{7,1},{8,14},{9,15},{10,... | collective-permute-start | bytes 196616 | tf_op jit(solution)/shard_map/ppermute | solution.py:13
  58.5 0.7 fusion.54
  59.3 1.5 %collective-permute-done.13 = f32[16,1024]{1,0:T(8,128)S(1)} collective-permute-done((f32[16,1024]{1,0:T(8,128)S(1)}, f32[16,1024]{1,0:T(8,128)S(1)}, u32[]{:S(2)}, u32[]{:S(2)}) %collective-permute-start.13) | collective-permute-done | bytes 65568 | tf_op jit(solution)/shard_map/ppermute | solution.py:13
  60.7 0.9 collective-permute-done.14
  61.8 1.5 %collective-permute-done.15 = f32[4,16,1024]{2,1,0:T(8,128)S(1)} collective-permute-done((f32[4,16,1024]{2,1,0:T(8,128)S(1)}, f32[4,16,1024]{2,1,0:T(8,128)S(1)}, u32[]{:S(2)}, u32[]{:S(2)}) %collective-permute-start.15) | collective-permute-done | bytes 262176 | tf_op jit(solution)/shard_map/ppermute | solution.py:13
  63.3 3.6 %multiply_multiply_fusion.1 = (f32[512,1024]{1,0:T(8,128)S(1)}, f32[512,1024]{1,0:T(8,128)S(1)}) fusion(f32[512,1024]{1,0:T(8,128)S(1)} %copy-done.4, f32[512,1024]{1,0:T(8,128)S(1)} %fusion.54, f32[512]{0:T(512)S(1)} %get-tuple-element.26, f32[512]{0:T(512)S(1)} %get-tuple-element.4, f32[512]{0:T(512)S(1)} %get-tuple-element.3, ...), kind=kOutput, calls=%fused_computation.18 | convolution fusion | flops 412155904 | bytes 12066816 | tf_op jit(solution)/shard_map/dot_general | solution.py:112
  67.0 0.7 fusion.50
  67.6 0.7 fusion.12
  68.8 2.0 %fusion.40 = f32[512,1024]{1,0:T(8,128)S(1)} fusion(f32[512,128]{1,0:T(8,128)S(1)} %bitcast.196, f32[3,128,1024]{2,1,0:T(8,128)} %param.12), kind=kOutput, calls=%fused_computation.58 | convolution fusion | flops 402653184 | bytes 2883584 | tf_op jit(solution)/shard_map/dot_general | solution.py:87
  70.8 1.8 %fusion.14 = f32[128,1024]{1,0:T(8,128)} fusion(f32[512,128]{1,0:T(8,128)S(1)} %bitcast.193, f32[512,1024]{1,0:T(8,128)S(1)} %fusion.40, f32[512]{0:T(512)S(1)} %add.183), kind=kOutput, calls=%fused_computation.22 | convolution fusion | flops 403701760 | bytes 2885632 | tf_op jit(solution)/shard_map/dot_general | solution.py:89
  73.0 0.8 slice_bitcast_fusion.6
  73.8 1.3 %collective-permute-start.18 = (f32[2,16,1024]{2,1,0:T(8,128)}, f32[2,16,1024]{2,1,0:T(8,128)S(1)}, u32[]{:S(2)}, u32[]{:S(2)}) collective-permute-start(f32[2,16,1024]{2,1,0:T(8,128)} %get-tuple-element.19), channel_id=1, source_target_pairs={{0,2},{1,3},{2,0},{3,1},{4,6},{5,7},{6,4},{7,5},{8,10},{9,11},{10,... | collective-permute-start | bytes 393224 | tf_op jit(solution)/shard_map/ppermute | solution.py:13
  75.0 1.3 %collective-permute-start.19 = (f32[2,16,1024]{2,1,0:T(8,128)}, f32[2,16,1024]{2,1,0:T(8,128)S(1)}, u32[]{:S(2)}, u32[]{:S(2)}) collective-permute-start(f32[2,16,1024]{2,1,0:T(8,128)} %get-tuple-element.21), channel_id=1, source_target_pairs={{0,4},{1,5},{2,6},{3,7},{4,0},{5,1},{6,2},{7,3},{8,12},{9,13},{10,... | collective-permute-start | bytes 393224 | tf_op jit(solution)/shard_map/ppermute | solution.py:13
  76.3 0.9 collective-permute-start.20
  77.2 0.5 fusion.92
  77.7 1.2 %pad_clamp_fusion = s32[1024]{0:T(1024)} fusion(s32[8]{0:T(128)} %fusion.92), kind=kLoop, calls=%fused_computation.151 | loop fusion | flops 1024 | bytes 4128 | tf_op jit(solution)/shard_map/gather | solution.py:111
  78.9 1.3 %add.215 = f32[128,1024]{1,0:T(8,128)S(1)} add(f32[128,1024]{1,0:T(8,128)} %fusion.14, f32[128,1024]{1,0:T(8,128)} %collective-permute-done.16) | non-fusion elementwise | flops 131072 | bytes 1572864 | tf_op jit(solution)/shard_map/add | solution.py:90
  80.2 1.2 %collective-permute-done.19 = f32[2,16,1024]{2,1,0:T(8,128)S(1)} collective-permute-done((f32[2,16,1024]{2,1,0:T(8,128)}, f32[2,16,1024]{2,1,0:T(8,128)S(1)}, u32[]{:S(2)}, u32[]{:S(2)}) %collective-permute-start.19) | collective-permute-done | bytes 131104 | tf_op jit(solution)/shard_map/ppermute | solution.py:13
  81.4 2.3 %collective-permute-done.20 = f32[2,16,1024]{2,1,0:T(8,128)S(1)} collective-permute-done((f32[2,16,1024]{2,1,0:T(8,128)}, f32[2,16,1024]{2,1,0:T(8,128)S(1)}, u32[]{:S(2)}, u32[]{:S(2)}) %collective-permute-start.20) | collective-permute-done | bytes 131104 | tf_op jit(solution)/shard_map/ppermute | solution.py:13
  83.8 2.7 %collective-permute-start.21 = (f32[2,16,1024]{2,1,0:T(8,128)S(1)}, f32[2,16,1024]{2,1,0:T(8,128)S(1)}, u32[]{:S(2)}, u32[]{:S(2)}) collective-permute-start(f32[2,16,1024]{2,1,0:T(8,128)S(1)} %fusion.61), channel_id=1, source_target_pairs={{0,8},{1,9},{2,10},{3,11},{4,12},{5,13},{6,14},{7,15},{8,0},{9,1},... | collective-permute-start | bytes 393224 | tf_op jit(solution)/shard_map/ppermute | solution.py:13
  86.5 2.1 %fusion.53 = f32[512,1024]{1,0:T(8,128)} fusion(f32[128,1024]{1,0:T(8,128)S(1)} %add.215, s32[512]{0:T(512)S(1)} %bitcast.228), kind=kOutput, calls=%fused_computation.75 | convolution fusion | flops 402718720 | bytes 2623488 | tf_op jit(solution)/shard_map/dot_general | solution.py:117
  88.6 3.7 %collective-permute-done.21 = f32[2,16,1024]{2,1,0:T(8,128)S(1)} collective-permute-done((f32[2,16,1024]{2,1,0:T(8,128)S(1)}, f32[2,16,1024]{2,1,0:T(8,128)S(1)}, u32[]{:S(2)}, u32[]{:S(2)}) %collective-permute-start.21) | collective-permute-done | bytes 131104 | tf_op jit(solution)/shard_map/ppermute | solution.py:13
  92.4 1.5 %collective-permute-start.22 = (f32[16,1024]{1,0:T(8,128)S(1)}, f32[16,1024]{1,0:T(8,128)S(1)}, u32[]{:S(2)}, u32[]{:S(2)}) collective-permute-start(f32[16,1024]{1,0:T(8,128)S(1)} %get-tuple-element.6), channel_id=1, source_target_pairs={{0,2},{1,3},{2,0},{3,1},{4,6},{5,7},{6,4},{7,5},{8,10},{9,11},{10,... | collective-permute-start | bytes 196616 | tf_op jit(solution)/shard_map/ppermute | solution.py:13
  93.9 2.1 %collective-permute-start.24 = (f32[16,1024]{1,0:T(8,128)S(1)}, f32[16,1024]{1,0:T(8,128)S(1)}, u32[]{:S(2)}, u32[]{:S(2)}) collective-permute-start(f32[16,1024]{1,0:T(8,128)S(1)} %get-tuple-element.6), channel_id=1, source_target_pairs={{0,6},{1,7},{2,4},{3,5},{4,2},{5,3},{6,0},{7,1},{8,14},{9,15},{10,... | collective-permute-start | bytes 196616 | tf_op jit(solution)/shard_map/ppermute | solution.py:13
  95.9 0.9 constant_dynamic-slice_fusion.2
  96.9 1.5 %gather_fusion = f32[8,16,1024]{2,1,0:T(8,128)} fusion(f32[8,16,1024]{2,1,0:T(8,128)S(1)} %constant_dynamic-update-slice_fusion.5, s32[1024]{0:T(1024)} %pad_clamp_fusion), kind=kCustom, calls=%fused_computation | custom fusion | bytes 1048608 | tf_op jit(solution)/shard_map/gather | solution.py:111
  98.4 0.6 collective-permute-done.24
  99.2 1.5 %collective-permute-done.25 = f32[4,16,1024]{2,1,0:T(8,128)S(1)} collective-permute-done((f32[4,16,1024]{2,1,0:T(8,128)S(1)}, f32[4,16,1024]{2,1,0:T(8,128)S(1)}, u32[]{:S(2)}, u32[]{:S(2)}) %collective-permute-start.25) | collective-permute-done | bytes 262176 | tf_op jit(solution)/shard_map/ppermute | solution.py:13
  100.7 0.7 gather_fusion.1
  101.4 0.9 constant_dynamic-slice_fusion
  102.5 5.3 %multiply_multiply_fusion = (f32[512,1024]{1,0:T(8,128)}, f32[512,1024]{1,0:T(8,128)}) fusion(f32[512,1024]{1,0:T(8,128)} %copy-done, f32[512,1024]{1,0:T(8,128)} %fusion.53, f32[512]{0:T(512)S(1)} %get-tuple-element.25, f32[512]{0:T(512)S(1)} %copy-done.9, f32[512]{0:T(512)S(1)} %get-tuple-element.3, bf16[512,3,1024]{2,0,1:T(8,128)(2,1)} %param.23, ...), kind=kOutput, calls=%fused_computation.17 | convolution fusion | flops 412155904 | bytes 12066816 | tf_op jit(solution)/shard_map/dot_general | solution.py:112
  107.8 0.6 pad_maximum_fusion.3
  (91 shorter events, 3.4 us)
Async XLA Ops:
  0.6 21.9 %copy-start.5 = (f32[3,128,1024]{2,1,0:T(8,128)S(1)}, f32[3,128,1024]{2,1,0:T(8,128)}, u32[]{:S(2)}) copy-start(f32[3,128,1024]{2,1,0:T(8,128)} %param.12) | copy-start | bytes 4718596
  5.3 7.9 %collective-permute-start = (f32[1,136,128]{2,1,0:T(8,128)S(1)}, f32[1,136,128]{2,1,0:T(8,128)S(1)}, u32[]{:S(2)}, u32[]{:S(2)}) collective-permute-start(f32[1,136,128]{2,1,0:T(8,128)S(1)} %bitcast.205), channel_id=1, source_target_pairs={{0,8},{1,9},{2,10},{3,11},{4,12},{5,13},{6,14},{7,15},{8,0},{9,1},... | collective-permute-start | bytes 208904 | tf_op jit(solution)/shard_map/ppermute | solution.py:13
  13.2 5.9 %collective-permute-start.1 = (f32[2,136,128]{2,1,0:T(8,128)S(1)}, f32[2,136,128]{2,1,0:T(8,128)S(1)}, u32[]{:S(2)}, u32[]{:S(2)}) collective-permute-start(f32[2,136,128]{2,1,0:T(8,128)S(1)} %pad_maximum_fusion.2), channel_id=1, source_target_pairs={{0,2},{1,3},{2,0},{3,1},{4,6},{5,7},{6,4},{7,5},{8,10},{9,11},{10,... | collective-permute-start | bytes 417800 | tf_op jit(solution)/shard_map/ppermute | solution.py:13
  15.0 5.1 %collective-permute-start.2 = (f32[2,136,128]{2,1,0:T(8,128)S(1)}, f32[2,136,128]{2,1,0:T(8,128)S(1)}, u32[]{:S(2)}, u32[]{:S(2)}) collective-permute-start(f32[2,136,128]{2,1,0:T(8,128)S(1)} %pad_maximum_fusion.2), channel_id=1, source_target_pairs={{0,4},{1,5},{2,6},{3,7},{4,0},{5,1},{6,2},{7,3},{8,12},{9,13},{10,... | collective-permute-start | bytes 417800 | tf_op jit(solution)/shard_map/ppermute | solution.py:13
  15.4 7.0 %collective-permute-start.3 = (f32[2,136,128]{2,1,0:T(8,128)S(1)}, f32[2,136,128]{2,1,0:T(8,128)S(1)}, u32[]{:S(2)}, u32[]{:S(2)}) collective-permute-start(f32[2,136,128]{2,1,0:T(8,128)S(1)} %pad_maximum_fusion.2), channel_id=1, source_target_pairs={{0,6},{1,7},{2,4},{3,5},{4,2},{5,3},{6,0},{7,1},{8,14},{9,15},{10,... | collective-permute-start | bytes 417800 | tf_op jit(solution)/shard_map/ppermute | solution.py:13
  23.5 1.1 %copy-start.7 = (s32[512,1]{0,1:T(1,128)S(1)}, s32[512,1]{0,1:T(1,128)}, u32[]{:S(2)}) copy-start(s32[512,1]{0,1:T(1,128)} %param.16) | copy-start | bytes 6148
  23.5 1.7 %copy-start.10 = (s32[512]{0:T(512)S(1)}, s32[512]{0:T(512)}, u32[]{:S(2)}) copy-start(s32[512]{0:T(512)} %param.17) | copy-start | bytes 6148
  23.5 1.7 %copy-start.12 = (f32[8]{0:T(128)S(1)}, f32[8]{0:T(128)}, u32[]{:S(2)}) copy-start(f32[8]{0:T(128)} %param.21) | copy-start | bytes 100
  23.5 1.7 %copy-start.13 = (f32[8]{0:T(128)S(1)}, f32[8]{0:T(128)}, u32[]{:S(2)}) copy-start(f32[8]{0:T(128)} %param.22) | copy-start | bytes 100
  24.5 2.0 %collective-permute-start.4 = (f32[128,1024]{1,0:T(8,128)S(1)}, f32[128,1024]{1,0:T(8,128)S(1)}, u32[]{:S(2)}, u32[]{:S(2)}) collective-permute-start(f32[128,1024]{1,0:T(8,128)S(1)} %fusion.24), channel_id=1, source_target_pairs={{0,1},{1,0},{2,3},{3,2},{4,5},{5,4},{6,7},{7,6},{8,9},{9,8},{10,11... | collective-permute-start | bytes 1572872 | tf_op jit(solution)/shard_map/ppermute | solution.py:13
  24.7 1.8 %collective-permute-start.5 = (f32[2,128]{1,0:T(2,128)S(1)}, f32[2,128]{1,0:T(2,128)S(1)}, u32[]{:S(2)}, u32[]{:S(2)}) collective-permute-start(f32[2,128]{1,0:T(2,128)S(1)} %slice_reduce_fusion), channel_id=1, source_target_pairs={{0,1},{1,0},{2,3},{3,2},{4,5},{5,4},{6,7},{7,6},{8,9},{9,8},{10,11... | collective-permute-start | bytes 3080 | tf_op jit(solution)/shard_map/ppermute | solution.py:13
  25.3 38.0 %copy-start.8 = (f32[512]{0:T(512)}, f32[512]{0:T(512)S(1)}, u32[]{:S(2)}) copy-start(f32[512]{0:T(512)S(1)} %get-tuple-element.4) | copy-start | bytes 6148
  26.5 1.3 %copy-start.11 = (f32[512]{0:T(512)S(1)}, f32[512]{0:T(512)}, u32[]{:S(2)}) copy-start(f32[512]{0:T(512)} %param.19) | copy-start | bytes 6148
  26.5 1.3 %copy-start.14 = (f32[512]{0:T(512)S(1)}, f32[512]{0:T(512)}, u32[]{:S(2)}) copy-start(f32[512]{0:T(512)} %param.20) | copy-start | bytes 6148
  27.8 3.6 %copy-start.6 = (f32[128,1024]{1,0:T(8,128)}, f32[128,1024]{1,0:T(8,128)S(1)}, u32[]{:S(2)}) copy-start(f32[128,1024]{1,0:T(8,128)S(1)} %fusion.37) | copy-start | bytes 1572868
  31.4 1.5 %copy-start.1 = (f32[512,1024]{1,0:T(8,128)}, f32[512,1024]{1,0:T(8,128)S(1)}, u32[]{:S(2)}) copy-start(f32[512,1024]{1,0:T(8,128)S(1)} %get-tuple-element.16) | copy-start | bytes 6291460
  31.4 2.0 %copy-start.3 = (f32[512,1024]{1,0:T(8,128)}, f32[512,1024]{1,0:T(8,128)S(1)}, u32[]{:S(2)}) copy-start(f32[512,1024]{1,0:T(8,128)S(1)} %get-tuple-element.15) | copy-start | bytes 6291460
  33.6 2.6 %collective-permute-start.7 = (f32[4,2,16,1024]{3,2,1,0:T(8,128)S(1)}, f32[4,2,16,1024]{3,2,1,0:T(8,128)S(1)}, u32[]{:S(2)}, u32[]{:S(2)}) collective-permute-start(f32[4,2,16,1024]{3,2,1,0:T(8,128)S(1)} %slice_bitcast_fusion.2), channel_id=1, source_target_pairs={{0,1},{1,0},{2,3},{3,2},{4,5},{5,4},{6,7},{7,6},{8,9},{9,8},{10,11... | collective-permute-start | bytes 1572872 | tf_op jit(solution)/shard_map/ppermute | solution.py:13
  35.7 12.6 %collective-permute-start.6 = (f32[128,1024]{1,0:T(8,128)S(1)}, f32[128,1024]{1,0:T(8,128)S(1)}, u32[]{:S(2)}, u32[]{:S(2)}) collective-permute-start(f32[128,1024]{1,0:T(8,128)S(1)} %fusion.20), channel_id=1, source_target_pairs={{0,1},{1,0},{2,3},{3,2},{4,5},{5,4},{6,7},{7,6},{8,9},{9,8},{10,11... | collective-permute-start | bytes 1572872 | tf_op jit(solution)/shard_map/ppermute | solution.py:13
  36.3 7.3 %collective-permute-start.10 = (f32[2,16,1024]{2,1,0:T(8,128)S(1)}, f32[2,16,1024]{2,1,0:T(8,128)S(1)}, u32[]{:S(2)}, u32[]{:S(2)}) collective-permute-start(f32[2,16,1024]{2,1,0:T(8,128)S(1)} %get-tuple-element.23), channel_id=1, source_target_pairs={{0,6},{1,7},{2,4},{3,5},{4,2},{5,3},{6,0},{7,1},{8,14},{9,15},{10,... | collective-permute-start | bytes 393224 | tf_op jit(solution)/shard_map/ppermute | solution.py:13
  38.1 7.5 %collective-permute-start.8 = (f32[2,16,1024]{2,1,0:T(8,128)S(1)}, f32[2,16,1024]{2,1,0:T(8,128)S(1)}, u32[]{:S(2)}, u32[]{:S(2)}) collective-permute-start(f32[2,16,1024]{2,1,0:T(8,128)S(1)} %get-tuple-element.22), channel_id=1, source_target_pairs={{0,2},{1,3},{2,0},{3,1},{4,6},{5,7},{6,4},{7,5},{8,10},{9,11},{10,... | collective-permute-start | bytes 393224 | tf_op jit(solution)/shard_map/ppermute | solution.py:13
  38.7 6.9 %collective-permute-start.9 = (f32[2,16,1024]{2,1,0:T(8,128)S(1)}, f32[2,16,1024]{2,1,0:T(8,128)S(1)}, u32[]{:S(2)}, u32[]{:S(2)}) collective-permute-start(f32[2,16,1024]{2,1,0:T(8,128)S(1)} %get-tuple-element.24), channel_id=1, source_target_pairs={{0,4},{1,5},{2,6},{3,7},{4,0},{5,1},{6,2},{7,3},{8,12},{9,13},{10,... | collective-permute-start | bytes 393224 | tf_op jit(solution)/shard_map/ppermute | solution.py:13
  45.6 9.2 %collective-permute-start.11 = (f32[2,16,1024]{2,1,0:T(8,128)S(1)}, f32[2,16,1024]{2,1,0:T(8,128)S(1)}, u32[]{:S(2)}, u32[]{:S(2)}) collective-permute-start(f32[2,16,1024]{2,1,0:T(8,128)S(1)} %fusion.64), channel_id=1, source_target_pairs={{0,8},{1,9},{2,10},{3,11},{4,12},{5,13},{6,14},{7,15},{8,0},{9,1},... | collective-permute-start | bytes 393224 | tf_op jit(solution)/shard_map/ppermute | solution.py:13
  54.9 8.5 %copy-start.4 = (f32[512,1024]{1,0:T(8,128)S(1)}, f32[512,1024]{1,0:T(8,128)}, u32[]{:S(2)}) copy-start(f32[512,1024]{1,0:T(8,128)} %copy-done.3) | copy-start | bytes 6291460
  54.9 8.4 %copy-start.2 = (f32[512,1024]{1,0:T(8,128)S(1)}, f32[512,1024]{1,0:T(8,128)}, u32[]{:S(2)}) copy-start(f32[512,1024]{1,0:T(8,128)} %copy-done.1) | copy-start | bytes 6291460
  55.0 4.3 %collective-permute-start.12 = (f32[16,1024]{1,0:T(8,128)S(1)}, f32[16,1024]{1,0:T(8,128)S(1)}, u32[]{:S(2)}, u32[]{:S(2)}) collective-permute-start(f32[16,1024]{1,0:T(8,128)S(1)} %get-tuple-element.8), channel_id=1, source_target_pairs={{0,2},{1,3},{2,0},{3,1},{4,6},{5,7},{6,4},{7,5},{8,10},{9,11},{10,... | collective-permute-start | bytes 196616 | tf_op jit(solution)/shard_map/ppermute | solution.py:13
  56.5 4.3 %collective-permute-start.13 = (f32[16,1024]{1,0:T(8,128)S(1)}, f32[16,1024]{1,0:T(8,128)S(1)}, u32[]{:S(2)}, u32[]{:S(2)}) collective-permute-start(f32[16,1024]{1,0:T(8,128)S(1)} %get-tuple-element.8), channel_id=1, source_target_pairs={{0,4},{1,5},{2,6},{3,7},{4,0},{5,1},{6,2},{7,3},{8,12},{9,13},{10,... | collective-permute-start | bytes 196616 | tf_op jit(solution)/shard_map/ppermute | solution.py:13
  56.5 5.2 %collective-permute-start.14 = (f32[16,1024]{1,0:T(8,128)S(1)}, f32[16,1024]{1,0:T(8,128)S(1)}, u32[]{:S(2)}, u32[]{:S(2)}) collective-permute-start(f32[16,1024]{1,0:T(8,128)S(1)} %get-tuple-element.8), channel_id=1, source_target_pairs={{0,6},{1,7},{2,4},{3,5},{4,2},{5,3},{6,0},{7,1},{8,14},{9,15},{10,... | collective-permute-start | bytes 196616 | tf_op jit(solution)/shard_map/ppermute | solution.py:13
  61.7 1.6 %collective-permute-start.15 = (f32[4,16,1024]{2,1,0:T(8,128)S(1)}, f32[4,16,1024]{2,1,0:T(8,128)S(1)}, u32[]{:S(2)}, u32[]{:S(2)}) collective-permute-start(f32[4,16,1024]{2,1,0:T(8,128)S(1)} %pad_maximum_fusion), channel_id=1, source_target_pairs={{0,1},{1,0},{2,3},{3,2},{4,5},{5,4},{6,7},{7,6},{8,9},{9,8},{10,11... | collective-permute-start | bytes 786440 | tf_op jit(solution)/shard_map/ppermute | solution.py:13
  67.0 1.4 %copy-start = (f32[512,1024]{1,0:T(8,128)}, f32[512,1024]{1,0:T(8,128)S(1)}, u32[]{:S(2)}) copy-start(f32[512,1024]{1,0:T(8,128)S(1)} %get-tuple-element.13) | copy-start | bytes 6291460
  68.6 4.4 %collective-permute-start.17 = (f32[4,2,16,1024]{3,2,1,0:T(8,128)S(1)}, f32[4,2,16,1024]{3,2,1,0:T(8,128)S(1)}, u32[]{:S(2)}, u32[]{:S(2)}) collective-permute-start(f32[4,2,16,1024]{3,2,1,0:T(8,128)S(1)} %slice_bitcast_fusion), channel_id=1, source_target_pairs={{0,1},{1,0},{2,3},{3,2},{4,5},{5,4},{6,7},{7,6},{8,9},{9,8},{10,11... | collective-permute-start | bytes 1572872 | tf_op jit(solution)/shard_map/ppermute | solution.py:13
  72.5 6.4 %collective-permute-start.16 = (f32[128,1024]{1,0:T(8,128)}, f32[128,1024]{1,0:T(8,128)}, u32[]{:S(2)}, u32[]{:S(2)}) collective-permute-start(f32[128,1024]{1,0:T(8,128)} %fusion.14), channel_id=1, source_target_pairs={{0,1},{1,0},{2,3},{3,2},{4,5},{5,4},{6,7},{7,6},{8,9},{9,8},{10,11... | collective-permute-start | bytes 1572872 | tf_op jit(solution)/shard_map/ppermute | solution.py:13
  73.8 6.4 %collective-permute-start.18 = (f32[2,16,1024]{2,1,0:T(8,128)}, f32[2,16,1024]{2,1,0:T(8,128)S(1)}, u32[]{:S(2)}, u32[]{:S(2)}) collective-permute-start(f32[2,16,1024]{2,1,0:T(8,128)} %get-tuple-element.19), channel_id=1, source_target_pairs={{0,2},{1,3},{2,0},{3,1},{4,6},{5,7},{6,4},{7,5},{8,10},{9,11},{10,... | collective-permute-start | bytes 393224 | tf_op jit(solution)/shard_map/ppermute | solution.py:13
  75.0 6.4 %collective-permute-start.19 = (f32[2,16,1024]{2,1,0:T(8,128)}, f32[2,16,1024]{2,1,0:T(8,128)S(1)}, u32[]{:S(2)}, u32[]{:S(2)}) collective-permute-start(f32[2,16,1024]{2,1,0:T(8,128)} %get-tuple-element.21), channel_id=1, source_target_pairs={{0,4},{1,5},{2,6},{3,7},{4,0},{5,1},{6,2},{7,3},{8,12},{9,13},{10,... | collective-permute-start | bytes 393224 | tf_op jit(solution)/shard_map/ppermute | solution.py:13
  76.3 7.4 %collective-permute-start.20 = (f32[2,16,1024]{2,1,0:T(8,128)}, f32[2,16,1024]{2,1,0:T(8,128)S(1)}, u32[]{:S(2)}, u32[]{:S(2)}) collective-permute-start(f32[2,16,1024]{2,1,0:T(8,128)} %get-tuple-element.20), channel_id=1, source_target_pairs={{0,6},{1,7},{2,4},{3,5},{4,2},{5,3},{6,0},{7,1},{8,14},{9,15},{10,... | collective-permute-start | bytes 393224 | tf_op jit(solution)/shard_map/ppermute | solution.py:13
  83.8 8.5 %collective-permute-start.21 = (f32[2,16,1024]{2,1,0:T(8,128)S(1)}, f32[2,16,1024]{2,1,0:T(8,128)S(1)}, u32[]{:S(2)}, u32[]{:S(2)}) collective-permute-start(f32[2,16,1024]{2,1,0:T(8,128)S(1)} %fusion.61), channel_id=1, source_target_pairs={{0,8},{1,9},{2,10},{3,11},{4,12},{5,13},{6,14},{7,15},{8,0},{9,1},... | collective-permute-start | bytes 393224 | tf_op jit(solution)/shard_map/ppermute | solution.py:13
  92.4 10.1 %copy-start.9 = (f32[512]{0:T(512)S(1)}, f32[512]{0:T(512)}, u32[]{:S(2)}) copy-start(f32[512]{0:T(512)} %copy-done.8) | copy-start | bytes 6148
  92.4 6.0 %collective-permute-start.22 = (f32[16,1024]{1,0:T(8,128)S(1)}, f32[16,1024]{1,0:T(8,128)S(1)}, u32[]{:S(2)}, u32[]{:S(2)}) collective-permute-start(f32[16,1024]{1,0:T(8,128)S(1)} %get-tuple-element.6), channel_id=1, source_target_pairs={{0,2},{1,3},{2,0},{3,1},{4,6},{5,7},{6,4},{7,5},{8,10},{9,11},{10,... | collective-permute-start | bytes 196616 | tf_op jit(solution)/shard_map/ppermute | solution.py:13
  93.9 4.6 %collective-permute-start.23 = (f32[16,1024]{1,0:T(8,128)S(1)}, f32[16,1024]{1,0:T(8,128)S(1)}, u32[]{:S(2)}, u32[]{:S(2)}) collective-permute-start(f32[16,1024]{1,0:T(8,128)S(1)} %get-tuple-element.6), channel_id=1, source_target_pairs={{0,4},{1,5},{2,6},{3,7},{4,0},{5,1},{6,2},{7,3},{8,12},{9,13},{10,... | collective-permute-start | bytes 196616 | tf_op jit(solution)/shard_map/ppermute | solution.py:13
  93.9 5.2 %collective-permute-start.24 = (f32[16,1024]{1,0:T(8,128)S(1)}, f32[16,1024]{1,0:T(8,128)S(1)}, u32[]{:S(2)}, u32[]{:S(2)}) collective-permute-start(f32[16,1024]{1,0:T(8,128)S(1)} %get-tuple-element.6), channel_id=1, source_target_pairs={{0,6},{1,7},{2,4},{3,5},{4,2},{5,3},{6,0},{7,1},{8,14},{9,15},{10,... | collective-permute-start | bytes 196616 | tf_op jit(solution)/shard_map/ppermute | solution.py:13
  99.1 1.6 %collective-permute-start.25 = (f32[4,16,1024]{2,1,0:T(8,128)S(1)}, f32[4,16,1024]{2,1,0:T(8,128)S(1)}, u32[]{:S(2)}, u32[]{:S(2)}) collective-permute-start(f32[4,16,1024]{2,1,0:T(8,128)S(1)} %pad_maximum_fusion.1), channel_id=1, source_target_pairs={{0,1},{1,0},{2,3},{3,2},{4,5},{5,4},{6,7},{7,6},{8,9},{9,8},{10,11... | collective-permute-start | bytes 786440 | tf_op jit(solution)/shard_map/ppermute | solution.py:13

commit v2 on v0

v2 whole, which is shorter than its diff:
```python
import functools

import jax
import jax.numpy as jnp
from jax import lax
from jax.experimental import pallas as pl
from jax.experimental.pallas import tpu as pltpu
from jax.sharding import PartitionSpec as P

F32, BF16 = jnp.float32, jnp.bfloat16
SQUARE = (2, 4, 6)
VMEM = pl.BlockSpec(memory_space=pltpu.VMEM)
SMEM = pl.BlockSpec(memory_space=pltpu.SMEM)
ANY = pl.BlockSpec(memory_space=pl.ANY)
ROW = (((1,), (1,)), ((), ()))


def swap(x, offset):
    n = lax.axis_size("pol")
    return lax.ppermute(x, "pol", [(i, i ^ offset) for i in range(n)])


def far_offsets():
    n = lax.axis_size("pol")
    return [1 << b for b in range(3, n.bit_length() - 1)]


def rate(ratio):
    x = 20.0 * (ratio - 1.05)
    return 0.01 + (jnp.maximum(x, 0.0) + jnp.log1p(jnp.exp(-jnp.abs(x)))) / 20.0


def halves(v):
    hi = v.astype(BF16)
    return hi, (v - hi.astype(F32)).astype(BF16)


def dot(a, b, dims=(((1,), (0,)), ((), ()))):
    return lax.dot_general(a, b, dims, preferred_element_type=F32)


def call(body, out, ins, name, flops=0, moved=0, scratch=(), out_specs=None, limit=24):
    return pl.pallas_call(
        body,
        out_shape=out,
        in_specs=ins,
        out_specs=out_specs if out_specs is not None else jax.tree.map(lambda _: VMEM, out),
        scratch_shapes=scratch,
        compiler_params=pltpu.CompilerParams(vmem_limit_bytes=limit << 20),
        cost_estimate=pl.CostEstimate(flops=flops, bytes_accessed=moved, transcendentals=0),
        name=name,
    )


def shaped(*dims, dtype=F32):
    return jax.ShapeDtypeStruct(dims, dtype)


def pack_body(load, hold, drift, fund, term, asset, liab, out):
    secs, funds = load.shape
    count = fund.shape[1]
    out[0:secs, :] = load[...]
    out[secs : 2 * secs, :] = hold[...]
    member = (lax.broadcasted_iota(jnp.int32, (funds, count), 0) == fund[...]).astype(BF16)
    at = lax.broadcasted_iota(jnp.int32, (8, count), 0)
    alive = (term[...] > 0).astype(F32)
    v = jnp.where(at < 3, asset[...] * alive, liab[...])
    one, rest = v.astype(BF16).astype(F32), v - v.astype(BF16).astype(F32)
    two = rest.astype(BF16).astype(F32)
    three = rest - two
    kind = jnp.where(at < 3, at, at - 3)
    rows = jnp.where(kind == 0, one, jnp.where(kind == 1, two, three))
    rows = jnp.where(at < 6, rows, 0.0).astype(BF16)
    out[2 * secs : 2 * secs + 8, :] = dot(rows, member, ROW)
    out[2 * secs + 6 : 2 * secs + 7, 0:secs] = drift[...]


def columns_body(base, guar, fund, kind, term, asset, liab, *outs):
    years = (len(outs) - 2) // 4
    member_t, member, base_w, guar_w = (outs[i * years : (i + 1) * years] for i in range(4))
    asset_w, liab_w = outs[-2:]
    funds, count = member_t[0].shape
    types = base.shape[0]
    base_row = jnp.zeros((1, count), F32)
    guar_row = jnp.zeros((1, count), F32)
    for t in range(types):
        base_row = jnp.where(kind[...] == t, base[t], base_row)
        guar_row = jnp.where(kind[...] == t, guar[t], guar_row)
    at = lax.broadcasted_iota(jnp.int32, (128, count), 0)
    rows = (fund[...].astype(F32), term[...].astype(F32), base_row, guar_row, asset[...], liab[...])
    stack = jnp.zeros((128, count), F32)
    for r, row in enumerate(rows):
        stack = jnp.where(at == r, row, stack)
    cols = jnp.transpose(stack)
    wide = lambda r: jnp.broadcast_to(cols[:, r : r + 1], (count, 128))
    fund_c, term_c, base_c, guar_c = wide(0), wide(1), wide(2), wide(3)
    asset_w[...] = wide(4)
    liab_w[...] = wide(5)
    hot_t = lax.broadcasted_iota(jnp.int32, (funds, count), 0) == fund[...]
    hot = lax.broadcasted_iota(jnp.int32, (count, funds), 1).astype(F32) == fund_c
    for y in range(years):
        alive = term_c > float(y)
        base_w[y][...] = jnp.where(alive, base_c, 0.0)
        guar_w[y][...] = jnp.where(alive, guar_c, 0.0)
        here = jnp.logical_and(hot, alive).astype(F32).astype(BF16)
        member[y][:, 0:funds] = here
        member[y][:, funds : 2 * funds] = here
        if y == 0:
            member_t[y][...] = hot_t.astype(F32).astype(BF16)
        else:
            member_t[y][...] = jnp.logical_and(hot_t, term[...] > y).astype(F32).astype(BF16)


def returns_body(year, first, secs, *refs):
    blocks, (shocks, part, sums), (load_hi, load_lo, hold_hi, hold_lo) = refs[:4], refs[4:7], refs[7:]
    funds, width = part.shape
    total = load_hi.shape[0]
    at = 0
    extra = jnp.zeros((8, funds), F32)
    fixed = jnp.zeros((8, funds), F32)
    for block in blocks:
        for b in range(block.shape[0]):
            load_hi[at : at + secs, :], load_lo[at : at + secs, :] = halves(block[b, 0:secs, :])
            hold = block[b, secs : 2 * secs, :]
            hold_hi[at : at + secs, :], hold_lo[at : at + secs, :] = halves(hold)
            tail = block[b, 2 * secs : 2 * secs + 8, :]
            extra = extra + tail
            fixed = fixed + jnp.dot(tail[:, 0:secs], hold, precision=lax.Precision.HIGHEST)
            at += secs
    sums[...] = extra
    row = lax.broadcasted_iota(jnp.int32, (128, funds), 0)
    fixed_col = jnp.transpose(jnp.where(row == 0, fixed[6:7, :], 0.0))[:, 0:1]
    step = min(256, width)
    group = min(512, total)
    for c in range(0, width, step):
        x_hi, x_lo = halves(shocks[year, :, first + c : first + c + step])
        acc = jnp.zeros((funds, step), F32)
        for g in range(0, total, group):
            lh, ll = load_hi[g : g + group, :], load_lo[g : g + group, :]
            z = dot(jnp.concatenate([lh, lh], 1), jnp.concatenate([x_hi, x_lo], 0)) + dot(ll, x_hi)
            t_hi, t_lo = halves(jnp.tanh(z))
            hh, hl = hold_hi[g : g + group, :], hold_lo[g : g + group, :]
            over = (((0,), (0,)), ((), ()))
            acc = acc + dot(hh, t_hi, over) + dot(hh, t_lo, over) + dot(hl, t_hi, over)
        part[:, c : c + step] = 0.25 * acc + fixed_col


def own_columns(me_ref, declared, first, out):
    paths, funds = out.shape
    width = declared.shape[1]
    spot = lax.broadcasted_iota(jnp.int32, (paths, width), 1) + first
    pick = spot == lax.broadcasted_iota(jnp.int32, (paths, width), 0) + me_ref[0] * paths
    pick = pick.astype(F32).astype(BF16)
    one, rest = declared.astype(BF16), declared - declared.astype(BF16).astype(F32)
    two, three = halves(rest)
    out[...] = dot(pick, one, ROW) + dot(pick, two, ROW) + dot(pick, three, ROW)


def slice_spot(me_ref, order, slice_funds):
    label = (order >> 2) | ((order & 3) << 1)
    return pl.multiple_of(((me_ref[0] & 7) ^ label) * slice_funds, slice_funds)


def advance(cols, c, step, table, member, base, guar, draw, asset, liab):
    wide = lambda v: jnp.concatenate([v] * (step // 128), 1)
    got = dot(member, table)
    growth, credit = got[:, 0:step], jnp.maximum(got[:, step:], wide(guar))
    lapse = jnp.minimum(wide(base) * (0.5 + draw.astype(F32)) * jnp.exp(5.0 * (growth - credit)), 0.5)
    stay = 1.0 - lapse
    return asset * (1.0 + growth) * stay, liab * (1.0 + credit) * stay


def table_of(growth, declared):
    g_hi, g_lo = halves(growth)
    d_hi, d_lo = halves(declared)
    return jnp.concatenate([jnp.concatenate([g_hi, d_hi], 1), jnp.concatenate([g_lo, d_lo], 1)], 0)


STEP, ROWS = 256, 256


def year_body(year, first, last, slice_funds, *refs):
    refs = list(refs)
    me = refs.pop(0)
    if year == 0:
        mine, other = refs.pop(0), refs.pop(0)
    else:
        near, far = refs.pop(0), refs.pop(0)
    part, peer = refs.pop(0), refs.pop(0)
    draws, member, base, guar = (refs.pop(0) for _ in range(4))
    states = [(refs.pop(0), refs.pop(0)) for _ in range(2 if last else 1)]
    if last:
        earlier = [refs.pop(0) for _ in range(2 * year)]
        out_a, out_l, out_r, declared, buf_a, buf_l, sem = refs
    else:
        member_t, member_ta = refs.pop(0), refs.pop(0)
        out_a, out_l, out_s, out_r, declared, acc = refs
    funds, width = declared.shape
    count = member.shape[0]
    if year == 0:
        sums = mine[...] + other[...]
        row = lax.broadcasted_iota(jnp.int32, (128, funds), 0)
        start_a = sums[0:1, :] + sums[1:2, :] + sums[2:3, :]
        start_l = sums[3:4, :] + sums[4:5, :] + sums[5:6, :]
        both = jnp.where(row == 0, start_a, jnp.where(row == 1, start_l, 0.0))
        both = jnp.transpose(both)
        ratio = both[:, 0:1] / both[:, 1:2]
        declared[...] = rate(ratio * (1.0 + (part[...] + peer[...])))
    else:
        for o in range(8):
            source = near if o < 4 else far
            declared[pl.ds(slice_spot(me, o, slice_funds), slice_funds), :] = source[
                o & 3, :, first : first + width
            ]
    if last:
        own = out_r.at[year]
        for y in range(year):
            out_r[y] = earlier[2 * y][...] + earlier[2 * y + 1][...]
    else:
        own = out_r
    copies = []
    for c in range(0, width, STEP):
        cut = slice(c, c + STEP)
        table = table_of(part[:, cut] + peer[:, cut], declared[:, cut])
        sum_a = sum_l = None
        for r in range(0, count, ROWS):
            rows = slice(r, r + ROWS)
            if year == 0:
                asset = jnp.concatenate([states[0][0][rows, :]] * (STEP // 128), 1)
                liab = jnp.concatenate([states[0][1][rows, :]] * (STEP // 128), 1)
            else:
                half = states[0][0].shape[1]
                held = states[c // half]
                at = slice(c % half, c % half + STEP)
                asset, liab = held[0][rows, at], held[1][rows, at]
            asset, liab = advance(
                None, c, STEP, table, member[rows, :], base[rows, :], guar[rows, :],
                draws[year, rows, first + c : first + c + STEP], asset, liab,
            )
            if last:
                buf_a[c // STEP, rows, :] = asset
                buf_l[c // STEP, rows, :] = liab
            else:
                out_a[rows, cut] = asset
                out_l[rows, cut] = liab
                a_hi, a_lo = halves(asset)
                l_hi, l_lo = halves(liab)
                ma, ml = member_ta[:, rows], member_t[:, rows]
                add_a = dot(ma, a_hi) + dot(ma, a_lo)
                add_l = dot(ml, l_hi) + dot(ml, l_lo)
                sum_a = add_a if sum_a is None else sum_a + add_a
                sum_l = add_l if sum_l is None else sum_l + add_l
        if last:
            for buf, out, k in ((buf_a, out_a, 0), (buf_l, out_l, 1)):
                copy = pltpu.make_async_copy(buf.at[c // STEP], out.at[:, cut], sem.at[k, c // STEP])
                copy.start()
                copies.append(copy)
        else:
            acc[0, :, cut] = sum_a
            acc[1, :, cut] = sum_l
    own_columns(me, declared[...], first, own)
    if last:
        for copy in copies:
            copy.wait()
    else:
        for o in range(8):
            for v in range(2):
                out_s[o // 4, o % 4, v] = acc[v, pl.ds(slice_spot(me, o, slice_funds), slice_funds), :]


def local(
    shocks,
    loadings,
    sec_drift,
    holdings,
    fund_of,
    product_type,
    term_years,
    asset_start,
    liab_start,
    base_lapse,
    guarantee,
    lapse_draw,
):
    years, _, paths = shocks.shape
    secs, funds = holdings.shape
    count = asset_start.shape[0]
    n = lax.axis_size("pol")
    me = lax.axis_index("pol")
    me_ref = me.astype(jnp.int32).reshape(1)
    slice_funds = funds // 8
    owned = paths // n
    half = paths // 2
    draws = lapse_draw.transpose(1, 0, 2)
    line = lambda v: v.reshape(1, count)
    fund, kind, term = line(fund_of), line(product_type), line(term_years)
    asset, liab = line(asset_start), line(liab_start)

    block = call(pack_body, shaped(2 * secs + 8, funds), [VMEM] * 7, "pack", 10**6, 10**5)(
        loadings, holdings, sec_drift.reshape(1, secs), fund, term, asset, liab
    )
    fund, kind, term, asset, liab, block = lax.optimization_barrier(
        (fund, kind, term, asset, liab, block)
    )
    block = block[None]
    for o in reversed(far_offsets()):
        block = jnp.concatenate([block, swap(block, o)])
    blocks = [block] + [swap(block, o) for o in SQUARE]

    wide = shaped(count, 128)
    made = call(
        columns_body,
        [shaped(funds, count, dtype=BF16)] * years
        + [shaped(count, 2 * funds, dtype=BF16)] * years
        + [wide] * (2 * years + 2),
        [SMEM] * 2 + [VMEM] * 5,
        "columns",
        10**6,
        4 * 10**6,
    )(base_lapse, guarantee, fund, kind, term, asset, liab)
    member_t, member, base_w, guar_w = (made[i * years : (i + 1) * years] for i in range(4))
    asset_w, liab_w = made[-2:]

    total = secs * n // 2

    def returns(year, first, width):
        part, sums = call(
            functools.partial(returns_body, year, first, secs),
            [shaped(funds, width), shaped(8, funds)],
            [VMEM] * 5,
            "returns",
            flops=2 * 6 * total * funds * width,
            moved=4 * funds * width,
            scratch=[pltpu.VMEM((total, funds), BF16)] * 4,
            limit=32,
        )(*blocks, shocks)
        return part, sums

    parts = [[returns(0, h * half, half) for h in range(2)]]
    sums = parts[0][0][1]
    parts[0] = [p for p, _ in parts[0]]
    parts += [[returns(y, 0, paths)[0]] for y in range(1, years)]
    peers = [[swap(p, 1) for p in ps] for ps in parts]
    other_sums = swap(sums, 1)

    state = [(asset_w, liab_w)] * 2
    rates = []
    for year in range(years):
        last = year + 1 == years
        if year == 0:
            head = [sums, other_sums]
        else:
            near = jnp.stack([own] + [swap(own, o) for o in SQUARE])
            head = [near, swap(near, 1)]
        shares = []
        for h in range(1 if last else 2):
            width = paths if last else half
            first = h * half
            if year == 0:
                pair = [parts[0][h], peers[0][h]]
            else:
                pair = [parts[year][0][:, first : first + width], peers[year][0][:, first : first + width]]
            ins = [me_ref] + head + pair + [draws, member[year], base_w[year], guar_w[year]]
            cost = dict(flops=2 * 2 * count * 2 * funds * width, moved=20 * count * width)
            if last:
                ins += [v for s in state for v in s] + [v for rs in rates for v in rs]
                out = [shaped(count, paths), shaped(count, paths), shaped(years, owned, funds)]
                out_specs = [ANY, ANY, VMEM]
                tiles = paths // STEP
                scratch = [pltpu.VMEM((funds, width), F32)]
                scratch += [pltpu.VMEM((tiles, count, STEP), F32)] * 2
                scratch += [pltpu.SemaphoreType.DMA((2, tiles))]
            else:
                ins += list(state[h]) + [member_t[0], member_t[year + 1]]
                out = [shaped(count, width)] * 2
                out += [shaped(2, 4, 2, slice_funds, width), shaped(owned, funds)]
                out_specs = None
                scratch = [pltpu.VMEM((funds, width), F32), pltpu.VMEM((2, funds, width), F32)]
            shares.append(
                call(
                    functools.partial(year_body, year, first, last, slice_funds),
                    out,
                    [SMEM] + [VMEM] * (len(ins) - 1),
                    "year",
                    scratch=scratch,
                    out_specs=out_specs,
                    limit=32,
                    **cost,
                )(*ins)
            )
        if last:
            assets, liability, credit = shares[0]
            return assets, liability, credit.transpose(0, 2, 1)
        state = [(s[0], s[1]) for s in shares]
        rates.append([s[3] for s in shares])
        held = jnp.concatenate([s[2][0] + swap(s[2][1], 1) for s in shares], -1)
        arrived = [swap(held[i + 1], o) for i, o in enumerate(SQUARE)]
        totals = held[0] + arrived[0] + arrived[1] + arrived[2]
        for o in far_offsets():
            totals = totals + swap(totals, o)
        here = lax.dynamic_slice_in_dim(
            parts[year + 1][0], (me & 7) * slice_funds, slice_funds, 0
        ) + lax.dynamic_slice_in_dim(
            peers[year + 1][0], (me & 7) * slice_funds, slice_funds, 0
        )
        own = rate(totals[0] * (1.0 + here) / totals[1])


def solution(mesh):
    in_specs = (
        P("grp", None, None),
        P("pol", None),
        P("pol"),
        P("pol", None),
        P("pol", None),
        P("pol"),
        P("pol"),
        P("pol"),
        P("pol"),
        P(),
        P(),
        P("pol", "grp", None),
    )
    out_specs = (P("pol", "grp"), P("pol", "grp"), P("grp", None, "pol"))
    return jax.shard_map(local, mesh=mesh, in_specs=in_specs, out_specs=out_specs, check_vma=False)
```

time: 432 us -> 122 us (0.28)
  waiting for transfers between devices: 367 us -> 40.9 us
  matrix products: 34.8 us -> 0 us
  starting transfers between devices: 0.34 us -> 31.5 us
  Pallas kernels: 0 us -> 24.1 us
  local copies, waits for them, and re-layouts: 6.66 us -> 20.9 us
  between operations: 14.1 us -> 1.32 us
  other arithmetic: 8.72 us -> 3.01 us
    psum x4 -> x0, waiting for transfers between devices: 367 us -> none  [the longest x3 271 us: local(): totals = lax.psum(fund_sums, 'pol')]
    ppermute x0 -> x29, waiting for transfers between devices: none -> 40.9 us  [swap(): return lax.ppermute(x, 'pol', [(i, i ^ offset) for i in range(n)])]
    dot_general x14 -> x0, matrix products: 34.8 us -> none  [the longest x3 15.3 us: local(): jnp.dot(member, declared, precision=highest)]
    ppermute x0 -> x29, starting transfers between devices: none -> 31.5 us  [swap(): return lax.ppermute(x, 'pol', [(i, i ^ offset) for i in range(n)])]
    pallas_call x0 -> x11, Pallas kernels: none -> 24.1 us  [the longest x5 13.8 us: local(): call(functools.partial(year_body, year, first, last, slice_funds), out, [...]
    unnamed x38 -> x104, local copies, waits for them, and re-layouts: 5.43 us -> 18.7 us
  transfers between devices with their start and end apart: 4 -> 29, of which waited for: 4 -> 19; matrix products, arithmetic and copies ran while one was open for 2% -> 3% of each run, Pallas kernels for 0% -> 14%
where the time goes in v2:
time: 122 us
  waiting for transfers between devices  40.9 us (34%)
  starting transfers between devices  31.5 us (26%)
  Pallas kernels  24.1 us (20%)
  local copies, waits for them, and re-layouts  20.9 us (17%)
  other arithmetic  3.01 us (2%)
  between operations  1.32 us (1%)
    ppermute x29, waiting for transfers between devices, swap(): return lax.ppermute(x, 'pol', [(i, i ^ offset) for i in range(n)])  40.9 us
    ppermute x29, starting transfers between devices, swap(): return lax.ppermute(x, 'pol', [(i, i ^ offset) for i in range(n)])  31.5 us
    unnamed x104, local copies, waits for them, and re-layouts  18.7 us
    pallas_call x5, Pallas kernels, local(): call(functools.partial(year_body, year, first, last, slice_funds), out, [...  13.8 us
    pallas_call x4, Pallas kernels, returns(): call(functools.partial(returns_body, year, first, secs), [shaped(funds, w...  8.84 us
  transfers between devices with their start and end apart: 29, of which 19 were waited for; matrix products, arithmetic and copies ran while one was open for 3% of the time, Pallas kernels for 14%

profile of v2, /device:TPU:0, one launch (start us, length us, event | category | flops | bytes accessed | tf_op | source)
XLA Modules:
  0.0 121.6 jit_solution(13407549378050797112)
XLA Ops:
  0.6 0.7 copy-done.38
  1.4 0.8 copy-done.39
  2.8 0.7 copy-done.42
  3.5 0.7 copy-done.44
  4.2 0.7 copy-done.46
  5.7 4.0 %collective-permute-start = (f32[1,136,128]{2,1,0:T(8,128)S(1)}, f32[1,136,128]{2,1,0:T(8,128)S(1)}, u32[]{:S(2)}, u32[]{:S(2)}) collective-permute-start(f32[1,136,128]{2,1,0:T(8,128)S(1)} %bitcast.103), channel_id=1, source_target_pairs={{0,8},{1,9},{2,10},{3,11},{4,12},{5,13},{6,14},{7,15},{8,0},{9,1},... | collective-permute-start | bytes 208904 | tf_op jit(solution)/shard_map/ppermute | solution.py:20
  9.7 3.8 %collective-permute-done = f32[1,136,128]{2,1,0:T(8,128)S(1)} collective-permute-done((f32[1,136,128]{2,1,0:T(8,128)S(1)}, f32[1,136,128]{2,1,0:T(8,128)S(1)}, u32[]{:S(2)}, u32[]{:S(2)}) %collective-permute-start) | collective-permute-done | bytes 69664 | tf_op jit(solution)/shard_map/ppermute | solution.py:20
  13.5 1.8 %collective-permute-start.1 = (f32[2,136,128]{2,1,0:T(8,128)S(1)}, f32[2,136,128]{2,1,0:T(8,128)S(1)}, u32[]{:S(2)}, u32[]{:S(2)}) collective-permute-start(f32[2,136,128]{2,1,0:T(8,128)S(1)} %pad_maximum_fusion.2.refs_0_), channel_id=1, source_target_pairs={{0,2},{1,3},{2,0},{3,1},{4,6},{5,7},{6,4},{7,5},{8,10},{9,11},{10,... | collective-permute-start | bytes 417800 | tf_op jit(solution)/shard_map/ppermute | solution.py:20
  15.7 1.4 %collective-permute-start.3 = (f32[2,136,128]{2,1,0:T(8,128)S(1)}, f32[2,136,128]{2,1,0:T(8,128)S(1)}, u32[]{:S(2)}, u32[]{:S(2)}) collective-permute-start(f32[2,136,128]{2,1,0:T(8,128)S(1)} %pad_maximum_fusion.2.refs_0_), channel_id=1, source_target_pairs={{0,6},{1,7},{2,4},{3,5},{4,2},{5,3},{6,0},{7,1},{8,14},{9,15},{10,... | collective-permute-start | bytes 417800 | tf_op jit(solution)/shard_map/ppermute | solution.py:20
  17.1 2.3 %collective-permute-done.1.refs_1_ = f32[2,136,128]{2,1,0:T(8,128)S(1)} collective-permute-done((f32[2,136,128]{2,1,0:T(8,128)S(1)}, f32[2,136,128]{2,1,0:T(8,128)S(1)}, u32[]{:S(2)}, u32[]{:S(2)}) %collective-permute-start.1) | collective-permute-done | bytes 139296 | tf_op jit(solution)/shard_map/ppermute | solution.py:20
  19.4 0.9 collective-permute-done.2.refs_2_
  20.4 2.3 %collective-permute-done.3.refs_3_ = f32[2,136,128]{2,1,0:T(8,128)S(1)} collective-permute-done((f32[2,136,128]{2,1,0:T(8,128)S(1)}, f32[2,136,128]{2,1,0:T(8,128)S(1)}, u32[]{:S(2)}, u32[]{:S(2)}) %collective-permute-start.3) | collective-permute-done | bytes 139296 | tf_op jit(solution)/shard_map/ppermute | solution.py:20
  22.7 1.4 %copy-done.1 = f32[3,128,1024]{2,1,0:T(8,128)S(1)} copy-done((f32[3,128,1024]{2,1,0:T(8,128)S(1)}, f32[3,128,1024]{2,1,0:T(8,128)}, u32[]{:S(2)}) %copy-start.1) | copy-done | bytes 1572888
  24.1 1.9 %returns.5 = (f32[128,512]{1,0:T(8,128)}, f32[8,128]{1,0:T(8,128)}) custom-call(f32[2,136,128]{2,1,0:T(8,128)S(1)} %pad_maximum_fusion.2.refs_0_, f32[2,136,128]{2,1,0:T(8,128)S(1)} %collective-permute-done.1.refs_1_, f32[2,136,128]{2,1,0:T(8,128)S(1)} %collective-permute-done.2.refs_2_, f32[2,136,128]{2,1,0:T(8,128)S(1)} %collective-permute-done.3.refs_3_, ...), custom_call_target="tpu_custom_call" | custom-call | flops 402653184 | bytes 262144 | tf_op jit(solution)/shard_map/returns/pallas_call | solution.py:327
  26.0 1.6 %returns.4 = (f32[128,512]{1,0:T(8,128)S(1)}, f32[8,128]{1,0:T(8,128)}) custom-call(f32[2,136,128]{2,1,0:T(8,128)S(1)} %pad_maximum_fusion.2.refs_0_, f32[2,136,128]{2,1,0:T(8,128)S(1)} %collective-permute-done.1.refs_1_, f32[2,136,128]{2,1,0:T(8,128)S(1)} %collective-permute-done.2.refs_2_, f32[2,136,128]{2,1,0:T(8,128)S(1)} %collective-permute-done.3.refs_3_, ...), custom_call_target="tpu_custom_call" | custom-call | flops 402653184 | bytes 262144 | tf_op jit(solution)/shard_map/returns/pallas_call | solution.py:327
  27.6 0.7 copy-done.32
  28.8 0.7 copy-done.41
  30.2 0.7 copy-done.45
  33.5 1.3 %columns.1 = (bf16[128,512]{1,0:T(8,128)(2,1)S(1)}, bf16[128,512]{1,0:T(8,128)(2,1)S(1)}, bf16[128,512]{1,0:T(8,128)(2,1)S(1)}, bf16[512,256]{1,0:T(8,128)(2,1)S...) custom-call(f32[8]{0:T(128)S(1)} %copy-done.50, ...), custom_call_target="tpu_custom_call" | custom-call | flops 1000000 | bytes 4000000 | tf_op jit(solution)/shard_map/columns/pallas_call | solution.py:311
  34.8 0.7 copy-done.12
  35.6 0.7 copy-done.14
  36.3 0.7 copy-done.16
  37.0 0.7 copy-done.26
  37.7 0.7 copy-done.28
  38.4 0.7 copy-done.30
  39.2 3.3 %year.6 = (f32[512,512]{1,0:T(8,128)S(1)}, f32[512,512]{1,0:T(8,128)S(1)}, f32[2,4,2,16,512]{4,3,2,1,0:T(8,128)S(1)}, f32[64,128]{1,0:T(8,128)S(1)}) custom-call(s32[1]{0:T(128)} %bitcast.refs_0_, f32[8,128]{1,0:T(8,128)} %get-tuple-element.48.refs_1_, f32[8,128]{1,0:T(8,128)} %collective-permute-done.4.refs_2_, f32[128,512]{1,0:T(8,128)} %get-tuple-element.63.refs_3_, ...), custom_call_target="tpu_custom_call" | custom-call | flops 268435456 | bytes 5242880 | tf_op jit(solution)/shard_map/year/pallas_call | solution.py:380
  42.5 1.0 copy-done.8
  43.5 1.0 copy-done.10
  45.7 2.9 %year.5 = (f32[512,512]{1,0:T(8,128)S(1)}, f32[512,512]{1,0:T(8,128)S(1)}, f32[2,4,2,16,512]{4,3,2,1,0:T(8,128)S(1)}, f32[64,128]{1,0:T(8,128)S(1)}) custom-call(s32[1]{0:T(128)} %bitcast.refs_0_, f32[8,128]{1,0:T(8,128)} %get-tuple-element.48.refs_1_, f32[8,128]{1,0:T(8,128)} %collective-permute-done.4.refs_2_, f32[128,512]{1,0:T(8,128)S(1)} %copy-done.33, ...), custom_call_target="tpu_custom_call" | custom-call | flops 268435456 | bytes 5242880 | tf_op jit(solution)/shard_map/year/pallas_call | solution.py:380
  48.9 2.9 %returns.6 = (f32[128,1024]{1,0:T(8,128)}, f32[8,128]{1,0:T(8,128)}) custom-call(f32[2,136,128]{2,1,0:T(8,128)S(1)} %pad_maximum_fusion.2.refs_0_, f32[2,136,128]{2,1,0:T(8,128)S(1)} %collective-permute-done.1.refs_1_, f32[2,136,128]{2,1,0:T(8,128)S(1)} %copy-done.19, f32[2,136,128]{2,1,0:T(8,128)S(1)} %copy-done.22, f32[3,128,1024]{2,1,0:T(8,128)S(1)} %copy-done.2), custom_call_target="tpu_custom_call" | custom-call | flops 805306368 | bytes 524288 | tf_op jit(solution)/shard_map/returns/pallas_call | solution.py:327
  52.2 0.9 collective-permute-start.10
  53.2 1.2 %collective-permute-start.11 = (f32[2,16,1024]{2,1,0:T(8,128)S(1)}, f32[2,16,1024]{2,1,0:T(8,128)S(1)}, u32[]{:S(2)}, u32[]{:S(2)}) collective-permute-start(f32[2,16,1024]{2,1,0:T(8,128)S(1)} %get-tuple-element.99), channel_id=1, source_target_pairs={{0,6},{1,7},{2,4},{3,5},{4,2},{5,3},{6,0},{7,1},{8,14},{9,15},{10,... | collective-permute-start | bytes 393224 | tf_op jit(solution)/shard_map/ppermute | solution.py:20
  54.4 1.4 %collective-permute-start.9 = (f32[2,16,1024]{2,1,0:T(8,128)S(1)}, f32[2,16,1024]{2,1,0:T(8,128)S(1)}, u32[]{:S(2)}, u32[]{:S(2)}) collective-permute-start(f32[2,16,1024]{2,1,0:T(8,128)S(1)} %get-tuple-element.98), channel_id=1, source_target_pairs={{0,2},{1,3},{2,0},{3,1},{4,6},{5,7},{6,4},{7,5},{8,10},{9,11},{10,... | collective-permute-start | bytes 393224 | tf_op jit(solution)/shard_map/ppermute | solution.py:20
  55.8 2.9 %collective-permute-done.10 = f32[2,16,1024]{2,1,0:T(8,128)S(1)} collective-permute-done((f32[2,16,1024]{2,1,0:T(8,128)S(1)}, f32[2,16,1024]{2,1,0:T(8,128)S(1)}, u32[]{:S(2)}, u32[]{:S(2)}) %collective-permute-start.10) | collective-permute-done | bytes 131104 | tf_op jit(solution)/shard_map/ppermute | solution.py:20
  58.6 2.2 %collective-permute-done.11 = f32[2,16,1024]{2,1,0:T(8,128)S(1)} collective-permute-done((f32[2,16,1024]{2,1,0:T(8,128)S(1)}, f32[2,16,1024]{2,1,0:T(8,128)S(1)}, u32[]{:S(2)}, u32[]{:S(2)}) %collective-permute-start.11) | collective-permute-done | bytes 131104 | tf_op jit(solution)/shard_map/ppermute | solution.py:20
  60.8 1.4 %collective-permute-done.9 = f32[2,16,1024]{2,1,0:T(8,128)S(1)} collective-permute-done((f32[2,16,1024]{2,1,0:T(8,128)S(1)}, f32[2,16,1024]{2,1,0:T(8,128)S(1)}, u32[]{:S(2)}, u32[]{:S(2)}) %collective-permute-start.9) | collective-permute-done | bytes 131104 | tf_op jit(solution)/shard_map/ppermute | solution.py:20
  62.2 0.7 fusion.15
  62.9 3.5 %collective-permute-start.12 = (f32[2,16,1024]{2,1,0:T(8,128)}, f32[2,16,1024]{2,1,0:T(8,128)}, u32[]{:S(2)}, u32[]{:S(2)}) collective-permute-start(f32[2,16,1024]{2,1,0:T(8,128)} %fusion.15), channel_id=1, source_target_pairs={{0,8},{1,9},{2,10},{3,11},{4,12},{5,13},{6,14},{7,15},{8,0},{9,1},... | collective-permute-start | bytes 393224 | tf_op jit(solution)/shard_map/ppermute | solution.py:20
  66.5 5.9 %collective-permute-done.12 = f32[2,16,1024]{2,1,0:T(8,128)} collective-permute-done((f32[2,16,1024]{2,1,0:T(8,128)}, f32[2,16,1024]{2,1,0:T(8,128)}, u32[]{:S(2)}, u32[]{:S(2)}) %collective-permute-start.12) | collective-permute-done | bytes 131104 | tf_op jit(solution)/shard_map/ppermute | solution.py:20
  72.4 1.0 add.73
  73.4 0.9 multiply_add_fusion.1
  75.5 2.4 %collective-permute-start.16 = (f32[16,1024]{1,0:T(8,128)S(1)}, f32[16,1024]{1,0:T(8,128)S(1)}, u32[]{:S(2)}, u32[]{:S(2)}) collective-permute-start(f32[16,1024]{1,0:T(8,128)S(1)} %multiply_add_fusion.1), channel_id=1, source_target_pairs={{0,6},{1,7},{2,4},{3,5},{4,2},{5,3},{6,0},{7,1},{8,14},{9,15},{10,... | collective-permute-start | bytes 196616 | tf_op jit(solution)/shard_map/ppermute | solution.py:20
  77.9 1.5 %collective-permute-done.14 = f32[16,1024]{1,0:T(8,128)S(1)} collective-permute-done((f32[16,1024]{1,0:T(8,128)S(1)}, f32[16,1024]{1,0:T(8,128)S(1)}, u32[]{:S(2)}, u32[]{:S(2)}) %collective-permute-start.14) | collective-permute-done | bytes 65568 | tf_op jit(solution)/shard_map/ppermute | solution.py:20
  79.7 1.1 collective-permute-done.16
  81.0 1.1 fusion.29
  82.0 1.1 fusion.28
  83.2 2.0 %year.8 = (f32[512,512]{1,0:T(8,128)S(1)}, f32[512,512]{1,0:T(8,128)S(1)}, f32[2,4,2,16,512]{4,3,2,1,0:T(8,128)S(1)}, f32[64,128]{1,0:T(8,128)S(1)}) custom-call(s32[1]{0:T(128)} %bitcast.refs_0_, f32[4,16,1024]{2,1,0:T(8,128)S(1)} %pad_maximum_fusion.refs_1_, f32[4,16,1024]{2,1,0:T(8,128)S(1)} %collective-permute-done.17.refs_2_, ...), custom_call_target="tpu_custom_call" | custom-call | flops 268435456 | bytes 5242880 | tf_op jit(solution)/shard_map/year/pallas_call | solution.py:380
  85.8 2.1 %year.7 = (f32[512,512]{1,0:T(8,128)S(1)}, f32[512,512]{1,0:T(8,128)S(1)}, f32[2,4,2,16,512]{4,3,2,1,0:T(8,128)S(1)}, f32[64,128]{1,0:T(8,128)S(1)}) custom-call(s32[1]{0:T(128)} %bitcast.refs_0_, f32[4,16,1024]{2,1,0:T(8,128)S(1)} %pad_maximum_fusion.refs_1_, f32[4,16,1024]{2,1,0:T(8,128)S(1)} %collective-permute-done.17.refs_2_, ...), custom_call_target="tpu_custom_call" | custom-call | flops 268435456 | bytes 5242880 | tf_op jit(solution)/shard_map/year/pallas_call | solution.py:380
  88.1 2.5 %returns.7 = (f32[128,1024]{1,0:T(8,128)S(1)}, f32[8,128]{1,0:T(8,128)}) custom-call(f32[2,136,128]{2,1,0:T(8,128)S(1)} %pad_maximum_fusion.2.refs_0_, f32[2,136,128]{2,1,0:T(8,128)S(1)} %collective-permute-done.1.refs_1_, f32[2,136,128]{2,1,0:T(8,128)S(1)} %copy-done.20, f32[2,136,128]{2,1,0:T(8,128)S(1)} %copy-done.23, f32[3,128,1024]{2,1,0:T(8,128)S(1)} %copy-done.3), custom_call_target="tpu_custom_call" | custom-call | flops 805306368 | bytes 524288 | tf_op jit(solution)/shard_map/returns/pallas_call | solution.py:327
  91.2 1.6 %collective-permute-start.20 = (f32[2,16,1024]{2,1,0:T(8,128)S(1)}, f32[2,16,1024]{2,1,0:T(8,128)S(1)}, u32[]{:S(2)}, u32[]{:S(2)}) collective-permute-start(f32[2,16,1024]{2,1,0:T(8,128)S(1)} %get-tuple-element.91), channel_id=1, source_target_pairs={{0,2},{1,3},{2,0},{3,1},{4,6},{5,7},{6,4},{7,5},{8,10},{9,11},{10,... | collective-permute-start | bytes 393224 | tf_op jit(solution)/shard_map/ppermute | solution.py:20
  92.8 1.3 %collective-permute-start.21 = (f32[2,16,1024]{2,1,0:T(8,128)S(1)}, f32[2,16,1024]{2,1,0:T(8,128)S(1)}, u32[]{:S(2)}, u32[]{:S(2)}) collective-permute-start(f32[2,16,1024]{2,1,0:T(8,128)S(1)} %get-tuple-element.93), channel_id=1, source_target_pairs={{0,4},{1,5},{2,6},{3,7},{4,0},{5,1},{6,2},{7,3},{8,12},{9,13},{10,... | collective-permute-start | bytes 393224 | tf_op jit(solution)/shard_map/ppermute | solution.py:20
  94.1 0.7 collective-permute-start.22
  94.8 2.0 %collective-permute-done.20 = f32[2,16,1024]{2,1,0:T(8,128)S(1)} collective-permute-done((f32[2,16,1024]{2,1,0:T(8,128)S(1)}, f32[2,16,1024]{2,1,0:T(8,128)S(1)}, u32[]{:S(2)}, u32[]{:S(2)}) %collective-permute-start.20) | collective-permute-done | bytes 131104 | tf_op jit(solution)/shard_map/ppermute | solution.py:20
  96.7 2.4 %collective-permute-done.21 = f32[2,16,1024]{2,1,0:T(8,128)S(1)} collective-permute-done((f32[2,16,1024]{2,1,0:T(8,128)S(1)}, f32[2,16,1024]{2,1,0:T(8,128)S(1)}, u32[]{:S(2)}, u32[]{:S(2)}) %collective-permute-start.21) | collective-permute-done | bytes 131104 | tf_op jit(solution)/shard_map/ppermute | solution.py:20
  99.2 1.6 %collective-permute-done.22 = f32[2,16,1024]{2,1,0:T(8,128)S(1)} collective-permute-done((f32[2,16,1024]{2,1,0:T(8,128)S(1)}, f32[2,16,1024]{2,1,0:T(8,128)S(1)}, u32[]{:S(2)}, u32[]{:S(2)}) %collective-permute-start.22) | collective-permute-done | bytes 131104 | tf_op jit(solution)/shard_map/ppermute | solution.py:20
  100.7 3.3 %collective-permute-start.23 = (f32[2,16,1024]{2,1,0:T(8,128)S(1)}, f32[2,16,1024]{2,1,0:T(8,128)S(1)}, u32[]{:S(2)}, u32[]{:S(2)}) collective-permute-start(f32[2,16,1024]{2,1,0:T(8,128)S(1)} %fusion.6), channel_id=1, source_target_pairs={{0,8},{1,9},{2,10},{3,11},{4,12},{5,13},{6,14},{7,15},{8,0},{9,1},... | collective-permute-start | bytes 393224 | tf_op jit(solution)/shard_map/ppermute | solution.py:20
  104.0 5.4 %collective-permute-done.23 = f32[2,16,1024]{2,1,0:T(8,128)S(1)} collective-permute-done((f32[2,16,1024]{2,1,0:T(8,128)S(1)}, f32[2,16,1024]{2,1,0:T(8,128)S(1)}, u32[]{:S(2)}, u32[]{:S(2)}) %collective-permute-start.23) | collective-permute-done | bytes 131104 | tf_op jit(solution)/shard_map/ppermute | solution.py:20
  109.5 1.7 %collective-permute-start.25 = (f32[16,1024]{1,0:T(8,128)S(1)}, f32[16,1024]{1,0:T(8,128)S(1)}, u32[]{:S(2)}, u32[]{:S(2)}) collective-permute-start(f32[16,1024]{1,0:T(8,128)S(1)} %multiply_add_fusion), channel_id=1, source_target_pairs={{0,2},{1,3},{2,0},{3,1},{4,6},{5,7},{6,4},{7,5},{8,10},{9,11},{10,... | collective-permute-start | bytes 196616 | tf_op jit(solution)/shard_map/ppermute | solution.py:20
  111.2 1.9 %collective-permute-start.27 = (f32[16,1024]{1,0:T(8,128)S(1)}, f32[16,1024]{1,0:T(8,128)S(1)}, u32[]{:S(2)}, u32[]{:S(2)}) collective-permute-start(f32[16,1024]{1,0:T(8,128)S(1)} %multiply_add_fusion), channel_id=1, source_target_pairs={{0,6},{1,7},{2,4},{3,5},{4,2},{5,3},{6,0},{7,1},{8,14},{9,15},{10,... | collective-permute-start | bytes 196616 | tf_op jit(solution)/shard_map/ppermute | solution.py:20
  113.0 0.8 collective-permute-done.25
  113.8 1.6 %collective-permute-done.26 = f32[16,1024]{1,0:T(8,128)S(1)} collective-permute-done((f32[16,1024]{1,0:T(8,128)S(1)}, f32[16,1024]{1,0:T(8,128)S(1)}, u32[]{:S(2)}, u32[]{:S(2)}) %collective-permute-start.26) | collective-permute-done | bytes 65568 | tf_op jit(solution)/shard_map/ppermute | solution.py:20
  115.4 0.9 collective-permute-done.27
  116.4 1.5 %collective-permute-done.28.refs_2_ = f32[4,16,1024]{2,1,0:T(8,128)S(1)} collective-permute-done((f32[4,16,1024]{2,1,0:T(8,128)S(1)}, f32[4,16,1024]{2,1,0:T(8,128)S(1)}, u32[]{:S(2)}, u32[]{:S(2)}) %collective-permute-start.28) | collective-permute-done | bytes 262176 | tf_op jit(solution)/shard_map/ppermute | solution.py:20
  118.0 3.5 %year.9 = (f32[512,1024]{1,0:T(8,128)}, f32[512,1024]{1,0:T(8,128)}, f32[3,64,128]{2,1,0:T(8,128)}) custom-call(s32[1]{0:T(128)} %bitcast.refs_0_, f32[4,16,1024]{2,1,0:T(8,128)S(1)} %pad_maximum_fusion.1.refs_1_, f32[4,16,1024]{2,1,0:T(8,128)S(1)} %collective-permute-done.28.refs_2_, f32[128,1024]{1,0:T(8,128)S(1)} %get-tuple-element.76.refs_3_, ...), custom_call_target="tpu_custom_call" | custom-call | flops 536870912 | bytes 10485760 | tf_op jit(solution)/shard_map/year/pallas_call | solution.py:380
  (130 shorter events, 10.8 us)
Async XLA Ops:
  0.6 0.8 copy-start.38
  1.4 0.8 copy-start.39
  5.7 7.8 %collective-permute-start = (f32[1,136,128]{2,1,0:T(8,128)S(1)}, f32[1,136,128]{2,1,0:T(8,128)S(1)}, u32[]{:S(2)}, u32[]{:S(2)}) collective-permute-start(f32[1,136,128]{2,1,0:T(8,128)S(1)} %bitcast.103), channel_id=1, source_target_pairs={{0,8},{1,9},{2,10},{3,11},{4,12},{5,13},{6,14},{7,15},{8,0},{9,1},... | collective-permute-start | bytes 208904 | tf_op jit(solution)/shard_map/ppermute | solution.py:20
  13.5 25.6 %copy-start = (bf16[512,3,1024]{2,0,1:T(8,128)(2,1)S(1)}, bf16[512,3,1024]{2,0,1:T(8,128)(2,1)}, u32[]{:S(2)}) copy-start(bf16[512,3,1024]{2,0,1:T(8,128)(2,1)} %param.23) | copy-start | bytes 9437188
  13.5 5.9 %collective-permute-start.1 = (f32[2,136,128]{2,1,0:T(8,128)S(1)}, f32[2,136,128]{2,1,0:T(8,128)S(1)}, u32[]{:S(2)}, u32[]{:S(2)}) collective-permute-start(f32[2,136,128]{2,1,0:T(8,128)S(1)} %pad_maximum_fusion.2.refs_0_), channel_id=1, source_target_pairs={{0,2},{1,3},{2,0},{3,1},{4,6},{5,7},{6,4},{7,5},{8,10},{9,11},{10,... | collective-permute-start | bytes 417800 | tf_op jit(solution)/shard_map/ppermute | solution.py:20
  15.3 5.1 %collective-permute-start.2 = (f32[2,136,128]{2,1,0:T(8,128)S(1)}, f32[2,136,128]{2,1,0:T(8,128)S(1)}, u32[]{:S(2)}, u32[]{:S(2)}) collective-permute-start(f32[2,136,128]{2,1,0:T(8,128)S(1)} %pad_maximum_fusion.2.refs_0_), channel_id=1, source_target_pairs={{0,4},{1,5},{2,6},{3,7},{4,0},{5,1},{6,2},{7,3},{8,12},{9,13},{10,... | collective-permute-start | bytes 417800 | tf_op jit(solution)/shard_map/ppermute | solution.py:20
  15.7 7.0 %collective-permute-start.3 = (f32[2,136,128]{2,1,0:T(8,128)S(1)}, f32[2,136,128]{2,1,0:T(8,128)S(1)}, u32[]{:S(2)}, u32[]{:S(2)}) collective-permute-start(f32[2,136,128]{2,1,0:T(8,128)S(1)} %pad_maximum_fusion.2.refs_0_), channel_id=1, source_target_pairs={{0,6},{1,7},{2,4},{3,5},{4,2},{5,3},{6,0},{7,1},{8,14},{9,15},{10,... | collective-permute-start | bytes 417800 | tf_op jit(solution)/shard_map/ppermute | solution.py:20
  20.4 7.2 %copy-start.18 = (f32[2,136,128]{2,1,0:T(8,128)}, f32[2,136,128]{2,1,0:T(8,128)S(1)}, u32[]{:S(2)}) copy-start(f32[2,136,128]{2,1,0:T(8,128)S(1)} %collective-permute-done.2.refs_2_) | copy-start | bytes 417796
  22.7 1.4 %copy-start.1 = (f32[3,128,1024]{2,1,0:T(8,128)S(1)}, f32[3,128,1024]{2,1,0:T(8,128)}, u32[]{:S(2)}) copy-start(f32[3,128,1024]{2,1,0:T(8,128)} %refs_4_.7) | copy-start | bytes 4718596
  24.1 3.5 %copy-start.21 = (f32[2,136,128]{2,1,0:T(8,128)}, f32[2,136,128]{2,1,0:T(8,128)S(1)}, u32[]{:S(2)}) copy-start(f32[2,136,128]{2,1,0:T(8,128)S(1)} %collective-permute-done.3.refs_3_) | copy-start | bytes 417796
  26.0 13.2 %collective-permute-start.7 = (f32[128,512]{1,0:T(8,128)}, f32[128,512]{1,0:T(8,128)}, u32[]{:S(2)}, u32[]{:S(2)}) collective-permute-start(f32[128,512]{1,0:T(8,128)} %get-tuple-element.63.refs_3_), channel_id=1, source_target_pairs={{0,1},{1,0},{2,3},{3,2},{4,5},{5,4},{6,7},{7,6},{8,9},{9,8},{10,11... | collective-permute-start | bytes 786440 | tf_op jit(solution)/shard_map/ppermute | solution.py:20
  28.3 10.8 %collective-permute-start.4 = (f32[8,128]{1,0:T(8,128)}, f32[8,128]{1,0:T(8,128)}, u32[]{:S(2)}, u32[]{:S(2)}) collective-permute-start(f32[8,128]{1,0:T(8,128)} %get-tuple-element.48.refs_1_), channel_id=1, source_target_pairs={{0,1},{1,0},{2,3},{3,2},{4,5},{5,4},{6,7},{7,6},{8,9},{9,8},{10,11... | collective-permute-start | bytes 12296 | tf_op jit(solution)/shard_map/ppermute | solution.py:20
  34.8 0.7 copy-start.12
  37.0 0.7 copy-start.26
  37.7 0.7 copy-start.28
  39.1 3.4 %copy-start.24 = (bf16[128,512]{1,0:T(8,128)(2,1)}, bf16[128,512]{1,0:T(8,128)(2,1)S(1)}, u32[]{:S(2)}) copy-start(bf16[128,512]{1,0:T(8,128)(2,1)S(1)} %get-tuple-element.71.refs_12_) | copy-start | bytes 393220
  39.1 6.5 %collective-permute-start.5 = (f32[128,512]{1,0:T(8,128)}, f32[128,512]{1,0:T(8,128)S(1)}, u32[]{:S(2)}, u32[]{:S(2)}) collective-permute-start(f32[128,512]{1,0:T(8,128)} %copy-done.32), channel_id=1, source_target_pairs={{0,1},{1,0},{2,3},{3,2},{4,5},{5,4},{6,7},{7,6},{8,9},{9,8},{10,11... | collective-permute-start | bytes 786440 | tf_op jit(solution)/shard_map/ppermute | solution.py:20
  39.2 6.5 %copy-start.33 = (f32[128,512]{1,0:T(8,128)S(1)}, f32[128,512]{1,0:T(8,128)}, u32[]{:S(2)}) copy-start(f32[128,512]{1,0:T(8,128)} %copy-done.32) | copy-start | bytes 786436
  42.5 1.0 copy-start.8
  43.5 1.0 copy-start.10
  45.1 3.8 %copy-start.2 = (f32[3,128,1024]{2,1,0:T(8,128)S(1)}, f32[3,128,1024]{2,1,0:T(8,128)}, u32[]{:S(2)}) copy-start(f32[3,128,1024]{2,1,0:T(8,128)} %refs_4_.7) | copy-start | bytes 4718596
  45.1 3.8 %copy-start.19 = (f32[2,136,128]{2,1,0:T(8,128)S(1)}, f32[2,136,128]{2,1,0:T(8,128)}, u32[]{:S(2)}) copy-start(f32[2,136,128]{2,1,0:T(8,128)} %copy-done.18) | copy-start | bytes 417796
  45.1 3.7 %copy-start.22 = (f32[2,136,128]{2,1,0:T(8,128)S(1)}, f32[2,136,128]{2,1,0:T(8,128)}, u32[]{:S(2)}) copy-start(f32[2,136,128]{2,1,0:T(8,128)} %copy-done.21) | copy-start | bytes 417796
  45.1 7.0 %collective-permute-start.8 = (f32[4,2,16,512]{3,2,1,0:T(8,128)S(1)}, f32[4,2,16,512]{3,2,1,0:T(8,128)S(1)}, u32[]{:S(2)}, u32[]{:S(2)}) collective-permute-start(f32[4,2,16,512]{3,2,1,0:T(8,128)S(1)} %slice_bitcast_fusion.2), channel_id=1, source_target_pairs={{0,1},{1,0},{2,3},{3,2},{4,5},{5,4},{6,7},{7,6},{8,9},{9,8},{10,11... | collective-permute-start | bytes 786440 | tf_op jit(solution)/shard_map/ppermute | solution.py:20
  48.6 3.5 %copy-start.4 = (f32[512,512]{1,0:T(8,128)}, f32[512,512]{1,0:T(8,128)S(1)}, u32[]{:S(2)}) copy-start(f32[512,512]{1,0:T(8,128)S(1)} %get-tuple-element.69.refs_9_) | copy-start | bytes 3145732
  48.6 3.5 %copy-start.6 = (f32[512,512]{1,0:T(8,128)}, f32[512,512]{1,0:T(8,128)S(1)}, u32[]{:S(2)}) copy-start(f32[512,512]{1,0:T(8,128)S(1)} %get-tuple-element.70.refs_10_) | copy-start | bytes 3145732
  48.6 3.5 %copy-start.36 = (f32[64,128]{1,0:T(8,128)}, f32[64,128]{1,0:T(8,128)S(1)}, u32[]{:S(2)}) copy-start(f32[64,128]{1,0:T(8,128)S(1)} %get-tuple-element.84.refs_13_) | copy-start | bytes 98308
  48.6 3.5 %collective-permute-start.6 = (f32[4,2,16,512]{3,2,1,0:T(8,128)S(1)}, f32[4,2,16,512]{3,2,1,0:T(8,128)S(1)}, u32[]{:S(2)}, u32[]{:S(2)}) collective-permute-start(f32[4,2,16,512]{3,2,1,0:T(8,128)S(1)} %slice_bitcast_fusion.3), channel_id=1, source_target_pairs={{0,1},{1,0},{2,3},{3,2},{4,5},{5,4},{6,7},{7,6},{8,9},{9,8},{10,11... | collective-permute-start | bytes 786440 | tf_op jit(solution)/shard_map/ppermute | solution.py:20
  51.7 21.7 %collective-permute-start.13 = (f32[128,1024]{1,0:T(8,128)}, f32[128,1024]{1,0:T(8,128)}, u32[]{:S(2)}, u32[]{:S(2)}) collective-permute-start(f32[128,1024]{1,0:T(8,128)} %get-tuple-element.65), channel_id=1, source_target_pairs={{0,1},{1,0},{2,3},{3,2},{4,5},{5,4},{6,7},{7,6},{8,9},{9,8},{10,11... | collective-permute-start | bytes 1572872 | tf_op jit(solution)/shard_map/ppermute | solution.py:20
  52.2 6.4 %collective-permute-start.10 = (f32[2,16,1024]{2,1,0:T(8,128)S(1)}, f32[2,16,1024]{2,1,0:T(8,128)S(1)}, u32[]{:S(2)}, u32[]{:S(2)}) collective-permute-start(f32[2,16,1024]{2,1,0:T(8,128)S(1)} %get-tuple-element.100), channel_id=1, source_target_pairs={{0,4},{1,5},{2,6},{3,7},{4,0},{5,1},{6,2},{7,3},{8,12},{9,13},{10,... | collective-permute-start | bytes 393224 | tf_op jit(solution)/shard_map/ppermute | solution.py:20
  53.2 7.7 %collective-permute-start.11 = (f32[2,16,1024]{2,1,0:T(8,128)S(1)}, f32[2,16,1024]{2,1,0:T(8,128)S(1)}, u32[]{:S(2)}, u32[]{:S(2)}) collective-permute-start(f32[2,16,1024]{2,1,0:T(8,128)S(1)} %get-tuple-element.99), channel_id=1, source_target_pairs={{0,6},{1,7},{2,4},{3,5},{4,2},{5,3},{6,0},{7,1},{8,14},{9,15},{10,... | collective-permute-start | bytes 393224 | tf_op jit(solution)/shard_map/ppermute | solution.py:20
  54.4 7.8 %collective-permute-start.9 = (f32[2,16,1024]{2,1,0:T(8,128)S(1)}, f32[2,16,1024]{2,1,0:T(8,128)S(1)}, u32[]{:S(2)}, u32[]{:S(2)}) collective-permute-start(f32[2,16,1024]{2,1,0:T(8,128)S(1)} %get-tuple-element.98), channel_id=1, source_target_pairs={{0,2},{1,3},{2,0},{3,1},{4,6},{5,7},{6,4},{7,5},{8,10},{9,11},{10,... | collective-permute-start | bytes 393224 | tf_op jit(solution)/shard_map/ppermute | solution.py:20
  62.9 9.5 %collective-permute-start.12 = (f32[2,16,1024]{2,1,0:T(8,128)}, f32[2,16,1024]{2,1,0:T(8,128)}, u32[]{:S(2)}, u32[]{:S(2)}) collective-permute-start(f32[2,16,1024]{2,1,0:T(8,128)} %fusion.15), channel_id=1, source_target_pairs={{0,8},{1,9},{2,10},{3,11},{4,12},{5,13},{6,14},{7,15},{8,0},{9,1},... | collective-permute-start | bytes 393224 | tf_op jit(solution)/shard_map/ppermute | solution.py:20
  66.4 16.7 %copy-start.9 = (f32[512,512]{1,0:T(8,128)S(1)}, f32[512,512]{1,0:T(8,128)}, u32[]{:S(2)}) copy-start(f32[512,512]{1,0:T(8,128)} %copy-done.8) | copy-start | bytes 3145732
  66.4 16.7 %copy-start.11 = (f32[512,512]{1,0:T(8,128)S(1)}, f32[512,512]{1,0:T(8,128)}, u32[]{:S(2)}) copy-start(f32[512,512]{1,0:T(8,128)} %copy-done.10) | copy-start | bytes 3145732
  66.4 16.7 %copy-start.13 = (bf16[512,256]{1,0:T(8,128)(2,1)S(1)}, bf16[512,256]{1,0:T(8,128)(2,1)}, u32[]{:S(2)}) copy-start(bf16[512,256]{1,0:T(8,128)(2,1)} %copy-done.12) | copy-start | bytes 786436
  66.5 16.7 %copy-start.15 = (f32[512,128]{1,0:T(8,128)S(1)}, f32[512,128]{1,0:T(8,128)}, u32[]{:S(2)}) copy-start(f32[512,128]{1,0:T(8,128)} %copy-done.14) | copy-start | bytes 786436
  66.5 16.7 %copy-start.17 = (f32[512,128]{1,0:T(8,128)S(1)}, f32[512,128]{1,0:T(8,128)}, u32[]{:S(2)}) copy-start(f32[512,128]{1,0:T(8,128)} %copy-done.16) | copy-start | bytes 786436
  66.5 16.7 %copy-start.25 = (bf16[128,512]{1,0:T(8,128)(2,1)S(1)}, bf16[128,512]{1,0:T(8,128)(2,1)}, u32[]{:S(2)}) copy-start(bf16[128,512]{1,0:T(8,128)(2,1)} %copy-done.24) | copy-start | bytes 393220
  74.4 5.0 %collective-permute-start.14 = (f32[16,1024]{1,0:T(8,128)S(1)}, f32[16,1024]{1,0:T(8,128)S(1)}, u32[]{:S(2)}, u32[]{:S(2)}) collective-permute-start(f32[16,1024]{1,0:T(8,128)S(1)} %multiply_add_fusion.1), channel_id=1, source_target_pairs={{0,2},{1,3},{2,0},{3,1},{4,6},{5,7},{6,4},{7,5},{8,10},{9,11},{10,... | collective-permute-start | bytes 196616 | tf_op jit(solution)/shard_map/ppermute | solution.py:20
  74.8 4.9 %collective-permute-start.15 = (f32[16,1024]{1,0:T(8,128)S(1)}, f32[16,1024]{1,0:T(8,128)S(1)}, u32[]{:S(2)}, u32[]{:S(2)}) collective-permute-start(f32[16,1024]{1,0:T(8,128)S(1)} %multiply_add_fusion.1), channel_id=1, source_target_pairs={{0,4},{1,5},{2,6},{3,7},{4,0},{5,1},{6,2},{7,3},{8,12},{9,13},{10,... | collective-permute-start | bytes 196616 | tf_op jit(solution)/shard_map/ppermute | solution.py:20
  75.5 5.4 %collective-permute-start.16 = (f32[16,1024]{1,0:T(8,128)S(1)}, f32[16,1024]{1,0:T(8,128)S(1)}, u32[]{:S(2)}, u32[]{:S(2)}) collective-permute-start(f32[16,1024]{1,0:T(8,128)S(1)} %multiply_add_fusion.1), channel_id=1, source_target_pairs={{0,6},{1,7},{2,4},{3,5},{4,2},{5,3},{6,0},{7,1},{8,14},{9,15},{10,... | collective-permute-start | bytes 196616 | tf_op jit(solution)/shard_map/ppermute | solution.py:20
  80.9 2.2 %collective-permute-start.17 = (f32[4,16,1024]{2,1,0:T(8,128)S(1)}, f32[4,16,1024]{2,1,0:T(8,128)S(1)}, u32[]{:S(2)}, u32[]{:S(2)}) collective-permute-start(f32[4,16,1024]{2,1,0:T(8,128)S(1)} %pad_maximum_fusion.refs_1_), channel_id=1, source_target_pairs={{0,1},{1,0},{2,3},{3,2},{4,5},{5,4},{6,7},{7,6},{8,9},{9,8},{10,11... | collective-permute-start | bytes 786440 | tf_op jit(solution)/shard_map/ppermute | solution.py:20
  83.2 2.6 %copy-start.5 = (f32[512,512]{1,0:T(8,128)S(1)}, f32[512,512]{1,0:T(8,128)}, u32[]{:S(2)}) copy-start(f32[512,512]{1,0:T(8,128)} %copy-done.4) | copy-start | bytes 3145732
  83.2 2.6 %copy-start.7 = (f32[512,512]{1,0:T(8,128)S(1)}, f32[512,512]{1,0:T(8,128)}, u32[]{:S(2)}) copy-start(f32[512,512]{1,0:T(8,128)} %copy-done.6) | copy-start | bytes 3145732
  85.2 5.8 %collective-permute-start.19 = (f32[4,2,16,512]{3,2,1,0:T(8,128)S(1)}, f32[4,2,16,512]{3,2,1,0:T(8,128)S(1)}, u32[]{:S(2)}, u32[]{:S(2)}) collective-permute-start(f32[4,2,16,512]{3,2,1,0:T(8,128)S(1)} %slice_bitcast_fusion), channel_id=1, source_target_pairs={{0,1},{1,0},{2,3},{3,2},{4,5},{5,4},{6,7},{7,6},{8,9},{9,8},{10,11... | collective-permute-start | bytes 786440 | tf_op jit(solution)/shard_map/ppermute | solution.py:20
  85.8 2.3 %copy-start.3 = (f32[3,128,1024]{2,1,0:T(8,128)S(1)}, f32[3,128,1024]{2,1,0:T(8,128)}, u32[]{:S(2)}) copy-start(f32[3,128,1024]{2,1,0:T(8,128)} %refs_4_.7) | copy-start | bytes 4718596
  85.8 2.3 %copy-start.20 = (f32[2,136,128]{2,1,0:T(8,128)S(1)}, f32[2,136,128]{2,1,0:T(8,128)}, u32[]{:S(2)}) copy-start(f32[2,136,128]{2,1,0:T(8,128)} %copy-done.18) | copy-start | bytes 417796
  85.8 2.3 %copy-start.23 = (f32[2,136,128]{2,1,0:T(8,128)S(1)}, f32[2,136,128]{2,1,0:T(8,128)}, u32[]{:S(2)}) copy-start(f32[2,136,128]{2,1,0:T(8,128)} %copy-done.21) | copy-start | bytes 417796
  87.9 3.2 %collective-permute-start.18 = (f32[4,2,16,512]{3,2,1,0:T(8,128)S(1)}, f32[4,2,16,512]{3,2,1,0:T(8,128)S(1)}, u32[]{:S(2)}, u32[]{:S(2)}) collective-permute-start(f32[4,2,16,512]{3,2,1,0:T(8,128)S(1)} %slice_bitcast_fusion.1), channel_id=1, source_target_pairs={{0,1},{1,0},{2,3},{3,2},{4,5},{5,4},{6,7},{7,6},{8,9},{9,8},{10,11... | collective-permute-start | bytes 786440 | tf_op jit(solution)/shard_map/ppermute | solution.py:20
  90.5 18.9 %collective-permute-start.24 = (f32[128,1024]{1,0:T(8,128)S(1)}, f32[128,1024]{1,0:T(8,128)S(1)}, u32[]{:S(2)}, u32[]{:S(2)}) collective-permute-start(f32[128,1024]{1,0:T(8,128)S(1)} %get-tuple-element.76.refs_3_), channel_id=1, source_target_pairs={{0,1},{1,0},{2,3},{3,2},{4,5},{5,4},{6,7},{7,6},{8,9},{9,8},{10,11... | collective-permute-start | bytes 1572872 | tf_op jit(solution)/shard_map/ppermute | solution.py:20
  91.1 26.9 %copy-start.27 = (bf16[512,256]{1,0:T(8,128)(2,1)S(1)}, bf16[512,256]{1,0:T(8,128)(2,1)}, u32[]{:S(2)}) copy-start(bf16[512,256]{1,0:T(8,128)(2,1)} %copy-done.26) | copy-start | bytes 786436
  91.1 26.9 %copy-start.29 = (f32[512,128]{1,0:T(8,128)S(1)}, f32[512,128]{1,0:T(8,128)}, u32[]{:S(2)}) copy-start(f32[512,128]{1,0:T(8,128)} %copy-done.28) | copy-start | bytes 786436
  91.1 26.9 %copy-start.31 = (f32[512,128]{1,0:T(8,128)S(1)}, f32[512,128]{1,0:T(8,128)}, u32[]{:S(2)}) copy-start(f32[512,128]{1,0:T(8,128)} %copy-done.30) | copy-start | bytes 786436
  91.1 26.9 %copy-start.35 = (f32[64,128]{1,0:T(8,128)S(1)}, f32[64,128]{1,0:T(8,128)}, u32[]{:S(2)}) copy-start(f32[64,128]{1,0:T(8,128)} %copy-done.34) | copy-start | bytes 98308
  91.1 26.9 %copy-start.37 = (f32[64,128]{1,0:T(8,128)S(1)}, f32[64,128]{1,0:T(8,128)}, u32[]{:S(2)}) copy-start(f32[64,128]{1,0:T(8,128)} %copy-done.36) | copy-start | bytes 98308
  91.2 5.5 %collective-permute-start.20 = (f32[2,16,1024]{2,1,0:T(8,128)S(1)}, f32[2,16,1024]{2,1,0:T(8,128)S(1)}, u32[]{:S(2)}, u32[]{:S(2)}) collective-permute-start(f32[2,16,1024]{2,1,0:T(8,128)S(1)} %get-tuple-element.91), channel_id=1, source_target_pairs={{0,2},{1,3},{2,0},{3,1},{4,6},{5,7},{6,4},{7,5},{8,10},{9,11},{10,... | collective-permute-start | bytes 393224 | tf_op jit(solution)/shard_map/ppermute | solution.py:20
  92.8 6.4 %collective-permute-start.21 = (f32[2,16,1024]{2,1,0:T(8,128)S(1)}, f32[2,16,1024]{2,1,0:T(8,128)S(1)}, u32[]{:S(2)}, u32[]{:S(2)}) collective-permute-start(f32[2,16,1024]{2,1,0:T(8,128)S(1)} %get-tuple-element.93), channel_id=1, source_target_pairs={{0,4},{1,5},{2,6},{3,7},{4,0},{5,1},{6,2},{7,3},{8,12},{9,13},{10,... | collective-permute-start | bytes 393224 | tf_op jit(solution)/shard_map/ppermute | solution.py:20
  94.1 6.6 %collective-permute-start.22 = (f32[2,16,1024]{2,1,0:T(8,128)S(1)}, f32[2,16,1024]{2,1,0:T(8,128)S(1)}, u32[]{:S(2)}, u32[]{:S(2)}) collective-permute-start(f32[2,16,1024]{2,1,0:T(8,128)S(1)} %get-tuple-element.92), channel_id=1, source_target_pairs={{0,6},{1,7},{2,4},{3,5},{4,2},{5,3},{6,0},{7,1},{8,14},{9,15},{10,... | collective-permute-start | bytes 393224 | tf_op jit(solution)/shard_map/ppermute | solution.py:20
  100.7 8.6 %collective-permute-start.23 = (f32[2,16,1024]{2,1,0:T(8,128)S(1)}, f32[2,16,1024]{2,1,0:T(8,128)S(1)}, u32[]{:S(2)}, u32[]{:S(2)}) collective-permute-start(f32[2,16,1024]{2,1,0:T(8,128)S(1)} %fusion.6), channel_id=1, source_target_pairs={{0,8},{1,9},{2,10},{3,11},{4,12},{5,13},{6,14},{7,15},{8,0},{9,1},... | collective-permute-start | bytes 393224 | tf_op jit(solution)/shard_map/ppermute | solution.py:20
  109.5 4.3 %collective-permute-start.25 = (f32[16,1024]{1,0:T(8,128)S(1)}, f32[16,1024]{1,0:T(8,128)S(1)}, u32[]{:S(2)}, u32[]{:S(2)}) collective-permute-start(f32[16,1024]{1,0:T(8,128)S(1)} %multiply_add_fusion), channel_id=1, source_target_pairs={{0,2},{1,3},{2,0},{3,1},{4,6},{5,7},{6,4},{7,5},{8,10},{9,11},{10,... | collective-permute-start | bytes 196616 | tf_op jit(solution)/shard_map/ppermute | solution.py:20
  111.2 4.3 %collective-permute-start.26 = (f32[16,1024]{1,0:T(8,128)S(1)}, f32[16,1024]{1,0:T(8,128)S(1)}, u32[]{:S(2)}, u32[]{:S(2)}) collective-permute-start(f32[16,1024]{1,0:T(8,128)S(1)} %multiply_add_fusion), channel_id=1, source_target_pairs={{0,4},{1,5},{2,6},{3,7},{4,0},{5,1},{6,2},{7,3},{8,12},{9,13},{10,... | collective-permute-start | bytes 196616 | tf_op jit(solution)/shard_map/ppermute | solution.py:20
  111.2 5.2 %collective-permute-start.27 = (f32[16,1024]{1,0:T(8,128)S(1)}, f32[16,1024]{1,0:T(8,128)S(1)}, u32[]{:S(2)}, u32[]{:S(2)}) collective-permute-start(f32[16,1024]{1,0:T(8,128)S(1)} %multiply_add_fusion), channel_id=1, source_target_pairs={{0,6},{1,7},{2,4},{3,5},{4,2},{5,3},{6,0},{7,1},{8,14},{9,15},{10,... | collective-permute-start | bytes 196616 | tf_op jit(solution)/shard_map/ppermute | solution.py:20
  116.4 1.6 %collective-permute-start.28 = (f32[4,16,1024]{2,1,0:T(8,128)S(1)}, f32[4,16,1024]{2,1,0:T(8,128)S(1)}, u32[]{:S(2)}, u32[]{:S(2)}) collective-permute-start(f32[4,16,1024]{2,1,0:T(8,128)S(1)} %pad_maximum_fusion.1.refs_1_), channel_id=1, source_target_pairs={{0,1},{1,0},{2,3},{3,2},{4,5},{5,4},{6,7},{7,6},{8,9},{9,8},{10,11... | collective-permute-start | bytes 786440 | tf_op jit(solution)/shard_map/ppermute | solution.py:20
  (17 other events, 11.5 us)

commit v3 on v2

--- a/solution.py
+++ b/solution.py
@@ -12,6 +12,7 @@
 VMEM = pl.BlockSpec(memory_space=pltpu.VMEM)
 SMEM = pl.BlockSpec(memory_space=pltpu.SMEM)
 ANY = pl.BlockSpec(memory_space=pl.ANY)
+HBM = pl.BlockSpec(memory_space=pltpu.HBM)
 ROW = (((1,), (1,)), ((), ()))
 
 
@@ -46,7 +47,7 @@
         in_specs=ins,
         out_specs=out_specs if out_specs is not None else jax.tree.map(lambda _: VMEM, out),
         scratch_shapes=scratch,
-        compiler_params=pltpu.CompilerParams(vmem_limit_bytes=limit << 20),
+        compiler_params=pltpu.CompilerParams(vmem_limit_bytes=int(limit * 2**20)),
         cost_estimate=pl.CostEstimate(flops=flops, bytes_accessed=moved, transcendentals=0),
         name=name,
     )
@@ -56,7 +57,14 @@
     return jax.ShapeDtypeStruct(dims, dtype)
 
 
-def pack_body(load, hold, drift, fund, term, asset, liab, out):
+def pack_body(*refs):
+    sources, (out, lines), held, sem = refs[1:11], refs[11:13], refs[13:23], refs[23]
+    copies = [pltpu.make_async_copy(s, h, sem.at[i]) for i, (s, h) in enumerate(zip(sources, held))]
+    for copy in copies:
+        copy.start()
+    for copy in copies:
+        copy.wait()
+    load, hold, drift, fund, term, asset, liab, kind, base, guar = held
     secs, funds = load.shape
     count = fund.shape[1]
     out[0:secs, :] = load[...]
@@ -68,51 +76,58 @@
     one, rest = v.astype(BF16).astype(F32), v - v.astype(BF16).astype(F32)
     two = rest.astype(BF16).astype(F32)
     three = rest - two
-    kind = jnp.where(at < 3, at, at - 3)
-    rows = jnp.where(kind == 0, one, jnp.where(kind == 1, two, three))
+    spot = jnp.where(at < 3, at, at - 3)
+    rows = jnp.where(spot == 0, one, jnp.where(spot == 1, two, three))
     rows = jnp.where(at < 6, rows, 0.0).astype(BF16)
     out[2 * secs : 2 * secs + 8, :] = dot(rows, member, ROW)
     out[2 * secs + 6 : 2 * secs + 7, 0:secs] = drift[...]
-
-
-def columns_body(base, guar, fund, kind, term, asset, liab, *outs):
-    years = (len(outs) - 2) // 4
-    member_t, member, base_w, guar_w = (outs[i * years : (i + 1) * years] for i in range(4))
-    asset_w, liab_w = outs[-2:]
-    funds, count = member_t[0].shape
-    types = base.shape[0]
     base_row = jnp.zeros((1, count), F32)
     guar_row = jnp.zeros((1, count), F32)
-    for t in range(types):
-        base_row = jnp.where(kind[...] == t, base[t], base_row)
-        guar_row = jnp.where(kind[...] == t, guar[t], guar_row)
-    at = lax.broadcasted_iota(jnp.int32, (128, count), 0)
-    rows = (fund[...].astype(F32), term[...].astype(F32), base_row, guar_row, asset[...], liab[...])
-    stack = jnp.zeros((128, count), F32)
-    for r, row in enumerate(rows):
+    for t in range(base.shape[1]):
+        base_row = jnp.where(kind[...] == t, base[:, t : t + 1], base_row)
+        guar_row = jnp.where(kind[...] == t, guar[:, t : t + 1], guar_row)
+    values = (fund[...].astype(F32), term[...].astype(F32), base_row, guar_row, asset[...], liab[...])
+    stack = jnp.zeros((8, count), F32)
+    for r, row in enumerate(values):
         stack = jnp.where(at == r, row, stack)
+    lines[...] = stack
+
+
+def columns_body(lines, block, shocks, member_t, member, wides, x_now, x_later, own, raw, sem):
+    own[0] = block[...]
+    years, funds, count = member_t.shape
+    fetch = pltpu.make_async_copy(shocks, raw, sem)
+    fetch.start()
+    stack = jnp.concatenate([lines[...], jnp.zeros((120, count), F32)], 0)
     cols = jnp.transpose(stack)
     wide = lambda r: jnp.broadcast_to(cols[:, r : r + 1], (count, 128))
     fund_c, term_c, base_c, guar_c = wide(0), wide(1), wide(2), wide(3)
-    asset_w[...] = wide(4)
-    liab_w[...] = wide(5)
-    hot_t = lax.broadcasted_iota(jnp.int32, (funds, count), 0) == fund[...]
+    wides[2 * years] = wide(4)
+    wides[2 * years + 1] = wide(5)
+    hot_t = lax.broadcasted_iota(jnp.int32, (funds, count), 0).astype(F32) == lines[0:1, :]
     hot = lax.broadcasted_iota(jnp.int32, (count, funds), 1).astype(F32) == fund_c
     for y in range(years):
         alive = term_c > float(y)
-        base_w[y][...] = jnp.where(alive, base_c, 0.0)
-        guar_w[y][...] = jnp.where(alive, guar_c, 0.0)
+        wides[2 * y] = jnp.where(alive, base_c, 0.0)
+        wides[2 * y + 1] = jnp.where(alive, guar_c, 0.0)
         here = jnp.logical_and(hot, alive).astype(F32).astype(BF16)
-        member[y][:, 0:funds] = here
-        member[y][:, funds : 2 * funds] = here
+        member[y, :, 0:funds] = here
+        member[y, :, funds : 2 * funds] = here
         if y == 0:
-            member_t[y][...] = hot_t.astype(F32).astype(BF16)
+            member_t[y] = hot_t.astype(F32).astype(BF16)
         else:
-            member_t[y][...] = jnp.logical_and(hot_t, term[...] > y).astype(F32).astype(BF16)
+            member_t[y] = jnp.logical_and(hot_t, lines[1:2, :] > float(y)).astype(F32).astype(BF16)
+    fetch.wait()
+    for y in range(years):
+        hi, lo = halves(raw[y])
+        if y == 0:
+            x_now[0], x_now[1] = hi, lo
+        else:
+            x_later[y - 1, 0], x_later[y - 1, 1] = hi, lo
 
 
 def returns_body(year, first, secs, *refs):
-    blocks, (shocks, part, sums), (load_hi, load_lo, hold_hi, hold_lo) = refs[:4], refs[4:7], refs[7:]
+    blocks, (xs, part, sums), (load_hi, load_lo, hold_hi, hold_lo) = refs[:4], refs[4:7], refs[7:]
     funds, width = part.shape
     total = load_hi.shape[0]
     at = 0
@@ -133,7 +148,8 @@
     step = min(256, width)
     group = min(512, total)
     for c in range(0, width, step):
-        x_hi, x_lo = halves(shocks[year, :, first + c : first + c + step])
+        cut = slice(first + c, first + c + step)
+        x_hi, x_lo = (xs[i, :, cut] if year == 0 else xs[year - 1, i, :, cut] for i in range(2))
         acc = jnp.zeros((funds, step), F32)
         for g in range(0, total, group):
             lh, ll = load_hi[g : g + group, :], load_lo[g : g + group, :]
@@ -161,7 +177,7 @@
     return pl.multiple_of(((me_ref[0] & 7) ^ label) * slice_funds, slice_funds)
 
 
-def advance(cols, c, step, table, member, base, guar, draw, asset, liab):
+def advance(step, table, member, base, guar, draw, asset, liab):
     wide = lambda v: jnp.concatenate([v] * (step // 128), 1)
     got = dot(member, table)
     growth, credit = got[:, 0:step], jnp.maximum(got[:, step:], wide(guar))
@@ -176,6 +192,16 @@
     return jnp.concatenate([jnp.concatenate([g_hi, d_hi], 1), jnp.concatenate([g_lo, d_lo], 1)], 0)
 
 
+def own_body(slice_funds, me, part, peer, *refs):
+    totals, out = refs[:-1], refs[-1]
+    rows = pl.ds(pl.multiple_of((me[0] & 7) * slice_funds, slice_funds), slice_funds)
+    growth = part[rows, :] + peer[rows, :]
+    asset, liab = totals[0][0], totals[0][1]
+    for t in totals[1:]:
+        asset, liab = asset + t[0], liab + t[1]
+    out[...] = rate(asset * (1.0 + growth) / liab)
+
+
 STEP, ROWS = 256, 256
 
 
@@ -185,18 +211,19 @@
     if year == 0:
         mine, other = refs.pop(0), refs.pop(0)
     else:
-        near, far = refs.pop(0), refs.pop(0)
+        slices = [refs.pop(0) for _ in range(8)]
     part, peer = refs.pop(0), refs.pop(0)
-    draws, member, base, guar = (refs.pop(0) for _ in range(4))
-    states = [(refs.pop(0), refs.pop(0)) for _ in range(2 if last else 1)]
+    draws, member, wides = refs.pop(0), refs.pop(0), refs.pop(0)
+    states = [(refs.pop(0), refs.pop(0)) for _ in range(0 if year == 0 else 2 if last else 1)]
+    lead = 0
     if last:
         earlier = [refs.pop(0) for _ in range(2 * year)]
         out_a, out_l, out_r, declared, buf_a, buf_l, sem = refs
     else:
-        member_t, member_ta = refs.pop(0), refs.pop(0)
+        member_t = refs.pop(0)
         out_a, out_l, out_s, out_r, declared, acc = refs
     funds, width = declared.shape
-    count = member.shape[0]
+    count = member.shape[1]
     if year == 0:
         sums = mine[...] + other[...]
         row = lax.broadcasted_iota(jnp.int32, (128, funds), 0)
@@ -207,11 +234,10 @@
         ratio = both[:, 0:1] / both[:, 1:2]
         declared[...] = rate(ratio * (1.0 + (part[...] + peer[...])))
     else:
+        lead = first
         for o in range(8):
-            source = near if o < 4 else far
-            declared[pl.ds(slice_spot(me, o, slice_funds), slice_funds), :] = source[
-                o & 3, :, first : first + width
-            ]
+            spot = pl.ds(slice_spot(me, o, slice_funds), slice_funds)
+            declared[spot, :] = slices[o][:, first : first + width]
     if last:
         own = out_r.at[year]
         for y in range(year):
@@ -221,20 +247,22 @@
     copies = []
     for c in range(0, width, STEP):
         cut = slice(c, c + STEP)
-        table = table_of(part[:, cut] + peer[:, cut], declared[:, cut])
+        there = slice(lead + c, lead + c + STEP)
+        table = table_of(part[:, there] + peer[:, there], declared[:, cut])
         sum_a = sum_l = None
         for r in range(0, count, ROWS):
             rows = slice(r, r + ROWS)
             if year == 0:
-                asset = jnp.concatenate([states[0][0][rows, :]] * (STEP // 128), 1)
-                liab = jnp.concatenate([states[0][1][rows, :]] * (STEP // 128), 1)
+                years = member.shape[0]
+                asset = jnp.concatenate([wides[2 * years, rows, :]] * (STEP // 128), 1)
+                liab = jnp.concatenate([wides[2 * years + 1, rows, :]] * (STEP // 128), 1)
             else:
                 half = states[0][0].shape[1]
                 held = states[c // half]
                 at = slice(c % half, c % half + STEP)
                 asset, liab = held[0][rows, at], held[1][rows, at]
             asset, liab = advance(
-                None, c, STEP, table, member[rows, :], base[rows, :], guar[rows, :],
+                STEP, table, member[year, rows, :], wides[2 * year, rows, :], wides[2 * year + 1, rows, :],
                 draws[year, rows, first + c : first + c + STEP], asset, liab,
             )
             if last:
@@ -245,7 +273,7 @@
                 out_l[rows, cut] = liab
                 a_hi, a_lo = halves(asset)
                 l_hi, l_lo = halves(liab)
-                ma, ml = member_ta[:, rows], member_t[:, rows]
+                ma, ml = member_t[year + 1, :, rows], member_t[0, :, rows]
                 add_a = dot(ma, a_hi) + dot(ma, a_lo)
                 add_l = dot(ml, l_hi) + dot(ml, l_lo)
                 sum_a = add_a if sum_a is None else sum_a + add_a
@@ -296,71 +324,77 @@
     fund, kind, term = line(fund_of), line(product_type), line(term_years)
     asset, liab = line(asset_start), line(liab_start)
 
-    block = call(pack_body, shaped(2 * secs + 8, funds), [VMEM] * 7, "pack", 10**6, 10**5)(
-        loadings, holdings, sec_drift.reshape(1, secs), fund, term, asset, liab
-    )
-    fund, kind, term, asset, liab, block = lax.optimization_barrier(
-        (fund, kind, term, asset, liab, block)
-    )
-    block = block[None]
-    for o in reversed(far_offsets()):
-        block = jnp.concatenate([block, swap(block, o)])
-    blocks = [block] + [swap(block, o) for o in SQUARE]
-
-    wide = shaped(count, 128)
-    made = call(
+    sources = [loadings, holdings, sec_drift.reshape(1, secs), fund, term, asset, liab, kind]
+    sources += [base_lapse.reshape(1, -1), guarantee.reshape(1, -1)]
+    block, lines = call(
+        pack_body,
+        [shaped(2 * secs + 8, funds), shaped(8, count)],
+        [SMEM] + [HBM] * 10,
+        "pack",
+        10**6,
+        10**5,
+        scratch=[pltpu.VMEM(v.shape, v.dtype) for v in sources] + [pltpu.SemaphoreType.DMA((10,))],
+        limit=60,
+    )(me_ref, *sources)
+    far = far_offsets()
+    came = swap(block[None], far[-1])
+    member_t, member, wides, x_now, x_later, block = call(
         columns_body,
-        [shaped(funds, count, dtype=BF16)] * years
-        + [shaped(count, 2 * funds, dtype=BF16)] * years
-        + [wide] * (2 * years + 2),
-        [SMEM] * 2 + [VMEM] * 5,
+        [
+            shaped(years, funds, count, dtype=BF16),
+            shaped(years, count, 2 * funds, dtype=BF16),
+            shaped(2 * years + 2, count, 128),
+            shaped(2, *shocks.shape[1:], dtype=BF16),
+            shaped(years - 1, 2, *shocks.shape[1:], dtype=BF16),
+            shaped(1, *block.shape),
+        ],
+        [VMEM, VMEM, HBM],
         "columns",
         10**6,
         4 * 10**6,
-    )(base_lapse, guarantee, fund, kind, term, asset, liab)
-    member_t, member, base_w, guar_w = (made[i * years : (i + 1) * years] for i in range(4))
-    asset_w, liab_w = made[-2:]
+        scratch=[pltpu.VMEM(shocks.shape, F32), pltpu.SemaphoreType.DMA],
+        limit=8,
+    )(lines, block, shocks)
+    came, block = lax.optimization_barrier((came, block))
+    block = jnp.concatenate([block, came])
+    for o in reversed(far[:-1]):
+        block = jnp.concatenate([block, swap(block, o)])
+    blocks = [block] + [swap(block, o) for o in SQUARE]
 
     total = secs * n // 2
 
-    def returns(year, first, width):
+    def returns(year, first, width, blocks, xs):
         part, sums = call(
             functools.partial(returns_body, year, first, secs),
             [shaped(funds, width), shaped(8, funds)],
             [VMEM] * 5,
             "returns",
-            flops=2 * 6 * total * funds * width,
-            moved=4 * funds * width,
             scratch=[pltpu.VMEM((total, funds), BF16)] * 4,
-            limit=32,
-        )(*blocks, shocks)
+            limit=8 * max(1, min(6, total // 512)),
+        )(*blocks, xs)
         return part, sums
 
-    parts = [[returns(0, h * half, half) for h in range(2)]]
-    sums = parts[0][0][1]
-    parts[0] = [p for p, _ in parts[0]]
-    parts += [[returns(y, 0, paths)[0]] for y in range(1, years)]
-    peers = [[swap(p, 1) for p in ps] for ps in parts]
+    firsts = [returns(0, h * half, half, blocks, x_now) for h in range(2)]
+    sums = firsts[0][1]
+    part = [p for p, _ in firsts]
+    peer = [swap(p, 1) for p in part]
     other_sums = swap(sums, 1)
 
-    state = [(asset_w, liab_w)] * 2
+    state = None
     rates = []
     for year in range(years):
         last = year + 1 == years
         if year == 0:
             head = [sums, other_sums]
         else:
-            near = jnp.stack([own] + [swap(own, o) for o in SQUARE])
-            head = [near, swap(near, 1)]
+            near = [own] + [swap(own, o) for o in SQUARE]
+            head = near + [swap(v, 1) for v in near]
         shares = []
         for h in range(1 if last else 2):
             width = paths if last else half
             first = h * half
-            if year == 0:
-                pair = [parts[0][h], peers[0][h]]
-            else:
-                pair = [parts[year][0][:, first : first + width], peers[year][0][:, first : first + width]]
-            ins = [me_ref] + head + pair + [draws, member[year], base_w[year], guar_w[year]]
+            pair = [part[h], peer[h]] if year == 0 else [part, peer]
+            ins = [me_ref] + head + pair + [draws, member, wides]
             cost = dict(flops=2 * 2 * count * 2 * funds * width, moved=20 * count * width)
             if last:
                 ins += [v for s in state for v in s] + [v for rs in rates for v in rs]
@@ -371,7 +405,7 @@
                 scratch += [pltpu.VMEM((tiles, count, STEP), F32)] * 2
                 scratch += [pltpu.SemaphoreType.DMA((2, tiles))]
             else:
-                ins += list(state[h]) + [member_t[0], member_t[year + 1]]
+                ins += ([] if year == 0 else list(state[h])) + [member_t]
                 out = [shaped(count, width)] * 2
                 out += [shaped(2, 4, 2, slice_funds, width), shaped(owned, funds)]
                 out_specs = None
@@ -384,7 +418,7 @@
                     "year",
                     scratch=scratch,
                     out_specs=out_specs,
-                    limit=32,
+                    limit=16 if last else 8,
                     **cost,
                 )(*ins)
             )
@@ -394,16 +428,26 @@
         state = [(s[0], s[1]) for s in shares]
         rates.append([s[3] for s in shares])
         held = jnp.concatenate([s[2][0] + swap(s[2][1], 1) for s in shares], -1)
+        x_later, held = lax.optimization_barrier((x_later, held))
+        if year == 0:
+            blocks, held = lax.optimization_barrier((blocks, held))
+            others = [swap(b, 1) for b in blocks]
         arrived = [swap(held[i + 1], o) for i, o in enumerate(SQUARE)]
         totals = held[0] + arrived[0] + arrived[1] + arrived[2]
-        for o in far_offsets():
+        for o in far[:-1]:
             totals = totals + swap(totals, o)
-        here = lax.dynamic_slice_in_dim(
-            parts[year + 1][0], (me & 7) * slice_funds, slice_funds, 0
-        ) + lax.dynamic_slice_in_dim(
-            peers[year + 1][0], (me & 7) * slice_funds, slice_funds, 0
-        )
-        own = rate(totals[0] * (1.0 + here) / totals[1])
+        totals = [totals] + [swap(totals, o) for o in far[-1:]]
+        part = returns(year + 1, 0, paths, blocks, x_later)[0]
+        peer = returns(year + 1, 0, paths, others, x_later)[0]
+        own = call(
+            functools.partial(own_body, slice_funds),
+            shaped(slice_funds, paths),
+            [SMEM] + [VMEM] * (2 + len(totals)),
+            "own",
+            10**6,
+            10**6,
+            limit=2,
+        )(me_ref, part, peer, *totals)
 
 
 def solution(mesh):

time: 122 us -> 93.7 us (0.77)
  local copies, waits for them, and re-layouts: 20.9 us -> 3.16 us
  waiting for transfers between devices: 40.9 us -> 30.7 us
  Pallas kernels: 24.1 us -> 28.2 us
  other arithmetic: 3.01 us -> 0.29 us
  starting transfers between devices: 31.5 us -> 30.1 us
    unnamed x104 -> x9, local copies, waits for them, and re-layouts: 18.7 us -> 3.02 us
    ppermute x29 -> x37, waiting for transfers between devices: 40.9 us -> 30.7 us  [swap(): return lax.ppermute(x, 'pol', [(i, i ^ offset) for i in range(n)])]
    pallas_call x4 -> x6, Pallas kernels: 8.84 us -> 12.7 us  [returns(): call(functools.partial(returns_body, year, first, secs), [shaped(funds, w...]
    slice x2 -> x0, local copies, waits for them, and re-layouts: 2.13 us -> none  [the longest x1 1.07 us: local(): peers[year][0][:, first:first + width]]
    add x4 -> x0, other arithmetic: 2.02 us -> none  [the longest x2 1.02 us: rate(): return 0.01 + (jnp.maximum(x, 0.0) + jnp.log1p(jnp.exp(-jnp.abs(x)))) / 20.0]
    pallas_call x2 -> x4, Pallas kernels: 1.44 us -> 3.1 us  [the longest x1 1.82 us: local(): call(pack_body, [shaped(2 * secs + 8, funds), shaped(8, count)], [SMEM] +...]
    ppermute x29 -> x37, starting transfers between devices: 31.5 us -> 30.1 us  [swap(): return lax.ppermute(x, 'pol', [(i, i ^ offset) for i in range(n)])]
    pallas_call x5, Pallas kernels: 13.8 us -> 12.4 us  [local(): call(functools.partial(year_body, year, first, last, slice_funds), out, [...]
  transfers between devices with their start and end apart: 29 -> 37, of which waited for: 19 -> 20; matrix products, arithmetic and copies ran while one was open for 3% -> 0% of each run, Pallas kernels for 14% -> 21%
where the time goes in v3:
time: 93.7 us; the launch traced here: 93.5 us
  waiting for transfers between devices  30.7 us (33%)
  starting transfers between devices  30.1 us (32%)
  Pallas kernels  28.2 us (30%)
  local copies, waits for them, and re-layouts  3.16 us (3%)
  between operations  1.06 us (1%)
    ppermute x37, waiting for transfers between devices, swap(): return lax.ppermute(x, 'pol', [(i, i ^ offset) for i in range(n)])  30.7 us
    ppermute x37, starting transfers between devices, swap(): return lax.ppermute(x, 'pol', [(i, i ^ offset) for i in range(n)])  30.1 us
    pallas_call x6, Pallas kernels, returns(): call(functools.partial(returns_body, year, first, secs), [shaped(funds, w...  12.7 us
    pallas_call x5, Pallas kernels, local(): call(functools.partial(year_body, year, first, last, slice_funds), out, [...  12.4 us
    unnamed x9, local copies, waits for them, and re-layouts  3.02 us
  transfers between devices with their start and end apart: 37, of which 20 were waited for; matrix products, arithmetic and copies ran while one was open for 0% of the time, Pallas kernels for 21%

profile of v3, /device:TPU:0, one launch (start us, length us, event | category | flops | bytes accessed | tf_op | source)
XLA Modules:
  0.0 93.5 jit_solution(7126654138550450817)
XLA Ops:
  0.6 1.8 %pack.1 = (f32[136,128]{1,0:T(8,128)}, f32[8,512]{1,0:T(8,128)}) custom-call(s32[1]{0:T(128)} %bitcast.refs_0_.me, f32[64,128]{1,0:T(8,128)} %refs_1_.1, f32[64,128]{1,0:T(8,128)} %refs_2_.1, f32[1,64]{1,0:T(1,128)} %bitcast.63, s32[1,512]{1,0:T(1,128)} %bitcast.58, s32[1,512]{1,0:T(1,128)} %bitcast.59, f32[1,512]{1,0:T(1,128)} %bitcast.60, ...), custom_call_target="tpu_custom_call" | custom-call | flops 1000000 | bytes 100000 | tf_op jit(solution)/shard_map/pack/pallas_call | solution.py:329
  2.5 4.1 %collective-permute-start = (f32[1,136,128]{2,1,0:T(8,128)}, f32[1,136,128]{2,1,0:T(8,128)S(1)}, u32[]{:S(2)}, u32[]{:S(2)}) collective-permute-start(f32[1,136,128]{2,1,0:T(8,128)} %bitcast.57), channel_id=1, source_target_pairs={{0,8},{1,9},{2,10},{3,11},{4,12},{5,13},{6,14},{7,15},{8,0},{9,1},... | collective-permute-start | bytes 208904 | tf_op jit(solution)/shard_map/ppermute | solution.py:21
  6.6 1.4 %copy-done.1 = f32[3,128,1024]{2,1,0:T(8,128)S(1)} copy-done((f32[3,128,1024]{2,1,0:T(8,128)S(1)}, f32[3,128,1024]{2,1,0:T(8,128)}, u32[]{:S(2)}) %copy-start.1) | copy-done | bytes 1572888
  8.0 0.9 copy-done.2
  8.9 0.7 copy-done.3
  9.6 1.1 %columns.1 = (bf16[3,128,512]{2,1,0:T(8,128)(2,1)S(1)}, bf16[3,512,256]{2,1,0:T(8,128)(2,1)S(1)}, f32[8,512,128]{2,1,0:T(8,128)S(1)}, bf16[2,128,1024]{2,1,0:T(8...) custom-call(f32[8,512]{1,0:T(8,128)S(1)} %copy-done.3, f32[136,128]{1,0:T(8,128)S(1)} %copy-done.2, ...), custom_call_target="tpu_custom_call" | custom-call | flops 1000000 | bytes 4000000 | tf_op jit(solution)/shard_map/columns/pallas_call | solution.py:341
  10.8 1.6 %collective-permute-start.1 = (f32[2,136,128]{2,1,0:T(8,128)S(1)}, f32[2,136,128]{2,1,0:T(8,128)S(1)}, u32[]{:S(2)}, u32[]{:S(2)}) collective-permute-start(f32[2,136,128]{2,1,0:T(8,128)S(1)} %constant_dynamic-update-slice_fusion.refs_0_), channel_id=1, source_target_pairs={{0,2},{1,3},{2,0},{3,1},{4,6},{5,7},{6,4},{7,5},{8,10},{9,11},{10,... | collective-permute-start | bytes 417800 | tf_op jit(solution)/shard_map/ppermute | solution.py:21
  12.4 1.6 %collective-permute-start.2 = (f32[2,136,128]{2,1,0:T(8,128)S(1)}, f32[2,136,128]{2,1,0:T(8,128)S(1)}, u32[]{:S(2)}, u32[]{:S(2)}) collective-permute-start(f32[2,136,128]{2,1,0:T(8,128)S(1)} %constant_dynamic-update-slice_fusion.refs_0_), channel_id=1, source_target_pairs={{0,4},{1,5},{2,6},{3,7},{4,0},{5,1},{6,2},{7,3},{8,12},{9,13},{10,... | collective-permute-start | bytes 417800 | tf_op jit(solution)/shard_map/ppermute | solution.py:21
  13.9 0.4 collective-permute-start.3
  14.3 1.6 %collective-permute-done.1.refs_1_ = f32[2,136,128]{2,1,0:T(8,128)S(1)} collective-permute-done((f32[2,136,128]{2,1,0:T(8,128)S(1)}, f32[2,136,128]{2,1,0:T(8,128)S(1)}, u32[]{:S(2)}, u32[]{:S(2)}) %collective-permute-start.1) | collective-permute-done | bytes 139296 | tf_op jit(solution)/shard_map/ppermute | solution.py:21
  16.0 2.7 %collective-permute-done.2.refs_2_ = f32[2,136,128]{2,1,0:T(8,128)S(1)} collective-permute-done((f32[2,136,128]{2,1,0:T(8,128)S(1)}, f32[2,136,128]{2,1,0:T(8,128)S(1)}, u32[]{:S(2)}, u32[]{:S(2)}) %collective-permute-start.2) | collective-permute-done | bytes 139296 | tf_op jit(solution)/shard_map/ppermute | solution.py:21
  18.7 1.7 %collective-permute-done.3.refs_3_ = f32[2,136,128]{2,1,0:T(8,128)S(1)} collective-permute-done((f32[2,136,128]{2,1,0:T(8,128)S(1)}, f32[2,136,128]{2,1,0:T(8,128)S(1)}, u32[]{:S(2)}, u32[]{:S(2)}) %collective-permute-start.3) | collective-permute-done | bytes 139296 | tf_op jit(solution)/shard_map/ppermute | solution.py:21
  20.3 1.2 %returns.6 = (f32[128,512]{1,0:T(8,128)S(1)}, f32[8,128]{1,0:T(8,128)S(1)}) custom-call(f32[2,136,128]{2,1,0:T(8,128)S(1)} %constant_dynamic-update-slice_fusion.refs_0_, f32[2,136,128]{2,1,0:T(8,128)S(1)} %collective-permute-done.1.refs_1_, f32[2,136,128]{2,1,0:T(8,128)S(1)} %collective-permute-done.2.refs_2_, ...), custom_call_target="tpu_custom_call" | custom-call | tf_op jit(solution)/shard_map/returns/pallas_call | solution.py:367
  21.6 0.5 collective-permute-start.4
  22.1 1.6 %returns.7 = (f32[128,512]{1,0:T(8,128)S(1)}, f32[8,128]{1,0:T(8,128)}) custom-call(f32[2,136,128]{2,1,0:T(8,128)S(1)} %constant_dynamic-update-slice_fusion.refs_0_, f32[2,136,128]{2,1,0:T(8,128)S(1)} %collective-permute-done.1.refs_1_, f32[2,136,128]{2,1,0:T(8,128)S(1)} %collective-permute-done.2.refs_2_, ...), custom_call_target="tpu_custom_call" | custom-call | tf_op jit(solution)/shard_map/returns/pallas_call | solution.py:367
  23.7 0.1 collective-permute-start.7
  23.8 2.3 %year.5 = (f32[512,512]{1,0:T(8,128)S(1)}, f32[512,512]{1,0:T(8,128)S(1)}, f32[2,4,2,16,512]{4,3,2,1,0:T(8,128)S(1)}, f32[64,128]{1,0:T(8,128)S(1)}) custom-call(s32[1]{0:T(128)} %bitcast.refs_0_.me, f32[8,128]{1,0:T(8,128)S(1)} %get-tuple-element.55.refs_1_, f32[8,128]{1,0:T(8,128)S(1)} %collective-permute-done.4.refs_2_, ...), custom_call_target="tpu_custom_call" | custom-call | flops 268435456 | bytes 5242880 | tf_op jit(solution)/shard_map/year/pallas_call | solution.py:414
  26.1 0.5 collective-permute-start.6
  26.6 2.3 %year.6 = (f32[512,512]{1,0:T(8,128)S(1)}, f32[512,512]{1,0:T(8,128)S(1)}, f32[2,4,2,16,512]{4,3,2,1,0:T(8,128)S(1)}, f32[64,128]{1,0:T(8,128)S(1)}) custom-call(s32[1]{0:T(128)} %bitcast.refs_0_.me, f32[8,128]{1,0:T(8,128)S(1)} %get-tuple-element.55.refs_1_, f32[8,128]{1,0:T(8,128)S(1)} %collective-permute-done.4.refs_2_, ...), custom_call_target="tpu_custom_call" | custom-call | flops 268435456 | bytes 5242880 | tf_op jit(solution)/shard_map/year/pallas_call | solution.py:414
  28.9 0.1 collective-permute-start.8
  29.1 1.4 %collective-permute-done.8 = f32[4,2,16,512]{3,2,1,0:T(8,128)S(1)} collective-permute-done((f32[4,2,16,512]{3,2,1,0:T(8,128)S(1)}, f32[4,2,16,512]{3,2,1,0:T(8,128)S(1)}, u32[]{:S(2)}, u32[]{:S(2)}) %collective-permute-start.8) | collective-permute-done | bytes 262176 | tf_op jit(solution)/shard_map/ppermute | solution.py:21
  30.6 1.4 %collective-permute-start.13 = (f32[2,16,1024]{2,1,0:T(8,128)S(1)}, f32[2,16,1024]{2,1,0:T(8,128)S(1)}, u32[]{:S(2)}, u32[]{:S(2)}) collective-permute-start(f32[2,16,1024]{2,1,0:T(8,128)S(1)} %get-tuple-element.96), channel_id=1, source_target_pairs={{0,2},{1,3},{2,0},{3,1},{4,6},{5,7},{6,4},{7,5},{8,10},{9,11},{10,... | collective-permute-start | bytes 393224 | tf_op jit(solution)/shard_map/ppermute | solution.py:21
  32.0 1.6 %collective-permute-start.14 = (f32[2,16,1024]{2,1,0:T(8,128)S(1)}, f32[2,16,1024]{2,1,0:T(8,128)S(1)}, u32[]{:S(2)}, u32[]{:S(2)}) collective-permute-start(f32[2,16,1024]{2,1,0:T(8,128)S(1)} %get-tuple-element.98), channel_id=1, source_target_pairs={{0,4},{1,5},{2,6},{3,7},{4,0},{5,1},{6,2},{7,3},{8,12},{9,13},{10,... | collective-permute-start | bytes 393224 | tf_op jit(solution)/shard_map/ppermute | solution.py:21
  33.6 0.6 collective-permute-start.15
  34.2 0.5 collective-permute-start.11
  34.7 1.5 %collective-permute-done.13 = f32[2,16,1024]{2,1,0:T(8,128)S(1)} collective-permute-done((f32[2,16,1024]{2,1,0:T(8,128)S(1)}, f32[2,16,1024]{2,1,0:T(8,128)S(1)}, u32[]{:S(2)}, u32[]{:S(2)}) %collective-permute-start.13) | collective-permute-done | bytes 131104 | tf_op jit(solution)/shard_map/ppermute | solution.py:21
  36.2 2.1 %collective-permute-done.14 = f32[2,16,1024]{2,1,0:T(8,128)S(1)} collective-permute-done((f32[2,16,1024]{2,1,0:T(8,128)S(1)}, f32[2,16,1024]{2,1,0:T(8,128)S(1)}, u32[]{:S(2)}, u32[]{:S(2)}) %collective-permute-start.14) | collective-permute-done | bytes 131104 | tf_op jit(solution)/shard_map/ppermute | solution.py:21
  38.4 1.8 %collective-permute-done.15 = f32[2,16,1024]{2,1,0:T(8,128)S(1)} collective-permute-done((f32[2,16,1024]{2,1,0:T(8,128)S(1)}, f32[2,16,1024]{2,1,0:T(8,128)S(1)}, u32[]{:S(2)}, u32[]{:S(2)}) %collective-permute-start.15) | collective-permute-done | bytes 131104 | tf_op jit(solution)/shard_map/ppermute | solution.py:21
  40.3 2.1 %collective-permute-start.16 = (f32[2,16,1024]{2,1,0:T(8,128)S(1)}, f32[2,16,1024]{2,1,0:T(8,128)S(1)}, u32[]{:S(2)}, u32[]{:S(2)}) collective-permute-start(f32[2,16,1024]{2,1,0:T(8,128)S(1)} %fusion.3.refs_0_), channel_id=1, source_target_pairs={{0,8},{1,9},{2,10},{3,11},{4,12},{5,13},{6,14},{7,15},{8,0},{9,1},... | collective-permute-start | bytes 393224 | tf_op jit(solution)/shard_map/ppermute | solution.py:21
  42.3 2.5 %returns.8 = (f32[128,1024]{1,0:T(8,128)S(1)}, f32[8,128]{1,0:T(8,128)}) custom-call(f32[2,136,128]{2,1,0:T(8,128)S(1)} %constant_dynamic-update-slice_fusion.refs_0_, f32[2,136,128]{2,1,0:T(8,128)S(1)} %collective-permute-done.1.refs_1_, f32[2,136,128]{2,1,0:T(8,128)S(1)} %collective-permute-done.2.refs_2_, ...), custom_call_target="tpu_custom_call" | custom-call | tf_op jit(solution)/shard_map/returns/pallas_call | solution.py:367
  44.9 2.5 %returns.9 = (f32[128,1024]{1,0:T(8,128)S(1)}, f32[8,128]{1,0:T(8,128)}) custom-call(f32[2,136,128]{2,1,0:T(8,128)S(1)} %collective-permute-done.9.refs_0_, f32[2,136,128]{2,1,0:T(8,128)S(1)} %collective-permute-done.10.refs_1_, f32[2,136,128]{2,1,0:T(8,128)S(1)} %collective-permute-done.11.refs_2_, f32[2,136,128]{2,1,0:T(8,128)S(1)} %collective-permute-done.12.refs_3_, ...), custom_call_target="tpu_custom_call" | custom-call | tf_op jit(solution)/shard_map/returns/pallas_call | solution.py:367
  47.3 1.4 %collective-permute-done.16.refs_1_ = f32[2,16,1024]{2,1,0:T(8,128)S(1)} collective-permute-done((f32[2,16,1024]{2,1,0:T(8,128)S(1)}, f32[2,16,1024]{2,1,0:T(8,128)S(1)}, u32[]{:S(2)}, u32[]{:S(2)}) %collective-permute-start.16) | collective-permute-done | bytes 131104 | tf_op jit(solution)/shard_map/ppermute | solution.py:21
  48.8 0.1 own.2.refs_1_
  48.8 1.0 %collective-permute-start.17 = (f32[16,1024]{1,0:T(8,128)S(1)}, f32[16,1024]{1,0:T(8,128)S(1)}, u32[]{:S(2)}, u32[]{:S(2)}) collective-permute-start(f32[16,1024]{1,0:T(8,128)S(1)} %own.2.refs_1_), channel_id=1, source_target_pairs={{0,2},{1,3},{2,0},{3,1},{4,6},{5,7},{6,4},{7,5},{8,10},{9,11},{10,... | collective-permute-start | bytes 196616 | tf_op jit(solution)/shard_map/ppermute | solution.py:21
  49.9 0.9 collective-permute-start.18
  50.7 1.7 %collective-permute-start.19 = (f32[16,1024]{1,0:T(8,128)S(1)}, f32[16,1024]{1,0:T(8,128)S(1)}, u32[]{:S(2)}, u32[]{:S(2)}) collective-permute-start(f32[16,1024]{1,0:T(8,128)S(1)} %own.2.refs_1_), channel_id=1, source_target_pairs={{0,6},{1,7},{2,4},{3,5},{4,2},{5,3},{6,0},{7,1},{8,14},{9,15},{10,... | collective-permute-start | bytes 196616 | tf_op jit(solution)/shard_map/ppermute | solution.py:21
  52.4 1.5 %collective-permute-done.17.refs_2_ = f32[16,1024]{1,0:T(8,128)S(1)} collective-permute-done((f32[16,1024]{1,0:T(8,128)S(1)}, f32[16,1024]{1,0:T(8,128)S(1)}, u32[]{:S(2)}, u32[]{:S(2)}) %collective-permute-start.17) | collective-permute-done | bytes 65568 | tf_op jit(solution)/shard_map/ppermute | solution.py:21
  53.9 0.3 collective-permute-done.18.refs_3_
  54.1 0.3 collective-permute-start.22
  54.4 1.5 %collective-permute-done.19.refs_4_ = f32[16,1024]{1,0:T(8,128)S(1)} collective-permute-done((f32[16,1024]{1,0:T(8,128)S(1)}, f32[16,1024]{1,0:T(8,128)S(1)}, u32[]{:S(2)}, u32[]{:S(2)}) %collective-permute-start.19) | collective-permute-done | bytes 65568 | tf_op jit(solution)/shard_map/ppermute | solution.py:21
  55.9 1.2 %collective-permute-done.23.refs_8_ = f32[16,1024]{1,0:T(8,128)S(1)} collective-permute-done((f32[16,1024]{1,0:T(8,128)S(1)}, f32[16,1024]{1,0:T(8,128)S(1)}, u32[]{:S(2)}, u32[]{:S(2)}) %collective-permute-start.23) | collective-permute-done | bytes 65568 | tf_op jit(solution)/shard_map/ppermute | solution.py:21
  57.1 2.2 %year.7 = (f32[512,512]{1,0:T(8,128)S(1)}, f32[512,512]{1,0:T(8,128)S(1)}, f32[2,4,2,16,512]{4,3,2,1,0:T(8,128)S(1)}, f32[64,128]{1,0:T(8,128)S(1)}) custom-call(s32[1]{0:T(128)} %bitcast.refs_0_.me, f32[16,1024]{1,0:T(8,128)S(1)} %own.2.refs_1_, f32[16,1024]{1,0:T(8,128)S(1)} %collective-permute-done.17.refs_2_, ...), custom_call_target="tpu_custom_call" | custom-call | flops 268435456 | bytes 5242880 | tf_op jit(solution)/shard_map/year/pallas_call | solution.py:414
  59.4 0.2 collective-permute-start.24
  59.6 2.0 %year.8 = (f32[512,512]{1,0:T(8,128)S(1)}, f32[512,512]{1,0:T(8,128)S(1)}, f32[2,4,2,16,512]{4,3,2,1,0:T(8,128)S(1)}, f32[64,128]{1,0:T(8,128)S(1)}) custom-call(s32[1]{0:T(128)} %bitcast.refs_0_.me, f32[16,1024]{1,0:T(8,128)S(1)} %own.2.refs_1_, f32[16,1024]{1,0:T(8,128)S(1)} %collective-permute-done.17.refs_2_, ...), custom_call_target="tpu_custom_call" | custom-call | flops 268435456 | bytes 5242880 | tf_op jit(solution)/shard_map/year/pallas_call | solution.py:414
  61.7 0.4 collective-permute-start.25
  62.1 1.1 %collective-permute-done.25 = f32[4,2,16,512]{3,2,1,0:T(8,128)S(1)} collective-permute-done((f32[4,2,16,512]{3,2,1,0:T(8,128)S(1)}, f32[4,2,16,512]{3,2,1,0:T(8,128)S(1)}, u32[]{:S(2)}, u32[]{:S(2)}) %collective-permute-start.25) | collective-permute-done | bytes 262176 | tf_op jit(solution)/shard_map/ppermute | solution.py:21
  63.4 0.6 collective-permute-start.26
  64.0 1.7 %collective-permute-start.27 = (f32[2,16,1024]{2,1,0:T(8,128)S(1)}, f32[2,16,1024]{2,1,0:T(8,128)S(1)}, u32[]{:S(2)}, u32[]{:S(2)}) collective-permute-start(f32[2,16,1024]{2,1,0:T(8,128)S(1)} %get-tuple-element.95), channel_id=1, source_target_pairs={{0,4},{1,5},{2,6},{3,7},{4,0},{5,1},{6,2},{7,3},{8,12},{9,13},{10,... | collective-permute-start | bytes 393224 | tf_op jit(solution)/shard_map/ppermute | solution.py:21
  65.7 1.3 %collective-permute-start.28 = (f32[2,16,1024]{2,1,0:T(8,128)S(1)}, f32[2,16,1024]{2,1,0:T(8,128)S(1)}, u32[]{:S(2)}, u32[]{:S(2)}) collective-permute-start(f32[2,16,1024]{2,1,0:T(8,128)S(1)} %get-tuple-element.94), channel_id=1, source_target_pairs={{0,6},{1,7},{2,4},{3,5},{4,2},{5,3},{6,0},{7,1},{8,14},{9,15},{10,... | collective-permute-start | bytes 393224 | tf_op jit(solution)/shard_map/ppermute | solution.py:21
  66.9 2.3 %collective-permute-done.26 = f32[2,16,1024]{2,1,0:T(8,128)S(1)} collective-permute-done((f32[2,16,1024]{2,1,0:T(8,128)S(1)}, f32[2,16,1024]{2,1,0:T(8,128)S(1)}, u32[]{:S(2)}, u32[]{:S(2)}) %collective-permute-start.26) | collective-permute-done | bytes 131104 | tf_op jit(solution)/shard_map/ppermute | solution.py:21
  69.2 1.1 %collective-permute-done.27 = f32[2,16,1024]{2,1,0:T(8,128)S(1)} collective-permute-done((f32[2,16,1024]{2,1,0:T(8,128)S(1)}, f32[2,16,1024]{2,1,0:T(8,128)S(1)}, u32[]{:S(2)}, u32[]{:S(2)}) %collective-permute-start.27) | collective-permute-done | bytes 131104 | tf_op jit(solution)/shard_map/ppermute | solution.py:21
  70.3 2.9 %collective-permute-done.28 = f32[2,16,1024]{2,1,0:T(8,128)S(1)} collective-permute-done((f32[2,16,1024]{2,1,0:T(8,128)S(1)}, f32[2,16,1024]{2,1,0:T(8,128)S(1)}, u32[]{:S(2)}, u32[]{:S(2)}) %collective-permute-start.28) | collective-permute-done | bytes 131104 | tf_op jit(solution)/shard_map/ppermute | solution.py:21
  73.2 2.9 %collective-permute-start.29 = (f32[2,16,1024]{2,1,0:T(8,128)S(1)}, f32[2,16,1024]{2,1,0:T(8,128)S(1)}, u32[]{:S(2)}, u32[]{:S(2)}) collective-permute-start(f32[2,16,1024]{2,1,0:T(8,128)S(1)} %fusion.1.refs_0_), channel_id=1, source_target_pairs={{0,8},{1,9},{2,10},{3,11},{4,12},{5,13},{6,14},{7,15},{8,0},{9,1},... | collective-permute-start | bytes 393224 | tf_op jit(solution)/shard_map/ppermute | solution.py:21
  76.1 2.5 %returns.10 = (f32[128,1024]{1,0:T(8,128)S(1)}, f32[8,128]{1,0:T(8,128)}) custom-call(f32[2,136,128]{2,1,0:T(8,128)S(1)} %constant_dynamic-update-slice_fusion.refs_0_, f32[2,136,128]{2,1,0:T(8,128)S(1)} %collective-permute-done.1.refs_1_, f32[2,136,128]{2,1,0:T(8,128)S(1)} %collective-permute-done.2.refs_2_, ...), custom_call_target="tpu_custom_call" | custom-call | tf_op jit(solution)/shard_map/returns/pallas_call | solution.py:367
  78.6 2.5 %returns.11 = (f32[128,1024]{1,0:T(8,128)S(1)}, f32[8,128]{1,0:T(8,128)}) custom-call(f32[2,136,128]{2,1,0:T(8,128)S(1)} %collective-permute-done.9.refs_0_, f32[2,136,128]{2,1,0:T(8,128)S(1)} %collective-permute-done.10.refs_1_, f32[2,136,128]{2,1,0:T(8,128)S(1)} %collective-permute-done.11.refs_2_, f32[2,136,128]{2,1,0:T(8,128)S(1)} %collective-permute-done.12.refs_3_, ...), custom_call_target="tpu_custom_call" | custom-call | tf_op jit(solution)/shard_map/returns/pallas_call | solution.py:367
  81.1 0.7 collective-permute-done.29.refs_1_
  81.8 0.1 own.3.refs_1_
  81.9 0.7 collective-permute-start.30
  82.6 2.9 %collective-permute-start.32 = (f32[16,1024]{1,0:T(8,128)S(1)}, f32[16,1024]{1,0:T(8,128)S(1)}, u32[]{:S(2)}, u32[]{:S(2)}) collective-permute-start(f32[16,1024]{1,0:T(8,128)S(1)} %own.3.refs_1_), channel_id=1, source_target_pairs={{0,6},{1,7},{2,4},{3,5},{4,2},{5,3},{6,0},{7,1},{8,14},{9,15},{10,... | collective-permute-start | bytes 196616 | tf_op jit(solution)/shard_map/ppermute | solution.py:21
  85.5 1.5 %collective-permute-done.30.refs_2_ = f32[16,1024]{1,0:T(8,128)S(1)} collective-permute-done((f32[16,1024]{1,0:T(8,128)S(1)}, f32[16,1024]{1,0:T(8,128)S(1)}, u32[]{:S(2)}, u32[]{:S(2)}) %collective-permute-start.30) | collective-permute-done | bytes 65568 | tf_op jit(solution)/shard_map/ppermute | solution.py:21
  87.0 0.5 collective-permute-start.35
  87.5 0.9 %collective-permute-done.32.refs_4_ = f32[16,1024]{1,0:T(8,128)S(1)} collective-permute-done((f32[16,1024]{1,0:T(8,128)S(1)}, f32[16,1024]{1,0:T(8,128)S(1)}, u32[]{:S(2)}, u32[]{:S(2)}) %collective-permute-start.32) | collective-permute-done | bytes 65568 | tf_op jit(solution)/shard_map/ppermute | solution.py:21
  88.4 1.2 %collective-permute-done.36.refs_8_ = f32[16,1024]{1,0:T(8,128)S(1)} collective-permute-done((f32[16,1024]{1,0:T(8,128)S(1)}, f32[16,1024]{1,0:T(8,128)S(1)}, u32[]{:S(2)}, u32[]{:S(2)}) %collective-permute-start.36) | collective-permute-done | bytes 65568 | tf_op jit(solution)/shard_map/ppermute | solution.py:21
  89.7 3.6 %year.9 = (f32[512,1024]{1,0:T(8,128)}, f32[512,1024]{1,0:T(8,128)}, f32[3,64,128]{2,1,0:T(8,128)}) custom-call(s32[1]{0:T(128)} %bitcast.refs_0_.me, f32[16,1024]{1,0:T(8,128)S(1)} %own.3.refs_1_, f32[16,1024]{1,0:T(8,128)S(1)} %collective-permute-done.30.refs_2_, f32[16,1024]{1,0:T(8,128)S(1)} %collective-permute-done.31.refs_3_, ...), custom_call_target="tpu_custom_call" | custom-call | flops 536870912 | bytes 10485760 | tf_op jit(solution)/shard_map/year/pallas_call | solution.py:414
  (49 shorter events, 0.6 us)
Async XLA Ops:
  0.6 23.2 %copy-start = (bf16[512,3,1024]{2,0,1:T(8,128)(2,1)S(1)}, bf16[512,3,1024]{2,0,1:T(8,128)(2,1)}, u32[]{:S(2)}) copy-start(bf16[512,3,1024]{2,0,1:T(8,128)(2,1)} %param.23) | copy-start | bytes 9437188
  2.5 8.3 %collective-permute-start = (f32[1,136,128]{2,1,0:T(8,128)}, f32[1,136,128]{2,1,0:T(8,128)S(1)}, u32[]{:S(2)}, u32[]{:S(2)}) collective-permute-start(f32[1,136,128]{2,1,0:T(8,128)} %bitcast.57), channel_id=1, source_target_pairs={{0,8},{1,9},{2,10},{3,11},{4,12},{5,13},{6,14},{7,15},{8,0},{9,1},... | collective-permute-start | bytes 208904 | tf_op jit(solution)/shard_map/ppermute | solution.py:21
  6.6 1.4 %copy-start.1 = (f32[3,128,1024]{2,1,0:T(8,128)S(1)}, f32[3,128,1024]{2,1,0:T(8,128)}, u32[]{:S(2)}) copy-start(f32[3,128,1024]{2,1,0:T(8,128)} %shocks.1) | copy-start | bytes 4718596
  8.0 0.9 copy-start.2
  8.9 0.7 copy-start.3
  10.8 5.2 %collective-permute-start.1 = (f32[2,136,128]{2,1,0:T(8,128)S(1)}, f32[2,136,128]{2,1,0:T(8,128)S(1)}, u32[]{:S(2)}, u32[]{:S(2)}) collective-permute-start(f32[2,136,128]{2,1,0:T(8,128)S(1)} %constant_dynamic-update-slice_fusion.refs_0_), channel_id=1, source_target_pairs={{0,2},{1,3},{2,0},{3,1},{4,6},{5,7},{6,4},{7,5},{8,10},{9,11},{10,... | collective-permute-start | bytes 417800 | tf_op jit(solution)/shard_map/ppermute | solution.py:21
  12.4 6.3 %collective-permute-start.2 = (f32[2,136,128]{2,1,0:T(8,128)S(1)}, f32[2,136,128]{2,1,0:T(8,128)S(1)}, u32[]{:S(2)}, u32[]{:S(2)}) collective-permute-start(f32[2,136,128]{2,1,0:T(8,128)S(1)} %constant_dynamic-update-slice_fusion.refs_0_), channel_id=1, source_target_pairs={{0,4},{1,5},{2,6},{3,7},{4,0},{5,1},{6,2},{7,3},{8,12},{9,13},{10,... | collective-permute-start | bytes 417800 | tf_op jit(solution)/shard_map/ppermute | solution.py:21
  13.9 6.4 %collective-permute-start.3 = (f32[2,136,128]{2,1,0:T(8,128)S(1)}, f32[2,136,128]{2,1,0:T(8,128)S(1)}, u32[]{:S(2)}, u32[]{:S(2)}) collective-permute-start(f32[2,136,128]{2,1,0:T(8,128)S(1)} %constant_dynamic-update-slice_fusion.refs_0_), channel_id=1, source_target_pairs={{0,6},{1,7},{2,4},{3,5},{4,2},{5,3},{6,0},{7,1},{8,14},{9,15},{10,... | collective-permute-start | bytes 417800 | tf_op jit(solution)/shard_map/ppermute | solution.py:21
  21.5 2.3 %collective-permute-start.5 = (f32[128,512]{1,0:T(8,128)S(1)}, f32[128,512]{1,0:T(8,128)S(1)}, u32[]{:S(2)}, u32[]{:S(2)}) collective-permute-start(f32[128,512]{1,0:T(8,128)S(1)} %get-tuple-element.56.refs_3_), channel_id=1, source_target_pairs={{0,1},{1,0},{2,3},{3,2},{4,5},{5,4},{6,7},{7,6},{8,9},{9,8},{10,11... | collective-permute-start | bytes 786440 | tf_op jit(solution)/shard_map/ppermute | solution.py:21
  21.6 2.2 %collective-permute-start.4 = (f32[8,128]{1,0:T(8,128)S(1)}, f32[8,128]{1,0:T(8,128)S(1)}, u32[]{:S(2)}, u32[]{:S(2)}) collective-permute-start(f32[8,128]{1,0:T(8,128)S(1)} %get-tuple-element.55.refs_1_), channel_id=1, source_target_pairs={{0,1},{1,0},{2,3},{3,2},{4,5},{5,4},{6,7},{7,6},{8,9},{9,8},{10,11... | collective-permute-start | bytes 12296 | tf_op jit(solution)/shard_map/ppermute | solution.py:21
  23.7 2.9 %collective-permute-start.7 = (f32[128,512]{1,0:T(8,128)S(1)}, f32[128,512]{1,0:T(8,128)S(1)}, u32[]{:S(2)}, u32[]{:S(2)}) collective-permute-start(f32[128,512]{1,0:T(8,128)S(1)} %get-tuple-element.61.refs_3_), channel_id=1, source_target_pairs={{0,1},{1,0},{2,3},{3,2},{4,5},{5,4},{6,7},{7,6},{8,9},{9,8},{10,11... | collective-permute-start | bytes 786440 | tf_op jit(solution)/shard_map/ppermute | solution.py:21
  26.1 2.9 %collective-permute-start.6 = (f32[4,2,16,512]{3,2,1,0:T(8,128)S(1)}, f32[4,2,16,512]{3,2,1,0:T(8,128)S(1)}, u32[]{:S(2)}, u32[]{:S(2)}) collective-permute-start(f32[4,2,16,512]{3,2,1,0:T(8,128)S(1)} %slice_bitcast_fusion.3), channel_id=1, source_target_pairs={{0,1},{1,0},{2,3},{3,2},{4,5},{5,4},{6,7},{7,6},{8,9},{9,8},{10,11... | collective-permute-start | bytes 786440 | tf_op jit(solution)/shard_map/ppermute | solution.py:21
  28.9 1.6 %collective-permute-start.8 = (f32[4,2,16,512]{3,2,1,0:T(8,128)S(1)}, f32[4,2,16,512]{3,2,1,0:T(8,128)S(1)}, u32[]{:S(2)}, u32[]{:S(2)}) collective-permute-start(f32[4,2,16,512]{3,2,1,0:T(8,128)S(1)} %slice_bitcast_fusion.2), channel_id=1, source_target_pairs={{0,1},{1,0},{2,3},{3,2},{4,5},{5,4},{6,7},{7,6},{8,9},{9,8},{10,11... | collective-permute-start | bytes 786440 | tf_op jit(solution)/shard_map/ppermute | solution.py:21
  30.6 5.6 %collective-permute-start.13 = (f32[2,16,1024]{2,1,0:T(8,128)S(1)}, f32[2,16,1024]{2,1,0:T(8,128)S(1)}, u32[]{:S(2)}, u32[]{:S(2)}) collective-permute-start(f32[2,16,1024]{2,1,0:T(8,128)S(1)} %get-tuple-element.96), channel_id=1, source_target_pairs={{0,2},{1,3},{2,0},{3,1},{4,6},{5,7},{6,4},{7,5},{8,10},{9,11},{10,... | collective-permute-start | bytes 393224 | tf_op jit(solution)/shard_map/ppermute | solution.py:21
  32.0 6.4 %collective-permute-start.14 = (f32[2,16,1024]{2,1,0:T(8,128)S(1)}, f32[2,16,1024]{2,1,0:T(8,128)S(1)}, u32[]{:S(2)}, u32[]{:S(2)}) collective-permute-start(f32[2,16,1024]{2,1,0:T(8,128)S(1)} %get-tuple-element.98), channel_id=1, source_target_pairs={{0,4},{1,5},{2,6},{3,7},{4,0},{5,1},{6,2},{7,3},{8,12},{9,13},{10,... | collective-permute-start | bytes 393224 | tf_op jit(solution)/shard_map/ppermute | solution.py:21
  33.6 6.7 %collective-permute-start.15 = (f32[2,16,1024]{2,1,0:T(8,128)S(1)}, f32[2,16,1024]{2,1,0:T(8,128)S(1)}, u32[]{:S(2)}, u32[]{:S(2)}) collective-permute-start(f32[2,16,1024]{2,1,0:T(8,128)S(1)} %get-tuple-element.97), channel_id=1, source_target_pairs={{0,6},{1,7},{2,4},{3,5},{4,2},{5,3},{6,0},{7,1},{8,14},{9,15},{10,... | collective-permute-start | bytes 393224 | tf_op jit(solution)/shard_map/ppermute | solution.py:21
  34.2 10.7 %collective-permute-start.10 = (f32[2,136,128]{2,1,0:T(8,128)S(1)}, f32[2,136,128]{2,1,0:T(8,128)S(1)}, u32[]{:S(2)}, u32[]{:S(2)}) collective-permute-start(f32[2,136,128]{2,1,0:T(8,128)S(1)} %collective-permute-done.1.refs_1_), channel_id=1, source_target_pairs={{0,1},{1,0},{2,3},{3,2},{4,5},{5,4},{6,7},{7,6},{8,9},{9,8},{10,11... | collective-permute-start | bytes 417800 | tf_op jit(solution)/shard_map/ppermute | solution.py:21
  34.2 10.7 %collective-permute-start.11 = (f32[2,136,128]{2,1,0:T(8,128)S(1)}, f32[2,136,128]{2,1,0:T(8,128)S(1)}, u32[]{:S(2)}, u32[]{:S(2)}) collective-permute-start(f32[2,136,128]{2,1,0:T(8,128)S(1)} %collective-permute-done.2.refs_2_), channel_id=1, source_target_pairs={{0,1},{1,0},{2,3},{3,2},{4,5},{5,4},{6,7},{7,6},{8,9},{9,8},{10,11... | collective-permute-start | bytes 417800 | tf_op jit(solution)/shard_map/ppermute | solution.py:21
  36.2 8.6 %collective-permute-start.12 = (f32[2,136,128]{2,1,0:T(8,128)S(1)}, f32[2,136,128]{2,1,0:T(8,128)S(1)}, u32[]{:S(2)}, u32[]{:S(2)}) collective-permute-start(f32[2,136,128]{2,1,0:T(8,128)S(1)} %collective-permute-done.3.refs_3_), channel_id=1, source_target_pairs={{0,1},{1,0},{2,3},{3,2},{4,5},{5,4},{6,7},{7,6},{8,9},{9,8},{10,11... | collective-permute-start | bytes 417800 | tf_op jit(solution)/shard_map/ppermute | solution.py:21
  38.4 6.5 %collective-permute-start.9 = (f32[2,136,128]{2,1,0:T(8,128)S(1)}, f32[2,136,128]{2,1,0:T(8,128)S(1)}, u32[]{:S(2)}, u32[]{:S(2)}) collective-permute-start(f32[2,136,128]{2,1,0:T(8,128)S(1)} %constant_dynamic-update-slice_fusion.refs_0_), channel_id=1, source_target_pairs={{0,1},{1,0},{2,3},{3,2},{4,5},{5,4},{6,7},{7,6},{8,9},{9,8},{10,11... | collective-permute-start | bytes 417800 | tf_op jit(solution)/shard_map/ppermute | solution.py:21
  40.3 8.5 %collective-permute-start.16 = (f32[2,16,1024]{2,1,0:T(8,128)S(1)}, f32[2,16,1024]{2,1,0:T(8,128)S(1)}, u32[]{:S(2)}, u32[]{:S(2)}) collective-permute-start(f32[2,16,1024]{2,1,0:T(8,128)S(1)} %fusion.3.refs_0_), channel_id=1, source_target_pairs={{0,8},{1,9},{2,10},{3,11},{4,12},{5,13},{6,14},{7,15},{8,0},{9,1},... | collective-permute-start | bytes 393224 | tf_op jit(solution)/shard_map/ppermute | solution.py:21
  48.8 5.0 %collective-permute-start.17 = (f32[16,1024]{1,0:T(8,128)S(1)}, f32[16,1024]{1,0:T(8,128)S(1)}, u32[]{:S(2)}, u32[]{:S(2)}) collective-permute-start(f32[16,1024]{1,0:T(8,128)S(1)} %own.2.refs_1_), channel_id=1, source_target_pairs={{0,2},{1,3},{2,0},{3,1},{4,6},{5,7},{6,4},{7,5},{8,10},{9,11},{10,... | collective-permute-start | bytes 196616 | tf_op jit(solution)/shard_map/ppermute | solution.py:21
  49.9 4.3 %collective-permute-start.18 = (f32[16,1024]{1,0:T(8,128)S(1)}, f32[16,1024]{1,0:T(8,128)S(1)}, u32[]{:S(2)}, u32[]{:S(2)}) collective-permute-start(f32[16,1024]{1,0:T(8,128)S(1)} %own.2.refs_1_), channel_id=1, source_target_pairs={{0,4},{1,5},{2,6},{3,7},{4,0},{5,1},{6,2},{7,3},{8,12},{9,13},{10,... | collective-permute-start | bytes 196616 | tf_op jit(solution)/shard_map/ppermute | solution.py:21
  50.7 5.2 %collective-permute-start.19 = (f32[16,1024]{1,0:T(8,128)S(1)}, f32[16,1024]{1,0:T(8,128)S(1)}, u32[]{:S(2)}, u32[]{:S(2)}) collective-permute-start(f32[16,1024]{1,0:T(8,128)S(1)} %own.2.refs_1_), channel_id=1, source_target_pairs={{0,6},{1,7},{2,4},{3,5},{4,2},{5,3},{6,0},{7,1},{8,14},{9,15},{10,... | collective-permute-start | bytes 196616 | tf_op jit(solution)/shard_map/ppermute | solution.py:21
  52.4 3.5 %collective-permute-start.20 = (f32[16,1024]{1,0:T(8,128)S(1)}, f32[16,1024]{1,0:T(8,128)S(1)}, u32[]{:S(2)}, u32[]{:S(2)}) collective-permute-start(f32[16,1024]{1,0:T(8,128)S(1)} %own.2.refs_1_), channel_id=1, source_target_pairs={{0,1},{1,0},{2,3},{3,2},{4,5},{5,4},{6,7},{7,6},{8,9},{9,8},{10,11... | collective-permute-start | bytes 196616 | tf_op jit(solution)/shard_map/ppermute | solution.py:21
  53.9 2.0 %collective-permute-start.21 = (f32[16,1024]{1,0:T(8,128)S(1)}, f32[16,1024]{1,0:T(8,128)S(1)}, u32[]{:S(2)}, u32[]{:S(2)}) collective-permute-start(f32[16,1024]{1,0:T(8,128)S(1)} %collective-permute-done.17.refs_2_), channel_id=1, source_target_pairs={{0,1},{1,0},{2,3},{3,2},{4,5},{5,4},{6,7},{7,6},{8,9},{9,8},{10,11... | collective-permute-start | bytes 196616 | tf_op jit(solution)/shard_map/ppermute | solution.py:21
  54.1 1.8 %collective-permute-start.22 = (f32[16,1024]{1,0:T(8,128)S(1)}, f32[16,1024]{1,0:T(8,128)S(1)}, u32[]{:S(2)}, u32[]{:S(2)}) collective-permute-start(f32[16,1024]{1,0:T(8,128)S(1)} %collective-permute-done.18.refs_3_), channel_id=1, source_target_pairs={{0,1},{1,0},{2,3},{3,2},{4,5},{5,4},{6,7},{7,6},{8,9},{9,8},{10,11... | collective-permute-start | bytes 196616 | tf_op jit(solution)/shard_map/ppermute | solution.py:21
  55.9 1.3 %collective-permute-start.23 = (f32[16,1024]{1,0:T(8,128)S(1)}, f32[16,1024]{1,0:T(8,128)S(1)}, u32[]{:S(2)}, u32[]{:S(2)}) collective-permute-start(f32[16,1024]{1,0:T(8,128)S(1)} %collective-permute-done.19.refs_4_), channel_id=1, source_target_pairs={{0,1},{1,0},{2,3},{3,2},{4,5},{5,4},{6,7},{7,6},{8,9},{9,8},{10,11... | collective-permute-start | bytes 196616 | tf_op jit(solution)/shard_map/ppermute | solution.py:21
  59.4 2.7 %collective-permute-start.24 = (f32[4,2,16,512]{3,2,1,0:T(8,128)S(1)}, f32[4,2,16,512]{3,2,1,0:T(8,128)S(1)}, u32[]{:S(2)}, u32[]{:S(2)}) collective-permute-start(f32[4,2,16,512]{3,2,1,0:T(8,128)S(1)} %slice_bitcast_fusion.1), channel_id=1, source_target_pairs={{0,1},{1,0},{2,3},{3,2},{4,5},{5,4},{6,7},{7,6},{8,9},{9,8},{10,11... | collective-permute-start | bytes 786440 | tf_op jit(solution)/shard_map/ppermute | solution.py:21
  61.7 1.6 %collective-permute-start.25 = (f32[4,2,16,512]{3,2,1,0:T(8,128)S(1)}, f32[4,2,16,512]{3,2,1,0:T(8,128)S(1)}, u32[]{:S(2)}, u32[]{:S(2)}) collective-permute-start(f32[4,2,16,512]{3,2,1,0:T(8,128)S(1)} %slice_bitcast_fusion), channel_id=1, source_target_pairs={{0,1},{1,0},{2,3},{3,2},{4,5},{5,4},{6,7},{7,6},{8,9},{9,8},{10,11... | collective-permute-start | bytes 786440 | tf_op jit(solution)/shard_map/ppermute | solution.py:21
  63.4 5.8 %collective-permute-start.26 = (f32[2,16,1024]{2,1,0:T(8,128)S(1)}, f32[2,16,1024]{2,1,0:T(8,128)S(1)}, u32[]{:S(2)}, u32[]{:S(2)}) collective-permute-start(f32[2,16,1024]{2,1,0:T(8,128)S(1)} %get-tuple-element.93), channel_id=1, source_target_pairs={{0,2},{1,3},{2,0},{3,1},{4,6},{5,7},{6,4},{7,5},{8,10},{9,11},{10,... | collective-permute-start | bytes 393224 | tf_op jit(solution)/shard_map/ppermute | solution.py:21
  64.0 6.4 %collective-permute-start.27 = (f32[2,16,1024]{2,1,0:T(8,128)S(1)}, f32[2,16,1024]{2,1,0:T(8,128)S(1)}, u32[]{:S(2)}, u32[]{:S(2)}) collective-permute-start(f32[2,16,1024]{2,1,0:T(8,128)S(1)} %get-tuple-element.95), channel_id=1, source_target_pairs={{0,4},{1,5},{2,6},{3,7},{4,0},{5,1},{6,2},{7,3},{8,12},{9,13},{10,... | collective-permute-start | bytes 393224 | tf_op jit(solution)/shard_map/ppermute | solution.py:21
  65.7 7.5 %collective-permute-start.28 = (f32[2,16,1024]{2,1,0:T(8,128)S(1)}, f32[2,16,1024]{2,1,0:T(8,128)S(1)}, u32[]{:S(2)}, u32[]{:S(2)}) collective-permute-start(f32[2,16,1024]{2,1,0:T(8,128)S(1)} %get-tuple-element.94), channel_id=1, source_target_pairs={{0,6},{1,7},{2,4},{3,5},{4,2},{5,3},{6,0},{7,1},{8,14},{9,15},{10,... | collective-permute-start | bytes 393224 | tf_op jit(solution)/shard_map/ppermute | solution.py:21
  73.2 8.6 %collective-permute-start.29 = (f32[2,16,1024]{2,1,0:T(8,128)S(1)}, f32[2,16,1024]{2,1,0:T(8,128)S(1)}, u32[]{:S(2)}, u32[]{:S(2)}) collective-permute-start(f32[2,16,1024]{2,1,0:T(8,128)S(1)} %fusion.1.refs_0_), channel_id=1, source_target_pairs={{0,8},{1,9},{2,10},{3,11},{4,12},{5,13},{6,14},{7,15},{8,0},{9,1},... | collective-permute-start | bytes 393224 | tf_op jit(solution)/shard_map/ppermute | solution.py:21
  81.9 5.0 %collective-permute-start.30 = (f32[16,1024]{1,0:T(8,128)S(1)}, f32[16,1024]{1,0:T(8,128)S(1)}, u32[]{:S(2)}, u32[]{:S(2)}) collective-permute-start(f32[16,1024]{1,0:T(8,128)S(1)} %own.3.refs_1_), channel_id=1, source_target_pairs={{0,2},{1,3},{2,0},{3,1},{4,6},{5,7},{6,4},{7,5},{8,10},{9,11},{10,... | collective-permute-start | bytes 196616 | tf_op jit(solution)/shard_map/ppermute | solution.py:21
  82.6 4.4 %collective-permute-start.31 = (f32[16,1024]{1,0:T(8,128)S(1)}, f32[16,1024]{1,0:T(8,128)S(1)}, u32[]{:S(2)}, u32[]{:S(2)}) collective-permute-start(f32[16,1024]{1,0:T(8,128)S(1)} %own.3.refs_1_), channel_id=1, source_target_pairs={{0,4},{1,5},{2,6},{3,7},{4,0},{5,1},{6,2},{7,3},{8,12},{9,13},{10,... | collective-permute-start | bytes 196616 | tf_op jit(solution)/shard_map/ppermute | solution.py:21
  82.6 5.8 %collective-permute-start.32 = (f32[16,1024]{1,0:T(8,128)S(1)}, f32[16,1024]{1,0:T(8,128)S(1)}, u32[]{:S(2)}, u32[]{:S(2)}) collective-permute-start(f32[16,1024]{1,0:T(8,128)S(1)} %own.3.refs_1_), channel_id=1, source_target_pairs={{0,6},{1,7},{2,4},{3,5},{4,2},{5,3},{6,0},{7,1},{8,14},{9,15},{10,... | collective-permute-start | bytes 196616 | tf_op jit(solution)/shard_map/ppermute | solution.py:21
  85.5 2.9 %collective-permute-start.33 = (f32[16,1024]{1,0:T(8,128)S(1)}, f32[16,1024]{1,0:T(8,128)S(1)}, u32[]{:S(2)}, u32[]{:S(2)}) collective-permute-start(f32[16,1024]{1,0:T(8,128)S(1)} %own.3.refs_1_), channel_id=1, source_target_pairs={{0,1},{1,0},{2,3},{3,2},{4,5},{5,4},{6,7},{7,6},{8,9},{9,8},{10,11... | collective-permute-start | bytes 196616 | tf_op jit(solution)/shard_map/ppermute | solution.py:21
  86.9 1.5 %collective-permute-start.34 = (f32[16,1024]{1,0:T(8,128)S(1)}, f32[16,1024]{1,0:T(8,128)S(1)}, u32[]{:S(2)}, u32[]{:S(2)}) collective-permute-start(f32[16,1024]{1,0:T(8,128)S(1)} %collective-permute-done.30.refs_2_), channel_id=1, source_target_pairs={{0,1},{1,0},{2,3},{3,2},{4,5},{5,4},{6,7},{7,6},{8,9},{9,8},{10,11... | collective-permute-start | bytes 196616 | tf_op jit(solution)/shard_map/ppermute | solution.py:21
  87.0 1.5 %collective-permute-start.35 = (f32[16,1024]{1,0:T(8,128)S(1)}, f32[16,1024]{1,0:T(8,128)S(1)}, u32[]{:S(2)}, u32[]{:S(2)}) collective-permute-start(f32[16,1024]{1,0:T(8,128)S(1)} %collective-permute-done.31.refs_3_), channel_id=1, source_target_pairs={{0,1},{1,0},{2,3},{3,2},{4,5},{5,4},{6,7},{7,6},{8,9},{9,8},{10,11... | collective-permute-start | bytes 196616 | tf_op jit(solution)/shard_map/ppermute | solution.py:21
  88.4 1.3 %collective-permute-start.36 = (f32[16,1024]{1,0:T(8,128)S(1)}, f32[16,1024]{1,0:T(8,128)S(1)}, u32[]{:S(2)}, u32[]{:S(2)}) collective-permute-start(f32[16,1024]{1,0:T(8,128)S(1)} %collective-permute-done.32.refs_4_), channel_id=1, source_target_pairs={{0,1},{1,0},{2,3},{3,2},{4,5},{5,4},{6,7},{7,6},{8,9},{9,8},{10,11... | collective-permute-start | bytes 196616 | tf_op jit(solution)/shard_map/ppermute | solution.py:21

commit v4 on v3

--- a/solution.py
+++ b/solution.py
@@ -80,7 +80,10 @@
     rows = jnp.where(spot == 0, one, jnp.where(spot == 1, two, three))
     rows = jnp.where(at < 6, rows, 0.0).astype(BF16)
     out[2 * secs : 2 * secs + 8, :] = dot(rows, member, ROW)
-    out[2 * secs + 6 : 2 * secs + 7, 0:secs] = drift[...]
+    fixed = jnp.dot(
+        jnp.broadcast_to(drift[...], (8, secs)), hold[...], precision=lax.Precision.HIGHEST
+    )
+    out[2 * secs + 6 : 2 * secs + 7, :] = fixed[0:1, :]
     base_row = jnp.zeros((1, count), F32)
     guar_row = jnp.zeros((1, count), F32)
     for t in range(base.shape[1]):
@@ -126,39 +129,48 @@
             x_later[y - 1, 0], x_later[y - 1, 1] = hi, lo
 
 
-def returns_body(year, first, secs, *refs):
-    blocks, (xs, part, sums), (load_hi, load_lo, hold_hi, hold_lo) = refs[:4], refs[4:7], refs[7:]
+def returns_body(year, first, secs, begun, final, *refs):
+    *blocks, xs, part, sums, load_hi, load_lo, held, flip_hi, flip_lo = refs
+    if begun:
+        *blocks, before, sums_before = blocks
     funds, width = part.shape
     total = load_hi.shape[0]
     at = 0
-    extra = jnp.zeros((8, funds), F32)
-    fixed = jnp.zeros((8, funds), F32)
+    extra = sums_before[...] if begun else jnp.zeros((8, funds), F32)
     for block in blocks:
         for b in range(block.shape[0]):
             load_hi[at : at + secs, :], load_lo[at : at + secs, :] = halves(block[b, 0:secs, :])
-            hold = block[b, secs : 2 * secs, :]
-            hold_hi[at : at + secs, :], hold_lo[at : at + secs, :] = halves(hold)
-            tail = block[b, 2 * secs : 2 * secs + 8, :]
-            extra = extra + tail
-            fixed = fixed + jnp.dot(tail[:, 0:secs], hold, precision=lax.Precision.HIGHEST)
+            held[at : at + secs, :] = block[b, secs : 2 * secs, :]
+            extra = extra + block[b, 2 * secs : 2 * secs + 8, :]
             at += secs
     sums[...] = extra
-    row = lax.broadcasted_iota(jnp.int32, (128, funds), 0)
-    fixed_col = jnp.transpose(jnp.where(row == 0, fixed[6:7, :], 0.0))[:, 0:1]
+    for g in range(0, total, 128):
+        flip_hi[:, g : g + 128], flip_lo[:, g : g + 128] = halves(jnp.transpose(held[g : g + 128, :]))
+    if final:
+        row = lax.broadcasted_iota(jnp.int32, (128, funds), 0)
+        fixed = jnp.transpose(jnp.where(row == 0, extra[6:7, :], 0.0))[:, 0:1]
     step = min(256, width)
     group = min(512, total)
-    for c in range(0, width, step):
+
+    def exposed(c, g):
         cut = slice(first + c, first + c + step)
         x_hi, x_lo = (xs[i, :, cut] if year == 0 else xs[year - 1, i, :, cut] for i in range(2))
-        acc = jnp.zeros((funds, step), F32)
-        for g in range(0, total, group):
-            lh, ll = load_hi[g : g + group, :], load_lo[g : g + group, :]
-            z = dot(jnp.concatenate([lh, lh], 1), jnp.concatenate([x_hi, x_lo], 0)) + dot(ll, x_hi)
-            t_hi, t_lo = halves(jnp.tanh(z))
-            hh, hl = hold_hi[g : g + group, :], hold_lo[g : g + group, :]
-            over = (((0,), (0,)), ((), ()))
-            acc = acc + dot(hh, t_hi, over) + dot(hh, t_lo, over) + dot(hl, t_hi, over)
-        part[:, c : c + step] = 0.25 * acc + fixed_col
+        lh, ll = load_hi[g : g + group, :], load_lo[g : g + group, :]
+        return dot(jnp.concatenate([lh, lh], 1), jnp.concatenate([x_hi, x_lo], 0)) + dot(ll, x_hi)
+
+    spots = [(c, g) for c in range(0, width, step) for g in range(0, total, group)]
+    ahead = exposed(*spots[0])
+    for i, (c, g) in enumerate(spots):
+        now = ahead
+        ahead = exposed(*spots[i + 1]) if i + 1 < len(spots) else None
+        t_hi, t_lo = halves(jnp.tanh(now))
+        fh, fl = flip_hi[:, g : g + group], flip_lo[:, g : g + group]
+        new = 0.25 * dot(jnp.concatenate([fh, fh, fl], 1), jnp.concatenate([t_hi, t_lo, t_hi], 0))
+        acc = new if g == 0 else acc + new
+        if g + group == total:
+            if begun:
+                acc = acc + before[:, first + c : first + c + step]
+            part[:, c : c + step] = acc + fixed if final else acc
 
 
 def own_columns(me_ref, declared, first, out):
@@ -177,9 +189,8 @@
     return pl.multiple_of(((me_ref[0] & 7) ^ label) * slice_funds, slice_funds)
 
 
-def advance(step, table, member, base, guar, draw, asset, liab):
+def advance(step, got, base, guar, draw, asset, liab):
     wide = lambda v: jnp.concatenate([v] * (step // 128), 1)
-    got = dot(member, table)
     growth, credit = got[:, 0:step], jnp.maximum(got[:, step:], wide(guar))
     lapse = jnp.minimum(wide(base) * (0.5 + draw.astype(F32)) * jnp.exp(5.0 * (growth - credit)), 0.5)
     stay = 1.0 - lapse
@@ -202,7 +213,7 @@
     out[...] = rate(asset * (1.0 + growth) / liab)
 
 
-STEP, ROWS = 256, 256
+STEP, ROWS = 256, 512
 
 
 def year_body(year, first, last, slice_funds, *refs):
@@ -245,10 +256,17 @@
     else:
         own = out_r
     copies = []
+
+    def gathered(c):
+        there = slice(lead + c, lead + c + STEP)
+        table = table_of(part[:, there] + peer[:, there], declared[:, c : c + STEP])
+        return [dot(member[year, r : r + ROWS, :], table) for r in range(0, count, ROWS)]
+
+    ahead = gathered(0)
     for c in range(0, width, STEP):
         cut = slice(c, c + STEP)
-        there = slice(lead + c, lead + c + STEP)
-        table = table_of(part[:, there] + peer[:, there], declared[:, cut])
+        now = ahead
+        ahead = gathered(c + STEP) if c + STEP < width else None
         sum_a = sum_l = None
         for r in range(0, count, ROWS):
             rows = slice(r, r + ROWS)
@@ -262,7 +280,7 @@
                 at = slice(c % half, c % half + STEP)
                 asset, liab = held[0][rows, at], held[1][rows, at]
             asset, liab = advance(
-                STEP, table, member[year, rows, :], wides[2 * year, rows, :], wides[2 * year + 1, rows, :],
+                STEP, now[r // ROWS], wides[2 * year, rows, :], wides[2 * year + 1, rows, :],
                 draws[year, rows, first + c : first + c + STEP], asset, liab,
             )
             if last:
@@ -274,8 +292,8 @@
                 a_hi, a_lo = halves(asset)
                 l_hi, l_lo = halves(liab)
                 ma, ml = member_t[year + 1, :, rows], member_t[0, :, rows]
-                add_a = dot(ma, a_hi) + dot(ma, a_lo)
-                add_l = dot(ml, l_hi) + dot(ml, l_lo)
+                add_a = dot(jnp.concatenate([ma, ma], 1), jnp.concatenate([a_hi, a_lo], 0))
+                add_l = dot(jnp.concatenate([ml, ml], 1), jnp.concatenate([l_hi, l_lo], 0))
                 sum_a = add_a if sum_a is None else sum_a + add_a
                 sum_l = add_l if sum_l is None else sum_l + add_l
         if last:
@@ -361,20 +379,23 @@
         block = jnp.concatenate([block, swap(block, o)])
     blocks = [block] + [swap(block, o) for o in SQUARE]
 
-    total = secs * n // 2
-
-    def returns(year, first, width, blocks, xs):
-        part, sums = call(
-            functools.partial(returns_body, year, first, secs),
+    def returns(year, first, width, blocks, xs, before=(), final=True):
+        total = secs * sum(b.shape[0] for b in blocks)
+        return call(
+            functools.partial(returns_body, year, first, secs, len(before) > 0, final),
             [shaped(funds, width), shaped(8, funds)],
-            [VMEM] * 5,
+            [VMEM] * (len(blocks) + len(before) + 1),
             "returns",
-            scratch=[pltpu.VMEM((total, funds), BF16)] * 4,
+            scratch=[pltpu.VMEM((total, funds), BF16)] * 2
+            + [pltpu.VMEM((total, funds), F32)]
+            + [pltpu.VMEM((funds, total), BF16)] * 2,
             limit=8 * max(1, min(6, total // 512)),
-        )(*blocks, xs)
-        return part, sums
-
-    firsts = [returns(0, h * half, half, blocks, x_now) for h in range(2)]
+        )(*blocks, *before, xs)
+
+    before = ()
+    for b in blocks[:-1]:
+        before = returns(0, 0, paths, [b], x_now, before, False)
+    firsts = [returns(0, h * half, half, blocks[-1:], x_now, before) for h in range(2)]
     sums = firsts[0][1]
     part = [p for p, _ in firsts]
     peer = [swap(p, 1) for p in part]

time: 93.7 us -> 90.4 us (0.965)
  Pallas kernels: 28.2 us -> 21.3 us
  waiting for transfers between devices: 30.7 us -> 33.9 us
    pallas_call x6 -> x9, Pallas kernels: 12.7 us -> 7.94 us  [returns(): call(functools.partial(returns_body, year, first, secs, len(before) > 0,...]
    ppermute x37, waiting for transfers between devices: 30.7 us -> 33.9 us  [swap(): return lax.ppermute(x, 'pol', [(i, i ^ offset) for i in range(n)])]
    pallas_call x5, Pallas kernels: 12.4 us -> 10.4 us  [local(): call(functools.partial(year_body, year, first, last, slice_funds), out, [...]
  transfers between devices with their start and end apart: 37 -> 37, of which waited for: 20 -> 21; matrix products, arithmetic and copies ran while one was open for 0% -> 0% of each run, Pallas kernels for 21% -> 15%
where the time goes in v4:
time: 90.4 us; the launch traced here: 90.1 us
  waiting for transfers between devices  33.9 us (38%)
  starting transfers between devices  30.4 us (34%)
  Pallas kernels  21.3 us (24%)
  local copies, waits for them, and re-layouts  3.17 us (4%)
  between operations  1.09 us (1%)
    ppermute x37, waiting for transfers between devices, swap(): return lax.ppermute(x, 'pol', [(i, i ^ offset) for i in range(n)])  33.9 us
    ppermute x37, starting transfers between devices, swap(): return lax.ppermute(x, 'pol', [(i, i ^ offset) for i in range(n)])  30.4 us
    pallas_call x5, Pallas kernels, local(): call(functools.partial(year_body, year, first, last, slice_funds), out, [...  10.4 us
    pallas_call x9, Pallas kernels, returns(): call(functools.partial(returns_body, year, first, secs, len(before) > 0,...  7.94 us
    unnamed x9, local copies, waits for them, and re-layouts  3.02 us
  transfers between devices with their start and end apart: 37, of which 21 were waited for; matrix products, arithmetic and copies ran while one was open for 0% of the time, Pallas kernels for 15%

profile of v4, /device:TPU:0, one launch (start us, length us, event | category | flops | bytes accessed | tf_op | source)
XLA Modules:
  0.0 90.1 jit_solution(567632463536488025)
XLA Ops:
  0.6 1.7 %pack.1 = (f32[136,128]{1,0:T(8,128)}, f32[8,512]{1,0:T(8,128)}) custom-call(s32[1]{0:T(128)} %bitcast.refs_0_.me, f32[64,128]{1,0:T(8,128)} %refs_1_.1, f32[64,128]{1,0:T(8,128)} %refs_2_.1, f32[1,64]{1,0:T(1,128)} %bitcast.63, s32[1,512]{1,0:T(1,128)} %bitcast.58, s32[1,512]{1,0:T(1,128)} %bitcast.59, f32[1,512]{1,0:T(1,128)} %bitcast.60, ...), custom_call_target="tpu_custom_call" | custom-call | flops 1000000 | bytes 100000 | tf_op jit(solution)/shard_map/pack/pallas_call | solution.py:347
  2.4 4.1 %collective-permute-start = (f32[1,136,128]{2,1,0:T(8,128)}, f32[1,136,128]{2,1,0:T(8,128)S(1)}, u32[]{:S(2)}, u32[]{:S(2)}) collective-permute-start(f32[1,136,128]{2,1,0:T(8,128)} %bitcast.57), channel_id=1, source_target_pairs={{0,8},{1,9},{2,10},{3,11},{4,12},{5,13},{6,14},{7,15},{8,0},{9,1},... | collective-permute-start | bytes 208904 | tf_op jit(solution)/shard_map/ppermute | solution.py:21
  6.5 1.4 %copy-done.1 = f32[3,128,1024]{2,1,0:T(8,128)S(1)} copy-done((f32[3,128,1024]{2,1,0:T(8,128)S(1)}, f32[3,128,1024]{2,1,0:T(8,128)}, u32[]{:S(2)}) %copy-start.1) | copy-done | bytes 1572888
  7.9 0.9 copy-done.2
  8.7 0.7 copy-done.3
  9.5 1.1 %columns.1 = (bf16[3,128,512]{2,1,0:T(8,128)(2,1)S(1)}, bf16[3,512,256]{2,1,0:T(8,128)(2,1)S(1)}, f32[8,512,128]{2,1,0:T(8,128)S(1)}, bf16[2,128,1024]{2,1,0:T(8...) custom-call(f32[8,512]{1,0:T(8,128)S(1)} %copy-done.3, f32[136,128]{1,0:T(8,128)S(1)} %copy-done.2, ...), custom_call_target="tpu_custom_call" | custom-call | flops 1000000 | bytes 4000000 | tf_op jit(solution)/shard_map/columns/pallas_call | solution.py:359
  10.6 1.6 %collective-permute-start.1 = (f32[2,136,128]{2,1,0:T(8,128)S(1)}, f32[2,136,128]{2,1,0:T(8,128)S(1)}, u32[]{:S(2)}, u32[]{:S(2)}) collective-permute-start(f32[2,136,128]{2,1,0:T(8,128)S(1)} %constant_dynamic-update-slice_fusion.refs_0_), channel_id=1, source_target_pairs={{0,2},{1,3},{2,0},{3,1},{4,6},{5,7},{6,4},{7,5},{8,10},{9,11},{10,... | collective-permute-start | bytes 417800 | tf_op jit(solution)/shard_map/ppermute | solution.py:21
  12.2 1.6 %collective-permute-start.2 = (f32[2,136,128]{2,1,0:T(8,128)S(1)}, f32[2,136,128]{2,1,0:T(8,128)S(1)}, u32[]{:S(2)}, u32[]{:S(2)}) collective-permute-start(f32[2,136,128]{2,1,0:T(8,128)S(1)} %constant_dynamic-update-slice_fusion.refs_0_), channel_id=1, source_target_pairs={{0,4},{1,5},{2,6},{3,7},{4,0},{5,1},{6,2},{7,3},{8,12},{9,13},{10,... | collective-permute-start | bytes 417800 | tf_op jit(solution)/shard_map/ppermute | solution.py:21
  13.8 0.4 collective-permute-start.3
  14.2 0.6 returns.9
  14.8 1.1 %collective-permute-done.1.refs_0_.refs_1_ = f32[2,136,128]{2,1,0:T(8,128)S(1)} collective-permute-done((f32[2,136,128]{2,1,0:T(8,128)S(1)}, f32[2,136,128]{2,1,0:T(8,128)S(1)}, u32[]{:S(2)}, u32[]{:S(2)}) %collective-permute-start.1) | collective-permute-done | bytes 139296 | tf_op jit(solution)/shard_map/ppermute | solution.py:21
  15.8 0.6 returns.10
  16.4 2.1 %collective-permute-done.2.refs_0_.refs_2_ = f32[2,136,128]{2,1,0:T(8,128)S(1)} collective-permute-done((f32[2,136,128]{2,1,0:T(8,128)S(1)}, f32[2,136,128]{2,1,0:T(8,128)S(1)}, u32[]{:S(2)}, u32[]{:S(2)}) %collective-permute-start.2) | collective-permute-done | bytes 139296 | tf_op jit(solution)/shard_map/ppermute | solution.py:21
  18.5 0.6 returns.11
  19.1 1.1 %collective-permute-done.3.refs_0_.refs_3_ = f32[2,136,128]{2,1,0:T(8,128)S(1)} collective-permute-done((f32[2,136,128]{2,1,0:T(8,128)S(1)}, f32[2,136,128]{2,1,0:T(8,128)S(1)}, u32[]{:S(2)}, u32[]{:S(2)}) %collective-permute-start.3) | collective-permute-done | bytes 139296 | tf_op jit(solution)/shard_map/ppermute | solution.py:21
  20.2 0.5 returns.12
  20.8 0.5 collective-permute-start.4
  21.3 0.7 returns.13
  22.0 0.3 collective-permute-done.4.refs_2_
  22.3 1.8 %year.5 = (f32[512,512]{1,0:T(8,128)S(1)}, f32[512,512]{1,0:T(8,128)S(1)}, f32[2,4,2,16,512]{4,3,2,1,0:T(8,128)S(1)}, f32[64,128]{1,0:T(8,128)S(1)}) custom-call(s32[1]{0:T(128)} %bitcast.refs_0_.me, f32[8,128]{1,0:T(8,128)S(1)} %get-tuple-element.67.refs_1_, f32[8,128]{1,0:T(8,128)S(1)} %collective-permute-done.4.refs_2_, ...), custom_call_target="tpu_custom_call" | custom-call | flops 268435456 | bytes 5242880 | tf_op jit(solution)/shard_map/year/pallas_call | solution.py:435
  24.1 0.2 collective-permute-start.6
  24.3 1.8 %year.6 = (f32[512,512]{1,0:T(8,128)S(1)}, f32[512,512]{1,0:T(8,128)S(1)}, f32[2,4,2,16,512]{4,3,2,1,0:T(8,128)S(1)}, f32[64,128]{1,0:T(8,128)S(1)}) custom-call(s32[1]{0:T(128)} %bitcast.refs_0_.me, f32[8,128]{1,0:T(8,128)S(1)} %get-tuple-element.67.refs_1_, f32[8,128]{1,0:T(8,128)S(1)} %collective-permute-done.4.refs_2_, ...), custom_call_target="tpu_custom_call" | custom-call | flops 268435456 | bytes 5242880 | tf_op jit(solution)/shard_map/year/pallas_call | solution.py:435
  26.1 0.4 collective-permute-start.8
  26.6 1.1 %collective-permute-done.8 = f32[4,2,16,512]{3,2,1,0:T(8,128)S(1)} collective-permute-done((f32[4,2,16,512]{3,2,1,0:T(8,128)S(1)}, f32[4,2,16,512]{3,2,1,0:T(8,128)S(1)}, u32[]{:S(2)}, u32[]{:S(2)}) %collective-permute-start.8) | collective-permute-done | bytes 262176 | tf_op jit(solution)/shard_map/ppermute | solution.py:21
  27.8 1.4 %collective-permute-start.13 = (f32[2,16,1024]{2,1,0:T(8,128)S(1)}, f32[2,16,1024]{2,1,0:T(8,128)S(1)}, u32[]{:S(2)}, u32[]{:S(2)}) collective-permute-start(f32[2,16,1024]{2,1,0:T(8,128)S(1)} %get-tuple-element.108), channel_id=1, source_target_pairs={{0,2},{1,3},{2,0},{3,1},{4,6},{5,7},{6,4},{7,5},{8,10},{9,11},{10,... | collective-permute-start | bytes 393224 | tf_op jit(solution)/shard_map/ppermute | solution.py:21
  29.2 1.6 %collective-permute-start.14 = (f32[2,16,1024]{2,1,0:T(8,128)S(1)}, f32[2,16,1024]{2,1,0:T(8,128)S(1)}, u32[]{:S(2)}, u32[]{:S(2)}) collective-permute-start(f32[2,16,1024]{2,1,0:T(8,128)S(1)} %get-tuple-element.110), channel_id=1, source_target_pairs={{0,4},{1,5},{2,6},{3,7},{4,0},{5,1},{6,2},{7,3},{8,12},{9,13},{10,... | collective-permute-start | bytes 393224 | tf_op jit(solution)/shard_map/ppermute | solution.py:21
  30.8 0.6 collective-permute-start.15
  31.4 0.5 collective-permute-start.11
  31.9 1.8 %collective-permute-done.13 = f32[2,16,1024]{2,1,0:T(8,128)S(1)} collective-permute-done((f32[2,16,1024]{2,1,0:T(8,128)S(1)}, f32[2,16,1024]{2,1,0:T(8,128)S(1)}, u32[]{:S(2)}, u32[]{:S(2)}) %collective-permute-start.13) | collective-permute-done | bytes 131104 | tf_op jit(solution)/shard_map/ppermute | solution.py:21
  33.7 1.9 %collective-permute-done.14 = f32[2,16,1024]{2,1,0:T(8,128)S(1)} collective-permute-done((f32[2,16,1024]{2,1,0:T(8,128)S(1)}, f32[2,16,1024]{2,1,0:T(8,128)S(1)}, u32[]{:S(2)}, u32[]{:S(2)}) %collective-permute-start.14) | collective-permute-done | bytes 131104 | tf_op jit(solution)/shard_map/ppermute | solution.py:21
  35.6 2.1 %collective-permute-done.15 = f32[2,16,1024]{2,1,0:T(8,128)S(1)} collective-permute-done((f32[2,16,1024]{2,1,0:T(8,128)S(1)}, f32[2,16,1024]{2,1,0:T(8,128)S(1)}, u32[]{:S(2)}, u32[]{:S(2)}) %collective-permute-start.15) | collective-permute-done | bytes 131104 | tf_op jit(solution)/shard_map/ppermute | solution.py:21
  37.7 2.1 %collective-permute-start.16 = (f32[2,16,1024]{2,1,0:T(8,128)S(1)}, f32[2,16,1024]{2,1,0:T(8,128)S(1)}, u32[]{:S(2)}, u32[]{:S(2)}) collective-permute-start(f32[2,16,1024]{2,1,0:T(8,128)S(1)} %fusion.3.refs_0_), channel_id=1, source_target_pairs={{0,8},{1,9},{2,10},{3,11},{4,12},{5,13},{6,14},{7,15},{8,0},{9,1},... | collective-permute-start | bytes 393224 | tf_op jit(solution)/shard_map/ppermute | solution.py:21
  39.8 1.3 %returns.14 = (f32[128,1024]{1,0:T(8,128)S(1)}, f32[8,128]{1,0:T(8,128)}) custom-call(f32[2,136,128]{2,1,0:T(8,128)S(1)} %constant_dynamic-update-slice_fusion.refs_0_, f32[2,136,128]{2,1,0:T(8,128)S(1)} %collective-permute-done.1.refs_0_.refs_1_, f32[2,136,128]{2,1,0:T(8,128)S(1)} %collective-permute-done.2.refs_0_.refs_2_, ...), custom_call_target="tpu_custom_call" | custom-call | tf_op jit(solution)/shard_map/returns/pallas_call | solution.py:384
  41.1 1.3 %returns.15 = (f32[128,1024]{1,0:T(8,128)S(1)}, f32[8,128]{1,0:T(8,128)}) custom-call(f32[2,136,128]{2,1,0:T(8,128)S(1)} %collective-permute-done.9.refs_0_, f32[2,136,128]{2,1,0:T(8,128)S(1)} %collective-permute-done.10.refs_1_, f32[2,136,128]{2,1,0:T(8,128)S(1)} %collective-permute-done.11.refs_2_, f32[2,136,128]{2,1,0:T(8,128)S(1)} %collective-permute-done.12.refs_3_, ...), custom_call_target="tpu_custom_call" | custom-call | tf_op jit(solution)/shard_map/returns/pallas_call | solution.py:384
  42.4 3.8 %collective-permute-done.16.refs_1_ = f32[2,16,1024]{2,1,0:T(8,128)S(1)} collective-permute-done((f32[2,16,1024]{2,1,0:T(8,128)S(1)}, f32[2,16,1024]{2,1,0:T(8,128)S(1)}, u32[]{:S(2)}, u32[]{:S(2)}) %collective-permute-start.16) | collective-permute-done | bytes 131104 | tf_op jit(solution)/shard_map/ppermute | solution.py:21
  46.3 1.2 %collective-permute-start.17 = (f32[16,1024]{1,0:T(8,128)S(1)}, f32[16,1024]{1,0:T(8,128)S(1)}, u32[]{:S(2)}, u32[]{:S(2)}) collective-permute-start(f32[16,1024]{1,0:T(8,128)S(1)} %own.2.refs_1_), channel_id=1, source_target_pairs={{0,2},{1,3},{2,0},{3,1},{4,6},{5,7},{6,4},{7,5},{8,10},{9,11},{10,... | collective-permute-start | bytes 196616 | tf_op jit(solution)/shard_map/ppermute | solution.py:21
  47.5 0.3 collective-permute-start.18
  47.8 2.0 %collective-permute-start.19 = (f32[16,1024]{1,0:T(8,128)S(1)}, f32[16,1024]{1,0:T(8,128)S(1)}, u32[]{:S(2)}, u32[]{:S(2)}) collective-permute-start(f32[16,1024]{1,0:T(8,128)S(1)} %own.2.refs_1_), channel_id=1, source_target_pairs={{0,6},{1,7},{2,4},{3,5},{4,2},{5,3},{6,0},{7,1},{8,14},{9,15},{10,... | collective-permute-start | bytes 196616 | tf_op jit(solution)/shard_map/ppermute | solution.py:21
  49.8 0.8 collective-permute-done.17.refs_2_
  50.6 1.2 %collective-permute-done.18.refs_3_ = f32[16,1024]{1,0:T(8,128)S(1)} collective-permute-done((f32[16,1024]{1,0:T(8,128)S(1)}, f32[16,1024]{1,0:T(8,128)S(1)}, u32[]{:S(2)}, u32[]{:S(2)}) %collective-permute-start.18) | collective-permute-done | bytes 65568 | tf_op jit(solution)/shard_map/ppermute | solution.py:21
  51.8 1.2 %collective-permute-done.19.refs_4_ = f32[16,1024]{1,0:T(8,128)S(1)} collective-permute-done((f32[16,1024]{1,0:T(8,128)S(1)}, f32[16,1024]{1,0:T(8,128)S(1)}, u32[]{:S(2)}, u32[]{:S(2)}) %collective-permute-start.19) | collective-permute-done | bytes 65568 | tf_op jit(solution)/shard_map/ppermute | solution.py:21
  53.1 1.2 %collective-permute-done.23.refs_8_ = f32[16,1024]{1,0:T(8,128)S(1)} collective-permute-done((f32[16,1024]{1,0:T(8,128)S(1)}, f32[16,1024]{1,0:T(8,128)S(1)}, u32[]{:S(2)}, u32[]{:S(2)}) %collective-permute-start.23) | collective-permute-done | bytes 65568 | tf_op jit(solution)/shard_map/ppermute | solution.py:21
  54.3 1.5 %year.7 = (f32[512,512]{1,0:T(8,128)S(1)}, f32[512,512]{1,0:T(8,128)S(1)}, f32[2,4,2,16,512]{4,3,2,1,0:T(8,128)S(1)}, f32[64,128]{1,0:T(8,128)S(1)}) custom-call(s32[1]{0:T(128)} %bitcast.refs_0_.me, f32[16,1024]{1,0:T(8,128)S(1)} %own.2.refs_1_, f32[16,1024]{1,0:T(8,128)S(1)} %collective-permute-done.17.refs_2_, ...), custom_call_target="tpu_custom_call" | custom-call | flops 268435456 | bytes 5242880 | tf_op jit(solution)/shard_map/year/pallas_call | solution.py:435
  55.8 0.2 collective-permute-start.24
  56.1 1.7 %year.8 = (f32[512,512]{1,0:T(8,128)S(1)}, f32[512,512]{1,0:T(8,128)S(1)}, f32[2,4,2,16,512]{4,3,2,1,0:T(8,128)S(1)}, f32[64,128]{1,0:T(8,128)S(1)}) custom-call(s32[1]{0:T(128)} %bitcast.refs_0_.me, f32[16,1024]{1,0:T(8,128)S(1)} %own.2.refs_1_, f32[16,1024]{1,0:T(8,128)S(1)} %collective-permute-done.17.refs_2_, ...), custom_call_target="tpu_custom_call" | custom-call | flops 268435456 | bytes 5242880 | tf_op jit(solution)/shard_map/year/pallas_call | solution.py:435
  57.8 0.4 collective-permute-start.25
  58.3 1.1 %collective-permute-done.25 = f32[4,2,16,512]{3,2,1,0:T(8,128)S(1)} collective-permute-done((f32[4,2,16,512]{3,2,1,0:T(8,128)S(1)}, f32[4,2,16,512]{3,2,1,0:T(8,128)S(1)}, u32[]{:S(2)}, u32[]{:S(2)}) %collective-permute-start.25) | collective-permute-done | bytes 262176 | tf_op jit(solution)/shard_map/ppermute | solution.py:21
  59.5 1.0 %collective-permute-start.26 = (f32[2,16,1024]{2,1,0:T(8,128)S(1)}, f32[2,16,1024]{2,1,0:T(8,128)S(1)}, u32[]{:S(2)}, u32[]{:S(2)}) collective-permute-start(f32[2,16,1024]{2,1,0:T(8,128)S(1)} %get-tuple-element.105), channel_id=1, source_target_pairs={{0,2},{1,3},{2,0},{3,1},{4,6},{5,7},{6,4},{7,5},{8,10},{9,11},{10,... | collective-permute-start | bytes 393224 | tf_op jit(solution)/shard_map/ppermute | solution.py:21
  60.6 1.6 %collective-permute-start.27 = (f32[2,16,1024]{2,1,0:T(8,128)S(1)}, f32[2,16,1024]{2,1,0:T(8,128)S(1)}, u32[]{:S(2)}, u32[]{:S(2)}) collective-permute-start(f32[2,16,1024]{2,1,0:T(8,128)S(1)} %get-tuple-element.107), channel_id=1, source_target_pairs={{0,4},{1,5},{2,6},{3,7},{4,0},{5,1},{6,2},{7,3},{8,12},{9,13},{10,... | collective-permute-start | bytes 393224 | tf_op jit(solution)/shard_map/ppermute | solution.py:21
  62.2 0.9 %collective-permute-start.28 = (f32[2,16,1024]{2,1,0:T(8,128)S(1)}, f32[2,16,1024]{2,1,0:T(8,128)S(1)}, u32[]{:S(2)}, u32[]{:S(2)}) collective-permute-start(f32[2,16,1024]{2,1,0:T(8,128)S(1)} %get-tuple-element.106), channel_id=1, source_target_pairs={{0,6},{1,7},{2,4},{3,5},{4,2},{5,3},{6,0},{7,1},{8,14},{9,15},{10,... | collective-permute-start | bytes 393224 | tf_op jit(solution)/shard_map/ppermute | solution.py:21
  63.1 2.3 %collective-permute-done.26 = f32[2,16,1024]{2,1,0:T(8,128)S(1)} collective-permute-done((f32[2,16,1024]{2,1,0:T(8,128)S(1)}, f32[2,16,1024]{2,1,0:T(8,128)S(1)}, u32[]{:S(2)}, u32[]{:S(2)}) %collective-permute-start.26) | collective-permute-done | bytes 131104 | tf_op jit(solution)/shard_map/ppermute | solution.py:21
  65.4 1.5 %collective-permute-done.27 = f32[2,16,1024]{2,1,0:T(8,128)S(1)} collective-permute-done((f32[2,16,1024]{2,1,0:T(8,128)S(1)}, f32[2,16,1024]{2,1,0:T(8,128)S(1)}, u32[]{:S(2)}, u32[]{:S(2)}) %collective-permute-start.27) | collective-permute-done | bytes 131104 | tf_op jit(solution)/shard_map/ppermute | solution.py:21
  66.9 2.5 %collective-permute-done.28 = f32[2,16,1024]{2,1,0:T(8,128)S(1)} collective-permute-done((f32[2,16,1024]{2,1,0:T(8,128)S(1)}, f32[2,16,1024]{2,1,0:T(8,128)S(1)}, u32[]{:S(2)}, u32[]{:S(2)}) %collective-permute-start.28) | collective-permute-done | bytes 131104 | tf_op jit(solution)/shard_map/ppermute | solution.py:21
  69.4 3.4 %collective-permute-start.29 = (f32[2,16,1024]{2,1,0:T(8,128)S(1)}, f32[2,16,1024]{2,1,0:T(8,128)S(1)}, u32[]{:S(2)}, u32[]{:S(2)}) collective-permute-start(f32[2,16,1024]{2,1,0:T(8,128)S(1)} %fusion.1.refs_0_), channel_id=1, source_target_pairs={{0,8},{1,9},{2,10},{3,11},{4,12},{5,13},{6,14},{7,15},{8,0},{9,1},... | collective-permute-start | bytes 393224 | tf_op jit(solution)/shard_map/ppermute | solution.py:21
  72.8 1.3 %returns.16 = (f32[128,1024]{1,0:T(8,128)S(1)}, f32[8,128]{1,0:T(8,128)}) custom-call(f32[2,136,128]{2,1,0:T(8,128)S(1)} %constant_dynamic-update-slice_fusion.refs_0_, f32[2,136,128]{2,1,0:T(8,128)S(1)} %collective-permute-done.1.refs_0_.refs_1_, f32[2,136,128]{2,1,0:T(8,128)S(1)} %collective-permute-done.2.refs_0_.refs_2_, ...), custom_call_target="tpu_custom_call" | custom-call | tf_op jit(solution)/shard_map/returns/pallas_call | solution.py:384
  74.1 1.3 %returns.17 = (f32[128,1024]{1,0:T(8,128)S(1)}, f32[8,128]{1,0:T(8,128)}) custom-call(f32[2,136,128]{2,1,0:T(8,128)S(1)} %collective-permute-done.9.refs_0_, f32[2,136,128]{2,1,0:T(8,128)S(1)} %collective-permute-done.10.refs_1_, f32[2,136,128]{2,1,0:T(8,128)S(1)} %collective-permute-done.11.refs_2_, f32[2,136,128]{2,1,0:T(8,128)S(1)} %collective-permute-done.12.refs_3_, ...), custom_call_target="tpu_custom_call" | custom-call | tf_op jit(solution)/shard_map/returns/pallas_call | solution.py:384
  75.4 3.1 %collective-permute-done.29.refs_1_ = f32[2,16,1024]{2,1,0:T(8,128)S(1)} collective-permute-done((f32[2,16,1024]{2,1,0:T(8,128)S(1)}, f32[2,16,1024]{2,1,0:T(8,128)S(1)}, u32[]{:S(2)}, u32[]{:S(2)}) %collective-permute-start.29) | collective-permute-done | bytes 131104 | tf_op jit(solution)/shard_map/ppermute | solution.py:21
  78.6 0.7 collective-permute-start.30
  79.3 2.9 %collective-permute-start.32 = (f32[16,1024]{1,0:T(8,128)S(1)}, f32[16,1024]{1,0:T(8,128)S(1)}, u32[]{:S(2)}, u32[]{:S(2)}) collective-permute-start(f32[16,1024]{1,0:T(8,128)S(1)} %own.3.refs_1_), channel_id=1, source_target_pairs={{0,6},{1,7},{2,4},{3,5},{4,2},{5,3},{6,0},{7,1},{8,14},{9,15},{10,... | collective-permute-start | bytes 196616 | tf_op jit(solution)/shard_map/ppermute | solution.py:21
  82.2 1.5 %collective-permute-done.30.refs_2_ = f32[16,1024]{1,0:T(8,128)S(1)} collective-permute-done((f32[16,1024]{1,0:T(8,128)S(1)}, f32[16,1024]{1,0:T(8,128)S(1)}, u32[]{:S(2)}, u32[]{:S(2)}) %collective-permute-start.30) | collective-permute-done | bytes 65568 | tf_op jit(solution)/shard_map/ppermute | solution.py:21
  83.7 0.5 collective-permute-start.35
  84.2 0.9 %collective-permute-done.32.refs_4_ = f32[16,1024]{1,0:T(8,128)S(1)} collective-permute-done((f32[16,1024]{1,0:T(8,128)S(1)}, f32[16,1024]{1,0:T(8,128)S(1)}, u32[]{:S(2)}, u32[]{:S(2)}) %collective-permute-start.32) | collective-permute-done | bytes 65568 | tf_op jit(solution)/shard_map/ppermute | solution.py:21
  85.1 1.2 %collective-permute-done.36.refs_8_ = f32[16,1024]{1,0:T(8,128)S(1)} collective-permute-done((f32[16,1024]{1,0:T(8,128)S(1)}, f32[16,1024]{1,0:T(8,128)S(1)}, u32[]{:S(2)}, u32[]{:S(2)}) %collective-permute-start.36) | collective-permute-done | bytes 65568 | tf_op jit(solution)/shard_map/ppermute | solution.py:21
  86.4 3.6 %year.9 = (f32[512,1024]{1,0:T(8,128)}, f32[512,1024]{1,0:T(8,128)}, f32[3,64,128]{2,1,0:T(8,128)}) custom-call(s32[1]{0:T(128)} %bitcast.refs_0_.me, f32[16,1024]{1,0:T(8,128)S(1)} %own.3.refs_1_, f32[16,1024]{1,0:T(8,128)S(1)} %collective-permute-done.30.refs_2_, f32[16,1024]{1,0:T(8,128)S(1)} %collective-permute-done.31.refs_3_, ...), custom_call_target="tpu_custom_call" | custom-call | flops 536870912 | bytes 10485760 | tf_op jit(solution)/shard_map/year/pallas_call | solution.py:435
  (52 shorter events, 0.9 us)
Async XLA Ops:
  2.4 8.3 %collective-permute-start = (f32[1,136,128]{2,1,0:T(8,128)}, f32[1,136,128]{2,1,0:T(8,128)S(1)}, u32[]{:S(2)}, u32[]{:S(2)}) collective-permute-start(f32[1,136,128]{2,1,0:T(8,128)} %bitcast.57), channel_id=1, source_target_pairs={{0,8},{1,9},{2,10},{3,11},{4,12},{5,13},{6,14},{7,15},{8,0},{9,1},... | collective-permute-start | bytes 208904 | tf_op jit(solution)/shard_map/ppermute | solution.py:21
  6.5 1.4 %copy-start.1 = (f32[3,128,1024]{2,1,0:T(8,128)S(1)}, f32[3,128,1024]{2,1,0:T(8,128)}, u32[]{:S(2)}) copy-start(f32[3,128,1024]{2,1,0:T(8,128)} %shocks.1) | copy-start | bytes 4718596
  7.9 0.9 copy-start.2
  8.7 0.7 copy-start.3
  10.6 5.2 %collective-permute-start.1 = (f32[2,136,128]{2,1,0:T(8,128)S(1)}, f32[2,136,128]{2,1,0:T(8,128)S(1)}, u32[]{:S(2)}, u32[]{:S(2)}) collective-permute-start(f32[2,136,128]{2,1,0:T(8,128)S(1)} %constant_dynamic-update-slice_fusion.refs_0_), channel_id=1, source_target_pairs={{0,2},{1,3},{2,0},{3,1},{4,6},{5,7},{6,4},{7,5},{8,10},{9,11},{10,... | collective-permute-start | bytes 417800 | tf_op jit(solution)/shard_map/ppermute | solution.py:21
  12.2 6.3 %collective-permute-start.2 = (f32[2,136,128]{2,1,0:T(8,128)S(1)}, f32[2,136,128]{2,1,0:T(8,128)S(1)}, u32[]{:S(2)}, u32[]{:S(2)}) collective-permute-start(f32[2,136,128]{2,1,0:T(8,128)S(1)} %constant_dynamic-update-slice_fusion.refs_0_), channel_id=1, source_target_pairs={{0,4},{1,5},{2,6},{3,7},{4,0},{5,1},{6,2},{7,3},{8,12},{9,13},{10,... | collective-permute-start | bytes 417800 | tf_op jit(solution)/shard_map/ppermute | solution.py:21
  13.8 6.4 %collective-permute-start.3 = (f32[2,136,128]{2,1,0:T(8,128)S(1)}, f32[2,136,128]{2,1,0:T(8,128)S(1)}, u32[]{:S(2)}, u32[]{:S(2)}) collective-permute-start(f32[2,136,128]{2,1,0:T(8,128)S(1)} %constant_dynamic-update-slice_fusion.refs_0_), channel_id=1, source_target_pairs={{0,6},{1,7},{2,4},{3,5},{4,2},{5,3},{6,0},{7,1},{8,14},{9,15},{10,... | collective-permute-start | bytes 417800 | tf_op jit(solution)/shard_map/ppermute | solution.py:21
  15.8 6.5 %copy-start = (bf16[512,3,1024]{2,0,1:T(8,128)(2,1)S(1)}, bf16[512,3,1024]{2,0,1:T(8,128)(2,1)}, u32[]{:S(2)}) copy-start(bf16[512,3,1024]{2,0,1:T(8,128)(2,1)} %param.23) | copy-start | bytes 9437188
  20.7 1.6 %collective-permute-start.5 = (f32[128,512]{1,0:T(8,128)S(1)}, f32[128,512]{1,0:T(8,128)S(1)}, u32[]{:S(2)}, u32[]{:S(2)}) collective-permute-start(f32[128,512]{1,0:T(8,128)S(1)} %get-tuple-element.68.refs_3_), channel_id=1, source_target_pairs={{0,1},{1,0},{2,3},{3,2},{4,5},{5,4},{6,7},{7,6},{8,9},{9,8},{10,11... | collective-permute-start | bytes 786440 | tf_op jit(solution)/shard_map/ppermute | solution.py:21
  20.8 1.5 %collective-permute-start.4 = (f32[8,128]{1,0:T(8,128)S(1)}, f32[8,128]{1,0:T(8,128)S(1)}, u32[]{:S(2)}, u32[]{:S(2)}) collective-permute-start(f32[8,128]{1,0:T(8,128)S(1)} %get-tuple-element.67.refs_1_), channel_id=1, source_target_pairs={{0,1},{1,0},{2,3},{3,2},{4,5},{5,4},{6,7},{7,6},{8,9},{9,8},{10,11... | collective-permute-start | bytes 12296 | tf_op jit(solution)/shard_map/ppermute | solution.py:21
  21.9 2.4 %collective-permute-start.7 = (f32[128,512]{1,0:T(8,128)S(1)}, f32[128,512]{1,0:T(8,128)S(1)}, u32[]{:S(2)}, u32[]{:S(2)}) collective-permute-start(f32[128,512]{1,0:T(8,128)S(1)} %get-tuple-element.73.refs_3_), channel_id=1, source_target_pairs={{0,1},{1,0},{2,3},{3,2},{4,5},{5,4},{6,7},{7,6},{8,9},{9,8},{10,11... | collective-permute-start | bytes 786440 | tf_op jit(solution)/shard_map/ppermute | solution.py:21
  24.1 2.5 %collective-permute-start.6 = (f32[4,2,16,512]{3,2,1,0:T(8,128)S(1)}, f32[4,2,16,512]{3,2,1,0:T(8,128)S(1)}, u32[]{:S(2)}, u32[]{:S(2)}) collective-permute-start(f32[4,2,16,512]{3,2,1,0:T(8,128)S(1)} %slice_bitcast_fusion.3), channel_id=1, source_target_pairs={{0,1},{1,0},{2,3},{3,2},{4,5},{5,4},{6,7},{7,6},{8,9},{9,8},{10,11... | collective-permute-start | bytes 786440 | tf_op jit(solution)/shard_map/ppermute | solution.py:21
  26.1 1.6 %collective-permute-start.8 = (f32[4,2,16,512]{3,2,1,0:T(8,128)S(1)}, f32[4,2,16,512]{3,2,1,0:T(8,128)S(1)}, u32[]{:S(2)}, u32[]{:S(2)}) collective-permute-start(f32[4,2,16,512]{3,2,1,0:T(8,128)S(1)} %slice_bitcast_fusion.2), channel_id=1, source_target_pairs={{0,1},{1,0},{2,3},{3,2},{4,5},{5,4},{6,7},{7,6},{8,9},{9,8},{10,11... | collective-permute-start | bytes 786440 | tf_op jit(solution)/shard_map/ppermute | solution.py:21
  27.8 5.8 %collective-permute-start.13 = (f32[2,16,1024]{2,1,0:T(8,128)S(1)}, f32[2,16,1024]{2,1,0:T(8,128)S(1)}, u32[]{:S(2)}, u32[]{:S(2)}) collective-permute-start(f32[2,16,1024]{2,1,0:T(8,128)S(1)} %get-tuple-element.108), channel_id=1, source_target_pairs={{0,2},{1,3},{2,0},{3,1},{4,6},{5,7},{6,4},{7,5},{8,10},{9,11},{10,... | collective-permute-start | bytes 393224 | tf_op jit(solution)/shard_map/ppermute | solution.py:21
  29.2 6.4 %collective-permute-start.14 = (f32[2,16,1024]{2,1,0:T(8,128)S(1)}, f32[2,16,1024]{2,1,0:T(8,128)S(1)}, u32[]{:S(2)}, u32[]{:S(2)}) collective-permute-start(f32[2,16,1024]{2,1,0:T(8,128)S(1)} %get-tuple-element.110), channel_id=1, source_target_pairs={{0,4},{1,5},{2,6},{3,7},{4,0},{5,1},{6,2},{7,3},{8,12},{9,13},{10,... | collective-permute-start | bytes 393224 | tf_op jit(solution)/shard_map/ppermute | solution.py:21
  30.8 6.9 %collective-permute-start.15 = (f32[2,16,1024]{2,1,0:T(8,128)S(1)}, f32[2,16,1024]{2,1,0:T(8,128)S(1)}, u32[]{:S(2)}, u32[]{:S(2)}) collective-permute-start(f32[2,16,1024]{2,1,0:T(8,128)S(1)} %get-tuple-element.109), channel_id=1, source_target_pairs={{0,6},{1,7},{2,4},{3,5},{4,2},{5,3},{6,0},{7,1},{8,14},{9,15},{10,... | collective-permute-start | bytes 393224 | tf_op jit(solution)/shard_map/ppermute | solution.py:21
  31.4 9.7 %collective-permute-start.10 = (f32[2,136,128]{2,1,0:T(8,128)S(1)}, f32[2,136,128]{2,1,0:T(8,128)S(1)}, u32[]{:S(2)}, u32[]{:S(2)}) collective-permute-start(f32[2,136,128]{2,1,0:T(8,128)S(1)} %collective-permute-done.1.refs_0_.refs_1_), channel_id=1, source_target_pairs={{0,1},{1,0},{2,3},{3,2},{4,5},{5,4},{6,7},{7,6},{8,9},{9,8},{10,11... | collective-permute-start | bytes 417800 | tf_op jit(solution)/shard_map/ppermute | solution.py:21
  31.4 9.7 %collective-permute-start.11 = (f32[2,136,128]{2,1,0:T(8,128)S(1)}, f32[2,136,128]{2,1,0:T(8,128)S(1)}, u32[]{:S(2)}, u32[]{:S(2)}) collective-permute-start(f32[2,136,128]{2,1,0:T(8,128)S(1)} %collective-permute-done.2.refs_0_.refs_2_), channel_id=1, source_target_pairs={{0,1},{1,0},{2,3},{3,2},{4,5},{5,4},{6,7},{7,6},{8,9},{9,8},{10,11... | collective-permute-start | bytes 417800 | tf_op jit(solution)/shard_map/ppermute | solution.py:21
  33.7 7.4 %collective-permute-start.12 = (f32[2,136,128]{2,1,0:T(8,128)S(1)}, f32[2,136,128]{2,1,0:T(8,128)S(1)}, u32[]{:S(2)}, u32[]{:S(2)}) collective-permute-start(f32[2,136,128]{2,1,0:T(8,128)S(1)} %collective-permute-done.3.refs_0_.refs_3_), channel_id=1, source_target_pairs={{0,1},{1,0},{2,3},{3,2},{4,5},{5,4},{6,7},{7,6},{8,9},{9,8},{10,11... | collective-permute-start | bytes 417800 | tf_op jit(solution)/shard_map/ppermute | solution.py:21
  35.5 5.5 %collective-permute-start.9 = (f32[2,136,128]{2,1,0:T(8,128)S(1)}, f32[2,136,128]{2,1,0:T(8,128)S(1)}, u32[]{:S(2)}, u32[]{:S(2)}) collective-permute-start(f32[2,136,128]{2,1,0:T(8,128)S(1)} %constant_dynamic-update-slice_fusion.refs_0_), channel_id=1, source_target_pairs={{0,1},{1,0},{2,3},{3,2},{4,5},{5,4},{6,7},{7,6},{8,9},{9,8},{10,11... | collective-permute-start | bytes 417800 | tf_op jit(solution)/shard_map/ppermute | solution.py:21
  37.7 8.5 %collective-permute-start.16 = (f32[2,16,1024]{2,1,0:T(8,128)S(1)}, f32[2,16,1024]{2,1,0:T(8,128)S(1)}, u32[]{:S(2)}, u32[]{:S(2)}) collective-permute-start(f32[2,16,1024]{2,1,0:T(8,128)S(1)} %fusion.3.refs_0_), channel_id=1, source_target_pairs={{0,8},{1,9},{2,10},{3,11},{4,12},{5,13},{6,14},{7,15},{8,0},{9,1},... | collective-permute-start | bytes 393224 | tf_op jit(solution)/shard_map/ppermute | solution.py:21
  46.3 4.3 %collective-permute-start.17 = (f32[16,1024]{1,0:T(8,128)S(1)}, f32[16,1024]{1,0:T(8,128)S(1)}, u32[]{:S(2)}, u32[]{:S(2)}) collective-permute-start(f32[16,1024]{1,0:T(8,128)S(1)} %own.2.refs_1_), channel_id=1, source_target_pairs={{0,2},{1,3},{2,0},{3,1},{4,6},{5,7},{6,4},{7,5},{8,10},{9,11},{10,... | collective-permute-start | bytes 196616 | tf_op jit(solution)/shard_map/ppermute | solution.py:21
  47.5 4.3 %collective-permute-start.18 = (f32[16,1024]{1,0:T(8,128)S(1)}, f32[16,1024]{1,0:T(8,128)S(1)}, u32[]{:S(2)}, u32[]{:S(2)}) collective-permute-start(f32[16,1024]{1,0:T(8,128)S(1)} %own.2.refs_1_), channel_id=1, source_target_pairs={{0,4},{1,5},{2,6},{3,7},{4,0},{5,1},{6,2},{7,3},{8,12},{9,13},{10,... | collective-permute-start | bytes 196616 | tf_op jit(solution)/shard_map/ppermute | solution.py:21
  47.8 5.2 %collective-permute-start.19 = (f32[16,1024]{1,0:T(8,128)S(1)}, f32[16,1024]{1,0:T(8,128)S(1)}, u32[]{:S(2)}, u32[]{:S(2)}) collective-permute-start(f32[16,1024]{1,0:T(8,128)S(1)} %own.2.refs_1_), channel_id=1, source_target_pairs={{0,6},{1,7},{2,4},{3,5},{4,2},{5,3},{6,0},{7,1},{8,14},{9,15},{10,... | collective-permute-start | bytes 196616 | tf_op jit(solution)/shard_map/ppermute | solution.py:21
  49.8 3.2 %collective-permute-start.20 = (f32[16,1024]{1,0:T(8,128)S(1)}, f32[16,1024]{1,0:T(8,128)S(1)}, u32[]{:S(2)}, u32[]{:S(2)}) collective-permute-start(f32[16,1024]{1,0:T(8,128)S(1)} %own.2.refs_1_), channel_id=1, source_target_pairs={{0,1},{1,0},{2,3},{3,2},{4,5},{5,4},{6,7},{7,6},{8,9},{9,8},{10,11... | collective-permute-start | bytes 196616 | tf_op jit(solution)/shard_map/ppermute | solution.py:21
  50.6 2.4 %collective-permute-start.21 = (f32[16,1024]{1,0:T(8,128)S(1)}, f32[16,1024]{1,0:T(8,128)S(1)}, u32[]{:S(2)}, u32[]{:S(2)}) collective-permute-start(f32[16,1024]{1,0:T(8,128)S(1)} %collective-permute-done.17.refs_2_), channel_id=1, source_target_pairs={{0,1},{1,0},{2,3},{3,2},{4,5},{5,4},{6,7},{7,6},{8,9},{9,8},{10,11... | collective-permute-start | bytes 196616 | tf_op jit(solution)/shard_map/ppermute | solution.py:21
  51.8 1.3 %collective-permute-start.22 = (f32[16,1024]{1,0:T(8,128)S(1)}, f32[16,1024]{1,0:T(8,128)S(1)}, u32[]{:S(2)}, u32[]{:S(2)}) collective-permute-start(f32[16,1024]{1,0:T(8,128)S(1)} %collective-permute-done.18.refs_3_), channel_id=1, source_target_pairs={{0,1},{1,0},{2,3},{3,2},{4,5},{5,4},{6,7},{7,6},{8,9},{9,8},{10,11... | collective-permute-start | bytes 196616 | tf_op jit(solution)/shard_map/ppermute | solution.py:21
  53.0 1.3 %collective-permute-start.23 = (f32[16,1024]{1,0:T(8,128)S(1)}, f32[16,1024]{1,0:T(8,128)S(1)}, u32[]{:S(2)}, u32[]{:S(2)}) collective-permute-start(f32[16,1024]{1,0:T(8,128)S(1)} %collective-permute-done.19.refs_4_), channel_id=1, source_target_pairs={{0,1},{1,0},{2,3},{3,2},{4,5},{5,4},{6,7},{7,6},{8,9},{9,8},{10,11... | collective-permute-start | bytes 196616 | tf_op jit(solution)/shard_map/ppermute | solution.py:21
  55.8 2.4 %collective-permute-start.24 = (f32[4,2,16,512]{3,2,1,0:T(8,128)S(1)}, f32[4,2,16,512]{3,2,1,0:T(8,128)S(1)}, u32[]{:S(2)}, u32[]{:S(2)}) collective-permute-start(f32[4,2,16,512]{3,2,1,0:T(8,128)S(1)} %slice_bitcast_fusion.1), channel_id=1, source_target_pairs={{0,1},{1,0},{2,3},{3,2},{4,5},{5,4},{6,7},{7,6},{8,9},{9,8},{10,11... | collective-permute-start | bytes 786440 | tf_op jit(solution)/shard_map/ppermute | solution.py:21
  57.8 1.6 %collective-permute-start.25 = (f32[4,2,16,512]{3,2,1,0:T(8,128)S(1)}, f32[4,2,16,512]{3,2,1,0:T(8,128)S(1)}, u32[]{:S(2)}, u32[]{:S(2)}) collective-permute-start(f32[4,2,16,512]{3,2,1,0:T(8,128)S(1)} %slice_bitcast_fusion), channel_id=1, source_target_pairs={{0,1},{1,0},{2,3},{3,2},{4,5},{5,4},{6,7},{7,6},{8,9},{9,8},{10,11... | collective-permute-start | bytes 786440 | tf_op jit(solution)/shard_map/ppermute | solution.py:21
  59.5 5.8 %collective-permute-start.26 = (f32[2,16,1024]{2,1,0:T(8,128)S(1)}, f32[2,16,1024]{2,1,0:T(8,128)S(1)}, u32[]{:S(2)}, u32[]{:S(2)}) collective-permute-start(f32[2,16,1024]{2,1,0:T(8,128)S(1)} %get-tuple-element.105), channel_id=1, source_target_pairs={{0,2},{1,3},{2,0},{3,1},{4,6},{5,7},{6,4},{7,5},{8,10},{9,11},{10,... | collective-permute-start | bytes 393224 | tf_op jit(solution)/shard_map/ppermute | solution.py:21
  60.6 6.3 %collective-permute-start.27 = (f32[2,16,1024]{2,1,0:T(8,128)S(1)}, f32[2,16,1024]{2,1,0:T(8,128)S(1)}, u32[]{:S(2)}, u32[]{:S(2)}) collective-permute-start(f32[2,16,1024]{2,1,0:T(8,128)S(1)} %get-tuple-element.107), channel_id=1, source_target_pairs={{0,4},{1,5},{2,6},{3,7},{4,0},{5,1},{6,2},{7,3},{8,12},{9,13},{10,... | collective-permute-start | bytes 393224 | tf_op jit(solution)/shard_map/ppermute | solution.py:21
  62.2 7.2 %collective-permute-start.28 = (f32[2,16,1024]{2,1,0:T(8,128)S(1)}, f32[2,16,1024]{2,1,0:T(8,128)S(1)}, u32[]{:S(2)}, u32[]{:S(2)}) collective-permute-start(f32[2,16,1024]{2,1,0:T(8,128)S(1)} %get-tuple-element.106), channel_id=1, source_target_pairs={{0,6},{1,7},{2,4},{3,5},{4,2},{5,3},{6,0},{7,1},{8,14},{9,15},{10,... | collective-permute-start | bytes 393224 | tf_op jit(solution)/shard_map/ppermute | solution.py:21
  69.4 9.2 %collective-permute-start.29 = (f32[2,16,1024]{2,1,0:T(8,128)S(1)}, f32[2,16,1024]{2,1,0:T(8,128)S(1)}, u32[]{:S(2)}, u32[]{:S(2)}) collective-permute-start(f32[2,16,1024]{2,1,0:T(8,128)S(1)} %fusion.1.refs_0_), channel_id=1, source_target_pairs={{0,8},{1,9},{2,10},{3,11},{4,12},{5,13},{6,14},{7,15},{8,0},{9,1},... | collective-permute-start | bytes 393224 | tf_op jit(solution)/shard_map/ppermute | solution.py:21
  78.6 5.0 %collective-permute-start.30 = (f32[16,1024]{1,0:T(8,128)S(1)}, f32[16,1024]{1,0:T(8,128)S(1)}, u32[]{:S(2)}, u32[]{:S(2)}) collective-permute-start(f32[16,1024]{1,0:T(8,128)S(1)} %own.3.refs_1_), channel_id=1, source_target_pairs={{0,2},{1,3},{2,0},{3,1},{4,6},{5,7},{6,4},{7,5},{8,10},{9,11},{10,... | collective-permute-start | bytes 196616 | tf_op jit(solution)/shard_map/ppermute | solution.py:21
  79.3 4.4 %collective-permute-start.31 = (f32[16,1024]{1,0:T(8,128)S(1)}, f32[16,1024]{1,0:T(8,128)S(1)}, u32[]{:S(2)}, u32[]{:S(2)}) collective-permute-start(f32[16,1024]{1,0:T(8,128)S(1)} %own.3.refs_1_), channel_id=1, source_target_pairs={{0,4},{1,5},{2,6},{3,7},{4,0},{5,1},{6,2},{7,3},{8,12},{9,13},{10,... | collective-permute-start | bytes 196616 | tf_op jit(solution)/shard_map/ppermute | solution.py:21
  79.3 5.8 %collective-permute-start.32 = (f32[16,1024]{1,0:T(8,128)S(1)}, f32[16,1024]{1,0:T(8,128)S(1)}, u32[]{:S(2)}, u32[]{:S(2)}) collective-permute-start(f32[16,1024]{1,0:T(8,128)S(1)} %own.3.refs_1_), channel_id=1, source_target_pairs={{0,6},{1,7},{2,4},{3,5},{4,2},{5,3},{6,0},{7,1},{8,14},{9,15},{10,... | collective-permute-start | bytes 196616 | tf_op jit(solution)/shard_map/ppermute | solution.py:21
  82.2 2.9 %collective-permute-start.33 = (f32[16,1024]{1,0:T(8,128)S(1)}, f32[16,1024]{1,0:T(8,128)S(1)}, u32[]{:S(2)}, u32[]{:S(2)}) collective-permute-start(f32[16,1024]{1,0:T(8,128)S(1)} %own.3.refs_1_), channel_id=1, source_target_pairs={{0,1},{1,0},{2,3},{3,2},{4,5},{5,4},{6,7},{7,6},{8,9},{9,8},{10,11... | collective-permute-start | bytes 196616 | tf_op jit(solution)/shard_map/ppermute | solution.py:21
  83.7 1.5 %collective-permute-start.34 = (f32[16,1024]{1,0:T(8,128)S(1)}, f32[16,1024]{1,0:T(8,128)S(1)}, u32[]{:S(2)}, u32[]{:S(2)}) collective-permute-start(f32[16,1024]{1,0:T(8,128)S(1)} %collective-permute-done.30.refs_2_), channel_id=1, source_target_pairs={{0,1},{1,0},{2,3},{3,2},{4,5},{5,4},{6,7},{7,6},{8,9},{9,8},{10,11... | collective-permute-start | bytes 196616 | tf_op jit(solution)/shard_map/ppermute | solution.py:21
  83.7 1.5 %collective-permute-start.35 = (f32[16,1024]{1,0:T(8,128)S(1)}, f32[16,1024]{1,0:T(8,128)S(1)}, u32[]{:S(2)}, u32[]{:S(2)}) collective-permute-start(f32[16,1024]{1,0:T(8,128)S(1)} %collective-permute-done.31.refs_3_), channel_id=1, source_target_pairs={{0,1},{1,0},{2,3},{3,2},{4,5},{5,4},{6,7},{7,6},{8,9},{9,8},{10,11... | collective-permute-start | bytes 196616 | tf_op jit(solution)/shard_map/ppermute | solution.py:21
  85.1 1.3 %collective-permute-start.36 = (f32[16,1024]{1,0:T(8,128)S(1)}, f32[16,1024]{1,0:T(8,128)S(1)}, u32[]{:S(2)}, u32[]{:S(2)}) collective-permute-start(f32[16,1024]{1,0:T(8,128)S(1)} %collective-permute-done.32.refs_4_), channel_id=1, source_target_pairs={{0,1},{1,0},{2,3},{3,2},{4,5},{5,4},{6,7},{7,6},{8,9},{9,8},{10,11... | collective-permute-start | bytes 196616 | tf_op jit(solution)/shard_map/ppermute | solution.py:21

commit v5 on v4

--- a/solution.py
+++ b/solution.py
@@ -9,6 +9,8 @@
 
 F32, BF16 = jnp.float32, jnp.bfloat16
 SQUARE = (2, 4, 6)
+FIRST = (2, 4)
+FULL = ((4, 8), (8, 2))
 VMEM = pl.BlockSpec(memory_space=pltpu.VMEM)
 SMEM = pl.BlockSpec(memory_space=pltpu.SMEM)
 ANY = pl.BlockSpec(memory_space=pl.ANY)
@@ -16,9 +18,14 @@
 ROW = (((1,), (1,)), ((), ()))
 
 
-def swap(x, offset):
+def swap(x, offset, odd=None):
     n = lax.axis_size("pol")
-    return lax.ppermute(x, "pol", [(i, i ^ offset) for i in range(n)])
+    offsets = (offset, offset if odd is None else odd)
+    return lax.ppermute(x, "pol", [(i, i ^ offsets[i % 2]) for i in range(n)])
+
+
+def tie(x, other):
+    return lax.optimization_barrier((x, other))[0]
 
 
 def far_offsets():
@@ -184,9 +191,10 @@
     out[...] = dot(pick, one, ROW) + dot(pick, two, ROW) + dot(pick, three, ROW)
 
 
-def slice_spot(me_ref, order, slice_funds):
-    label = (order >> 2) | ((order & 3) << 1)
-    return pl.multiple_of(((me_ref[0] & 7) ^ label) * slice_funds, slice_funds)
+def slice_spot(me, order, slice_funds):
+    core = (me & 1) ^ (order >> 1)
+    side = ((me >> (1 + core)) & 1) ^ (order & 1)
+    return pl.multiple_of((2 * core + side) * slice_funds, slice_funds)
 
 
 def advance(step, got, base, guar, draw, asset, liab):
@@ -203,10 +211,11 @@
     return jnp.concatenate([jnp.concatenate([g_hi, d_hi], 1), jnp.concatenate([g_lo, d_lo], 1)], 0)
 
 
-def own_body(slice_funds, me, part, peer, *refs):
+def own_body(slice_funds, first, me, part, peer, *refs):
     totals, out = refs[:-1], refs[-1]
-    rows = pl.ds(pl.multiple_of((me[0] & 7) * slice_funds, slice_funds), slice_funds)
-    growth = part[rows, :] + peer[rows, :]
+    rows = pl.ds(slice_spot(me[0], 0, slice_funds), slice_funds)
+    cut = slice(first, first + out.shape[1])
+    growth = part[rows, cut] + peer[rows, cut]
     asset, liab = totals[0][0], totals[0][1]
     for t in totals[1:]:
         asset, liab = asset + t[0], liab + t[1]
@@ -222,17 +231,23 @@
     if year == 0:
         mine, other = refs.pop(0), refs.pop(0)
     else:
-        slices = [refs.pop(0) for _ in range(8)]
+        slices = [refs.pop(0) for _ in range(4)]
     part, peer = refs.pop(0), refs.pop(0)
     draws, member, wides = refs.pop(0), refs.pop(0), refs.pop(0)
-    states = [(refs.pop(0), refs.pop(0)) for _ in range(0 if year == 0 else 2 if last else 1)]
+    held = [refs.pop(0) for _ in range(2 if year else 0)]
     lead = 0
-    if last:
-        earlier = [refs.pop(0) for _ in range(2 * year)]
-        out_a, out_l, out_r, declared, buf_a, buf_l, sem = refs
+    copies = []
+    if last and first:
+        half_a, half_l, *earlier, out_a, out_l, out_r, declared, buf_a, buf_l, sem = refs
+        own = out_r.at[year]
+        for k, (half, out) in enumerate(((half_a, out_a), (half_l, out_l))):
+            copies.append(pltpu.make_async_copy(half, out.at[:, 0:first], sem.at[k, 0]))
+            copies[-1].start()
+    elif last:
+        out_a, out_l, own, declared = refs
     else:
         member_t = refs.pop(0)
-        out_a, out_l, out_s, out_r, declared, acc = refs
+        out_a, out_l, out_s, own, declared, acc = refs
     funds, width = declared.shape
     count = member.shape[1]
     if year == 0:
@@ -246,16 +261,11 @@
         declared[...] = rate(ratio * (1.0 + (part[...] + peer[...])))
     else:
         lead = first
-        for o in range(8):
-            spot = pl.ds(slice_spot(me, o, slice_funds), slice_funds)
-            declared[spot, :] = slices[o][:, first : first + width]
-    if last:
-        own = out_r.at[year]
+        for o in range(4):
+            declared[pl.ds(slice_spot(me[0], o, slice_funds), slice_funds), :] = slices[o][...]
+    if last and first:
         for y in range(year):
             out_r[y] = earlier[2 * y][...] + earlier[2 * y + 1][...]
-    else:
-        own = out_r
-    copies = []
 
     def gathered(c):
         there = slice(lead + c, lead + c + STEP)
@@ -275,20 +285,18 @@
                 asset = jnp.concatenate([wides[2 * years, rows, :]] * (STEP // 128), 1)
                 liab = jnp.concatenate([wides[2 * years + 1, rows, :]] * (STEP // 128), 1)
             else:
-                half = states[0][0].shape[1]
-                held = states[c // half]
-                at = slice(c % half, c % half + STEP)
-                asset, liab = held[0][rows, at], held[1][rows, at]
+                asset, liab = held[0][rows, cut], held[1][rows, cut]
             asset, liab = advance(
                 STEP, now[r // ROWS], wides[2 * year, rows, :], wides[2 * year + 1, rows, :],
                 draws[year, rows, first + c : first + c + STEP], asset, liab,
             )
-            if last:
+            if last and first:
                 buf_a[c // STEP, rows, :] = asset
                 buf_l[c // STEP, rows, :] = liab
             else:
                 out_a[rows, cut] = asset
                 out_l[rows, cut] = liab
+            if not last:
                 a_hi, a_lo = halves(asset)
                 l_hi, l_lo = halves(liab)
                 ma, ml = member_t[year + 1, :, rows], member_t[0, :, rows]
@@ -296,22 +304,26 @@
                 add_l = dot(jnp.concatenate([ml, ml], 1), jnp.concatenate([l_hi, l_lo], 0))
                 sum_a = add_a if sum_a is None else sum_a + add_a
                 sum_l = add_l if sum_l is None else sum_l + add_l
-        if last:
+        if last and first:
             for buf, out, k in ((buf_a, out_a, 0), (buf_l, out_l, 1)):
-                copy = pltpu.make_async_copy(buf.at[c // STEP], out.at[:, cut], sem.at[k, c // STEP])
+                copy = pltpu.make_async_copy(
+                    buf.at[c // STEP], out.at[:, first + c : first + c + STEP], sem.at[k, 1 + c // STEP]
+                )
                 copy.start()
                 copies.append(copy)
-        else:
+        elif not last:
             acc[0, :, cut] = sum_a
             acc[1, :, cut] = sum_l
     own_columns(me, declared[...], first, own)
-    if last:
-        for copy in copies:
-            copy.wait()
-    else:
-        for o in range(8):
+    if last and first:
+        out_r[year] = out_r[year] + earlier[2 * year][...]
+    for copy in copies:
+        copy.wait()
+    if not last:
+        for o in range(4):
             for v in range(2):
-                out_s[o // 4, o % 4, v] = acc[v, pl.ds(slice_spot(me, o, slice_funds), slice_funds), :]
+                spot = pl.ds(slice_spot(me[0], o, slice_funds), slice_funds)
+                out_s[o // 2, o % 2, v] = acc[v, spot, :]
 
 
 def local(
@@ -334,7 +346,7 @@
     n = lax.axis_size("pol")
     me = lax.axis_index("pol")
     me_ref = me.astype(jnp.int32).reshape(1)
-    slice_funds = funds // 8
+    slice_funds = funds // 4
     owned = paths // n
     half = paths // 2
     draws = lapse_draw.transpose(1, 0, 2)
@@ -401,74 +413,97 @@
     peer = [swap(p, 1) for p in part]
     other_sums = swap(sums, 1)
 
-    state = None
-    rates = []
-    for year in range(years):
-        last = year + 1 == years
-        if year == 0:
-            head = [sums, other_sums]
-        else:
-            near = [own] + [swap(own, o) for o in SQUARE]
-            head = near + [swap(v, 1) for v in near]
-        shares = []
-        for h in range(1 if last else 2):
-            width = paths if last else half
-            first = h * half
-            pair = [part[h], peer[h]] if year == 0 else [part, peer]
-            ins = [me_ref] + head + pair + [draws, member, wides]
-            cost = dict(flops=2 * 2 * count * 2 * funds * width, moved=20 * count * width)
-            if last:
-                ins += [v for s in state for v in s] + [v for rs in rates for v in rs]
+    later = {0: (part, peer)}
+    others = []
+    rates = [[None, None] for _ in range(years)]
+    final = []
+
+    def advance_half(h):
+        first = h * half
+        head, state = [sums, other_sums], []
+        other = yield sums
+        for year in range(years):
+            last = year + 1 == years
+            pair = [v[h] for v in later[0]] if year == 0 else list(later[year])
+            ins = [me_ref] + tie(head, other) + pair + [draws, member, wides] + state
+            specs = [SMEM] + [VMEM] * (len(ins) - 1)
+            scratch = [pltpu.VMEM((funds, half), F32)]
+            if last and h:
+                tiles = half // STEP
                 out = [shaped(count, paths), shaped(count, paths), shaped(years, owned, funds)]
                 out_specs = [ANY, ANY, VMEM]
-                tiles = paths // STEP
-                scratch = [pltpu.VMEM((funds, width), F32)]
                 scratch += [pltpu.VMEM((tiles, count, STEP), F32)] * 2
-                scratch += [pltpu.SemaphoreType.DMA((2, tiles))]
+                scratch += [pltpu.SemaphoreType.DMA((2, 1 + tiles))]
+                before = final[:2] + [v for rs in rates for v in rs if v is not None]
+                ins += before
+                specs += [VMEM] * len(before)
+            elif last:
+                out = [shaped(count, half), shaped(count, half), shaped(owned, funds)]
+                out_specs = [VMEM] * 3
             else:
-                ins += ([] if year == 0 else list(state[h])) + [member_t]
-                out = [shaped(count, width)] * 2
-                out += [shaped(2, 4, 2, slice_funds, width), shaped(owned, funds)]
-                out_specs = None
-                scratch = [pltpu.VMEM((funds, width), F32), pltpu.VMEM((2, funds, width), F32)]
-            shares.append(
-                call(
-                    functools.partial(year_body, year, first, last, slice_funds),
-                    out,
-                    [SMEM] + [VMEM] * (len(ins) - 1),
-                    "year",
-                    scratch=scratch,
-                    out_specs=out_specs,
-                    limit=16 if last else 8,
-                    **cost,
-                )(*ins)
-            )
-        if last:
-            assets, liability, credit = shares[0]
-            return assets, liability, credit.transpose(0, 2, 1)
-        state = [(s[0], s[1]) for s in shares]
-        rates.append([s[3] for s in shares])
-        held = jnp.concatenate([s[2][0] + swap(s[2][1], 1) for s in shares], -1)
-        x_later, held = lax.optimization_barrier((x_later, held))
-        if year == 0:
-            blocks, held = lax.optimization_barrier((blocks, held))
-            others = [swap(b, 1) for b in blocks]
-        arrived = [swap(held[i + 1], o) for i, o in enumerate(SQUARE)]
-        totals = held[0] + arrived[0] + arrived[1] + arrived[2]
-        for o in far[:-1]:
-            totals = totals + swap(totals, o)
-        totals = [totals] + [swap(totals, o) for o in far[-1:]]
-        part = returns(year + 1, 0, paths, blocks, x_later)[0]
-        peer = returns(year + 1, 0, paths, others, x_later)[0]
-        own = call(
-            functools.partial(own_body, slice_funds),
-            shaped(slice_funds, paths),
-            [SMEM] + [VMEM] * (2 + len(totals)),
-            "own",
-            10**6,
-            10**6,
-            limit=2,
-        )(me_ref, part, peer, *totals)
+                ins.append(member_t)
+                specs.append(VMEM)
+                out = [shaped(count, half)] * 2
+                out += [shaped(2, 2, 2, slice_funds, half), shaped(owned, funds)]
+                out_specs = [VMEM] * 4
+                scratch += [pltpu.VMEM((2, funds, half), F32)]
+            result = call(
+                functools.partial(year_body, year, first, last, slice_funds),
+                out,
+                specs,
+                "year",
+                flops=2 * 2 * count * 2 * funds * half,
+                moved=20 * count * half,
+                scratch=scratch,
+                out_specs=out_specs,
+                limit=10,
+            )(*ins)
+            if last:
+                final[:] = result
+                rates[year][h] = result[2]
+                yield result[2]
+                return
+            state, share, rates[year][h] = list(result[:2]), result[2], result[3]
+            other = yield share
+            held = share[0] + tie(swap(share[1], 1), other)
+            if year == 0 and h == 0:
+                others.extend(swap(b, 1) for b in tie(blocks, held))
+            other = yield held
+            held = held[0] + tie(swap(held[1], *FIRST), other)
+            other = yield held
+            *steps, closing = list(FULL) + [(o,) for o in far[1:]]
+            for i, step in enumerate(steps):
+                held = held + tie(swap(held, *step), other)
+                if i == 0 and h == 0:
+                    xs = tie(x_later, held)
+                    later[year + 1] = [
+                        returns(year + 1, 0, paths, b, xs)[0] for b in (blocks, others)
+                    ]
+                other = yield held
+            own = call(
+                functools.partial(own_body, slice_funds, first),
+                shaped(slice_funds, half),
+                [SMEM] + [VMEM] * 4,
+                "own",
+                10**6,
+                10**6,
+                limit=2,
+            )(me_ref, *later[year + 1], held, tie(swap(held, *closing), other))
+            other = yield own
+            near = tie(swap(own, *FIRST), other)
+            other = yield near
+            head = [own, near, swap(own, 1), swap(near, 1)]
+
+    running = [advance_half(h) for h in range(2)]
+    newest = [next(r) for r in running]
+    while running:
+        for h, r in enumerate(list(running)):
+            try:
+                newest[h] = r.send(newest[1 - h])
+            except StopIteration:
+                running.remove(r)
+    assets, liability, credit = final
+    return assets, liability, credit.transpose(0, 2, 1)
 
 
 def solution(mesh):

time: 90.4 us -> 88.2 us (0.976)
  waiting for transfers between devices: 33.9 us -> 24.7 us
  starting transfers between devices: 30.4 us -> 36.8 us
    ppermute x37 -> x39, waiting for transfers between devices: 33.9 us -> 24.7 us  [swap(): return lax.ppermute(x, 'pol', [(i, i ^ offsets[i % 2]) for i in range(n)])]
    ppermute x37 -> x39, starting transfers between devices: 30.4 us -> 36.8 us  [swap(): return lax.ppermute(x, 'pol', [(i, i ^ offsets[i % 2]) for i in range(n)])]
    pallas_call x7 -> x10, Pallas kernels: 10.5 us -> 10.9 us  [the longest x6 10.6 us: advance_half(): call(functools.partial(year_body, year, first, last, slice_funds), out, s...]
  transfers between devices with their start and end apart: 37 -> 39, of which waited for: 21 -> 17; matrix products, arithmetic and copies ran while one was open for 0% -> 1% of each run, Pallas kernels for 15% -> 19%
where the time goes in v5:
time: 88.2 us; the launch traced here: 87.9 us
  starting transfers between devices  36.8 us (42%)
  waiting for transfers between devices  24.7 us (28%)
  Pallas kernels  21.7 us (25%)
  local copies, waits for them, and re-layouts  3.16 us (4%)
  between operations  1.15 us (1%)
    ppermute x39, starting transfers between devices, swap(): return lax.ppermute(x, 'pol', [(i, i ^ offsets[i % 2]) for i in range(n)])  36.8 us
    ppermute x39, waiting for transfers between devices, swap(): return lax.ppermute(x, 'pol', [(i, i ^ offsets[i % 2]) for i in range(n)])  24.7 us
    pallas_call x6, Pallas kernels, advance_half(): call(functools.partial(year_body, year, first, last, slice_funds), out, s...  10.6 us
    pallas_call x9, Pallas kernels, returns(): call(functools.partial(returns_body, year, first, secs, len(before) > 0,...  7.95 us
    unnamed x9, local copies, waits for them, and re-layouts  3.02 us
  transfers between devices with their start and end apart: 39, of which 17 were waited for; matrix products, arithmetic and copies ran while one was open for 1% of the time, Pallas kernels for 19%

profile of v5, /device:TPU:0, one launch (start us, length us, event | category | flops | bytes accessed | tf_op | source)
XLA Modules:
  0.0 87.9 jit_solution(4863299664439045647)
XLA Ops:
  0.6 1.7 %pack.1 = (f32[136,128]{1,0:T(8,128)}, f32[8,512]{1,0:T(8,128)}) custom-call(s32[1]{0:T(128)} %bitcast.refs_0_.me, f32[64,128]{1,0:T(8,128)} %refs_1_.1, f32[64,128]{1,0:T(8,128)} %refs_2_.1, f32[1,64]{1,0:T(1,128)} %bitcast.64, s32[1,512]{1,0:T(1,128)} %bitcast.59, s32[1,512]{1,0:T(1,128)} %bitcast.60, f32[1,512]{1,0:T(1,128)} %bitcast.61, ...), custom_call_target="tpu_custom_call" | custom-call | flops 1000000 | bytes 100000 | tf_op jit(solution)/shard_map/pack/pallas_call | solution.py:359
  2.4 4.1 %collective-permute-start = (f32[1,136,128]{2,1,0:T(8,128)}, f32[1,136,128]{2,1,0:T(8,128)S(1)}, u32[]{:S(2)}, u32[]{:S(2)}) collective-permute-start(f32[1,136,128]{2,1,0:T(8,128)} %bitcast.58), channel_id=1, source_target_pairs={{0,8},{1,9},{2,10},{3,11},{4,12},{5,13},{6,14},{7,15},{8,0},{9,1},... | collective-permute-start | bytes 208904 | tf_op jit(solution)/shard_map/ppermute | solution.py:24
  6.5 1.4 %copy-done.1 = f32[3,128,1024]{2,1,0:T(8,128)S(1)} copy-done((f32[3,128,1024]{2,1,0:T(8,128)S(1)}, f32[3,128,1024]{2,1,0:T(8,128)}, u32[]{:S(2)}) %copy-start.1) | copy-done | bytes 1572888
  7.9 0.9 %copy-done.2 = f32[136,128]{1,0:T(8,128)S(1)} copy-done((f32[136,128]{1,0:T(8,128)S(1)}, f32[136,128]{1,0:T(8,128)}, u32[]{:S(2)}) %copy-start.2) | copy-done | bytes 69656
  8.7 0.7 copy-done.3
  9.5 1.1 %columns.1 = (bf16[3,128,512]{2,1,0:T(8,128)(2,1)S(1)}, bf16[3,512,256]{2,1,0:T(8,128)(2,1)S(1)}, f32[8,512,128]{2,1,0:T(8,128)S(1)}, bf16[2,128,1024]{2,1,0:T(8...) custom-call(f32[8,512]{1,0:T(8,128)S(1)} %copy-done.3, f32[136,128]{1,0:T(8,128)S(1)} %copy-done.2, ...), custom_call_target="tpu_custom_call" | custom-call | flops 1000000 | bytes 4000000 | tf_op jit(solution)/shard_map/columns/pallas_call | solution.py:371
  10.6 1.6 %collective-permute-start.1 = (f32[2,136,128]{2,1,0:T(8,128)S(1)}, f32[2,136,128]{2,1,0:T(8,128)S(1)}, u32[]{:S(2)}, u32[]{:S(2)}) collective-permute-start(f32[2,136,128]{2,1,0:T(8,128)S(1)} %constant_dynamic-update-slice_fusion.refs_0_), channel_id=1, source_target_pairs={{0,2},{1,3},{2,0},{3,1},{4,6},{5,7},{6,4},{7,5},{8,10},{9,11},{10,... | collective-permute-start | bytes 417800 | tf_op jit(solution)/shard_map/ppermute | solution.py:24
  12.2 1.6 %collective-permute-start.2 = (f32[2,136,128]{2,1,0:T(8,128)S(1)}, f32[2,136,128]{2,1,0:T(8,128)S(1)}, u32[]{:S(2)}, u32[]{:S(2)}) collective-permute-start(f32[2,136,128]{2,1,0:T(8,128)S(1)} %constant_dynamic-update-slice_fusion.refs_0_), channel_id=1, source_target_pairs={{0,4},{1,5},{2,6},{3,7},{4,0},{5,1},{6,2},{7,3},{8,12},{9,13},{10,... | collective-permute-start | bytes 417800 | tf_op jit(solution)/shard_map/ppermute | solution.py:24
  13.8 0.4 collective-permute-start.3
  14.2 0.6 returns.9
  14.8 1.1 %collective-permute-done.1.refs_0_.refs_1_ = f32[2,136,128]{2,1,0:T(8,128)S(1)} collective-permute-done((f32[2,136,128]{2,1,0:T(8,128)S(1)}, f32[2,136,128]{2,1,0:T(8,128)S(1)}, u32[]{:S(2)}, u32[]{:S(2)}) %collective-permute-start.1) | collective-permute-done | bytes 139296 | tf_op jit(solution)/shard_map/ppermute | solution.py:24
  15.8 0.6 returns.10
  16.4 2.1 %collective-permute-done.2.refs_0_.refs_2_ = f32[2,136,128]{2,1,0:T(8,128)S(1)} collective-permute-done((f32[2,136,128]{2,1,0:T(8,128)S(1)}, f32[2,136,128]{2,1,0:T(8,128)S(1)}, u32[]{:S(2)}, u32[]{:S(2)}) %collective-permute-start.2) | collective-permute-done | bytes 139296 | tf_op jit(solution)/shard_map/ppermute | solution.py:24
  18.5 0.6 returns.11
  19.1 1.1 %collective-permute-done.3.refs_0_.refs_3_ = f32[2,136,128]{2,1,0:T(8,128)S(1)} collective-permute-done((f32[2,136,128]{2,1,0:T(8,128)S(1)}, f32[2,136,128]{2,1,0:T(8,128)S(1)}, u32[]{:S(2)}, u32[]{:S(2)}) %collective-permute-start.3) | collective-permute-done | bytes 139296 | tf_op jit(solution)/shard_map/ppermute | solution.py:24
  20.2 0.5 returns.12
  20.8 0.5 collective-permute-start.4
  21.3 0.7 returns.13
  22.0 0.3 collective-permute-done.4.refs_2_
  22.3 1.8 %year.6 = (f32[512,512]{1,0:T(8,128)S(1)}, f32[512,512]{1,0:T(8,128)S(1)}, f32[2,2,2,32,512]{4,3,2,1,0:T(8,128)S(1)}, f32[64,128]{1,0:T(8,128)S(1)}) custom-call(s32[1]{0:T(128)} %bitcast.refs_0_.me, f32[8,128]{1,0:T(8,128)S(1)} %get-tuple-element.115.refs_1_, f32[8,128]{1,0:T(8,128)S(1)} %collective-permute-done.4.refs_2_, ...), custom_call_target="tpu_custom_call" | custom-call | flops 268435456 | bytes 5242880 | tf_op jit(solution)/shard_map/year/pallas_call | solution.py:450
  24.4 1.8 %year.7 = (f32[512,512]{1,0:T(8,128)S(1)}, f32[512,512]{1,0:T(8,128)S(1)}, f32[2,2,2,32,512]{4,3,2,1,0:T(8,128)S(1)}, f32[64,128]{1,0:T(8,128)S(1)}) custom-call(s32[1]{0:T(128)} %bitcast.refs_0_.me, f32[8,128]{1,0:T(8,128)S(1)} %get-tuple-element.115.refs_1_, f32[8,128]{1,0:T(8,128)S(1)} %collective-permute-done.4.refs_2_, ...), custom_call_target="tpu_custom_call" | custom-call | flops 268435456 | bytes 5242880 | tf_op jit(solution)/shard_map/year/pallas_call | solution.py:450
  26.2 0.4 collective-permute-start.9
  26.7 1.4 %collective-permute-start.8 = (f32[2,32,512]{2,1,0:T(8,128)S(1)}, f32[2,32,512]{2,1,0:T(8,128)S(1)}, u32[]{:S(2)}, u32[]{:S(2)}) collective-permute-start(f32[2,32,512]{2,1,0:T(8,128)S(1)} %slice_bitcast_fusion.10), channel_id=1, source_target_pairs={{0,2},{1,5},{2,0},{3,7},{4,6},{5,1},{6,4},{7,3},{8,10},{9,13},{10,... | collective-permute-start | bytes 393224 | tf_op jit(solution)/shard_map/ppermute | solution.py:24
  28.1 1.1 %collective-permute-start.11 = (f32[2,32,512]{2,1,0:T(8,128)S(1)}, f32[2,32,512]{2,1,0:T(8,128)S(1)}, u32[]{:S(2)}, u32[]{:S(2)}) collective-permute-start(f32[2,32,512]{2,1,0:T(8,128)S(1)} %slice_bitcast_fusion.8), channel_id=1, source_target_pairs={{0,2},{1,5},{2,0},{3,7},{4,6},{5,1},{6,4},{7,3},{8,10},{9,13},{10,... | collective-permute-start | bytes 393224 | tf_op jit(solution)/shard_map/ppermute | solution.py:24
  29.2 2.5 %collective-permute-done.8 = f32[2,32,512]{2,1,0:T(8,128)S(1)} collective-permute-done((f32[2,32,512]{2,1,0:T(8,128)S(1)}, f32[2,32,512]{2,1,0:T(8,128)S(1)}, u32[]{:S(2)}, u32[]{:S(2)}) %collective-permute-start.8) | collective-permute-done | bytes 131104 | tf_op jit(solution)/shard_map/ppermute | solution.py:24
  31.7 1.4 %collective-permute-start.10 = (f32[2,32,512]{2,1,0:T(8,128)S(1)}, f32[2,32,512]{2,1,0:T(8,128)S(1)}, u32[]{:S(2)}, u32[]{:S(2)}) collective-permute-start(f32[2,32,512]{2,1,0:T(8,128)S(1)} %fusion.3), channel_id=1, source_target_pairs={{0,4},{1,9},{2,6},{3,11},{4,0},{5,13},{6,2},{7,15},{8,12},{9,1},{1... | collective-permute-start | bytes 393224 | tf_op jit(solution)/shard_map/ppermute | solution.py:24
  33.2 1.6 %collective-permute-start.17 = (f32[2,32,512]{2,1,0:T(8,128)S(1)}, f32[2,32,512]{2,1,0:T(8,128)S(1)}, u32[]{:S(2)}, u32[]{:S(2)}) collective-permute-start(f32[2,32,512]{2,1,0:T(8,128)S(1)} %fusion.2), channel_id=1, source_target_pairs={{0,4},{1,9},{2,6},{3,11},{4,0},{5,13},{6,2},{7,15},{8,12},{9,1},{1... | collective-permute-start | bytes 393224 | tf_op jit(solution)/shard_map/ppermute | solution.py:24
  34.8 0.5 collective-permute-start.13
  35.3 1.8 %collective-permute-done.10 = f32[2,32,512]{2,1,0:T(8,128)S(1)} collective-permute-done((f32[2,32,512]{2,1,0:T(8,128)S(1)}, f32[2,32,512]{2,1,0:T(8,128)S(1)}, u32[]{:S(2)}, u32[]{:S(2)}) %collective-permute-start.10) | collective-permute-done | bytes 131104 | tf_op jit(solution)/shard_map/ppermute | solution.py:24
  37.1 0.2 collective-permute-start.15
  37.3 2.9 %collective-permute-done.17 = f32[2,32,512]{2,1,0:T(8,128)S(1)} collective-permute-done((f32[2,32,512]{2,1,0:T(8,128)S(1)}, f32[2,32,512]{2,1,0:T(8,128)S(1)}, u32[]{:S(2)}, u32[]{:S(2)}) %collective-permute-start.17) | collective-permute-done | bytes 131104 | tf_op jit(solution)/shard_map/ppermute | solution.py:24
  40.2 2.0 %collective-permute-start.16 = (f32[2,32,512]{2,1,0:T(8,128)S(1)}, f32[2,32,512]{2,1,0:T(8,128)S(1)}, u32[]{:S(2)}, u32[]{:S(2)}) collective-permute-start(f32[2,32,512]{2,1,0:T(8,128)S(1)} %add.40.refs_0_), channel_id=1, source_target_pairs={{0,8},{1,3},{2,10},{3,1},{4,12},{5,7},{6,14},{7,5},{8,0},{9,11},{1... | collective-permute-start | bytes 393224 | tf_op jit(solution)/shard_map/ppermute | solution.py:24
  42.2 1.0 %collective-permute-start.19 = (f32[2,32,512]{2,1,0:T(8,128)S(1)}, f32[2,32,512]{2,1,0:T(8,128)S(1)}, u32[]{:S(2)}, u32[]{:S(2)}) collective-permute-start(f32[2,32,512]{2,1,0:T(8,128)S(1)} %add.41.refs_0_), channel_id=1, source_target_pairs={{0,8},{1,3},{2,10},{3,1},{4,12},{5,7},{6,14},{7,5},{8,0},{9,11},{1... | collective-permute-start | bytes 393224 | tf_op jit(solution)/shard_map/ppermute | solution.py:24
  43.2 1.3 %returns.14 = (f32[128,1024]{1,0:T(8,128)S(1)}, f32[8,128]{1,0:T(8,128)}) custom-call(f32[2,136,128]{2,1,0:T(8,128)S(1)} %constant_dynamic-update-slice_fusion.refs_0_, f32[2,136,128]{2,1,0:T(8,128)S(1)} %collective-permute-done.1.refs_0_.refs_1_, f32[2,136,128]{2,1,0:T(8,128)S(1)} %collective-permute-done.2.refs_0_.refs_2_, ...), custom_call_target="tpu_custom_call" | custom-call | tf_op jit(solution)/shard_map/returns/pallas_call | solution.py:396
  44.5 1.3 %returns.15 = (f32[128,1024]{1,0:T(8,128)S(1)}, f32[8,128]{1,0:T(8,128)}) custom-call(f32[2,136,128]{2,1,0:T(8,128)S(1)} %collective-permute-done.12.refs_0_, f32[2,136,128]{2,1,0:T(8,128)S(1)} %collective-permute-done.13.refs_1_, f32[2,136,128]{2,1,0:T(8,128)S(1)} %collective-permute-done.14.refs_2_, f32[2,136,128]{2,1,0:T(8,128)S(1)} %collective-permute-done.15.refs_3_, ...), custom_call_target="tpu_custom_call" | custom-call | tf_op jit(solution)/shard_map/returns/pallas_call | solution.py:396
  45.8 1.7 %collective-permute-done.16.refs_1_ = f32[2,32,512]{2,1,0:T(8,128)S(1)} collective-permute-done((f32[2,32,512]{2,1,0:T(8,128)S(1)}, f32[2,32,512]{2,1,0:T(8,128)S(1)}, u32[]{:S(2)}, u32[]{:S(2)}) %collective-permute-start.16) | collective-permute-done | bytes 131104 | tf_op jit(solution)/shard_map/ppermute | solution.py:24
  47.6 1.3 %collective-permute-start.18 = (f32[32,512]{1,0:T(8,128)S(1)}, f32[32,512]{1,0:T(8,128)S(1)}, u32[]{:S(2)}, u32[]{:S(2)}) collective-permute-start(f32[32,512]{1,0:T(8,128)S(1)} %own.4.refs_1_), channel_id=1, source_target_pairs={{0,2},{1,5},{2,0},{3,7},{4,6},{5,1},{6,4},{7,3},{8,10},{9,13},{10,... | collective-permute-start | bytes 196616 | tf_op jit(solution)/shard_map/ppermute | solution.py:24
  48.9 0.3 collective-permute-done.19.refs_1_
  49.3 1.1 %collective-permute-start.22 = (f32[32,512]{1,0:T(8,128)S(1)}, f32[32,512]{1,0:T(8,128)S(1)}, u32[]{:S(2)}, u32[]{:S(2)}) collective-permute-start(f32[32,512]{1,0:T(8,128)S(1)} %own.5.refs_1_), channel_id=1, source_target_pairs={{0,2},{1,5},{2,0},{3,7},{4,6},{5,1},{6,4},{7,3},{8,10},{9,13},{10,... | collective-permute-start | bytes 196616 | tf_op jit(solution)/shard_map/ppermute | solution.py:24
  50.4 1.6 %collective-permute-done.18.refs_2_ = f32[32,512]{1,0:T(8,128)S(1)} collective-permute-done((f32[32,512]{1,0:T(8,128)S(1)}, f32[32,512]{1,0:T(8,128)S(1)}, u32[]{:S(2)}, u32[]{:S(2)}) %collective-permute-start.18) | collective-permute-done | bytes 65568 | tf_op jit(solution)/shard_map/ppermute | solution.py:24
  52.0 0.5 collective-permute-start.24
  52.5 1.2 %collective-permute-done.22.refs_2_ = f32[32,512]{1,0:T(8,128)S(1)} collective-permute-done((f32[32,512]{1,0:T(8,128)S(1)}, f32[32,512]{1,0:T(8,128)S(1)}, u32[]{:S(2)}, u32[]{:S(2)}) %collective-permute-start.22) | collective-permute-done | bytes 65568 | tf_op jit(solution)/shard_map/ppermute | solution.py:24
  53.7 1.6 %year.8 = (f32[512,512]{1,0:T(8,128)S(1)}, f32[512,512]{1,0:T(8,128)S(1)}, f32[2,2,2,32,512]{4,3,2,1,0:T(8,128)S(1)}, f32[64,128]{1,0:T(8,128)S(1)}) custom-call(s32[1]{0:T(128)} %bitcast.refs_0_.me, f32[32,512]{1,0:T(8,128)S(1)} %own.4.refs_1_, f32[32,512]{1,0:T(8,128)S(1)} %collective-permute-done.18.refs_2_, ...), custom_call_target="tpu_custom_call" | custom-call | flops 268435456 | bytes 5242880 | tf_op jit(solution)/shard_map/year/pallas_call | solution.py:450
  55.3 0.6 collective-permute-start.23
  55.9 1.7 %year.9 = (f32[512,512]{1,0:T(8,128)S(1)}, f32[512,512]{1,0:T(8,128)S(1)}, f32[2,2,2,32,512]{4,3,2,1,0:T(8,128)S(1)}, f32[64,128]{1,0:T(8,128)S(1)}) custom-call(s32[1]{0:T(128)} %bitcast.refs_0_.me, f32[32,512]{1,0:T(8,128)S(1)} %own.5.refs_1_, f32[32,512]{1,0:T(8,128)S(1)} %collective-permute-done.22.refs_2_, ...), custom_call_target="tpu_custom_call" | custom-call | flops 268435456 | bytes 5242880 | tf_op jit(solution)/shard_map/year/pallas_call | solution.py:450
  57.8 1.1 %collective-permute-start.26 = (f32[2,32,512]{2,1,0:T(8,128)S(1)}, f32[2,32,512]{2,1,0:T(8,128)S(1)}, u32[]{:S(2)}, u32[]{:S(2)}) collective-permute-start(f32[2,32,512]{2,1,0:T(8,128)S(1)} %slice_bitcast_fusion.6), channel_id=1, source_target_pairs={{0,2},{1,5},{2,0},{3,7},{4,6},{5,1},{6,4},{7,3},{8,10},{9,13},{10,... | collective-permute-start | bytes 393224 | tf_op jit(solution)/shard_map/ppermute | solution.py:24
  58.8 0.4 collective-permute-done.27
  59.3 1.1 %collective-permute-start.29 = (f32[2,32,512]{2,1,0:T(8,128)S(1)}, f32[2,32,512]{2,1,0:T(8,128)S(1)}, u32[]{:S(2)}, u32[]{:S(2)}) collective-permute-start(f32[2,32,512]{2,1,0:T(8,128)S(1)} %slice_bitcast_fusion.4), channel_id=1, source_target_pairs={{0,2},{1,5},{2,0},{3,7},{4,6},{5,1},{6,4},{7,3},{8,10},{9,13},{10,... | collective-permute-start | bytes 393224 | tf_op jit(solution)/shard_map/ppermute | solution.py:24
  60.4 2.4 %collective-permute-done.26 = f32[2,32,512]{2,1,0:T(8,128)S(1)} collective-permute-done((f32[2,32,512]{2,1,0:T(8,128)S(1)}, f32[2,32,512]{2,1,0:T(8,128)S(1)}, u32[]{:S(2)}, u32[]{:S(2)}) %collective-permute-start.26) | collective-permute-done | bytes 131104 | tf_op jit(solution)/shard_map/ppermute | solution.py:24
  62.8 2.2 %collective-permute-start.28 = (f32[2,32,512]{2,1,0:T(8,128)S(1)}, f32[2,32,512]{2,1,0:T(8,128)S(1)}, u32[]{:S(2)}, u32[]{:S(2)}) collective-permute-start(f32[2,32,512]{2,1,0:T(8,128)S(1)} %fusion.1), channel_id=1, source_target_pairs={{0,4},{1,9},{2,6},{3,11},{4,0},{5,13},{6,2},{7,15},{8,12},{9,1},{1... | collective-permute-start | bytes 393224 | tf_op jit(solution)/shard_map/ppermute | solution.py:24
  65.0 1.6 %collective-permute-start.30 = (f32[2,32,512]{2,1,0:T(8,128)S(1)}, f32[2,32,512]{2,1,0:T(8,128)S(1)}, u32[]{:S(2)}, u32[]{:S(2)}) collective-permute-start(f32[2,32,512]{2,1,0:T(8,128)S(1)} %fusion), channel_id=1, source_target_pairs={{0,4},{1,9},{2,6},{3,11},{4,0},{5,13},{6,2},{7,15},{8,12},{9,1},{1... | collective-permute-start | bytes 393224 | tf_op jit(solution)/shard_map/ppermute | solution.py:24
  66.6 2.8 %collective-permute-done.28 = f32[2,32,512]{2,1,0:T(8,128)S(1)} collective-permute-done((f32[2,32,512]{2,1,0:T(8,128)S(1)}, f32[2,32,512]{2,1,0:T(8,128)S(1)}, u32[]{:S(2)}, u32[]{:S(2)}) %collective-permute-start.28) | collective-permute-done | bytes 131104 | tf_op jit(solution)/shard_map/ppermute | solution.py:24
  69.5 2.1 %collective-permute-start.32 = (f32[2,32,512]{2,1,0:T(8,128)S(1)}, f32[2,32,512]{2,1,0:T(8,128)S(1)}, u32[]{:S(2)}, u32[]{:S(2)}) collective-permute-start(f32[2,32,512]{2,1,0:T(8,128)S(1)} %add.46.refs_0_), channel_id=1, source_target_pairs={{0,8},{1,3},{2,10},{3,1},{4,12},{5,7},{6,14},{7,5},{8,0},{9,11},{1... | collective-permute-start | bytes 393224 | tf_op jit(solution)/shard_map/ppermute | solution.py:24
  71.5 0.5 collective-permute-done.30
  72.1 2.2 %collective-permute-start.31 = (f32[2,32,512]{2,1,0:T(8,128)S(1)}, f32[2,32,512]{2,1,0:T(8,128)S(1)}, u32[]{:S(2)}, u32[]{:S(2)}) collective-permute-start(f32[2,32,512]{2,1,0:T(8,128)S(1)} %add.47.refs_0_), channel_id=1, source_target_pairs={{0,8},{1,3},{2,10},{3,1},{4,12},{5,7},{6,14},{7,5},{8,0},{9,11},{1... | collective-permute-start | bytes 393224 | tf_op jit(solution)/shard_map/ppermute | solution.py:24
  74.3 1.3 %returns.17 = (f32[128,1024]{1,0:T(8,128)S(1)}, f32[8,128]{1,0:T(8,128)}) custom-call(f32[2,136,128]{2,1,0:T(8,128)S(1)} %collective-permute-done.12.refs_0_, f32[2,136,128]{2,1,0:T(8,128)S(1)} %collective-permute-done.13.refs_1_, f32[2,136,128]{2,1,0:T(8,128)S(1)} %collective-permute-done.14.refs_2_, f32[2,136,128]{2,1,0:T(8,128)S(1)} %collective-permute-done.15.refs_3_, ...), custom_call_target="tpu_custom_call" | custom-call | tf_op jit(solution)/shard_map/returns/pallas_call | solution.py:396
  75.6 1.3 %returns.16 = (f32[128,1024]{1,0:T(8,128)S(1)}, f32[8,128]{1,0:T(8,128)}) custom-call(f32[2,136,128]{2,1,0:T(8,128)S(1)} %constant_dynamic-update-slice_fusion.refs_0_, f32[2,136,128]{2,1,0:T(8,128)S(1)} %collective-permute-done.1.refs_0_.refs_1_, f32[2,136,128]{2,1,0:T(8,128)S(1)} %collective-permute-done.2.refs_0_.refs_2_, ...), custom_call_target="tpu_custom_call" | custom-call | tf_op jit(solution)/shard_map/returns/pallas_call | solution.py:396
  77.0 1.5 %collective-permute-start.34 = (f32[32,512]{1,0:T(8,128)S(1)}, f32[32,512]{1,0:T(8,128)S(1)}, u32[]{:S(2)}, u32[]{:S(2)}) collective-permute-start(f32[32,512]{1,0:T(8,128)S(1)} %own.6.refs_1_), channel_id=1, source_target_pairs={{0,2},{1,5},{2,0},{3,7},{4,6},{5,1},{6,4},{7,3},{8,10},{9,13},{10,... | collective-permute-start | bytes 196616 | tf_op jit(solution)/shard_map/ppermute | solution.py:24
  78.6 2.8 %collective-permute-start.33 = (f32[32,512]{1,0:T(8,128)S(1)}, f32[32,512]{1,0:T(8,128)S(1)}, u32[]{:S(2)}, u32[]{:S(2)}) collective-permute-start(f32[32,512]{1,0:T(8,128)S(1)} %own.7.refs_1_), channel_id=1, source_target_pairs={{0,2},{1,5},{2,0},{3,7},{4,6},{5,1},{6,4},{7,3},{8,10},{9,13},{10,... | collective-permute-start | bytes 196616 | tf_op jit(solution)/shard_map/ppermute | solution.py:24
  81.4 0.5 collective-permute-start.38
  82.0 1.7 %collective-permute-done.33.refs_2_ = f32[32,512]{1,0:T(8,128)S(1)} collective-permute-done((f32[32,512]{1,0:T(8,128)S(1)}, f32[32,512]{1,0:T(8,128)S(1)}, u32[]{:S(2)}, u32[]{:S(2)}) %collective-permute-start.33) | collective-permute-done | bytes 65568 | tf_op jit(solution)/shard_map/ppermute | solution.py:24
  83.7 1.0 %year.10 = (f32[512,512]{1,0:T(8,128)S(1)}, f32[512,512]{1,0:T(8,128)S(1)}, f32[64,128]{1,0:T(8,128)S(1)}) custom-call(s32[1]{0:T(128)} %bitcast.refs_0_.me, f32[32,512]{1,0:T(8,128)S(1)} %own.6.refs_1_, f32[32,512]{1,0:T(8,128)S(1)} %collective-permute-done.34.refs_2_, f32[32,512]{1,0:T(8,128)S(1)} %collective-permute-done.37.refs_3_, ...), custom_call_target="tpu_custom_call" | custom-call | flops 268435456 | bytes 5242880 | tf_op jit(solution)/shard_map/year/pallas_call | solution.py:450
  84.7 0.3 collective-permute-done.36.refs_4_
  84.9 2.8 %year.11 = (f32[512,1024]{1,0:T(8,128)}, f32[512,1024]{1,0:T(8,128)}, f32[3,64,128]{2,1,0:T(8,128)}) custom-call(s32[1]{0:T(128)} %bitcast.refs_0_.me, f32[32,512]{1,0:T(8,128)S(1)} %own.7.refs_1_, f32[32,512]{1,0:T(8,128)S(1)} %collective-permute-done.33.refs_2_, f32[32,512]{1,0:T(8,128)S(1)} %collective-permute-done.35.refs_3_, ...), custom_call_target="tpu_custom_call" | custom-call | flops 268435456 | bytes 5242880 | tf_op jit(solution)/shard_map/year/pallas_call | solution.py:450
  (65 shorter events, 1.3 us)
Async XLA Ops:
  2.4 8.3 %collective-permute-start = (f32[1,136,128]{2,1,0:T(8,128)}, f32[1,136,128]{2,1,0:T(8,128)S(1)}, u32[]{:S(2)}, u32[]{:S(2)}) collective-permute-start(f32[1,136,128]{2,1,0:T(8,128)} %bitcast.58), channel_id=1, source_target_pairs={{0,8},{1,9},{2,10},{3,11},{4,12},{5,13},{6,14},{7,15},{8,0},{9,1},... | collective-permute-start | bytes 208904 | tf_op jit(solution)/shard_map/ppermute | solution.py:24
  6.5 1.4 %copy-start.1 = (f32[3,128,1024]{2,1,0:T(8,128)S(1)}, f32[3,128,1024]{2,1,0:T(8,128)}, u32[]{:S(2)}) copy-start(f32[3,128,1024]{2,1,0:T(8,128)} %shocks.1) | copy-start | bytes 4718596
  7.9 0.9 %copy-start.2 = (f32[136,128]{1,0:T(8,128)S(1)}, f32[136,128]{1,0:T(8,128)}, u32[]{:S(2)}) copy-start(f32[136,128]{1,0:T(8,128)} %get-tuple-element.94.block) | copy-start | bytes 208900
  8.7 0.7 copy-start.3
  10.6 5.2 %collective-permute-start.1 = (f32[2,136,128]{2,1,0:T(8,128)S(1)}, f32[2,136,128]{2,1,0:T(8,128)S(1)}, u32[]{:S(2)}, u32[]{:S(2)}) collective-permute-start(f32[2,136,128]{2,1,0:T(8,128)S(1)} %constant_dynamic-update-slice_fusion.refs_0_), channel_id=1, source_target_pairs={{0,2},{1,3},{2,0},{3,1},{4,6},{5,7},{6,4},{7,5},{8,10},{9,11},{10,... | collective-permute-start | bytes 417800 | tf_op jit(solution)/shard_map/ppermute | solution.py:24
  12.2 6.3 %collective-permute-start.2 = (f32[2,136,128]{2,1,0:T(8,128)S(1)}, f32[2,136,128]{2,1,0:T(8,128)S(1)}, u32[]{:S(2)}, u32[]{:S(2)}) collective-permute-start(f32[2,136,128]{2,1,0:T(8,128)S(1)} %constant_dynamic-update-slice_fusion.refs_0_), channel_id=1, source_target_pairs={{0,4},{1,5},{2,6},{3,7},{4,0},{5,1},{6,2},{7,3},{8,12},{9,13},{10,... | collective-permute-start | bytes 417800 | tf_op jit(solution)/shard_map/ppermute | solution.py:24
  13.8 6.4 %collective-permute-start.3 = (f32[2,136,128]{2,1,0:T(8,128)S(1)}, f32[2,136,128]{2,1,0:T(8,128)S(1)}, u32[]{:S(2)}, u32[]{:S(2)}) collective-permute-start(f32[2,136,128]{2,1,0:T(8,128)S(1)} %constant_dynamic-update-slice_fusion.refs_0_), channel_id=1, source_target_pairs={{0,6},{1,7},{2,4},{3,5},{4,2},{5,3},{6,0},{7,1},{8,14},{9,15},{10,... | collective-permute-start | bytes 417800 | tf_op jit(solution)/shard_map/ppermute | solution.py:24
  15.8 6.5 %copy-start = (bf16[512,3,1024]{2,0,1:T(8,128)(2,1)S(1)}, bf16[512,3,1024]{2,0,1:T(8,128)(2,1)}, u32[]{:S(2)}) copy-start(bf16[512,3,1024]{2,0,1:T(8,128)(2,1)} %param.23) | copy-start | bytes 9437188
  20.7 1.6 %collective-permute-start.5 = (f32[128,512]{1,0:T(8,128)S(1)}, f32[128,512]{1,0:T(8,128)S(1)}, u32[]{:S(2)}, u32[]{:S(2)}) collective-permute-start(f32[128,512]{1,0:T(8,128)S(1)} %get-tuple-element.110.refs_3_), channel_id=1, source_target_pairs={{0,1},{1,0},{2,3},{3,2},{4,5},{5,4},{6,7},{7,6},{8,9},{9,8},{10,11... | collective-permute-start | bytes 786440 | tf_op jit(solution)/shard_map/ppermute | solution.py:24
  20.8 1.5 %collective-permute-start.4 = (f32[8,128]{1,0:T(8,128)S(1)}, f32[8,128]{1,0:T(8,128)S(1)}, u32[]{:S(2)}, u32[]{:S(2)}) collective-permute-start(f32[8,128]{1,0:T(8,128)S(1)} %get-tuple-element.115.refs_1_), channel_id=1, source_target_pairs={{0,1},{1,0},{2,3},{3,2},{4,5},{5,4},{6,7},{7,6},{8,9},{9,8},{10,11... | collective-permute-start | bytes 12296 | tf_op jit(solution)/shard_map/ppermute | solution.py:24
  21.9 2.4 %collective-permute-start.7 = (f32[128,512]{1,0:T(8,128)S(1)}, f32[128,512]{1,0:T(8,128)S(1)}, u32[]{:S(2)}, u32[]{:S(2)}) collective-permute-start(f32[128,512]{1,0:T(8,128)S(1)} %get-tuple-element.117.refs_3_), channel_id=1, source_target_pairs={{0,1},{1,0},{2,3},{3,2},{4,5},{5,4},{6,7},{7,6},{8,9},{9,8},{10,11... | collective-permute-start | bytes 786440 | tf_op jit(solution)/shard_map/ppermute | solution.py:24
  24.2 2.5 %collective-permute-start.6 = (f32[2,2,32,512]{3,2,1,0:T(8,128)S(1)}, f32[2,2,32,512]{3,2,1,0:T(8,128)S(1)}, u32[]{:S(2)}, u32[]{:S(2)}) collective-permute-start(f32[2,2,32,512]{3,2,1,0:T(8,128)S(1)} %slice_bitcast_fusion.3), channel_id=1, source_target_pairs={{0,1},{1,0},{2,3},{3,2},{4,5},{5,4},{6,7},{7,6},{8,9},{9,8},{10,11... | collective-permute-start | bytes 786440 | tf_op jit(solution)/shard_map/ppermute | solution.py:24
  26.2 1.9 %collective-permute-start.9 = (f32[2,2,32,512]{3,2,1,0:T(8,128)S(1)}, f32[2,2,32,512]{3,2,1,0:T(8,128)S(1)}, u32[]{:S(2)}, u32[]{:S(2)}) collective-permute-start(f32[2,2,32,512]{3,2,1,0:T(8,128)S(1)} %slice_bitcast_fusion.2), channel_id=1, source_target_pairs={{0,1},{1,0},{2,3},{3,2},{4,5},{5,4},{6,7},{7,6},{8,9},{9,8},{10,11... | collective-permute-start | bytes 786440 | tf_op jit(solution)/shard_map/ppermute | solution.py:24
  26.7 5.0 %collective-permute-start.8 = (f32[2,32,512]{2,1,0:T(8,128)S(1)}, f32[2,32,512]{2,1,0:T(8,128)S(1)}, u32[]{:S(2)}, u32[]{:S(2)}) collective-permute-start(f32[2,32,512]{2,1,0:T(8,128)S(1)} %slice_bitcast_fusion.10), channel_id=1, source_target_pairs={{0,2},{1,5},{2,0},{3,7},{4,6},{5,1},{6,4},{7,3},{8,10},{9,13},{10,... | collective-permute-start | bytes 393224 | tf_op jit(solution)/shard_map/ppermute | solution.py:24
  28.1 5.1 %collective-permute-start.11 = (f32[2,32,512]{2,1,0:T(8,128)S(1)}, f32[2,32,512]{2,1,0:T(8,128)S(1)}, u32[]{:S(2)}, u32[]{:S(2)}) collective-permute-start(f32[2,32,512]{2,1,0:T(8,128)S(1)} %slice_bitcast_fusion.8), channel_id=1, source_target_pairs={{0,2},{1,5},{2,0},{3,7},{4,6},{5,1},{6,4},{7,3},{8,10},{9,13},{10,... | collective-permute-start | bytes 393224 | tf_op jit(solution)/shard_map/ppermute | solution.py:24
  31.7 5.3 %collective-permute-start.10 = (f32[2,32,512]{2,1,0:T(8,128)S(1)}, f32[2,32,512]{2,1,0:T(8,128)S(1)}, u32[]{:S(2)}, u32[]{:S(2)}) collective-permute-start(f32[2,32,512]{2,1,0:T(8,128)S(1)} %fusion.3), channel_id=1, source_target_pairs={{0,4},{1,9},{2,6},{3,11},{4,0},{5,13},{6,2},{7,15},{8,12},{9,1},{1... | collective-permute-start | bytes 393224 | tf_op jit(solution)/shard_map/ppermute | solution.py:24
  33.2 7.0 %collective-permute-start.17 = (f32[2,32,512]{2,1,0:T(8,128)S(1)}, f32[2,32,512]{2,1,0:T(8,128)S(1)}, u32[]{:S(2)}, u32[]{:S(2)}) collective-permute-start(f32[2,32,512]{2,1,0:T(8,128)S(1)} %fusion.2), channel_id=1, source_target_pairs={{0,4},{1,9},{2,6},{3,11},{4,0},{5,13},{6,2},{7,15},{8,12},{9,1},{1... | collective-permute-start | bytes 393224 | tf_op jit(solution)/shard_map/ppermute | solution.py:24
  34.8 7.4 %collective-permute-start.12 = (f32[2,136,128]{2,1,0:T(8,128)S(1)}, f32[2,136,128]{2,1,0:T(8,128)S(1)}, u32[]{:S(2)}, u32[]{:S(2)}) collective-permute-start(f32[2,136,128]{2,1,0:T(8,128)S(1)} %constant_dynamic-update-slice_fusion.refs_0_), channel_id=1, source_target_pairs={{0,1},{1,0},{2,3},{3,2},{4,5},{5,4},{6,7},{7,6},{8,9},{9,8},{10,11... | collective-permute-start | bytes 417800 | tf_op jit(solution)/shard_map/ppermute | solution.py:24
  34.8 9.7 %collective-permute-start.13 = (f32[2,136,128]{2,1,0:T(8,128)S(1)}, f32[2,136,128]{2,1,0:T(8,128)S(1)}, u32[]{:S(2)}, u32[]{:S(2)}) collective-permute-start(f32[2,136,128]{2,1,0:T(8,128)S(1)} %collective-permute-done.1.refs_0_.refs_1_), channel_id=1, source_target_pairs={{0,1},{1,0},{2,3},{3,2},{4,5},{5,4},{6,7},{7,6},{8,9},{9,8},{10,11... | collective-permute-start | bytes 417800 | tf_op jit(solution)/shard_map/ppermute | solution.py:24
  35.3 9.2 %collective-permute-start.14 = (f32[2,136,128]{2,1,0:T(8,128)S(1)}, f32[2,136,128]{2,1,0:T(8,128)S(1)}, u32[]{:S(2)}, u32[]{:S(2)}) collective-permute-start(f32[2,136,128]{2,1,0:T(8,128)S(1)} %collective-permute-done.2.refs_0_.refs_2_), channel_id=1, source_target_pairs={{0,1},{1,0},{2,3},{3,2},{4,5},{5,4},{6,7},{7,6},{8,9},{9,8},{10,11... | collective-permute-start | bytes 417800 | tf_op jit(solution)/shard_map/ppermute | solution.py:24
  37.1 7.5 %collective-permute-start.15 = (f32[2,136,128]{2,1,0:T(8,128)S(1)}, f32[2,136,128]{2,1,0:T(8,128)S(1)}, u32[]{:S(2)}, u32[]{:S(2)}) collective-permute-start(f32[2,136,128]{2,1,0:T(8,128)S(1)} %collective-permute-done.3.refs_0_.refs_3_), channel_id=1, source_target_pairs={{0,1},{1,0},{2,3},{3,2},{4,5},{5,4},{6,7},{7,6},{8,9},{9,8},{10,11... | collective-permute-start | bytes 417800 | tf_op jit(solution)/shard_map/ppermute | solution.py:24
  40.2 7.4 %collective-permute-start.16 = (f32[2,32,512]{2,1,0:T(8,128)S(1)}, f32[2,32,512]{2,1,0:T(8,128)S(1)}, u32[]{:S(2)}, u32[]{:S(2)}) collective-permute-start(f32[2,32,512]{2,1,0:T(8,128)S(1)} %add.40.refs_0_), channel_id=1, source_target_pairs={{0,8},{1,3},{2,10},{3,1},{4,12},{5,7},{6,14},{7,5},{8,0},{9,11},{1... | collective-permute-start | bytes 393224 | tf_op jit(solution)/shard_map/ppermute | solution.py:24
  42.2 7.0 %collective-permute-start.19 = (f32[2,32,512]{2,1,0:T(8,128)S(1)}, f32[2,32,512]{2,1,0:T(8,128)S(1)}, u32[]{:S(2)}, u32[]{:S(2)}) collective-permute-start(f32[2,32,512]{2,1,0:T(8,128)S(1)} %add.41.refs_0_), channel_id=1, source_target_pairs={{0,8},{1,3},{2,10},{3,1},{4,12},{5,7},{6,14},{7,5},{8,0},{9,11},{1... | collective-permute-start | bytes 393224 | tf_op jit(solution)/shard_map/ppermute | solution.py:24
  47.6 4.3 %collective-permute-start.18 = (f32[32,512]{1,0:T(8,128)S(1)}, f32[32,512]{1,0:T(8,128)S(1)}, u32[]{:S(2)}, u32[]{:S(2)}) collective-permute-start(f32[32,512]{1,0:T(8,128)S(1)} %own.4.refs_1_), channel_id=1, source_target_pairs={{0,2},{1,5},{2,0},{3,7},{4,6},{5,1},{6,4},{7,3},{8,10},{9,13},{10,... | collective-permute-start | bytes 196616 | tf_op jit(solution)/shard_map/ppermute | solution.py:24
  49.3 4.3 %collective-permute-start.22 = (f32[32,512]{1,0:T(8,128)S(1)}, f32[32,512]{1,0:T(8,128)S(1)}, u32[]{:S(2)}, u32[]{:S(2)}) collective-permute-start(f32[32,512]{1,0:T(8,128)S(1)} %own.5.refs_1_), channel_id=1, source_target_pairs={{0,2},{1,5},{2,0},{3,7},{4,6},{5,1},{6,4},{7,3},{8,10},{9,13},{10,... | collective-permute-start | bytes 196616 | tf_op jit(solution)/shard_map/ppermute | solution.py:24
  50.4 3.3 %collective-permute-start.20 = (f32[32,512]{1,0:T(8,128)S(1)}, f32[32,512]{1,0:T(8,128)S(1)}, u32[]{:S(2)}, u32[]{:S(2)}) collective-permute-start(f32[32,512]{1,0:T(8,128)S(1)} %own.4.refs_1_), channel_id=1, source_target_pairs={{0,1},{1,0},{2,3},{3,2},{4,5},{5,4},{6,7},{7,6},{8,9},{9,8},{10,11... | collective-permute-start | bytes 196616 | tf_op jit(solution)/shard_map/ppermute | solution.py:24
  52.0 1.7 %collective-permute-start.21 = (f32[32,512]{1,0:T(8,128)S(1)}, f32[32,512]{1,0:T(8,128)S(1)}, u32[]{:S(2)}, u32[]{:S(2)}) collective-permute-start(f32[32,512]{1,0:T(8,128)S(1)} %collective-permute-done.18.refs_2_), channel_id=1, source_target_pairs={{0,1},{1,0},{2,3},{3,2},{4,5},{5,4},{6,7},{7,6},{8,9},{9,8},{10,11... | collective-permute-start | bytes 196616 | tf_op jit(solution)/shard_map/ppermute | solution.py:24
  52.0 3.3 %collective-permute-start.24 = (f32[32,512]{1,0:T(8,128)S(1)}, f32[32,512]{1,0:T(8,128)S(1)}, u32[]{:S(2)}, u32[]{:S(2)}) collective-permute-start(f32[32,512]{1,0:T(8,128)S(1)} %own.5.refs_1_), channel_id=1, source_target_pairs={{0,1},{1,0},{2,3},{3,2},{4,5},{5,4},{6,7},{7,6},{8,9},{9,8},{10,11... | collective-permute-start | bytes 196616 | tf_op jit(solution)/shard_map/ppermute | solution.py:24
  53.7 1.6 %collective-permute-start.25 = (f32[32,512]{1,0:T(8,128)S(1)}, f32[32,512]{1,0:T(8,128)S(1)}, u32[]{:S(2)}, u32[]{:S(2)}) collective-permute-start(f32[32,512]{1,0:T(8,128)S(1)} %collective-permute-done.22.refs_2_), channel_id=1, source_target_pairs={{0,1},{1,0},{2,3},{3,2},{4,5},{5,4},{6,7},{7,6},{8,9},{9,8},{10,11... | collective-permute-start | bytes 196616 | tf_op jit(solution)/shard_map/ppermute | solution.py:24
  55.3 2.4 %collective-permute-start.23 = (f32[2,2,32,512]{3,2,1,0:T(8,128)S(1)}, f32[2,2,32,512]{3,2,1,0:T(8,128)S(1)}, u32[]{:S(2)}, u32[]{:S(2)}) collective-permute-start(f32[2,2,32,512]{3,2,1,0:T(8,128)S(1)} %slice_bitcast_fusion.1), channel_id=1, source_target_pairs={{0,1},{1,0},{2,3},{3,2},{4,5},{5,4},{6,7},{7,6},{8,9},{9,8},{10,11... | collective-permute-start | bytes 786440 | tf_op jit(solution)/shard_map/ppermute | solution.py:24
  57.6 1.6 %collective-permute-start.27 = (f32[2,2,32,512]{3,2,1,0:T(8,128)S(1)}, f32[2,2,32,512]{3,2,1,0:T(8,128)S(1)}, u32[]{:S(2)}, u32[]{:S(2)}) collective-permute-start(f32[2,2,32,512]{3,2,1,0:T(8,128)S(1)} %slice_bitcast_fusion), channel_id=1, source_target_pairs={{0,1},{1,0},{2,3},{3,2},{4,5},{5,4},{6,7},{7,6},{8,9},{9,8},{10,11... | collective-permute-start | bytes 786440 | tf_op jit(solution)/shard_map/ppermute | solution.py:24
  57.8 5.0 %collective-permute-start.26 = (f32[2,32,512]{2,1,0:T(8,128)S(1)}, f32[2,32,512]{2,1,0:T(8,128)S(1)}, u32[]{:S(2)}, u32[]{:S(2)}) collective-permute-start(f32[2,32,512]{2,1,0:T(8,128)S(1)} %slice_bitcast_fusion.6), channel_id=1, source_target_pairs={{0,2},{1,5},{2,0},{3,7},{4,6},{5,1},{6,4},{7,3},{8,10},{9,13},{10,... | collective-permute-start | bytes 393224 | tf_op jit(solution)/shard_map/ppermute | solution.py:24
  59.3 5.8 %collective-permute-start.29 = (f32[2,32,512]{2,1,0:T(8,128)S(1)}, f32[2,32,512]{2,1,0:T(8,128)S(1)}, u32[]{:S(2)}, u32[]{:S(2)}) collective-permute-start(f32[2,32,512]{2,1,0:T(8,128)S(1)} %slice_bitcast_fusion.4), channel_id=1, source_target_pairs={{0,2},{1,5},{2,0},{3,7},{4,6},{5,1},{6,4},{7,3},{8,10},{9,13},{10,... | collective-permute-start | bytes 393224 | tf_op jit(solution)/shard_map/ppermute | solution.py:24
  62.8 6.6 %collective-permute-start.28 = (f32[2,32,512]{2,1,0:T(8,128)S(1)}, f32[2,32,512]{2,1,0:T(8,128)S(1)}, u32[]{:S(2)}, u32[]{:S(2)}) collective-permute-start(f32[2,32,512]{2,1,0:T(8,128)S(1)} %fusion.1), channel_id=1, source_target_pairs={{0,4},{1,9},{2,6},{3,11},{4,0},{5,13},{6,2},{7,15},{8,12},{9,1},{1... | collective-permute-start | bytes 393224 | tf_op jit(solution)/shard_map/ppermute | solution.py:24
  65.0 7.0 %collective-permute-start.30 = (f32[2,32,512]{2,1,0:T(8,128)S(1)}, f32[2,32,512]{2,1,0:T(8,128)S(1)}, u32[]{:S(2)}, u32[]{:S(2)}) collective-permute-start(f32[2,32,512]{2,1,0:T(8,128)S(1)} %fusion), channel_id=1, source_target_pairs={{0,4},{1,9},{2,6},{3,11},{4,0},{5,13},{6,2},{7,15},{8,12},{9,1},{1... | collective-permute-start | bytes 393224 | tf_op jit(solution)/shard_map/ppermute | solution.py:24
  69.5 7.4 %collective-permute-start.32 = (f32[2,32,512]{2,1,0:T(8,128)S(1)}, f32[2,32,512]{2,1,0:T(8,128)S(1)}, u32[]{:S(2)}, u32[]{:S(2)}) collective-permute-start(f32[2,32,512]{2,1,0:T(8,128)S(1)} %add.46.refs_0_), channel_id=1, source_target_pairs={{0,8},{1,3},{2,10},{3,1},{4,12},{5,7},{6,14},{7,5},{8,0},{9,11},{1... | collective-permute-start | bytes 393224 | tf_op jit(solution)/shard_map/ppermute | solution.py:24
  72.1 6.4 %collective-permute-start.31 = (f32[2,32,512]{2,1,0:T(8,128)S(1)}, f32[2,32,512]{2,1,0:T(8,128)S(1)}, u32[]{:S(2)}, u32[]{:S(2)}) collective-permute-start(f32[2,32,512]{2,1,0:T(8,128)S(1)} %add.47.refs_0_), channel_id=1, source_target_pairs={{0,8},{1,3},{2,10},{3,1},{4,12},{5,7},{6,14},{7,5},{8,0},{9,11},{1... | collective-permute-start | bytes 393224 | tf_op jit(solution)/shard_map/ppermute | solution.py:24
  77.0 4.5 %collective-permute-start.34 = (f32[32,512]{1,0:T(8,128)S(1)}, f32[32,512]{1,0:T(8,128)S(1)}, u32[]{:S(2)}, u32[]{:S(2)}) collective-permute-start(f32[32,512]{1,0:T(8,128)S(1)} %own.6.refs_1_), channel_id=1, source_target_pairs={{0,2},{1,5},{2,0},{3,7},{4,6},{5,1},{6,4},{7,3},{8,10},{9,13},{10,... | collective-permute-start | bytes 196616 | tf_op jit(solution)/shard_map/ppermute | solution.py:24
  78.6 5.1 %collective-permute-start.33 = (f32[32,512]{1,0:T(8,128)S(1)}, f32[32,512]{1,0:T(8,128)S(1)}, u32[]{:S(2)}, u32[]{:S(2)}) collective-permute-start(f32[32,512]{1,0:T(8,128)S(1)} %own.7.refs_1_), channel_id=1, source_target_pairs={{0,2},{1,5},{2,0},{3,7},{4,6},{5,1},{6,4},{7,3},{8,10},{9,13},{10,... | collective-permute-start | bytes 196616 | tf_op jit(solution)/shard_map/ppermute | solution.py:24
  81.4 2.3 %collective-permute-start.37 = (f32[32,512]{1,0:T(8,128)S(1)}, f32[32,512]{1,0:T(8,128)S(1)}, u32[]{:S(2)}, u32[]{:S(2)}) collective-permute-start(f32[32,512]{1,0:T(8,128)S(1)} %own.6.refs_1_), channel_id=1, source_target_pairs={{0,1},{1,0},{2,3},{3,2},{4,5},{5,4},{6,7},{7,6},{8,9},{9,8},{10,11... | collective-permute-start | bytes 196616 | tf_op jit(solution)/shard_map/ppermute | solution.py:24
  81.4 2.2 %collective-permute-start.38 = (f32[32,512]{1,0:T(8,128)S(1)}, f32[32,512]{1,0:T(8,128)S(1)}, u32[]{:S(2)}, u32[]{:S(2)}) collective-permute-start(f32[32,512]{1,0:T(8,128)S(1)} %collective-permute-done.34.refs_2_), channel_id=1, source_target_pairs={{0,1},{1,0},{2,3},{3,2},{4,5},{5,4},{6,7},{7,6},{8,9},{9,8},{10,11... | collective-permute-start | bytes 196616 | tf_op jit(solution)/shard_map/ppermute | solution.py:24
  82.0 2.7 %collective-permute-start.35 = (f32[32,512]{1,0:T(8,128)S(1)}, f32[32,512]{1,0:T(8,128)S(1)}, u32[]{:S(2)}, u32[]{:S(2)}) collective-permute-start(f32[32,512]{1,0:T(8,128)S(1)} %own.7.refs_1_), channel_id=1, source_target_pairs={{0,1},{1,0},{2,3},{3,2},{4,5},{5,4},{6,7},{7,6},{8,9},{9,8},{10,11... | collective-permute-start | bytes 196616 | tf_op jit(solution)/shard_map/ppermute | solution.py:24
  83.7 1.3 %collective-permute-start.36 = (f32[32,512]{1,0:T(8,128)S(1)}, f32[32,512]{1,0:T(8,128)S(1)}, u32[]{:S(2)}, u32[]{:S(2)}) collective-permute-start(f32[32,512]{1,0:T(8,128)S(1)} %collective-permute-done.33.refs_2_), channel_id=1, source_target_pairs={{0,1},{1,0},{2,3},{3,2},{4,5},{5,4},{6,7},{7,6},{8,9},{9,8},{10,11... | collective-permute-start | bytes 196616 | tf_op jit(solution)/shard_map/ppermute | solution.py:24

commit v6 on v5

--- a/solution.py
+++ b/solution.py
@@ -464,21 +464,26 @@
                 yield result[2]
                 return
             state, share, rates[year][h] = list(result[:2]), result[2], result[3]
+            if year == 0 and h == 1:
+                others.append(swap(jnp.concatenate(tie(blocks, share)), 1))
             other = yield share
             held = share[0] + tie(swap(share[1], 1), other)
-            if year == 0 and h == 0:
-                others.extend(swap(b, 1) for b in tie(blocks, held))
             other = yield held
-            held = held[0] + tie(swap(held[1], *FIRST), other)
+            came = tie(swap(held[1], *FIRST), other)
+            if h == 0:
+                made = returns(year + 1, 0, paths, blocks, tie(x_later, held))[0]
+                came, made, ready = lax.optimization_barrier((came, made, list(others)))
+                later[year + 1] = [made]
+            held = held[0] + came
             other = yield held
             *steps, closing = list(FULL) + [(o,) for o in far[1:]]
             for i, step in enumerate(steps):
-                held = held + tie(swap(held, *step), other)
+                came = tie(swap(held, *step), other)
                 if i == 0 and h == 0:
-                    xs = tie(x_later, held)
-                    later[year + 1] = [
-                        returns(year + 1, 0, paths, b, xs)[0] for b in (blocks, others)
-                    ]
+                    made = returns(year + 1, 0, paths, ready, tie(x_later, held))[0]
+                    came, made = lax.optimization_barrier((came, made))
+                    later[year + 1].append(made)
+                held = held + came
                 other = yield held
             own = call(
                 functools.partial(own_body, slice_funds, first),

time: 88.2 us -> 84.9 us (0.963)
  waiting for transfers between devices: 24.7 us -> 21.6 us
    ppermute x39 -> x36, waiting for transfers between devices: 24.7 us -> 21.6 us  [swap(): return lax.ppermute(x, 'pol', [(i, i ^ offsets[i % 2]) for i in range(n)])]
    ppermute x39 -> x36, starting transfers between devices: 36.8 us -> 36.7 us  [swap(): return lax.ppermute(x, 'pol', [(i, i ^ offsets[i % 2]) for i in range(n)])]
  transfers between devices with their start and end apart: 39 -> 36, of which waited for: 17 -> 17; matrix products, arithmetic and copies ran while one was open for 1% -> 1% of each run, Pallas kernels for 19% -> 20%
where the time goes in v6:
time: 84.9 us; the launch traced here: 84.6 us
  starting transfers between devices  36.7 us (43%)
  Pallas kernels  21.7 us (26%)
  waiting for transfers between devices  21.6 us (25%)
  local copies, waits for them, and re-layouts  3.16 us (4%)
  between operations  1.11 us (1%)
    ppermute x36, starting transfers between devices, swap(): return lax.ppermute(x, 'pol', [(i, i ^ offsets[i % 2]) for i in range(n)])  36.7 us
    ppermute x36, waiting for transfers between devices, swap(): return lax.ppermute(x, 'pol', [(i, i ^ offsets[i % 2]) for i in range(n)])  21.6 us
    pallas_call x6, Pallas kernels, advance_half(): call(functools.partial(year_body, year, first, last, slice_funds), out, s...  10.6 us
    pallas_call x9, Pallas kernels, returns(): call(functools.partial(returns_body, year, first, secs, len(before) > 0,...  7.95 us
    unnamed x9, local copies, waits for them, and re-layouts  3.02 us
    pallas_call x1, Pallas kernels, local(): call(pack_body, [shaped(2 * secs + 8, funds), shaped(8, count)], [SMEM] +...  1.71 us
  transfers between devices with their start and end apart: 36, of which 17 were waited for; matrix products, arithmetic and copies ran while one was open for 1% of the time, Pallas kernels for 20%

profile of v6, /device:TPU:0, one launch (start us, length us, event | category | flops | bytes accessed | tf_op | source)
XLA Modules:
  0.0 84.6 jit_solution(4078382363914044493)
XLA Ops:
  0.6 1.7 %pack.1 = (f32[136,128]{1,0:T(8,128)}, f32[8,512]{1,0:T(8,128)}) custom-call(s32[1]{0:T(128)} %bitcast.refs_0_.me, f32[64,128]{1,0:T(8,128)} %refs_1_.1, f32[64,128]{1,0:T(8,128)} %refs_2_.1, f32[1,64]{1,0:T(1,128)} %bitcast.64, s32[1,512]{1,0:T(1,128)} %bitcast.59, s32[1,512]{1,0:T(1,128)} %bitcast.60, f32[1,512]{1,0:T(1,128)} %bitcast.61, ...), custom_call_target="tpu_custom_call" | custom-call | flops 1000000 | bytes 100000 | tf_op jit(solution)/shard_map/pack/pallas_call | solution.py:359
  2.4 4.1 %collective-permute-start = (f32[1,136,128]{2,1,0:T(8,128)}, f32[1,136,128]{2,1,0:T(8,128)S(1)}, u32[]{:S(2)}, u32[]{:S(2)}) collective-permute-start(f32[1,136,128]{2,1,0:T(8,128)} %bitcast.58), channel_id=1, source_target_pairs={{0,8},{1,9},{2,10},{3,11},{4,12},{5,13},{6,14},{7,15},{8,0},{9,1},... | collective-permute-start | bytes 208904 | tf_op jit(solution)/shard_map/ppermute | solution.py:24
  6.5 1.4 %copy-done.1 = f32[3,128,1024]{2,1,0:T(8,128)S(1)} copy-done((f32[3,128,1024]{2,1,0:T(8,128)S(1)}, f32[3,128,1024]{2,1,0:T(8,128)}, u32[]{:S(2)}) %copy-start.1) | copy-done | bytes 1572888
  7.9 0.9 %copy-done.2 = f32[136,128]{1,0:T(8,128)S(1)} copy-done((f32[136,128]{1,0:T(8,128)S(1)}, f32[136,128]{1,0:T(8,128)}, u32[]{:S(2)}) %copy-start.2) | copy-done | bytes 69656
  8.7 0.7 copy-done.3
  9.5 1.1 %columns.1 = (bf16[3,128,512]{2,1,0:T(8,128)(2,1)S(1)}, bf16[3,512,256]{2,1,0:T(8,128)(2,1)S(1)}, f32[8,512,128]{2,1,0:T(8,128)S(1)}, bf16[2,128,1024]{2,1,0:T(8...) custom-call(f32[8,512]{1,0:T(8,128)S(1)} %copy-done.3, f32[136,128]{1,0:T(8,128)S(1)} %copy-done.2, ...), custom_call_target="tpu_custom_call" | custom-call | flops 1000000 | bytes 4000000 | tf_op jit(solution)/shard_map/columns/pallas_call | solution.py:371
  10.6 1.6 %collective-permute-start.3 = (f32[2,136,128]{2,1,0:T(8,128)S(1)}, f32[2,136,128]{2,1,0:T(8,128)S(1)}, u32[]{:S(2)}, u32[]{:S(2)}) collective-permute-start(f32[2,136,128]{2,1,0:T(8,128)S(1)} %constant_dynamic-update-slice_fusion.refs_0_), channel_id=1, source_target_pairs={{0,2},{1,3},{2,0},{3,1},{4,6},{5,7},{6,4},{7,5},{8,10},{9,11},{10,... | collective-permute-start | bytes 417800 | tf_op jit(solution)/shard_map/ppermute | solution.py:24
  12.2 1.6 %collective-permute-start.2 = (f32[2,136,128]{2,1,0:T(8,128)S(1)}, f32[2,136,128]{2,1,0:T(8,128)S(1)}, u32[]{:S(2)}, u32[]{:S(2)}) collective-permute-start(f32[2,136,128]{2,1,0:T(8,128)S(1)} %constant_dynamic-update-slice_fusion.refs_0_), channel_id=1, source_target_pairs={{0,4},{1,5},{2,6},{3,7},{4,0},{5,1},{6,2},{7,3},{8,12},{9,13},{10,... | collective-permute-start | bytes 417800 | tf_op jit(solution)/shard_map/ppermute | solution.py:24
  13.8 0.4 collective-permute-start.1
  14.2 0.6 returns.9
  14.8 1.1 %collective-permute-done.3.refs_0_.refs_1_ = f32[2,136,128]{2,1,0:T(8,128)S(1)} collective-permute-done((f32[2,136,128]{2,1,0:T(8,128)S(1)}, f32[2,136,128]{2,1,0:T(8,128)S(1)}, u32[]{:S(2)}, u32[]{:S(2)}) %collective-permute-start.3) | collective-permute-done | bytes 139296 | tf_op jit(solution)/shard_map/ppermute | solution.py:24
  15.8 0.6 returns.10
  16.4 2.1 %collective-permute-done.2.refs_0_.refs_2_ = f32[2,136,128]{2,1,0:T(8,128)S(1)} collective-permute-done((f32[2,136,128]{2,1,0:T(8,128)S(1)}, f32[2,136,128]{2,1,0:T(8,128)S(1)}, u32[]{:S(2)}, u32[]{:S(2)}) %collective-permute-start.2) | collective-permute-done | bytes 139296 | tf_op jit(solution)/shard_map/ppermute | solution.py:24
  18.5 0.6 returns.11
  19.1 1.1 %collective-permute-done.1.refs_0_.refs_3_ = f32[2,136,128]{2,1,0:T(8,128)S(1)} collective-permute-done((f32[2,136,128]{2,1,0:T(8,128)S(1)}, f32[2,136,128]{2,1,0:T(8,128)S(1)}, u32[]{:S(2)}, u32[]{:S(2)}) %collective-permute-start.1) | collective-permute-done | bytes 139296 | tf_op jit(solution)/shard_map/ppermute | solution.py:24
  20.2 0.5 returns.12
  20.8 0.5 collective-permute-start.4
  21.3 0.7 returns.13
  22.0 0.3 collective-permute-done.4.refs_2_
  22.3 1.8 %year.6 = (f32[512,512]{1,0:T(8,128)S(1)}, f32[512,512]{1,0:T(8,128)S(1)}, f32[2,2,2,32,512]{4,3,2,1,0:T(8,128)S(1)}, f32[64,128]{1,0:T(8,128)S(1)}) custom-call(s32[1]{0:T(128)} %bitcast.refs_0_.me, f32[8,128]{1,0:T(8,128)S(1)} %get-tuple-element.126.refs_1_, f32[8,128]{1,0:T(8,128)S(1)} %collective-permute-done.4.refs_2_, ...), custom_call_target="tpu_custom_call" | custom-call | flops 268435456 | bytes 5242880 | tf_op jit(solution)/shard_map/year/pallas_call | solution.py:450
  24.1 0.2 collective-permute-start.6
  24.3 1.8 %year.7 = (f32[512,512]{1,0:T(8,128)S(1)}, f32[512,512]{1,0:T(8,128)S(1)}, f32[2,2,2,32,512]{4,3,2,1,0:T(8,128)S(1)}, f32[64,128]{1,0:T(8,128)S(1)}) custom-call(s32[1]{0:T(128)} %bitcast.refs_0_.me, f32[8,128]{1,0:T(8,128)S(1)} %get-tuple-element.126.refs_1_, f32[8,128]{1,0:T(8,128)S(1)} %collective-permute-done.4.refs_2_, ...), custom_call_target="tpu_custom_call" | custom-call | flops 268435456 | bytes 5242880 | tf_op jit(solution)/shard_map/year/pallas_call | solution.py:450
  26.1 0.4 collective-permute-start.9
  26.6 0.2 collective-permute-start.10
  26.9 1.4 %collective-permute-start.8 = (f32[2,32,512]{2,1,0:T(8,128)S(1)}, f32[2,32,512]{2,1,0:T(8,128)S(1)}, u32[]{:S(2)}, u32[]{:S(2)}) collective-permute-start(f32[2,32,512]{2,1,0:T(8,128)S(1)} %slice_bitcast_fusion.11), channel_id=1, source_target_pairs={{0,2},{1,5},{2,0},{3,7},{4,6},{5,1},{6,4},{7,3},{8,10},{9,13},{10,... | collective-permute-start | bytes 393224 | tf_op jit(solution)/shard_map/ppermute | solution.py:24
  28.3 0.9 %collective-permute-start.12 = (f32[2,32,512]{2,1,0:T(8,128)S(1)}, f32[2,32,512]{2,1,0:T(8,128)S(1)}, u32[]{:S(2)}, u32[]{:S(2)}) collective-permute-start(f32[2,32,512]{2,1,0:T(8,128)S(1)} %slice_bitcast_fusion.8), channel_id=1, source_target_pairs={{0,2},{1,5},{2,0},{3,7},{4,6},{5,1},{6,4},{7,3},{8,10},{9,13},{10,... | collective-permute-start | bytes 393224 | tf_op jit(solution)/shard_map/ppermute | solution.py:24
  29.2 1.3 %returns.14 = (f32[128,1024]{1,0:T(8,128)S(1)}, f32[8,128]{1,0:T(8,128)}) custom-call(f32[2,136,128]{2,1,0:T(8,128)S(1)} %constant_dynamic-update-slice_fusion.refs_0_, f32[2,136,128]{2,1,0:T(8,128)S(1)} %collective-permute-done.3.refs_0_.refs_1_, f32[2,136,128]{2,1,0:T(8,128)S(1)} %collective-permute-done.2.refs_0_.refs_2_, ...), custom_call_target="tpu_custom_call" | custom-call | tf_op jit(solution)/shard_map/returns/pallas_call | solution.py:396
  30.4 1.5 %collective-permute-done.8 = f32[2,32,512]{2,1,0:T(8,128)S(1)} collective-permute-done((f32[2,32,512]{2,1,0:T(8,128)S(1)}, f32[2,32,512]{2,1,0:T(8,128)S(1)}, u32[]{:S(2)}, u32[]{:S(2)}) %collective-permute-start.8) | collective-permute-done | bytes 131104 | tf_op jit(solution)/shard_map/ppermute | solution.py:24
  31.9 1.4 %collective-permute-start.11 = (f32[2,32,512]{2,1,0:T(8,128)S(1)}, f32[2,32,512]{2,1,0:T(8,128)S(1)}, u32[]{:S(2)}, u32[]{:S(2)}) collective-permute-start(f32[2,32,512]{2,1,0:T(8,128)S(1)} %fusion.3), channel_id=1, source_target_pairs={{0,4},{1,9},{2,6},{3,11},{4,0},{5,13},{6,2},{7,15},{8,12},{9,1},{1... | collective-permute-start | bytes 393224 | tf_op jit(solution)/shard_map/ppermute | solution.py:24
  33.4 1.6 %collective-permute-start.14 = (f32[2,32,512]{2,1,0:T(8,128)S(1)}, f32[2,32,512]{2,1,0:T(8,128)S(1)}, u32[]{:S(2)}, u32[]{:S(2)}) collective-permute-start(f32[2,32,512]{2,1,0:T(8,128)S(1)} %fusion.2), channel_id=1, source_target_pairs={{0,4},{1,9},{2,6},{3,11},{4,0},{5,13},{6,2},{7,15},{8,12},{9,1},{1... | collective-permute-start | bytes 393224 | tf_op jit(solution)/shard_map/ppermute | solution.py:24
  35.0 1.3 %returns.15 = (f32[128,1024]{1,0:T(8,128)S(1)}, f32[8,128]{1,0:T(8,128)}) custom-call(f32[8,136,128]{2,1,0:T(8,128)S(1)} %collective-permute-done.10.refs_0_, bf16[2,2,128,1024]{3,2,1,0:T(8,128)(2,1)S(1)} %get-tuple-element.178.refs_4_.refs_1_), custom_call_target="tpu_custom_call" | custom-call | tf_op jit(solution)/shard_map/returns/pallas_call | solution.py:396
  36.3 1.2 %collective-permute-done.11 = f32[2,32,512]{2,1,0:T(8,128)S(1)} collective-permute-done((f32[2,32,512]{2,1,0:T(8,128)S(1)}, f32[2,32,512]{2,1,0:T(8,128)S(1)}, u32[]{:S(2)}, u32[]{:S(2)}) %collective-permute-start.11) | collective-permute-done | bytes 131104 | tf_op jit(solution)/shard_map/ppermute | solution.py:24
  37.5 2.5 %collective-permute-start.13 = (f32[2,32,512]{2,1,0:T(8,128)S(1)}, f32[2,32,512]{2,1,0:T(8,128)S(1)}, u32[]{:S(2)}, u32[]{:S(2)}) collective-permute-start(f32[2,32,512]{2,1,0:T(8,128)S(1)} %add.40.refs_0_), channel_id=1, source_target_pairs={{0,8},{1,3},{2,10},{3,1},{4,12},{5,7},{6,14},{7,5},{8,0},{9,11},{1... | collective-permute-start | bytes 393224 | tf_op jit(solution)/shard_map/ppermute | solution.py:24
  40.0 0.7 collective-permute-done.14
  40.7 1.9 %collective-permute-start.16 = (f32[2,32,512]{2,1,0:T(8,128)S(1)}, f32[2,32,512]{2,1,0:T(8,128)S(1)}, u32[]{:S(2)}, u32[]{:S(2)}) collective-permute-start(f32[2,32,512]{2,1,0:T(8,128)S(1)} %add.41.refs_0_), channel_id=1, source_target_pairs={{0,8},{1,3},{2,10},{3,1},{4,12},{5,7},{6,14},{7,5},{8,0},{9,11},{1... | collective-permute-start | bytes 393224 | tf_op jit(solution)/shard_map/ppermute | solution.py:24
  42.5 0.9 %collective-permute-done.13.refs_1_ = f32[2,32,512]{2,1,0:T(8,128)S(1)} collective-permute-done((f32[2,32,512]{2,1,0:T(8,128)S(1)}, f32[2,32,512]{2,1,0:T(8,128)S(1)}, u32[]{:S(2)}, u32[]{:S(2)}) %collective-permute-start.13) | collective-permute-done | bytes 131104 | tf_op jit(solution)/shard_map/ppermute | solution.py:24
  43.5 1.6 %collective-permute-start.15 = (f32[32,512]{1,0:T(8,128)S(1)}, f32[32,512]{1,0:T(8,128)S(1)}, u32[]{:S(2)}, u32[]{:S(2)}) collective-permute-start(f32[32,512]{1,0:T(8,128)S(1)} %own.4.refs_1_), channel_id=1, source_target_pairs={{0,2},{1,5},{2,0},{3,7},{4,6},{5,1},{6,4},{7,3},{8,10},{9,13},{10,... | collective-permute-start | bytes 196616 | tf_op jit(solution)/shard_map/ppermute | solution.py:24
  45.1 2.0 %collective-permute-done.16.refs_1_ = f32[2,32,512]{2,1,0:T(8,128)S(1)} collective-permute-done((f32[2,32,512]{2,1,0:T(8,128)S(1)}, f32[2,32,512]{2,1,0:T(8,128)S(1)}, u32[]{:S(2)}, u32[]{:S(2)}) %collective-permute-start.16) | collective-permute-done | bytes 131104 | tf_op jit(solution)/shard_map/ppermute | solution.py:24
  47.2 1.4 %collective-permute-start.19 = (f32[32,512]{1,0:T(8,128)S(1)}, f32[32,512]{1,0:T(8,128)S(1)}, u32[]{:S(2)}, u32[]{:S(2)}) collective-permute-start(f32[32,512]{1,0:T(8,128)S(1)} %own.5.refs_1_), channel_id=1, source_target_pairs={{0,2},{1,5},{2,0},{3,7},{4,6},{5,1},{6,4},{7,3},{8,10},{9,13},{10,... | collective-permute-start | bytes 196616 | tf_op jit(solution)/shard_map/ppermute | solution.py:24
  48.6 0.5 collective-permute-start.18
  49.1 2.4 %collective-permute-done.19.refs_2_ = f32[32,512]{1,0:T(8,128)S(1)} collective-permute-done((f32[32,512]{1,0:T(8,128)S(1)}, f32[32,512]{1,0:T(8,128)S(1)}, u32[]{:S(2)}, u32[]{:S(2)}) %collective-permute-start.19) | collective-permute-done | bytes 65568 | tf_op jit(solution)/shard_map/ppermute | solution.py:24
  51.5 1.6 %year.8 = (f32[512,512]{1,0:T(8,128)S(1)}, f32[512,512]{1,0:T(8,128)S(1)}, f32[2,2,2,32,512]{4,3,2,1,0:T(8,128)S(1)}, f32[64,128]{1,0:T(8,128)S(1)}) custom-call(s32[1]{0:T(128)} %bitcast.refs_0_.me, f32[32,512]{1,0:T(8,128)S(1)} %own.4.refs_1_, f32[32,512]{1,0:T(8,128)S(1)} %collective-permute-done.15.refs_2_, ...), custom_call_target="tpu_custom_call" | custom-call | flops 268435456 | bytes 5242880 | tf_op jit(solution)/shard_map/year/pallas_call | solution.py:450
  53.1 0.6 collective-permute-start.20
  53.7 1.7 %year.9 = (f32[512,512]{1,0:T(8,128)S(1)}, f32[512,512]{1,0:T(8,128)S(1)}, f32[2,2,2,32,512]{4,3,2,1,0:T(8,128)S(1)}, f32[64,128]{1,0:T(8,128)S(1)}) custom-call(s32[1]{0:T(128)} %bitcast.refs_0_.me, f32[32,512]{1,0:T(8,128)S(1)} %own.5.refs_1_, f32[32,512]{1,0:T(8,128)S(1)} %collective-permute-done.19.refs_2_, ...), custom_call_target="tpu_custom_call" | custom-call | flops 268435456 | bytes 5242880 | tf_op jit(solution)/shard_map/year/pallas_call | solution.py:450
  55.6 1.4 %collective-permute-start.23 = (f32[2,32,512]{2,1,0:T(8,128)S(1)}, f32[2,32,512]{2,1,0:T(8,128)S(1)}, u32[]{:S(2)}, u32[]{:S(2)}) collective-permute-start(f32[2,32,512]{2,1,0:T(8,128)S(1)} %slice_bitcast_fusion.7), channel_id=1, source_target_pairs={{0,2},{1,5},{2,0},{3,7},{4,6},{5,1},{6,4},{7,3},{8,10},{9,13},{10,... | collective-permute-start | bytes 393224 | tf_op jit(solution)/shard_map/ppermute | solution.py:24
  57.1 1.4 %collective-permute-start.26 = (f32[2,32,512]{2,1,0:T(8,128)S(1)}, f32[2,32,512]{2,1,0:T(8,128)S(1)}, u32[]{:S(2)}, u32[]{:S(2)}) collective-permute-start(f32[2,32,512]{2,1,0:T(8,128)S(1)} %slice_bitcast_fusion.4), channel_id=1, source_target_pairs={{0,2},{1,5},{2,0},{3,7},{4,6},{5,1},{6,4},{7,3},{8,10},{9,13},{10,... | collective-permute-start | bytes 393224 | tf_op jit(solution)/shard_map/ppermute | solution.py:24
  58.5 1.3 %returns.16 = (f32[128,1024]{1,0:T(8,128)S(1)}, f32[8,128]{1,0:T(8,128)}) custom-call(f32[2,136,128]{2,1,0:T(8,128)S(1)} %constant_dynamic-update-slice_fusion.refs_0_, f32[2,136,128]{2,1,0:T(8,128)S(1)} %collective-permute-done.3.refs_0_.refs_1_, f32[2,136,128]{2,1,0:T(8,128)S(1)} %collective-permute-done.2.refs_0_.refs_2_, ...), custom_call_target="tpu_custom_call" | custom-call | tf_op jit(solution)/shard_map/returns/pallas_call | solution.py:396
  59.8 0.8 collective-permute-done.23
  60.6 1.8 %collective-permute-start.25 = (f32[2,32,512]{2,1,0:T(8,128)S(1)}, f32[2,32,512]{2,1,0:T(8,128)S(1)}, u32[]{:S(2)}, u32[]{:S(2)}) collective-permute-start(f32[2,32,512]{2,1,0:T(8,128)S(1)} %fusion.1), channel_id=1, source_target_pairs={{0,4},{1,9},{2,6},{3,11},{4,0},{5,13},{6,2},{7,15},{8,12},{9,1},{1... | collective-permute-start | bytes 393224 | tf_op jit(solution)/shard_map/ppermute | solution.py:24
  62.5 1.6 %collective-permute-start.27 = (f32[2,32,512]{2,1,0:T(8,128)S(1)}, f32[2,32,512]{2,1,0:T(8,128)S(1)}, u32[]{:S(2)}, u32[]{:S(2)}) collective-permute-start(f32[2,32,512]{2,1,0:T(8,128)S(1)} %fusion), channel_id=1, source_target_pairs={{0,4},{1,9},{2,6},{3,11},{4,0},{5,13},{6,2},{7,15},{8,12},{9,1},{1... | collective-permute-start | bytes 393224 | tf_op jit(solution)/shard_map/ppermute | solution.py:24
  64.1 1.3 %returns.17 = (f32[128,1024]{1,0:T(8,128)S(1)}, f32[8,128]{1,0:T(8,128)}) custom-call(f32[8,136,128]{2,1,0:T(8,128)S(1)} %collective-permute-done.10.refs_0_, bf16[2,2,128,1024]{3,2,1,0:T(8,128)(2,1)S(1)} %get-tuple-element.178.refs_4_.refs_1_), custom_call_target="tpu_custom_call" | custom-call | tf_op jit(solution)/shard_map/returns/pallas_call | solution.py:396
  65.4 1.8 %collective-permute-done.25 = f32[2,32,512]{2,1,0:T(8,128)S(1)} collective-permute-done((f32[2,32,512]{2,1,0:T(8,128)S(1)}, f32[2,32,512]{2,1,0:T(8,128)S(1)}, u32[]{:S(2)}, u32[]{:S(2)}) %collective-permute-start.25) | collective-permute-done | bytes 131104 | tf_op jit(solution)/shard_map/ppermute | solution.py:24
  67.2 2.1 %collective-permute-start.29 = (f32[2,32,512]{2,1,0:T(8,128)S(1)}, f32[2,32,512]{2,1,0:T(8,128)S(1)}, u32[]{:S(2)}, u32[]{:S(2)}) collective-permute-start(f32[2,32,512]{2,1,0:T(8,128)S(1)} %add.46.refs_0_), channel_id=1, source_target_pairs={{0,8},{1,3},{2,10},{3,1},{4,12},{5,7},{6,14},{7,5},{8,0},{9,11},{1... | collective-permute-start | bytes 393224 | tf_op jit(solution)/shard_map/ppermute | solution.py:24
  69.2 0.5 collective-permute-done.27
  69.8 2.2 %collective-permute-start.28 = (f32[2,32,512]{2,1,0:T(8,128)S(1)}, f32[2,32,512]{2,1,0:T(8,128)S(1)}, u32[]{:S(2)}, u32[]{:S(2)}) collective-permute-start(f32[2,32,512]{2,1,0:T(8,128)S(1)} %add.47.refs_0_), channel_id=1, source_target_pairs={{0,8},{1,3},{2,10},{3,1},{4,12},{5,7},{6,14},{7,5},{8,0},{9,11},{1... | collective-permute-start | bytes 393224 | tf_op jit(solution)/shard_map/ppermute | solution.py:24
  72.0 2.5 %collective-permute-done.29.refs_1_ = f32[2,32,512]{2,1,0:T(8,128)S(1)} collective-permute-done((f32[2,32,512]{2,1,0:T(8,128)S(1)}, f32[2,32,512]{2,1,0:T(8,128)S(1)}, u32[]{:S(2)}, u32[]{:S(2)}) %collective-permute-start.29) | collective-permute-done | bytes 131104 | tf_op jit(solution)/shard_map/ppermute | solution.py:24
  74.6 1.4 %collective-permute-start.31 = (f32[32,512]{1,0:T(8,128)S(1)}, f32[32,512]{1,0:T(8,128)S(1)}, u32[]{:S(2)}, u32[]{:S(2)}) collective-permute-start(f32[32,512]{1,0:T(8,128)S(1)} %own.6.refs_1_), channel_id=1, source_target_pairs={{0,2},{1,5},{2,0},{3,7},{4,6},{5,1},{6,4},{7,3},{8,10},{9,13},{10,... | collective-permute-start | bytes 196616 | tf_op jit(solution)/shard_map/ppermute | solution.py:24
  76.0 1.3 %collective-permute-start.30 = (f32[32,512]{1,0:T(8,128)S(1)}, f32[32,512]{1,0:T(8,128)S(1)}, u32[]{:S(2)}, u32[]{:S(2)}) collective-permute-start(f32[32,512]{1,0:T(8,128)S(1)} %own.7.refs_1_), channel_id=1, source_target_pairs={{0,2},{1,5},{2,0},{3,7},{4,6},{5,1},{6,4},{7,3},{8,10},{9,13},{10,... | collective-permute-start | bytes 196616 | tf_op jit(solution)/shard_map/ppermute | solution.py:24
  77.4 1.5 %collective-permute-done.31.refs_2_ = f32[32,512]{1,0:T(8,128)S(1)} collective-permute-done((f32[32,512]{1,0:T(8,128)S(1)}, f32[32,512]{1,0:T(8,128)S(1)}, u32[]{:S(2)}, u32[]{:S(2)}) %collective-permute-start.31) | collective-permute-done | bytes 65568 | tf_op jit(solution)/shard_map/ppermute | solution.py:24
  78.9 0.5 collective-permute-start.32
  79.4 0.9 %collective-permute-done.30.refs_2_ = f32[32,512]{1,0:T(8,128)S(1)} collective-permute-done((f32[32,512]{1,0:T(8,128)S(1)}, f32[32,512]{1,0:T(8,128)S(1)}, u32[]{:S(2)}, u32[]{:S(2)}) %collective-permute-start.30) | collective-permute-done | bytes 65568 | tf_op jit(solution)/shard_map/ppermute | solution.py:24
  80.4 1.0 %year.10 = (f32[512,512]{1,0:T(8,128)S(1)}, f32[512,512]{1,0:T(8,128)S(1)}, f32[64,128]{1,0:T(8,128)S(1)}) custom-call(s32[1]{0:T(128)} %bitcast.refs_0_.me, f32[32,512]{1,0:T(8,128)S(1)} %own.6.refs_1_, f32[32,512]{1,0:T(8,128)S(1)} %collective-permute-done.31.refs_2_, f32[32,512]{1,0:T(8,128)S(1)} %collective-permute-done.34.refs_3_, ...), custom_call_target="tpu_custom_call" | custom-call | flops 268435456 | bytes 5242880 | tf_op jit(solution)/shard_map/year/pallas_call | solution.py:450
  81.4 0.3 collective-permute-done.33.refs_4_
  81.6 2.8 %year.11 = (f32[512,1024]{1,0:T(8,128)}, f32[512,1024]{1,0:T(8,128)}, f32[3,64,128]{2,1,0:T(8,128)}) custom-call(s32[1]{0:T(128)} %bitcast.refs_0_.me, f32[32,512]{1,0:T(8,128)S(1)} %own.7.refs_1_, f32[32,512]{1,0:T(8,128)S(1)} %collective-permute-done.30.refs_2_, f32[32,512]{1,0:T(8,128)S(1)} %collective-permute-done.32.refs_3_, ...), custom_call_target="tpu_custom_call" | custom-call | flops 268435456 | bytes 5242880 | tf_op jit(solution)/shard_map/year/pallas_call | solution.py:450
  (60 shorter events, 1.1 us)
Async XLA Ops:
  2.4 8.3 %collective-permute-start = (f32[1,136,128]{2,1,0:T(8,128)}, f32[1,136,128]{2,1,0:T(8,128)S(1)}, u32[]{:S(2)}, u32[]{:S(2)}) collective-permute-start(f32[1,136,128]{2,1,0:T(8,128)} %bitcast.58), channel_id=1, source_target_pairs={{0,8},{1,9},{2,10},{3,11},{4,12},{5,13},{6,14},{7,15},{8,0},{9,1},... | collective-permute-start | bytes 208904 | tf_op jit(solution)/shard_map/ppermute | solution.py:24
  6.5 1.4 %copy-start.1 = (f32[3,128,1024]{2,1,0:T(8,128)S(1)}, f32[3,128,1024]{2,1,0:T(8,128)}, u32[]{:S(2)}) copy-start(f32[3,128,1024]{2,1,0:T(8,128)} %shocks.1) | copy-start | bytes 4718596
  7.9 0.9 %copy-start.2 = (f32[136,128]{1,0:T(8,128)S(1)}, f32[136,128]{1,0:T(8,128)}, u32[]{:S(2)}) copy-start(f32[136,128]{1,0:T(8,128)} %get-tuple-element.106.block) | copy-start | bytes 208900
  8.7 0.7 copy-start.3
  10.6 5.2 %collective-permute-start.3 = (f32[2,136,128]{2,1,0:T(8,128)S(1)}, f32[2,136,128]{2,1,0:T(8,128)S(1)}, u32[]{:S(2)}, u32[]{:S(2)}) collective-permute-start(f32[2,136,128]{2,1,0:T(8,128)S(1)} %constant_dynamic-update-slice_fusion.refs_0_), channel_id=1, source_target_pairs={{0,2},{1,3},{2,0},{3,1},{4,6},{5,7},{6,4},{7,5},{8,10},{9,11},{10,... | collective-permute-start | bytes 417800 | tf_op jit(solution)/shard_map/ppermute | solution.py:24
  12.2 6.3 %collective-permute-start.2 = (f32[2,136,128]{2,1,0:T(8,128)S(1)}, f32[2,136,128]{2,1,0:T(8,128)S(1)}, u32[]{:S(2)}, u32[]{:S(2)}) collective-permute-start(f32[2,136,128]{2,1,0:T(8,128)S(1)} %constant_dynamic-update-slice_fusion.refs_0_), channel_id=1, source_target_pairs={{0,4},{1,5},{2,6},{3,7},{4,0},{5,1},{6,2},{7,3},{8,12},{9,13},{10,... | collective-permute-start | bytes 417800 | tf_op jit(solution)/shard_map/ppermute | solution.py:24
  13.8 6.4 %collective-permute-start.1 = (f32[2,136,128]{2,1,0:T(8,128)S(1)}, f32[2,136,128]{2,1,0:T(8,128)S(1)}, u32[]{:S(2)}, u32[]{:S(2)}) collective-permute-start(f32[2,136,128]{2,1,0:T(8,128)S(1)} %constant_dynamic-update-slice_fusion.refs_0_), channel_id=1, source_target_pairs={{0,6},{1,7},{2,4},{3,5},{4,2},{5,3},{6,0},{7,1},{8,14},{9,15},{10,... | collective-permute-start | bytes 417800 | tf_op jit(solution)/shard_map/ppermute | solution.py:24
  15.8 6.5 %copy-start = (bf16[512,3,1024]{2,0,1:T(8,128)(2,1)S(1)}, bf16[512,3,1024]{2,0,1:T(8,128)(2,1)}, u32[]{:S(2)}) copy-start(bf16[512,3,1024]{2,0,1:T(8,128)(2,1)} %param.23) | copy-start | bytes 9437188
  20.7 1.6 %collective-permute-start.5 = (f32[128,512]{1,0:T(8,128)S(1)}, f32[128,512]{1,0:T(8,128)S(1)}, u32[]{:S(2)}, u32[]{:S(2)}) collective-permute-start(f32[128,512]{1,0:T(8,128)S(1)} %get-tuple-element.121.refs_3_), channel_id=1, source_target_pairs={{0,1},{1,0},{2,3},{3,2},{4,5},{5,4},{6,7},{7,6},{8,9},{9,8},{10,11... | collective-permute-start | bytes 786440 | tf_op jit(solution)/shard_map/ppermute | solution.py:24
  20.8 1.5 %collective-permute-start.4 = (f32[8,128]{1,0:T(8,128)S(1)}, f32[8,128]{1,0:T(8,128)S(1)}, u32[]{:S(2)}, u32[]{:S(2)}) collective-permute-start(f32[8,128]{1,0:T(8,128)S(1)} %get-tuple-element.126.refs_1_), channel_id=1, source_target_pairs={{0,1},{1,0},{2,3},{3,2},{4,5},{5,4},{6,7},{7,6},{8,9},{9,8},{10,11... | collective-permute-start | bytes 12296 | tf_op jit(solution)/shard_map/ppermute | solution.py:24
  21.9 2.4 %collective-permute-start.7 = (f32[128,512]{1,0:T(8,128)S(1)}, f32[128,512]{1,0:T(8,128)S(1)}, u32[]{:S(2)}, u32[]{:S(2)}) collective-permute-start(f32[128,512]{1,0:T(8,128)S(1)} %get-tuple-element.128.refs_3_), channel_id=1, source_target_pairs={{0,1},{1,0},{2,3},{3,2},{4,5},{5,4},{6,7},{7,6},{8,9},{9,8},{10,11... | collective-permute-start | bytes 786440 | tf_op jit(solution)/shard_map/ppermute | solution.py:24
  24.1 2.7 %collective-permute-start.6 = (f32[2,2,32,512]{3,2,1,0:T(8,128)S(1)}, f32[2,2,32,512]{3,2,1,0:T(8,128)S(1)}, u32[]{:S(2)}, u32[]{:S(2)}) collective-permute-start(f32[2,2,32,512]{3,2,1,0:T(8,128)S(1)} %slice_bitcast_fusion.3), channel_id=1, source_target_pairs={{0,1},{1,0},{2,3},{3,2},{4,5},{5,4},{6,7},{7,6},{8,9},{9,8},{10,11... | collective-permute-start | bytes 786440 | tf_op jit(solution)/shard_map/ppermute | solution.py:24
  26.1 2.1 %collective-permute-start.9 = (f32[2,2,32,512]{3,2,1,0:T(8,128)S(1)}, f32[2,2,32,512]{3,2,1,0:T(8,128)S(1)}, u32[]{:S(2)}, u32[]{:S(2)}) collective-permute-start(f32[2,2,32,512]{3,2,1,0:T(8,128)S(1)} %slice_bitcast_fusion.2), channel_id=1, source_target_pairs={{0,1},{1,0},{2,3},{3,2},{4,5},{5,4},{6,7},{7,6},{8,9},{9,8},{10,11... | collective-permute-start | bytes 786440 | tf_op jit(solution)/shard_map/ppermute | solution.py:24
  26.6 5.3 %collective-permute-start.10 = (f32[8,136,128]{2,1,0:T(8,128)S(1)}, f32[8,136,128]{2,1,0:T(8,128)S(1)}, u32[]{:S(2)}, u32[]{:S(2)}) collective-permute-start(f32[8,136,128]{2,1,0:T(8,128)S(1)} %pad_maximum_fusion), channel_id=1, source_target_pairs={{0,1},{1,0},{2,3},{3,2},{4,5},{5,4},{6,7},{7,6},{8,9},{9,8},{10,11... | collective-permute-start | bytes 1671176 | tf_op jit(solution)/shard_map/ppermute | solution.py:24
  26.9 5.0 %collective-permute-start.8 = (f32[2,32,512]{2,1,0:T(8,128)S(1)}, f32[2,32,512]{2,1,0:T(8,128)S(1)}, u32[]{:S(2)}, u32[]{:S(2)}) collective-permute-start(f32[2,32,512]{2,1,0:T(8,128)S(1)} %slice_bitcast_fusion.11), channel_id=1, source_target_pairs={{0,2},{1,5},{2,0},{3,7},{4,6},{5,1},{6,4},{7,3},{8,10},{9,13},{10,... | collective-permute-start | bytes 393224 | tf_op jit(solution)/shard_map/ppermute | solution.py:24
  28.3 5.1 %collective-permute-start.12 = (f32[2,32,512]{2,1,0:T(8,128)S(1)}, f32[2,32,512]{2,1,0:T(8,128)S(1)}, u32[]{:S(2)}, u32[]{:S(2)}) collective-permute-start(f32[2,32,512]{2,1,0:T(8,128)S(1)} %slice_bitcast_fusion.8), channel_id=1, source_target_pairs={{0,2},{1,5},{2,0},{3,7},{4,6},{5,1},{6,4},{7,3},{8,10},{9,13},{10,... | collective-permute-start | bytes 393224 | tf_op jit(solution)/shard_map/ppermute | solution.py:24
  31.9 5.5 %collective-permute-start.11 = (f32[2,32,512]{2,1,0:T(8,128)S(1)}, f32[2,32,512]{2,1,0:T(8,128)S(1)}, u32[]{:S(2)}, u32[]{:S(2)}) collective-permute-start(f32[2,32,512]{2,1,0:T(8,128)S(1)} %fusion.3), channel_id=1, source_target_pairs={{0,4},{1,9},{2,6},{3,11},{4,0},{5,13},{6,2},{7,15},{8,12},{9,1},{1... | collective-permute-start | bytes 393224 | tf_op jit(solution)/shard_map/ppermute | solution.py:24
  33.4 7.2 %collective-permute-start.14 = (f32[2,32,512]{2,1,0:T(8,128)S(1)}, f32[2,32,512]{2,1,0:T(8,128)S(1)}, u32[]{:S(2)}, u32[]{:S(2)}) collective-permute-start(f32[2,32,512]{2,1,0:T(8,128)S(1)} %fusion.2), channel_id=1, source_target_pairs={{0,4},{1,9},{2,6},{3,11},{4,0},{5,13},{6,2},{7,15},{8,12},{9,1},{1... | collective-permute-start | bytes 393224 | tf_op jit(solution)/shard_map/ppermute | solution.py:24
  37.5 5.9 %collective-permute-start.13 = (f32[2,32,512]{2,1,0:T(8,128)S(1)}, f32[2,32,512]{2,1,0:T(8,128)S(1)}, u32[]{:S(2)}, u32[]{:S(2)}) collective-permute-start(f32[2,32,512]{2,1,0:T(8,128)S(1)} %add.40.refs_0_), channel_id=1, source_target_pairs={{0,8},{1,3},{2,10},{3,1},{4,12},{5,7},{6,14},{7,5},{8,0},{9,11},{1... | collective-permute-start | bytes 393224 | tf_op jit(solution)/shard_map/ppermute | solution.py:24
  40.7 6.4 %collective-permute-start.16 = (f32[2,32,512]{2,1,0:T(8,128)S(1)}, f32[2,32,512]{2,1,0:T(8,128)S(1)}, u32[]{:S(2)}, u32[]{:S(2)}) collective-permute-start(f32[2,32,512]{2,1,0:T(8,128)S(1)} %add.41.refs_0_), channel_id=1, source_target_pairs={{0,8},{1,3},{2,10},{3,1},{4,12},{5,7},{6,14},{7,5},{8,0},{9,11},{1... | collective-permute-start | bytes 393224 | tf_op jit(solution)/shard_map/ppermute | solution.py:24
  43.5 5.1 %collective-permute-start.15 = (f32[32,512]{1,0:T(8,128)S(1)}, f32[32,512]{1,0:T(8,128)S(1)}, u32[]{:S(2)}, u32[]{:S(2)}) collective-permute-start(f32[32,512]{1,0:T(8,128)S(1)} %own.4.refs_1_), channel_id=1, source_target_pairs={{0,2},{1,5},{2,0},{3,7},{4,6},{5,1},{6,4},{7,3},{8,10},{9,13},{10,... | collective-permute-start | bytes 196616 | tf_op jit(solution)/shard_map/ppermute | solution.py:24
  47.2 4.3 %collective-permute-start.19 = (f32[32,512]{1,0:T(8,128)S(1)}, f32[32,512]{1,0:T(8,128)S(1)}, u32[]{:S(2)}, u32[]{:S(2)}) collective-permute-start(f32[32,512]{1,0:T(8,128)S(1)} %own.5.refs_1_), channel_id=1, source_target_pairs={{0,2},{1,5},{2,0},{3,7},{4,6},{5,1},{6,4},{7,3},{8,10},{9,13},{10,... | collective-permute-start | bytes 196616 | tf_op jit(solution)/shard_map/ppermute | solution.py:24
  48.6 2.9 %collective-permute-start.17 = (f32[32,512]{1,0:T(8,128)S(1)}, f32[32,512]{1,0:T(8,128)S(1)}, u32[]{:S(2)}, u32[]{:S(2)}) collective-permute-start(f32[32,512]{1,0:T(8,128)S(1)} %own.4.refs_1_), channel_id=1, source_target_pairs={{0,1},{1,0},{2,3},{3,2},{4,5},{5,4},{6,7},{7,6},{8,9},{9,8},{10,11... | collective-permute-start | bytes 196616 | tf_op jit(solution)/shard_map/ppermute | solution.py:24
  48.6 2.9 %collective-permute-start.18 = (f32[32,512]{1,0:T(8,128)S(1)}, f32[32,512]{1,0:T(8,128)S(1)}, u32[]{:S(2)}, u32[]{:S(2)}) collective-permute-start(f32[32,512]{1,0:T(8,128)S(1)} %collective-permute-done.15.refs_2_), channel_id=1, source_target_pairs={{0,1},{1,0},{2,3},{3,2},{4,5},{5,4},{6,7},{7,6},{8,9},{9,8},{10,11... | collective-permute-start | bytes 196616 | tf_op jit(solution)/shard_map/ppermute | solution.py:24
  49.1 4.0 %collective-permute-start.21 = (f32[32,512]{1,0:T(8,128)S(1)}, f32[32,512]{1,0:T(8,128)S(1)}, u32[]{:S(2)}, u32[]{:S(2)}) collective-permute-start(f32[32,512]{1,0:T(8,128)S(1)} %own.5.refs_1_), channel_id=1, source_target_pairs={{0,1},{1,0},{2,3},{3,2},{4,5},{5,4},{6,7},{7,6},{8,9},{9,8},{10,11... | collective-permute-start | bytes 196616 | tf_op jit(solution)/shard_map/ppermute | solution.py:24
  51.5 1.6 %collective-permute-start.22 = (f32[32,512]{1,0:T(8,128)S(1)}, f32[32,512]{1,0:T(8,128)S(1)}, u32[]{:S(2)}, u32[]{:S(2)}) collective-permute-start(f32[32,512]{1,0:T(8,128)S(1)} %collective-permute-done.19.refs_2_), channel_id=1, source_target_pairs={{0,1},{1,0},{2,3},{3,2},{4,5},{5,4},{6,7},{7,6},{8,9},{9,8},{10,11... | collective-permute-start | bytes 196616 | tf_op jit(solution)/shard_map/ppermute | solution.py:24
  53.1 2.4 %collective-permute-start.20 = (f32[2,2,32,512]{3,2,1,0:T(8,128)S(1)}, f32[2,2,32,512]{3,2,1,0:T(8,128)S(1)}, u32[]{:S(2)}, u32[]{:S(2)}) collective-permute-start(f32[2,2,32,512]{3,2,1,0:T(8,128)S(1)} %slice_bitcast_fusion.1), channel_id=1, source_target_pairs={{0,1},{1,0},{2,3},{3,2},{4,5},{5,4},{6,7},{7,6},{8,9},{9,8},{10,11... | collective-permute-start | bytes 786440 | tf_op jit(solution)/shard_map/ppermute | solution.py:24
  55.4 1.6 %collective-permute-start.24 = (f32[2,2,32,512]{3,2,1,0:T(8,128)S(1)}, f32[2,2,32,512]{3,2,1,0:T(8,128)S(1)}, u32[]{:S(2)}, u32[]{:S(2)}) collective-permute-start(f32[2,2,32,512]{3,2,1,0:T(8,128)S(1)} %slice_bitcast_fusion), channel_id=1, source_target_pairs={{0,1},{1,0},{2,3},{3,2},{4,5},{5,4},{6,7},{7,6},{8,9},{9,8},{10,11... | collective-permute-start | bytes 786440 | tf_op jit(solution)/shard_map/ppermute | solution.py:24
  55.6 5.0 %collective-permute-start.23 = (f32[2,32,512]{2,1,0:T(8,128)S(1)}, f32[2,32,512]{2,1,0:T(8,128)S(1)}, u32[]{:S(2)}, u32[]{:S(2)}) collective-permute-start(f32[2,32,512]{2,1,0:T(8,128)S(1)} %slice_bitcast_fusion.7), channel_id=1, source_target_pairs={{0,2},{1,5},{2,0},{3,7},{4,6},{5,1},{6,4},{7,3},{8,10},{9,13},{10,... | collective-permute-start | bytes 393224 | tf_op jit(solution)/shard_map/ppermute | solution.py:24
  57.1 5.4 %collective-permute-start.26 = (f32[2,32,512]{2,1,0:T(8,128)S(1)}, f32[2,32,512]{2,1,0:T(8,128)S(1)}, u32[]{:S(2)}, u32[]{:S(2)}) collective-permute-start(f32[2,32,512]{2,1,0:T(8,128)S(1)} %slice_bitcast_fusion.4), channel_id=1, source_target_pairs={{0,2},{1,5},{2,0},{3,7},{4,6},{5,1},{6,4},{7,3},{8,10},{9,13},{10,... | collective-permute-start | bytes 393224 | tf_op jit(solution)/shard_map/ppermute | solution.py:24
  60.6 6.5 %collective-permute-start.25 = (f32[2,32,512]{2,1,0:T(8,128)S(1)}, f32[2,32,512]{2,1,0:T(8,128)S(1)}, u32[]{:S(2)}, u32[]{:S(2)}) collective-permute-start(f32[2,32,512]{2,1,0:T(8,128)S(1)} %fusion.1), channel_id=1, source_target_pairs={{0,4},{1,9},{2,6},{3,11},{4,0},{5,13},{6,2},{7,15},{8,12},{9,1},{1... | collective-permute-start | bytes 393224 | tf_op jit(solution)/shard_map/ppermute | solution.py:24
  62.5 7.3 %collective-permute-start.27 = (f32[2,32,512]{2,1,0:T(8,128)S(1)}, f32[2,32,512]{2,1,0:T(8,128)S(1)}, u32[]{:S(2)}, u32[]{:S(2)}) collective-permute-start(f32[2,32,512]{2,1,0:T(8,128)S(1)} %fusion), channel_id=1, source_target_pairs={{0,4},{1,9},{2,6},{3,11},{4,0},{5,13},{6,2},{7,15},{8,12},{9,1},{1... | collective-permute-start | bytes 393224 | tf_op jit(solution)/shard_map/ppermute | solution.py:24
  67.2 7.3 %collective-permute-start.29 = (f32[2,32,512]{2,1,0:T(8,128)S(1)}, f32[2,32,512]{2,1,0:T(8,128)S(1)}, u32[]{:S(2)}, u32[]{:S(2)}) collective-permute-start(f32[2,32,512]{2,1,0:T(8,128)S(1)} %add.46.refs_0_), channel_id=1, source_target_pairs={{0,8},{1,3},{2,10},{3,1},{4,12},{5,7},{6,14},{7,5},{8,0},{9,11},{1... | collective-permute-start | bytes 393224 | tf_op jit(solution)/shard_map/ppermute | solution.py:24
  69.8 6.2 %collective-permute-start.28 = (f32[2,32,512]{2,1,0:T(8,128)S(1)}, f32[2,32,512]{2,1,0:T(8,128)S(1)}, u32[]{:S(2)}, u32[]{:S(2)}) collective-permute-start(f32[2,32,512]{2,1,0:T(8,128)S(1)} %add.47.refs_0_), channel_id=1, source_target_pairs={{0,8},{1,3},{2,10},{3,1},{4,12},{5,7},{6,14},{7,5},{8,0},{9,11},{1... | collective-permute-start | bytes 393224 | tf_op jit(solution)/shard_map/ppermute | solution.py:24
  74.6 4.3 %collective-permute-start.31 = (f32[32,512]{1,0:T(8,128)S(1)}, f32[32,512]{1,0:T(8,128)S(1)}, u32[]{:S(2)}, u32[]{:S(2)}) collective-permute-start(f32[32,512]{1,0:T(8,128)S(1)} %own.6.refs_1_), channel_id=1, source_target_pairs={{0,2},{1,5},{2,0},{3,7},{4,6},{5,1},{6,4},{7,3},{8,10},{9,13},{10,... | collective-permute-start | bytes 196616 | tf_op jit(solution)/shard_map/ppermute | solution.py:24
  76.0 4.3 %collective-permute-start.30 = (f32[32,512]{1,0:T(8,128)S(1)}, f32[32,512]{1,0:T(8,128)S(1)}, u32[]{:S(2)}, u32[]{:S(2)}) collective-permute-start(f32[32,512]{1,0:T(8,128)S(1)} %own.7.refs_1_), channel_id=1, source_target_pairs={{0,2},{1,5},{2,0},{3,7},{4,6},{5,1},{6,4},{7,3},{8,10},{9,13},{10,... | collective-permute-start | bytes 196616 | tf_op jit(solution)/shard_map/ppermute | solution.py:24
  77.4 3.0 %collective-permute-start.34 = (f32[32,512]{1,0:T(8,128)S(1)}, f32[32,512]{1,0:T(8,128)S(1)}, u32[]{:S(2)}, u32[]{:S(2)}) collective-permute-start(f32[32,512]{1,0:T(8,128)S(1)} %own.6.refs_1_), channel_id=1, source_target_pairs={{0,1},{1,0},{2,3},{3,2},{4,5},{5,4},{6,7},{7,6},{8,9},{9,8},{10,11... | collective-permute-start | bytes 196616 | tf_op jit(solution)/shard_map/ppermute | solution.py:24
  78.9 1.5 %collective-permute-start.35 = (f32[32,512]{1,0:T(8,128)S(1)}, f32[32,512]{1,0:T(8,128)S(1)}, u32[]{:S(2)}, u32[]{:S(2)}) collective-permute-start(f32[32,512]{1,0:T(8,128)S(1)} %collective-permute-done.31.refs_2_), channel_id=1, source_target_pairs={{0,1},{1,0},{2,3},{3,2},{4,5},{5,4},{6,7},{7,6},{8,9},{9,8},{10,11... | collective-permute-start | bytes 196616 | tf_op jit(solution)/shard_map/ppermute | solution.py:24
  78.9 2.4 %collective-permute-start.32 = (f32[32,512]{1,0:T(8,128)S(1)}, f32[32,512]{1,0:T(8,128)S(1)}, u32[]{:S(2)}, u32[]{:S(2)}) collective-permute-start(f32[32,512]{1,0:T(8,128)S(1)} %own.7.refs_1_), channel_id=1, source_target_pairs={{0,1},{1,0},{2,3},{3,2},{4,5},{5,4},{6,7},{7,6},{8,9},{9,8},{10,11... | collective-permute-start | bytes 196616 | tf_op jit(solution)/shard_map/ppermute | solution.py:24
  80.4 1.3 %collective-permute-start.33 = (f32[32,512]{1,0:T(8,128)S(1)}, f32[32,512]{1,0:T(8,128)S(1)}, u32[]{:S(2)}, u32[]{:S(2)}) collective-permute-start(f32[32,512]{1,0:T(8,128)S(1)} %collective-permute-done.30.refs_2_), channel_id=1, source_target_pairs={{0,1},{1,0},{2,3},{3,2},{4,5},{5,4},{6,7},{7,6},{8,9},{9,8},{10,11... | collective-permute-start | bytes 196616 | tf_op jit(solution)/shard_map/ppermute | solution.py:24

commit v7 on v6

--- a/solution.py
+++ b/solution.py
@@ -238,8 +238,7 @@
     lead = 0
     copies = []
     if last and first:
-        half_a, half_l, *earlier, out_a, out_l, out_r, declared, buf_a, buf_l, sem = refs
-        own = out_r.at[year]
+        half_a, half_l, *earlier, out_a, out_l, out_r, declared, buf_a, buf_l, rates, sem = refs
         for k, (half, out) in enumerate(((half_a, out_a), (half_l, out_l))):
             copies.append(pltpu.make_async_copy(half, out.at[:, 0:first], sem.at[k, 0]))
             copies[-1].start()
@@ -264,8 +263,12 @@
         for o in range(4):
             declared[pl.ds(slice_spot(me[0], o, slice_funds), slice_funds), :] = slices[o][...]
     if last and first:
+        own_columns(me, declared[...], first, rates.at[year])
+        rates[year] = rates[year] + earlier[2 * year][...]
         for y in range(year):
-            out_r[y] = earlier[2 * y][...] + earlier[2 * y + 1][...]
+            rates[y] = earlier[2 * y][...] + earlier[2 * y + 1][...]
+        copies.append(pltpu.make_async_copy(rates, out_r, sem.at[2, 0]))
+        copies[-1].start()
 
     def gathered(c):
         there = slice(lead + c, lead + c + STEP)
@@ -314,9 +317,8 @@
         elif not last:
             acc[0, :, cut] = sum_a
             acc[1, :, cut] = sum_l
-    own_columns(me, declared[...], first, own)
-    if last and first:
-        out_r[year] = out_r[year] + earlier[2 * year][...]
+    if not (last and first):
+        own_columns(me, declared[...], first, own)
     for copy in copies:
         copy.wait()
     if not last:
@@ -431,9 +433,10 @@
             if last and h:
                 tiles = half // STEP
                 out = [shaped(count, paths), shaped(count, paths), shaped(years, owned, funds)]
-                out_specs = [ANY, ANY, VMEM]
+                out_specs = [ANY] * 3
                 scratch += [pltpu.VMEM((tiles, count, STEP), F32)] * 2
-                scratch += [pltpu.SemaphoreType.DMA((2, 1 + tiles))]
+                scratch += [pltpu.VMEM((years, owned, funds), F32)]
+                scratch += [pltpu.SemaphoreType.DMA((3, 1 + tiles))]
                 before = final[:2] + [v for rs in rates for v in rs if v is not None]
                 ins += before
                 specs += [VMEM] * len(before)

time: 84.9 us -> 84.2 us (level)
  no operation moved by 1% of the time
where the time goes in v7:
time: 84.2 us; the launch traced here: 83.9 us
  starting transfers between devices  36.7 us (44%)
  waiting for transfers between devices  21.6 us (26%)
  Pallas kernels  21 us (25%)
  local copies, waits for them, and re-layouts  3.16 us (4%)
  between operations  1.11 us (1%)
    ppermute x36, starting transfers between devices, swap(): return lax.ppermute(x, 'pol', [(i, i ^ offsets[i % 2]) for i in range(n)])  36.7 us
    ppermute x36, waiting for transfers between devices, swap(): return lax.ppermute(x, 'pol', [(i, i ^ offsets[i % 2]) for i in range(n)])  21.6 us
    pallas_call x6, Pallas kernels, advance_half(): call(functools.partial(year_body, year, first, last, slice_funds), out, s...  9.95 us
    pallas_call x9, Pallas kernels, returns(): call(functools.partial(returns_body, year, first, secs, len(before) > 0,...  7.95 us
    unnamed x9, local copies, waits for them, and re-layouts  3.02 us
    pallas_call x1, Pallas kernels, local(): call(pack_body, [shaped(2 * secs + 8, funds), shaped(8, count)], [SMEM] +...  1.71 us
  transfers between devices with their start and end apart: 36, of which 17 were waited for; matrix products, arithmetic and copies ran while one was open for 1% of the time, Pallas kernels for 20%

profile of v7, /device:TPU:0, one launch (start us, length us, event | category | flops | bytes accessed | tf_op | source)
XLA Modules:
  0.0 83.9 jit_solution(11297515900579308807)
XLA Ops:
  0.6 1.7 %pack.1 = (f32[136,128]{1,0:T(8,128)}, f32[8,512]{1,0:T(8,128)}) custom-call(s32[1]{0:T(128)} %bitcast.refs_0_.me, f32[64,128]{1,0:T(8,128)} %refs_1_.1, f32[64,128]{1,0:T(8,128)} %refs_2_.1, f32[1,64]{1,0:T(1,128)} %bitcast.64, s32[1,512]{1,0:T(1,128)} %bitcast.59, s32[1,512]{1,0:T(1,128)} %bitcast.60, f32[1,512]{1,0:T(1,128)} %bitcast.61, ...), custom_call_target="tpu_custom_call" | custom-call | flops 1000000 | bytes 100000 | tf_op jit(solution)/shard_map/pack/pallas_call | solution.py:361
  2.4 4.1 %collective-permute-start = (f32[1,136,128]{2,1,0:T(8,128)}, f32[1,136,128]{2,1,0:T(8,128)S(1)}, u32[]{:S(2)}, u32[]{:S(2)}) collective-permute-start(f32[1,136,128]{2,1,0:T(8,128)} %bitcast.58), channel_id=1, source_target_pairs={{0,8},{1,9},{2,10},{3,11},{4,12},{5,13},{6,14},{7,15},{8,0},{9,1},... | collective-permute-start | bytes 208904 | tf_op jit(solution)/shard_map/ppermute | solution.py:24
  6.5 1.4 %copy-done.1 = f32[3,128,1024]{2,1,0:T(8,128)S(1)} copy-done((f32[3,128,1024]{2,1,0:T(8,128)S(1)}, f32[3,128,1024]{2,1,0:T(8,128)}, u32[]{:S(2)}) %copy-start.1) | copy-done | bytes 1572888
  7.9 0.9 %copy-done.2 = f32[136,128]{1,0:T(8,128)S(1)} copy-done((f32[136,128]{1,0:T(8,128)S(1)}, f32[136,128]{1,0:T(8,128)}, u32[]{:S(2)}) %copy-start.2) | copy-done | bytes 69656
  8.7 0.7 copy-done.3
  9.5 1.1 %columns.1 = (bf16[3,128,512]{2,1,0:T(8,128)(2,1)S(1)}, bf16[3,512,256]{2,1,0:T(8,128)(2,1)S(1)}, f32[8,512,128]{2,1,0:T(8,128)S(1)}, bf16[2,128,1024]{2,1,0:T(8...) custom-call(f32[8,512]{1,0:T(8,128)S(1)} %copy-done.3, f32[136,128]{1,0:T(8,128)S(1)} %copy-done.2, ...), custom_call_target="tpu_custom_call" | custom-call | flops 1000000 | bytes 4000000 | tf_op jit(solution)/shard_map/columns/pallas_call | solution.py:373
  10.6 1.6 %collective-permute-start.3 = (f32[2,136,128]{2,1,0:T(8,128)S(1)}, f32[2,136,128]{2,1,0:T(8,128)S(1)}, u32[]{:S(2)}, u32[]{:S(2)}) collective-permute-start(f32[2,136,128]{2,1,0:T(8,128)S(1)} %constant_dynamic-update-slice_fusion.refs_0_), channel_id=1, source_target_pairs={{0,2},{1,3},{2,0},{3,1},{4,6},{5,7},{6,4},{7,5},{8,10},{9,11},{10,... | collective-permute-start | bytes 417800 | tf_op jit(solution)/shard_map/ppermute | solution.py:24
  12.2 1.6 %collective-permute-start.2 = (f32[2,136,128]{2,1,0:T(8,128)S(1)}, f32[2,136,128]{2,1,0:T(8,128)S(1)}, u32[]{:S(2)}, u32[]{:S(2)}) collective-permute-start(f32[2,136,128]{2,1,0:T(8,128)S(1)} %constant_dynamic-update-slice_fusion.refs_0_), channel_id=1, source_target_pairs={{0,4},{1,5},{2,6},{3,7},{4,0},{5,1},{6,2},{7,3},{8,12},{9,13},{10,... | collective-permute-start | bytes 417800 | tf_op jit(solution)/shard_map/ppermute | solution.py:24
  13.8 0.4 collective-permute-start.1
  14.2 0.6 returns.9
  14.8 1.1 %collective-permute-done.3.refs_0_.refs_1_ = f32[2,136,128]{2,1,0:T(8,128)S(1)} collective-permute-done((f32[2,136,128]{2,1,0:T(8,128)S(1)}, f32[2,136,128]{2,1,0:T(8,128)S(1)}, u32[]{:S(2)}, u32[]{:S(2)}) %collective-permute-start.3) | collective-permute-done | bytes 139296 | tf_op jit(solution)/shard_map/ppermute | solution.py:24
  15.8 0.6 returns.10
  16.4 2.1 %collective-permute-done.2.refs_0_.refs_2_ = f32[2,136,128]{2,1,0:T(8,128)S(1)} collective-permute-done((f32[2,136,128]{2,1,0:T(8,128)S(1)}, f32[2,136,128]{2,1,0:T(8,128)S(1)}, u32[]{:S(2)}, u32[]{:S(2)}) %collective-permute-start.2) | collective-permute-done | bytes 139296 | tf_op jit(solution)/shard_map/ppermute | solution.py:24
  18.5 0.6 returns.11
  19.1 1.1 %collective-permute-done.1.refs_0_.refs_3_ = f32[2,136,128]{2,1,0:T(8,128)S(1)} collective-permute-done((f32[2,136,128]{2,1,0:T(8,128)S(1)}, f32[2,136,128]{2,1,0:T(8,128)S(1)}, u32[]{:S(2)}, u32[]{:S(2)}) %collective-permute-start.1) | collective-permute-done | bytes 139296 | tf_op jit(solution)/shard_map/ppermute | solution.py:24
  20.2 0.5 returns.12
  20.8 0.5 collective-permute-start.4
  21.3 0.7 returns.13
  22.0 0.3 collective-permute-done.4.refs_2_
  22.3 1.8 %year.6 = (f32[512,512]{1,0:T(8,128)S(1)}, f32[512,512]{1,0:T(8,128)S(1)}, f32[2,2,2,32,512]{4,3,2,1,0:T(8,128)S(1)}, f32[64,128]{1,0:T(8,128)S(1)}) custom-call(s32[1]{0:T(128)} %bitcast.refs_0_.me, f32[8,128]{1,0:T(8,128)S(1)} %get-tuple-element.126.refs_1_, f32[8,128]{1,0:T(8,128)S(1)} %collective-permute-done.4.refs_2_, ...), custom_call_target="tpu_custom_call" | custom-call | flops 268435456 | bytes 5242880 | tf_op jit(solution)/shard_map/year/pallas_call | solution.py:453
  24.1 0.2 collective-permute-start.6
  24.3 1.8 %year.7 = (f32[512,512]{1,0:T(8,128)S(1)}, f32[512,512]{1,0:T(8,128)S(1)}, f32[2,2,2,32,512]{4,3,2,1,0:T(8,128)S(1)}, f32[64,128]{1,0:T(8,128)S(1)}) custom-call(s32[1]{0:T(128)} %bitcast.refs_0_.me, f32[8,128]{1,0:T(8,128)S(1)} %get-tuple-element.126.refs_1_, f32[8,128]{1,0:T(8,128)S(1)} %collective-permute-done.4.refs_2_, ...), custom_call_target="tpu_custom_call" | custom-call | flops 268435456 | bytes 5242880 | tf_op jit(solution)/shard_map/year/pallas_call | solution.py:453
  26.1 0.4 collective-permute-start.9
  26.6 0.2 collective-permute-start.10
  26.9 1.4 %collective-permute-start.8 = (f32[2,32,512]{2,1,0:T(8,128)S(1)}, f32[2,32,512]{2,1,0:T(8,128)S(1)}, u32[]{:S(2)}, u32[]{:S(2)}) collective-permute-start(f32[2,32,512]{2,1,0:T(8,128)S(1)} %slice_bitcast_fusion.11), channel_id=1, source_target_pairs={{0,2},{1,5},{2,0},{3,7},{4,6},{5,1},{6,4},{7,3},{8,10},{9,13},{10,... | collective-permute-start | bytes 393224 | tf_op jit(solution)/shard_map/ppermute | solution.py:24
  28.3 0.9 %collective-permute-start.12 = (f32[2,32,512]{2,1,0:T(8,128)S(1)}, f32[2,32,512]{2,1,0:T(8,128)S(1)}, u32[]{:S(2)}, u32[]{:S(2)}) collective-permute-start(f32[2,32,512]{2,1,0:T(8,128)S(1)} %slice_bitcast_fusion.8), channel_id=1, source_target_pairs={{0,2},{1,5},{2,0},{3,7},{4,6},{5,1},{6,4},{7,3},{8,10},{9,13},{10,... | collective-permute-start | bytes 393224 | tf_op jit(solution)/shard_map/ppermute | solution.py:24
  29.2 1.3 %returns.14 = (f32[128,1024]{1,0:T(8,128)S(1)}, f32[8,128]{1,0:T(8,128)}) custom-call(f32[2,136,128]{2,1,0:T(8,128)S(1)} %constant_dynamic-update-slice_fusion.refs_0_, f32[2,136,128]{2,1,0:T(8,128)S(1)} %collective-permute-done.3.refs_0_.refs_1_, f32[2,136,128]{2,1,0:T(8,128)S(1)} %collective-permute-done.2.refs_0_.refs_2_, ...), custom_call_target="tpu_custom_call" | custom-call | tf_op jit(solution)/shard_map/returns/pallas_call | solution.py:398
  30.4 1.5 %collective-permute-done.8 = f32[2,32,512]{2,1,0:T(8,128)S(1)} collective-permute-done((f32[2,32,512]{2,1,0:T(8,128)S(1)}, f32[2,32,512]{2,1,0:T(8,128)S(1)}, u32[]{:S(2)}, u32[]{:S(2)}) %collective-permute-start.8) | collective-permute-done | bytes 131104 | tf_op jit(solution)/shard_map/ppermute | solution.py:24
  31.9 1.4 %collective-permute-start.11 = (f32[2,32,512]{2,1,0:T(8,128)S(1)}, f32[2,32,512]{2,1,0:T(8,128)S(1)}, u32[]{:S(2)}, u32[]{:S(2)}) collective-permute-start(f32[2,32,512]{2,1,0:T(8,128)S(1)} %fusion.3), channel_id=1, source_target_pairs={{0,4},{1,9},{2,6},{3,11},{4,0},{5,13},{6,2},{7,15},{8,12},{9,1},{1... | collective-permute-start | bytes 393224 | tf_op jit(solution)/shard_map/ppermute | solution.py:24
  33.4 1.6 %collective-permute-start.14 = (f32[2,32,512]{2,1,0:T(8,128)S(1)}, f32[2,32,512]{2,1,0:T(8,128)S(1)}, u32[]{:S(2)}, u32[]{:S(2)}) collective-permute-start(f32[2,32,512]{2,1,0:T(8,128)S(1)} %fusion.2), channel_id=1, source_target_pairs={{0,4},{1,9},{2,6},{3,11},{4,0},{5,13},{6,2},{7,15},{8,12},{9,1},{1... | collective-permute-start | bytes 393224 | tf_op jit(solution)/shard_map/ppermute | solution.py:24
  35.0 1.3 %returns.15 = (f32[128,1024]{1,0:T(8,128)S(1)}, f32[8,128]{1,0:T(8,128)}) custom-call(f32[8,136,128]{2,1,0:T(8,128)S(1)} %collective-permute-done.10.refs_0_, bf16[2,2,128,1024]{3,2,1,0:T(8,128)(2,1)S(1)} %get-tuple-element.178.refs_4_.refs_1_), custom_call_target="tpu_custom_call" | custom-call | tf_op jit(solution)/shard_map/returns/pallas_call | solution.py:398
  36.3 1.2 %collective-permute-done.11 = f32[2,32,512]{2,1,0:T(8,128)S(1)} collective-permute-done((f32[2,32,512]{2,1,0:T(8,128)S(1)}, f32[2,32,512]{2,1,0:T(8,128)S(1)}, u32[]{:S(2)}, u32[]{:S(2)}) %collective-permute-start.11) | collective-permute-done | bytes 131104 | tf_op jit(solution)/shard_map/ppermute | solution.py:24
  37.5 2.5 %collective-permute-start.13 = (f32[2,32,512]{2,1,0:T(8,128)S(1)}, f32[2,32,512]{2,1,0:T(8,128)S(1)}, u32[]{:S(2)}, u32[]{:S(2)}) collective-permute-start(f32[2,32,512]{2,1,0:T(8,128)S(1)} %add.40.refs_0_), channel_id=1, source_target_pairs={{0,8},{1,3},{2,10},{3,1},{4,12},{5,7},{6,14},{7,5},{8,0},{9,11},{1... | collective-permute-start | bytes 393224 | tf_op jit(solution)/shard_map/ppermute | solution.py:24
  40.0 0.7 collective-permute-done.14
  40.7 1.9 %collective-permute-start.16 = (f32[2,32,512]{2,1,0:T(8,128)S(1)}, f32[2,32,512]{2,1,0:T(8,128)S(1)}, u32[]{:S(2)}, u32[]{:S(2)}) collective-permute-start(f32[2,32,512]{2,1,0:T(8,128)S(1)} %add.41.refs_0_), channel_id=1, source_target_pairs={{0,8},{1,3},{2,10},{3,1},{4,12},{5,7},{6,14},{7,5},{8,0},{9,11},{1... | collective-permute-start | bytes 393224 | tf_op jit(solution)/shard_map/ppermute | solution.py:24
  42.5 0.9 %collective-permute-done.13.refs_1_ = f32[2,32,512]{2,1,0:T(8,128)S(1)} collective-permute-done((f32[2,32,512]{2,1,0:T(8,128)S(1)}, f32[2,32,512]{2,1,0:T(8,128)S(1)}, u32[]{:S(2)}, u32[]{:S(2)}) %collective-permute-start.13) | collective-permute-done | bytes 131104 | tf_op jit(solution)/shard_map/ppermute | solution.py:24
  43.5 1.6 %collective-permute-start.15 = (f32[32,512]{1,0:T(8,128)S(1)}, f32[32,512]{1,0:T(8,128)S(1)}, u32[]{:S(2)}, u32[]{:S(2)}) collective-permute-start(f32[32,512]{1,0:T(8,128)S(1)} %own.4.refs_1_), channel_id=1, source_target_pairs={{0,2},{1,5},{2,0},{3,7},{4,6},{5,1},{6,4},{7,3},{8,10},{9,13},{10,... | collective-permute-start | bytes 196616 | tf_op jit(solution)/shard_map/ppermute | solution.py:24
  45.1 2.0 %collective-permute-done.16.refs_1_ = f32[2,32,512]{2,1,0:T(8,128)S(1)} collective-permute-done((f32[2,32,512]{2,1,0:T(8,128)S(1)}, f32[2,32,512]{2,1,0:T(8,128)S(1)}, u32[]{:S(2)}, u32[]{:S(2)}) %collective-permute-start.16) | collective-permute-done | bytes 131104 | tf_op jit(solution)/shard_map/ppermute | solution.py:24
  47.2 1.4 %collective-permute-start.19 = (f32[32,512]{1,0:T(8,128)S(1)}, f32[32,512]{1,0:T(8,128)S(1)}, u32[]{:S(2)}, u32[]{:S(2)}) collective-permute-start(f32[32,512]{1,0:T(8,128)S(1)} %own.5.refs_1_), channel_id=1, source_target_pairs={{0,2},{1,5},{2,0},{3,7},{4,6},{5,1},{6,4},{7,3},{8,10},{9,13},{10,... | collective-permute-start | bytes 196616 | tf_op jit(solution)/shard_map/ppermute | solution.py:24
  48.6 0.5 collective-permute-start.18
  49.1 2.4 %collective-permute-done.19.refs_2_ = f32[32,512]{1,0:T(8,128)S(1)} collective-permute-done((f32[32,512]{1,0:T(8,128)S(1)}, f32[32,512]{1,0:T(8,128)S(1)}, u32[]{:S(2)}, u32[]{:S(2)}) %collective-permute-start.19) | collective-permute-done | bytes 65568 | tf_op jit(solution)/shard_map/ppermute | solution.py:24
  51.5 1.6 %year.8 = (f32[512,512]{1,0:T(8,128)S(1)}, f32[512,512]{1,0:T(8,128)S(1)}, f32[2,2,2,32,512]{4,3,2,1,0:T(8,128)S(1)}, f32[64,128]{1,0:T(8,128)S(1)}) custom-call(s32[1]{0:T(128)} %bitcast.refs_0_.me, f32[32,512]{1,0:T(8,128)S(1)} %own.4.refs_1_, f32[32,512]{1,0:T(8,128)S(1)} %collective-permute-done.15.refs_2_, ...), custom_call_target="tpu_custom_call" | custom-call | flops 268435456 | bytes 5242880 | tf_op jit(solution)/shard_map/year/pallas_call | solution.py:453
  53.1 0.6 collective-permute-start.20
  53.7 1.7 %year.9 = (f32[512,512]{1,0:T(8,128)S(1)}, f32[512,512]{1,0:T(8,128)S(1)}, f32[2,2,2,32,512]{4,3,2,1,0:T(8,128)S(1)}, f32[64,128]{1,0:T(8,128)S(1)}) custom-call(s32[1]{0:T(128)} %bitcast.refs_0_.me, f32[32,512]{1,0:T(8,128)S(1)} %own.5.refs_1_, f32[32,512]{1,0:T(8,128)S(1)} %collective-permute-done.19.refs_2_, ...), custom_call_target="tpu_custom_call" | custom-call | flops 268435456 | bytes 5242880 | tf_op jit(solution)/shard_map/year/pallas_call | solution.py:453
  55.6 1.4 %collective-permute-start.23 = (f32[2,32,512]{2,1,0:T(8,128)S(1)}, f32[2,32,512]{2,1,0:T(8,128)S(1)}, u32[]{:S(2)}, u32[]{:S(2)}) collective-permute-start(f32[2,32,512]{2,1,0:T(8,128)S(1)} %slice_bitcast_fusion.7), channel_id=1, source_target_pairs={{0,2},{1,5},{2,0},{3,7},{4,6},{5,1},{6,4},{7,3},{8,10},{9,13},{10,... | collective-permute-start | bytes 393224 | tf_op jit(solution)/shard_map/ppermute | solution.py:24
  57.1 1.4 %collective-permute-start.26 = (f32[2,32,512]{2,1,0:T(8,128)S(1)}, f32[2,32,512]{2,1,0:T(8,128)S(1)}, u32[]{:S(2)}, u32[]{:S(2)}) collective-permute-start(f32[2,32,512]{2,1,0:T(8,128)S(1)} %slice_bitcast_fusion.4), channel_id=1, source_target_pairs={{0,2},{1,5},{2,0},{3,7},{4,6},{5,1},{6,4},{7,3},{8,10},{9,13},{10,... | collective-permute-start | bytes 393224 | tf_op jit(solution)/shard_map/ppermute | solution.py:24
  58.5 1.3 %returns.16 = (f32[128,1024]{1,0:T(8,128)S(1)}, f32[8,128]{1,0:T(8,128)}) custom-call(f32[2,136,128]{2,1,0:T(8,128)S(1)} %constant_dynamic-update-slice_fusion.refs_0_, f32[2,136,128]{2,1,0:T(8,128)S(1)} %collective-permute-done.3.refs_0_.refs_1_, f32[2,136,128]{2,1,0:T(8,128)S(1)} %collective-permute-done.2.refs_0_.refs_2_, ...), custom_call_target="tpu_custom_call" | custom-call | tf_op jit(solution)/shard_map/returns/pallas_call | solution.py:398
  59.8 0.8 collective-permute-done.23
  60.6 1.8 %collective-permute-start.25 = (f32[2,32,512]{2,1,0:T(8,128)S(1)}, f32[2,32,512]{2,1,0:T(8,128)S(1)}, u32[]{:S(2)}, u32[]{:S(2)}) collective-permute-start(f32[2,32,512]{2,1,0:T(8,128)S(1)} %fusion.1), channel_id=1, source_target_pairs={{0,4},{1,9},{2,6},{3,11},{4,0},{5,13},{6,2},{7,15},{8,12},{9,1},{1... | collective-permute-start | bytes 393224 | tf_op jit(solution)/shard_map/ppermute | solution.py:24
  62.5 1.6 %collective-permute-start.27 = (f32[2,32,512]{2,1,0:T(8,128)S(1)}, f32[2,32,512]{2,1,0:T(8,128)S(1)}, u32[]{:S(2)}, u32[]{:S(2)}) collective-permute-start(f32[2,32,512]{2,1,0:T(8,128)S(1)} %fusion), channel_id=1, source_target_pairs={{0,4},{1,9},{2,6},{3,11},{4,0},{5,13},{6,2},{7,15},{8,12},{9,1},{1... | collective-permute-start | bytes 393224 | tf_op jit(solution)/shard_map/ppermute | solution.py:24
  64.1 1.3 %returns.17 = (f32[128,1024]{1,0:T(8,128)S(1)}, f32[8,128]{1,0:T(8,128)}) custom-call(f32[8,136,128]{2,1,0:T(8,128)S(1)} %collective-permute-done.10.refs_0_, bf16[2,2,128,1024]{3,2,1,0:T(8,128)(2,1)S(1)} %get-tuple-element.178.refs_4_.refs_1_), custom_call_target="tpu_custom_call" | custom-call | tf_op jit(solution)/shard_map/returns/pallas_call | solution.py:398
  65.4 1.8 %collective-permute-done.25 = f32[2,32,512]{2,1,0:T(8,128)S(1)} collective-permute-done((f32[2,32,512]{2,1,0:T(8,128)S(1)}, f32[2,32,512]{2,1,0:T(8,128)S(1)}, u32[]{:S(2)}, u32[]{:S(2)}) %collective-permute-start.25) | collective-permute-done | bytes 131104 | tf_op jit(solution)/shard_map/ppermute | solution.py:24
  67.2 2.1 %collective-permute-start.29 = (f32[2,32,512]{2,1,0:T(8,128)S(1)}, f32[2,32,512]{2,1,0:T(8,128)S(1)}, u32[]{:S(2)}, u32[]{:S(2)}) collective-permute-start(f32[2,32,512]{2,1,0:T(8,128)S(1)} %add.46.refs_0_), channel_id=1, source_target_pairs={{0,8},{1,3},{2,10},{3,1},{4,12},{5,7},{6,14},{7,5},{8,0},{9,11},{1... | collective-permute-start | bytes 393224 | tf_op jit(solution)/shard_map/ppermute | solution.py:24
  69.2 0.5 collective-permute-done.27
  69.8 2.2 %collective-permute-start.28 = (f32[2,32,512]{2,1,0:T(8,128)S(1)}, f32[2,32,512]{2,1,0:T(8,128)S(1)}, u32[]{:S(2)}, u32[]{:S(2)}) collective-permute-start(f32[2,32,512]{2,1,0:T(8,128)S(1)} %add.47.refs_0_), channel_id=1, source_target_pairs={{0,8},{1,3},{2,10},{3,1},{4,12},{5,7},{6,14},{7,5},{8,0},{9,11},{1... | collective-permute-start | bytes 393224 | tf_op jit(solution)/shard_map/ppermute | solution.py:24
  72.0 2.5 %collective-permute-done.29.refs_1_ = f32[2,32,512]{2,1,0:T(8,128)S(1)} collective-permute-done((f32[2,32,512]{2,1,0:T(8,128)S(1)}, f32[2,32,512]{2,1,0:T(8,128)S(1)}, u32[]{:S(2)}, u32[]{:S(2)}) %collective-permute-start.29) | collective-permute-done | bytes 131104 | tf_op jit(solution)/shard_map/ppermute | solution.py:24
  74.6 1.4 %collective-permute-start.31 = (f32[32,512]{1,0:T(8,128)S(1)}, f32[32,512]{1,0:T(8,128)S(1)}, u32[]{:S(2)}, u32[]{:S(2)}) collective-permute-start(f32[32,512]{1,0:T(8,128)S(1)} %own.6.refs_1_), channel_id=1, source_target_pairs={{0,2},{1,5},{2,0},{3,7},{4,6},{5,1},{6,4},{7,3},{8,10},{9,13},{10,... | collective-permute-start | bytes 196616 | tf_op jit(solution)/shard_map/ppermute | solution.py:24
  76.0 1.3 %collective-permute-start.30 = (f32[32,512]{1,0:T(8,128)S(1)}, f32[32,512]{1,0:T(8,128)S(1)}, u32[]{:S(2)}, u32[]{:S(2)}) collective-permute-start(f32[32,512]{1,0:T(8,128)S(1)} %own.7.refs_1_), channel_id=1, source_target_pairs={{0,2},{1,5},{2,0},{3,7},{4,6},{5,1},{6,4},{7,3},{8,10},{9,13},{10,... | collective-permute-start | bytes 196616 | tf_op jit(solution)/shard_map/ppermute | solution.py:24
  77.4 1.5 %collective-permute-done.31.refs_2_ = f32[32,512]{1,0:T(8,128)S(1)} collective-permute-done((f32[32,512]{1,0:T(8,128)S(1)}, f32[32,512]{1,0:T(8,128)S(1)}, u32[]{:S(2)}, u32[]{:S(2)}) %collective-permute-start.31) | collective-permute-done | bytes 65568 | tf_op jit(solution)/shard_map/ppermute | solution.py:24
  78.9 0.5 collective-permute-start.32
  79.4 0.9 %collective-permute-done.30.refs_2_ = f32[32,512]{1,0:T(8,128)S(1)} collective-permute-done((f32[32,512]{1,0:T(8,128)S(1)}, f32[32,512]{1,0:T(8,128)S(1)}, u32[]{:S(2)}, u32[]{:S(2)}) %collective-permute-start.30) | collective-permute-done | bytes 65568 | tf_op jit(solution)/shard_map/ppermute | solution.py:24
  80.4 1.0 %year.10 = (f32[512,512]{1,0:T(8,128)S(1)}, f32[512,512]{1,0:T(8,128)S(1)}, f32[64,128]{1,0:T(8,128)S(1)}) custom-call(s32[1]{0:T(128)} %bitcast.refs_0_.me, f32[32,512]{1,0:T(8,128)S(1)} %own.6.refs_1_, f32[32,512]{1,0:T(8,128)S(1)} %collective-permute-done.31.refs_2_, f32[32,512]{1,0:T(8,128)S(1)} %collective-permute-done.34.refs_3_, ...), custom_call_target="tpu_custom_call" | custom-call | flops 268435456 | bytes 5242880 | tf_op jit(solution)/shard_map/year/pallas_call | solution.py:453
  81.4 0.3 collective-permute-done.33.refs_4_
  81.6 2.1 %year.11 = (f32[512,1024]{1,0:T(8,128)}, f32[512,1024]{1,0:T(8,128)}, f32[3,64,128]{2,1,0:T(8,128)}) custom-call(s32[1]{0:T(128)} %bitcast.refs_0_.me, f32[32,512]{1,0:T(8,128)S(1)} %own.7.refs_1_, f32[32,512]{1,0:T(8,128)S(1)} %collective-permute-done.30.refs_2_, f32[32,512]{1,0:T(8,128)S(1)} %collective-permute-done.32.refs_3_, ...), custom_call_target="tpu_custom_call" | custom-call | flops 268435456 | bytes 5242880 | tf_op jit(solution)/shard_map/year/pallas_call | solution.py:453
  (60 shorter events, 1.1 us)
Async XLA Ops:
  2.4 8.3 %collective-permute-start = (f32[1,136,128]{2,1,0:T(8,128)}, f32[1,136,128]{2,1,0:T(8,128)S(1)}, u32[]{:S(2)}, u32[]{:S(2)}) collective-permute-start(f32[1,136,128]{2,1,0:T(8,128)} %bitcast.58), channel_id=1, source_target_pairs={{0,8},{1,9},{2,10},{3,11},{4,12},{5,13},{6,14},{7,15},{8,0},{9,1},... | collective-permute-start | bytes 208904 | tf_op jit(solution)/shard_map/ppermute | solution.py:24
  6.5 1.4 %copy-start.1 = (f32[3,128,1024]{2,1,0:T(8,128)S(1)}, f32[3,128,1024]{2,1,0:T(8,128)}, u32[]{:S(2)}) copy-start(f32[3,128,1024]{2,1,0:T(8,128)} %shocks.1) | copy-start | bytes 4718596
  7.9 0.9 %copy-start.2 = (f32[136,128]{1,0:T(8,128)S(1)}, f32[136,128]{1,0:T(8,128)}, u32[]{:S(2)}) copy-start(f32[136,128]{1,0:T(8,128)} %get-tuple-element.106.block) | copy-start | bytes 208900
  8.7 0.7 copy-start.3
  10.6 5.2 %collective-permute-start.3 = (f32[2,136,128]{2,1,0:T(8,128)S(1)}, f32[2,136,128]{2,1,0:T(8,128)S(1)}, u32[]{:S(2)}, u32[]{:S(2)}) collective-permute-start(f32[2,136,128]{2,1,0:T(8,128)S(1)} %constant_dynamic-update-slice_fusion.refs_0_), channel_id=1, source_target_pairs={{0,2},{1,3},{2,0},{3,1},{4,6},{5,7},{6,4},{7,5},{8,10},{9,11},{10,... | collective-permute-start | bytes 417800 | tf_op jit(solution)/shard_map/ppermute | solution.py:24
  12.2 6.3 %collective-permute-start.2 = (f32[2,136,128]{2,1,0:T(8,128)S(1)}, f32[2,136,128]{2,1,0:T(8,128)S(1)}, u32[]{:S(2)}, u32[]{:S(2)}) collective-permute-start(f32[2,136,128]{2,1,0:T(8,128)S(1)} %constant_dynamic-update-slice_fusion.refs_0_), channel_id=1, source_target_pairs={{0,4},{1,5},{2,6},{3,7},{4,0},{5,1},{6,2},{7,3},{8,12},{9,13},{10,... | collective-permute-start | bytes 417800 | tf_op jit(solution)/shard_map/ppermute | solution.py:24
  13.8 6.4 %collective-permute-start.1 = (f32[2,136,128]{2,1,0:T(8,128)S(1)}, f32[2,136,128]{2,1,0:T(8,128)S(1)}, u32[]{:S(2)}, u32[]{:S(2)}) collective-permute-start(f32[2,136,128]{2,1,0:T(8,128)S(1)} %constant_dynamic-update-slice_fusion.refs_0_), channel_id=1, source_target_pairs={{0,6},{1,7},{2,4},{3,5},{4,2},{5,3},{6,0},{7,1},{8,14},{9,15},{10,... | collective-permute-start | bytes 417800 | tf_op jit(solution)/shard_map/ppermute | solution.py:24
  15.8 6.5 %copy-start = (bf16[512,3,1024]{2,0,1:T(8,128)(2,1)S(1)}, bf16[512,3,1024]{2,0,1:T(8,128)(2,1)}, u32[]{:S(2)}) copy-start(bf16[512,3,1024]{2,0,1:T(8,128)(2,1)} %param.23) | copy-start | bytes 9437188
  20.7 1.6 %collective-permute-start.5 = (f32[128,512]{1,0:T(8,128)S(1)}, f32[128,512]{1,0:T(8,128)S(1)}, u32[]{:S(2)}, u32[]{:S(2)}) collective-permute-start(f32[128,512]{1,0:T(8,128)S(1)} %get-tuple-element.121.refs_3_), channel_id=1, source_target_pairs={{0,1},{1,0},{2,3},{3,2},{4,5},{5,4},{6,7},{7,6},{8,9},{9,8},{10,11... | collective-permute-start | bytes 786440 | tf_op jit(solution)/shard_map/ppermute | solution.py:24
  20.8 1.5 %collective-permute-start.4 = (f32[8,128]{1,0:T(8,128)S(1)}, f32[8,128]{1,0:T(8,128)S(1)}, u32[]{:S(2)}, u32[]{:S(2)}) collective-permute-start(f32[8,128]{1,0:T(8,128)S(1)} %get-tuple-element.126.refs_1_), channel_id=1, source_target_pairs={{0,1},{1,0},{2,3},{3,2},{4,5},{5,4},{6,7},{7,6},{8,9},{9,8},{10,11... | collective-permute-start | bytes 12296 | tf_op jit(solution)/shard_map/ppermute | solution.py:24
  21.9 2.4 %collective-permute-start.7 = (f32[128,512]{1,0:T(8,128)S(1)}, f32[128,512]{1,0:T(8,128)S(1)}, u32[]{:S(2)}, u32[]{:S(2)}) collective-permute-start(f32[128,512]{1,0:T(8,128)S(1)} %get-tuple-element.128.refs_3_), channel_id=1, source_target_pairs={{0,1},{1,0},{2,3},{3,2},{4,5},{5,4},{6,7},{7,6},{8,9},{9,8},{10,11... | collective-permute-start | bytes 786440 | tf_op jit(solution)/shard_map/ppermute | solution.py:24
  24.1 2.7 %collective-permute-start.6 = (f32[2,2,32,512]{3,2,1,0:T(8,128)S(1)}, f32[2,2,32,512]{3,2,1,0:T(8,128)S(1)}, u32[]{:S(2)}, u32[]{:S(2)}) collective-permute-start(f32[2,2,32,512]{3,2,1,0:T(8,128)S(1)} %slice_bitcast_fusion.3), channel_id=1, source_target_pairs={{0,1},{1,0},{2,3},{3,2},{4,5},{5,4},{6,7},{7,6},{8,9},{9,8},{10,11... | collective-permute-start | bytes 786440 | tf_op jit(solution)/shard_map/ppermute | solution.py:24
  26.1 2.1 %collective-permute-start.9 = (f32[2,2,32,512]{3,2,1,0:T(8,128)S(1)}, f32[2,2,32,512]{3,2,1,0:T(8,128)S(1)}, u32[]{:S(2)}, u32[]{:S(2)}) collective-permute-start(f32[2,2,32,512]{3,2,1,0:T(8,128)S(1)} %slice_bitcast_fusion.2), channel_id=1, source_target_pairs={{0,1},{1,0},{2,3},{3,2},{4,5},{5,4},{6,7},{7,6},{8,9},{9,8},{10,11... | collective-permute-start | bytes 786440 | tf_op jit(solution)/shard_map/ppermute | solution.py:24
  26.6 5.3 %collective-permute-start.10 = (f32[8,136,128]{2,1,0:T(8,128)S(1)}, f32[8,136,128]{2,1,0:T(8,128)S(1)}, u32[]{:S(2)}, u32[]{:S(2)}) collective-permute-start(f32[8,136,128]{2,1,0:T(8,128)S(1)} %pad_maximum_fusion), channel_id=1, source_target_pairs={{0,1},{1,0},{2,3},{3,2},{4,5},{5,4},{6,7},{7,6},{8,9},{9,8},{10,11... | collective-permute-start | bytes 1671176 | tf_op jit(solution)/shard_map/ppermute | solution.py:24
  26.9 5.0 %collective-permute-start.8 = (f32[2,32,512]{2,1,0:T(8,128)S(1)}, f32[2,32,512]{2,1,0:T(8,128)S(1)}, u32[]{:S(2)}, u32[]{:S(2)}) collective-permute-start(f32[2,32,512]{2,1,0:T(8,128)S(1)} %slice_bitcast_fusion.11), channel_id=1, source_target_pairs={{0,2},{1,5},{2,0},{3,7},{4,6},{5,1},{6,4},{7,3},{8,10},{9,13},{10,... | collective-permute-start | bytes 393224 | tf_op jit(solution)/shard_map/ppermute | solution.py:24
  28.3 5.1 %collective-permute-start.12 = (f32[2,32,512]{2,1,0:T(8,128)S(1)}, f32[2,32,512]{2,1,0:T(8,128)S(1)}, u32[]{:S(2)}, u32[]{:S(2)}) collective-permute-start(f32[2,32,512]{2,1,0:T(8,128)S(1)} %slice_bitcast_fusion.8), channel_id=1, source_target_pairs={{0,2},{1,5},{2,0},{3,7},{4,6},{5,1},{6,4},{7,3},{8,10},{9,13},{10,... | collective-permute-start | bytes 393224 | tf_op jit(solution)/shard_map/ppermute | solution.py:24
  31.9 5.5 %collective-permute-start.11 = (f32[2,32,512]{2,1,0:T(8,128)S(1)}, f32[2,32,512]{2,1,0:T(8,128)S(1)}, u32[]{:S(2)}, u32[]{:S(2)}) collective-permute-start(f32[2,32,512]{2,1,0:T(8,128)S(1)} %fusion.3), channel_id=1, source_target_pairs={{0,4},{1,9},{2,6},{3,11},{4,0},{5,13},{6,2},{7,15},{8,12},{9,1},{1... | collective-permute-start | bytes 393224 | tf_op jit(solution)/shard_map/ppermute | solution.py:24
  33.4 7.2 %collective-permute-start.14 = (f32[2,32,512]{2,1,0:T(8,128)S(1)}, f32[2,32,512]{2,1,0:T(8,128)S(1)}, u32[]{:S(2)}, u32[]{:S(2)}) collective-permute-start(f32[2,32,512]{2,1,0:T(8,128)S(1)} %fusion.2), channel_id=1, source_target_pairs={{0,4},{1,9},{2,6},{3,11},{4,0},{5,13},{6,2},{7,15},{8,12},{9,1},{1... | collective-permute-start | bytes 393224 | tf_op jit(solution)/shard_map/ppermute | solution.py:24
  37.5 5.9 %collective-permute-start.13 = (f32[2,32,512]{2,1,0:T(8,128)S(1)}, f32[2,32,512]{2,1,0:T(8,128)S(1)}, u32[]{:S(2)}, u32[]{:S(2)}) collective-permute-start(f32[2,32,512]{2,1,0:T(8,128)S(1)} %add.40.refs_0_), channel_id=1, source_target_pairs={{0,8},{1,3},{2,10},{3,1},{4,12},{5,7},{6,14},{7,5},{8,0},{9,11},{1... | collective-permute-start | bytes 393224 | tf_op jit(solution)/shard_map/ppermute | solution.py:24
  40.7 6.4 %collective-permute-start.16 = (f32[2,32,512]{2,1,0:T(8,128)S(1)}, f32[2,32,512]{2,1,0:T(8,128)S(1)}, u32[]{:S(2)}, u32[]{:S(2)}) collective-permute-start(f32[2,32,512]{2,1,0:T(8,128)S(1)} %add.41.refs_0_), channel_id=1, source_target_pairs={{0,8},{1,3},{2,10},{3,1},{4,12},{5,7},{6,14},{7,5},{8,0},{9,11},{1... | collective-permute-start | bytes 393224 | tf_op jit(solution)/shard_map/ppermute | solution.py:24
  43.5 5.1 %collective-permute-start.15 = (f32[32,512]{1,0:T(8,128)S(1)}, f32[32,512]{1,0:T(8,128)S(1)}, u32[]{:S(2)}, u32[]{:S(2)}) collective-permute-start(f32[32,512]{1,0:T(8,128)S(1)} %own.4.refs_1_), channel_id=1, source_target_pairs={{0,2},{1,5},{2,0},{3,7},{4,6},{5,1},{6,4},{7,3},{8,10},{9,13},{10,... | collective-permute-start | bytes 196616 | tf_op jit(solution)/shard_map/ppermute | solution.py:24
  47.2 4.3 %collective-permute-start.19 = (f32[32,512]{1,0:T(8,128)S(1)}, f32[32,512]{1,0:T(8,128)S(1)}, u32[]{:S(2)}, u32[]{:S(2)}) collective-permute-start(f32[32,512]{1,0:T(8,128)S(1)} %own.5.refs_1_), channel_id=1, source_target_pairs={{0,2},{1,5},{2,0},{3,7},{4,6},{5,1},{6,4},{7,3},{8,10},{9,13},{10,... | collective-permute-start | bytes 196616 | tf_op jit(solution)/shard_map/ppermute | solution.py:24
  48.6 2.9 %collective-permute-start.17 = (f32[32,512]{1,0:T(8,128)S(1)}, f32[32,512]{1,0:T(8,128)S(1)}, u32[]{:S(2)}, u32[]{:S(2)}) collective-permute-start(f32[32,512]{1,0:T(8,128)S(1)} %own.4.refs_1_), channel_id=1, source_target_pairs={{0,1},{1,0},{2,3},{3,2},{4,5},{5,4},{6,7},{7,6},{8,9},{9,8},{10,11... | collective-permute-start | bytes 196616 | tf_op jit(solution)/shard_map/ppermute | solution.py:24
  48.6 2.9 %collective-permute-start.18 = (f32[32,512]{1,0:T(8,128)S(1)}, f32[32,512]{1,0:T(8,128)S(1)}, u32[]{:S(2)}, u32[]{:S(2)}) collective-permute-start(f32[32,512]{1,0:T(8,128)S(1)} %collective-permute-done.15.refs_2_), channel_id=1, source_target_pairs={{0,1},{1,0},{2,3},{3,2},{4,5},{5,4},{6,7},{7,6},{8,9},{9,8},{10,11... | collective-permute-start | bytes 196616 | tf_op jit(solution)/shard_map/ppermute | solution.py:24
  49.1 4.0 %collective-permute-start.21 = (f32[32,512]{1,0:T(8,128)S(1)}, f32[32,512]{1,0:T(8,128)S(1)}, u32[]{:S(2)}, u32[]{:S(2)}) collective-permute-start(f32[32,512]{1,0:T(8,128)S(1)} %own.5.refs_1_), channel_id=1, source_target_pairs={{0,1},{1,0},{2,3},{3,2},{4,5},{5,4},{6,7},{7,6},{8,9},{9,8},{10,11... | collective-permute-start | bytes 196616 | tf_op jit(solution)/shard_map/ppermute | solution.py:24
  51.5 1.6 %collective-permute-start.22 = (f32[32,512]{1,0:T(8,128)S(1)}, f32[32,512]{1,0:T(8,128)S(1)}, u32[]{:S(2)}, u32[]{:S(2)}) collective-permute-start(f32[32,512]{1,0:T(8,128)S(1)} %collective-permute-done.19.refs_2_), channel_id=1, source_target_pairs={{0,1},{1,0},{2,3},{3,2},{4,5},{5,4},{6,7},{7,6},{8,9},{9,8},{10,11... | collective-permute-start | bytes 196616 | tf_op jit(solution)/shard_map/ppermute | solution.py:24
  53.1 2.4 %collective-permute-start.20 = (f32[2,2,32,512]{3,2,1,0:T(8,128)S(1)}, f32[2,2,32,512]{3,2,1,0:T(8,128)S(1)}, u32[]{:S(2)}, u32[]{:S(2)}) collective-permute-start(f32[2,2,32,512]{3,2,1,0:T(8,128)S(1)} %slice_bitcast_fusion.1), channel_id=1, source_target_pairs={{0,1},{1,0},{2,3},{3,2},{4,5},{5,4},{6,7},{7,6},{8,9},{9,8},{10,11... | collective-permute-start | bytes 786440 | tf_op jit(solution)/shard_map/ppermute | solution.py:24
  55.4 1.6 %collective-permute-start.24 = (f32[2,2,32,512]{3,2,1,0:T(8,128)S(1)}, f32[2,2,32,512]{3,2,1,0:T(8,128)S(1)}, u32[]{:S(2)}, u32[]{:S(2)}) collective-permute-start(f32[2,2,32,512]{3,2,1,0:T(8,128)S(1)} %slice_bitcast_fusion), channel_id=1, source_target_pairs={{0,1},{1,0},{2,3},{3,2},{4,5},{5,4},{6,7},{7,6},{8,9},{9,8},{10,11... | collective-permute-start | bytes 786440 | tf_op jit(solution)/shard_map/ppermute | solution.py:24
  55.6 5.0 %collective-permute-start.23 = (f32[2,32,512]{2,1,0:T(8,128)S(1)}, f32[2,32,512]{2,1,0:T(8,128)S(1)}, u32[]{:S(2)}, u32[]{:S(2)}) collective-permute-start(f32[2,32,512]{2,1,0:T(8,128)S(1)} %slice_bitcast_fusion.7), channel_id=1, source_target_pairs={{0,2},{1,5},{2,0},{3,7},{4,6},{5,1},{6,4},{7,3},{8,10},{9,13},{10,... | collective-permute-start | bytes 393224 | tf_op jit(solution)/shard_map/ppermute | solution.py:24
  57.1 5.4 %collective-permute-start.26 = (f32[2,32,512]{2,1,0:T(8,128)S(1)}, f32[2,32,512]{2,1,0:T(8,128)S(1)}, u32[]{:S(2)}, u32[]{:S(2)}) collective-permute-start(f32[2,32,512]{2,1,0:T(8,128)S(1)} %slice_bitcast_fusion.4), channel_id=1, source_target_pairs={{0,2},{1,5},{2,0},{3,7},{4,6},{5,1},{6,4},{7,3},{8,10},{9,13},{10,... | collective-permute-start | bytes 393224 | tf_op jit(solution)/shard_map/ppermute | solution.py:24
  60.6 6.5 %collective-permute-start.25 = (f32[2,32,512]{2,1,0:T(8,128)S(1)}, f32[2,32,512]{2,1,0:T(8,128)S(1)}, u32[]{:S(2)}, u32[]{:S(2)}) collective-permute-start(f32[2,32,512]{2,1,0:T(8,128)S(1)} %fusion.1), channel_id=1, source_target_pairs={{0,4},{1,9},{2,6},{3,11},{4,0},{5,13},{6,2},{7,15},{8,12},{9,1},{1... | collective-permute-start | bytes 393224 | tf_op jit(solution)/shard_map/ppermute | solution.py:24
  62.5 7.3 %collective-permute-start.27 = (f32[2,32,512]{2,1,0:T(8,128)S(1)}, f32[2,32,512]{2,1,0:T(8,128)S(1)}, u32[]{:S(2)}, u32[]{:S(2)}) collective-permute-start(f32[2,32,512]{2,1,0:T(8,128)S(1)} %fusion), channel_id=1, source_target_pairs={{0,4},{1,9},{2,6},{3,11},{4,0},{5,13},{6,2},{7,15},{8,12},{9,1},{1... | collective-permute-start | bytes 393224 | tf_op jit(solution)/shard_map/ppermute | solution.py:24
  67.2 7.3 %collective-permute-start.29 = (f32[2,32,512]{2,1,0:T(8,128)S(1)}, f32[2,32,512]{2,1,0:T(8,128)S(1)}, u32[]{:S(2)}, u32[]{:S(2)}) collective-permute-start(f32[2,32,512]{2,1,0:T(8,128)S(1)} %add.46.refs_0_), channel_id=1, source_target_pairs={{0,8},{1,3},{2,10},{3,1},{4,12},{5,7},{6,14},{7,5},{8,0},{9,11},{1... | collective-permute-start | bytes 393224 | tf_op jit(solution)/shard_map/ppermute | solution.py:24
  69.8 6.2 %collective-permute-start.28 = (f32[2,32,512]{2,1,0:T(8,128)S(1)}, f32[2,32,512]{2,1,0:T(8,128)S(1)}, u32[]{:S(2)}, u32[]{:S(2)}) collective-permute-start(f32[2,32,512]{2,1,0:T(8,128)S(1)} %add.47.refs_0_), channel_id=1, source_target_pairs={{0,8},{1,3},{2,10},{3,1},{4,12},{5,7},{6,14},{7,5},{8,0},{9,11},{1... | collective-permute-start | bytes 393224 | tf_op jit(solution)/shard_map/ppermute | solution.py:24
  74.6 4.3 %collective-permute-start.31 = (f32[32,512]{1,0:T(8,128)S(1)}, f32[32,512]{1,0:T(8,128)S(1)}, u32[]{:S(2)}, u32[]{:S(2)}) collective-permute-start(f32[32,512]{1,0:T(8,128)S(1)} %own.6.refs_1_), channel_id=1, source_target_pairs={{0,2},{1,5},{2,0},{3,7},{4,6},{5,1},{6,4},{7,3},{8,10},{9,13},{10,... | collective-permute-start | bytes 196616 | tf_op jit(solution)/shard_map/ppermute | solution.py:24
  76.0 4.3 %collective-permute-start.30 = (f32[32,512]{1,0:T(8,128)S(1)}, f32[32,512]{1,0:T(8,128)S(1)}, u32[]{:S(2)}, u32[]{:S(2)}) collective-permute-start(f32[32,512]{1,0:T(8,128)S(1)} %own.7.refs_1_), channel_id=1, source_target_pairs={{0,2},{1,5},{2,0},{3,7},{4,6},{5,1},{6,4},{7,3},{8,10},{9,13},{10,... | collective-permute-start | bytes 196616 | tf_op jit(solution)/shard_map/ppermute | solution.py:24
  77.4 3.0 %collective-permute-start.34 = (f32[32,512]{1,0:T(8,128)S(1)}, f32[32,512]{1,0:T(8,128)S(1)}, u32[]{:S(2)}, u32[]{:S(2)}) collective-permute-start(f32[32,512]{1,0:T(8,128)S(1)} %own.6.refs_1_), channel_id=1, source_target_pairs={{0,1},{1,0},{2,3},{3,2},{4,5},{5,4},{6,7},{7,6},{8,9},{9,8},{10,11... | collective-permute-start | bytes 196616 | tf_op jit(solution)/shard_map/ppermute | solution.py:24
  78.9 1.5 %collective-permute-start.35 = (f32[32,512]{1,0:T(8,128)S(1)}, f32[32,512]{1,0:T(8,128)S(1)}, u32[]{:S(2)}, u32[]{:S(2)}) collective-permute-start(f32[32,512]{1,0:T(8,128)S(1)} %collective-permute-done.31.refs_2_), channel_id=1, source_target_pairs={{0,1},{1,0},{2,3},{3,2},{4,5},{5,4},{6,7},{7,6},{8,9},{9,8},{10,11... | collective-permute-start | bytes 196616 | tf_op jit(solution)/shard_map/ppermute | solution.py:24
  78.9 2.4 %collective-permute-start.32 = (f32[32,512]{1,0:T(8,128)S(1)}, f32[32,512]{1,0:T(8,128)S(1)}, u32[]{:S(2)}, u32[]{:S(2)}) collective-permute-start(f32[32,512]{1,0:T(8,128)S(1)} %own.7.refs_1_), channel_id=1, source_target_pairs={{0,1},{1,0},{2,3},{3,2},{4,5},{5,4},{6,7},{7,6},{8,9},{9,8},{10,11... | collective-permute-start | bytes 196616 | tf_op jit(solution)/shard_map/ppermute | solution.py:24
  80.4 1.3 %collective-permute-start.33 = (f32[32,512]{1,0:T(8,128)S(1)}, f32[32,512]{1,0:T(8,128)S(1)}, u32[]{:S(2)}, u32[]{:S(2)}) collective-permute-start(f32[32,512]{1,0:T(8,128)S(1)} %collective-permute-done.30.refs_2_), channel_id=1, source_target_pairs={{0,1},{1,0},{2,3},{3,2},{4,5},{5,4},{6,7},{7,6},{8,9},{9,8},{10,11... | collective-permute-start | bytes 196616 | tf_op jit(solution)/shard_map/ppermute | solution.py:24

commit v8 on v7

--- a/solution.py
+++ b/solution.py
@@ -191,6 +191,10 @@
     out[...] = dot(pick, one, ROW) + dot(pick, two, ROW) + dot(pick, three, ROW)
 
 
+def rates_body(first, me, declared, out):
+    own_columns(me, declared[...], first, out)
+
+
 def slice_spot(me, order, slice_funds):
     core = (me & 1) ^ (order >> 1)
     side = ((me >> (1 + core)) & 1) ^ (order & 1)
@@ -246,7 +250,7 @@
         out_a, out_l, own, declared = refs
     else:
         member_t = refs.pop(0)
-        out_a, out_l, out_s, own, declared, acc = refs
+        out_a, out_l, out_s, declared, acc = refs
     funds, width = declared.shape
     count = member.shape[1]
     if year == 0:
@@ -317,7 +321,7 @@
         elif not last:
             acc[0, :, cut] = sum_a
             acc[1, :, cut] = sum_l
-    if not (last and first):
+    if last and not first:
         own_columns(me, declared[...], first, own)
     for copy in copies:
         copy.wait()
@@ -447,9 +451,9 @@
                 ins.append(member_t)
                 specs.append(VMEM)
                 out = [shaped(count, half)] * 2
-                out += [shaped(2, 2, 2, slice_funds, half), shaped(owned, funds)]
+                out += [shaped(2, 2, 2, slice_funds, half), shaped(funds, half)]
                 out_specs = [VMEM] * 4
-                scratch += [pltpu.VMEM((2, funds, half), F32)]
+                scratch = [pltpu.VMEM((2, funds, half), F32)]
             result = call(
                 functools.partial(year_body, year, first, last, slice_funds),
                 out,
@@ -466,7 +470,7 @@
                 rates[year][h] = result[2]
                 yield result[2]
                 return
-            state, share, rates[year][h] = list(result[:2]), result[2], result[3]
+            state, share, declared = list(result[:2]), result[2], result[3]
             if year == 0 and h == 1:
                 others.append(swap(jnp.concatenate(tie(blocks, share)), 1))
             other = yield share
@@ -478,10 +482,19 @@
                 came, made, ready = lax.optimization_barrier((came, made, list(others)))
                 later[year + 1] = [made]
             held = held[0] + came
+            rates[year][h] = call(
+                functools.partial(rates_body, first),
+                shaped(owned, funds),
+                [SMEM, VMEM],
+                "rates",
+                limit=4,
+            )(me_ref, tie(declared, held))
             other = yield held
             *steps, closing = list(FULL) + [(o,) for o in far[1:]]
             for i, step in enumerate(steps):
                 came = tie(swap(held, *step), other)
+                if i == 0:
+                    came, rates[year][h] = lax.optimization_barrier((came, rates[year][h]))
                 if i == 0 and h == 0:
                     made = returns(year + 1, 0, paths, ready, tie(x_later, held))[0]
                     came, made = lax.optimization_barrier((came, made))

time: 84.2 us -> 83.6 us (level)
  waiting for transfers between devices: 21.6 us -> 19.2 us
  starting transfers between devices: 36.7 us -> 37.8 us
    ppermute x36, waiting for transfers between devices: 21.6 us -> 19.2 us  [swap(): return lax.ppermute(x, 'pol', [(i, i ^ offsets[i % 2]) for i in range(n)])]
    ppermute x36, starting transfers between devices: 36.7 us -> 37.8 us  [swap(): return lax.ppermute(x, 'pol', [(i, i ^ offsets[i % 2]) for i in range(n)])]
    pallas_call x0 -> x4, Pallas kernels: none -> 1.03 us  [advance_half(): call(functools.partial(rates_body, first), shaped(owned, funds), [SMEM, V...]
  transfers between devices with their start and end apart: 36 -> 36, of which waited for: 17 -> 17; matrix products, arithmetic and copies ran while one was open for 1% -> 1% of each run, Pallas kernels for 20% -> 21%
where the time goes in v8:
time: 83.6 us; the launch traced here: 83.3 us
  starting transfers between devices  37.8 us (45%)
  Pallas kernels  21.7 us (26%)
  waiting for transfers between devices  19.2 us (23%)
  local copies, waits for them, and re-layouts  3.14 us (4%)
  between operations  1.15 us (1%)
    ppermute x36, starting transfers between devices, swap(): return lax.ppermute(x, 'pol', [(i, i ^ offsets[i % 2]) for i in range(n)])  37.8 us
    ppermute x36, waiting for transfers between devices, swap(): return lax.ppermute(x, 'pol', [(i, i ^ offsets[i % 2]) for i in range(n)])  19.2 us
    pallas_call x6, Pallas kernels, advance_half(): call(functools.partial(year_body, year, first, last, slice_funds), out, s...  9.56 us
    pallas_call x9, Pallas kernels, returns(): call(functools.partial(returns_body, year, first, secs, len(before) > 0,...  7.95 us
    unnamed x9, local copies, waits for them, and re-layouts  3.02 us
    pallas_call x1, Pallas kernels, local(): call(pack_body, [shaped(2 * secs + 8, funds), shaped(8, count)], [SMEM] +...  1.71 us
  transfers between devices with their start and end apart: 36, of which 17 were waited for; matrix products, arithmetic and copies ran while one was open for 1% of the time, Pallas kernels for 21%

profile of v8, /device:TPU:0, one launch (start us, length us, event | category | flops | bytes accessed | tf_op | source)
XLA Modules:
  0.0 83.3 jit_solution(4513192884030425130)
XLA Ops:
  0.6 1.7 %pack.1 = (f32[136,128]{1,0:T(8,128)}, f32[8,512]{1,0:T(8,128)}) custom-call(s32[1]{0:T(128)} %bitcast.refs_0_.me, f32[64,128]{1,0:T(8,128)} %refs_1_.1, f32[64,128]{1,0:T(8,128)} %refs_2_.1, f32[1,64]{1,0:T(1,128)} %bitcast.64, s32[1,512]{1,0:T(1,128)} %bitcast.59, s32[1,512]{1,0:T(1,128)} %bitcast.60, f32[1,512]{1,0:T(1,128)} %bitcast.61, ...), custom_call_target="tpu_custom_call" | custom-call | flops 1000000 | bytes 100000 | tf_op jit(solution)/shard_map/pack/pallas_call | solution.py:365
  2.4 4.1 %collective-permute-start = (f32[1,136,128]{2,1,0:T(8,128)}, f32[1,136,128]{2,1,0:T(8,128)S(1)}, u32[]{:S(2)}, u32[]{:S(2)}) collective-permute-start(f32[1,136,128]{2,1,0:T(8,128)} %bitcast.58), channel_id=1, source_target_pairs={{0,8},{1,9},{2,10},{3,11},{4,12},{5,13},{6,14},{7,15},{8,0},{9,1},... | collective-permute-start | bytes 208904 | tf_op jit(solution)/shard_map/ppermute | solution.py:24
  6.5 1.4 %copy-done.1 = f32[3,128,1024]{2,1,0:T(8,128)S(1)} copy-done((f32[3,128,1024]{2,1,0:T(8,128)S(1)}, f32[3,128,1024]{2,1,0:T(8,128)}, u32[]{:S(2)}) %copy-start.1) | copy-done | bytes 1572888
  7.9 0.9 %copy-done.2 = f32[136,128]{1,0:T(8,128)S(1)} copy-done((f32[136,128]{1,0:T(8,128)S(1)}, f32[136,128]{1,0:T(8,128)}, u32[]{:S(2)}) %copy-start.2) | copy-done | bytes 69656
  8.7 0.7 copy-done.3
  9.5 1.1 %columns.1 = (bf16[3,128,512]{2,1,0:T(8,128)(2,1)S(1)}, bf16[3,512,256]{2,1,0:T(8,128)(2,1)S(1)}, f32[8,512,128]{2,1,0:T(8,128)S(1)}, bf16[2,128,1024]{2,1,0:T(8...) custom-call(f32[8,512]{1,0:T(8,128)S(1)} %copy-done.3, f32[136,128]{1,0:T(8,128)S(1)} %copy-done.2, ...), custom_call_target="tpu_custom_call" | custom-call | flops 1000000 | bytes 4000000 | tf_op jit(solution)/shard_map/columns/pallas_call | solution.py:377
  10.6 1.6 %collective-permute-start.3 = (f32[2,136,128]{2,1,0:T(8,128)S(1)}, f32[2,136,128]{2,1,0:T(8,128)S(1)}, u32[]{:S(2)}, u32[]{:S(2)}) collective-permute-start(f32[2,136,128]{2,1,0:T(8,128)S(1)} %constant_dynamic-update-slice_fusion.refs_0_), channel_id=1, source_target_pairs={{0,2},{1,3},{2,0},{3,1},{4,6},{5,7},{6,4},{7,5},{8,10},{9,11},{10,... | collective-permute-start | bytes 417800 | tf_op jit(solution)/shard_map/ppermute | solution.py:24
  12.2 1.6 %collective-permute-start.2 = (f32[2,136,128]{2,1,0:T(8,128)S(1)}, f32[2,136,128]{2,1,0:T(8,128)S(1)}, u32[]{:S(2)}, u32[]{:S(2)}) collective-permute-start(f32[2,136,128]{2,1,0:T(8,128)S(1)} %constant_dynamic-update-slice_fusion.refs_0_), channel_id=1, source_target_pairs={{0,4},{1,5},{2,6},{3,7},{4,0},{5,1},{6,2},{7,3},{8,12},{9,13},{10,... | collective-permute-start | bytes 417800 | tf_op jit(solution)/shard_map/ppermute | solution.py:24
  13.8 0.4 collective-permute-start.1
  14.2 0.6 returns.9
  14.8 1.1 %collective-permute-done.3.refs_0_.refs_1_ = f32[2,136,128]{2,1,0:T(8,128)S(1)} collective-permute-done((f32[2,136,128]{2,1,0:T(8,128)S(1)}, f32[2,136,128]{2,1,0:T(8,128)S(1)}, u32[]{:S(2)}, u32[]{:S(2)}) %collective-permute-start.3) | collective-permute-done | bytes 139296 | tf_op jit(solution)/shard_map/ppermute | solution.py:24
  15.8 0.6 returns.10
  16.4 2.1 %collective-permute-done.2.refs_0_.refs_2_ = f32[2,136,128]{2,1,0:T(8,128)S(1)} collective-permute-done((f32[2,136,128]{2,1,0:T(8,128)S(1)}, f32[2,136,128]{2,1,0:T(8,128)S(1)}, u32[]{:S(2)}, u32[]{:S(2)}) %collective-permute-start.2) | collective-permute-done | bytes 139296 | tf_op jit(solution)/shard_map/ppermute | solution.py:24
  18.5 0.6 returns.11
  19.1 1.1 %collective-permute-done.1.refs_0_.refs_3_ = f32[2,136,128]{2,1,0:T(8,128)S(1)} collective-permute-done((f32[2,136,128]{2,1,0:T(8,128)S(1)}, f32[2,136,128]{2,1,0:T(8,128)S(1)}, u32[]{:S(2)}, u32[]{:S(2)}) %collective-permute-start.1) | collective-permute-done | bytes 139296 | tf_op jit(solution)/shard_map/ppermute | solution.py:24
  20.2 0.5 returns.12
  20.8 0.5 collective-permute-start.4
  21.3 0.7 returns.13
  22.0 0.3 collective-permute-done.4.refs_2_
  22.3 1.7 %year.6 = (f32[512,512]{1,0:T(8,128)S(1)}, f32[512,512]{1,0:T(8,128)S(1)}, f32[2,2,2,32,512]{4,3,2,1,0:T(8,128)S(1)}, f32[128,512]{1,0:T(8,128)S(1)}) custom-call(s32[1]{0:T(128)} %bitcast.refs_0_.me, f32[8,128]{1,0:T(8,128)S(1)} %get-tuple-element.138.refs_1_, f32[8,128]{1,0:T(8,128)S(1)} %collective-permute-done.4.refs_2_, ...), custom_call_target="tpu_custom_call" | custom-call | flops 268435456 | bytes 5242880 | tf_op jit(solution)/shard_map/year/pallas_call | solution.py:457
  24.3 1.7 %year.7 = (f32[512,512]{1,0:T(8,128)S(1)}, f32[512,512]{1,0:T(8,128)S(1)}, f32[2,2,2,32,512]{4,3,2,1,0:T(8,128)S(1)}, f32[128,512]{1,0:T(8,128)S(1)}) custom-call(s32[1]{0:T(128)} %bitcast.refs_0_.me, f32[8,128]{1,0:T(8,128)S(1)} %get-tuple-element.138.refs_1_, f32[8,128]{1,0:T(8,128)S(1)} %collective-permute-done.4.refs_2_, ...), custom_call_target="tpu_custom_call" | custom-call | flops 268435456 | bytes 5242880 | tf_op jit(solution)/shard_map/year/pallas_call | solution.py:457
  26.0 0.4 collective-permute-start.9
  26.7 1.4 %collective-permute-start.8 = (f32[2,32,512]{2,1,0:T(8,128)S(1)}, f32[2,32,512]{2,1,0:T(8,128)S(1)}, u32[]{:S(2)}, u32[]{:S(2)}) collective-permute-start(f32[2,32,512]{2,1,0:T(8,128)S(1)} %slice_bitcast_fusion.11), channel_id=1, source_target_pairs={{0,2},{1,5},{2,0},{3,7},{4,6},{5,1},{6,4},{7,3},{8,10},{9,13},{10,... | collective-permute-start | bytes 393224 | tf_op jit(solution)/shard_map/ppermute | solution.py:24
  28.2 0.9 %collective-permute-start.12 = (f32[2,32,512]{2,1,0:T(8,128)S(1)}, f32[2,32,512]{2,1,0:T(8,128)S(1)}, u32[]{:S(2)}, u32[]{:S(2)}) collective-permute-start(f32[2,32,512]{2,1,0:T(8,128)S(1)} %slice_bitcast_fusion.8), channel_id=1, source_target_pairs={{0,2},{1,5},{2,0},{3,7},{4,6},{5,1},{6,4},{7,3},{8,10},{9,13},{10,... | collective-permute-start | bytes 393224 | tf_op jit(solution)/shard_map/ppermute | solution.py:24
  29.0 1.3 %returns.14 = (f32[128,1024]{1,0:T(8,128)S(1)}, f32[8,128]{1,0:T(8,128)}) custom-call(f32[2,136,128]{2,1,0:T(8,128)S(1)} %constant_dynamic-update-slice_fusion.refs_0_, f32[2,136,128]{2,1,0:T(8,128)S(1)} %collective-permute-done.3.refs_0_.refs_1_, f32[2,136,128]{2,1,0:T(8,128)S(1)} %collective-permute-done.2.refs_0_.refs_2_, ...), custom_call_target="tpu_custom_call" | custom-call | tf_op jit(solution)/shard_map/returns/pallas_call | solution.py:402
  30.3 1.5 %collective-permute-done.8 = f32[2,32,512]{2,1,0:T(8,128)S(1)} collective-permute-done((f32[2,32,512]{2,1,0:T(8,128)S(1)}, f32[2,32,512]{2,1,0:T(8,128)S(1)}, u32[]{:S(2)}, u32[]{:S(2)}) %collective-permute-start.8) | collective-permute-done | bytes 131104 | tf_op jit(solution)/shard_map/ppermute | solution.py:24
  31.8 1.4 %collective-permute-start.11 = (f32[2,32,512]{2,1,0:T(8,128)S(1)}, f32[2,32,512]{2,1,0:T(8,128)S(1)}, u32[]{:S(2)}, u32[]{:S(2)}) collective-permute-start(f32[2,32,512]{2,1,0:T(8,128)S(1)} %fusion.3), channel_id=1, source_target_pairs={{0,4},{1,9},{2,6},{3,11},{4,0},{5,13},{6,2},{7,15},{8,12},{9,1},{1... | collective-permute-start | bytes 393224 | tf_op jit(solution)/shard_map/ppermute | solution.py:24
  33.3 1.6 %collective-permute-start.14 = (f32[2,32,512]{2,1,0:T(8,128)S(1)}, f32[2,32,512]{2,1,0:T(8,128)S(1)}, u32[]{:S(2)}, u32[]{:S(2)}) collective-permute-start(f32[2,32,512]{2,1,0:T(8,128)S(1)} %fusion.2), channel_id=1, source_target_pairs={{0,4},{1,9},{2,6},{3,11},{4,0},{5,13},{6,2},{7,15},{8,12},{9,1},{1... | collective-permute-start | bytes 393224 | tf_op jit(solution)/shard_map/ppermute | solution.py:24
  34.9 0.3 rates.4.refs_14_
  35.1 1.3 %returns.15 = (f32[128,1024]{1,0:T(8,128)S(1)}, f32[8,128]{1,0:T(8,128)}) custom-call(f32[8,136,128]{2,1,0:T(8,128)S(1)} %collective-permute-done.10.refs_0_, bf16[2,2,128,1024]{3,2,1,0:T(8,128)(2,1)S(1)} %get-tuple-element.199.refs_4_.refs_1_), custom_call_target="tpu_custom_call" | custom-call | tf_op jit(solution)/shard_map/returns/pallas_call | solution.py:402
  36.4 0.9 %collective-permute-done.11 = f32[2,32,512]{2,1,0:T(8,128)S(1)} collective-permute-done((f32[2,32,512]{2,1,0:T(8,128)S(1)}, f32[2,32,512]{2,1,0:T(8,128)S(1)}, u32[]{:S(2)}, u32[]{:S(2)}) %collective-permute-start.11) | collective-permute-done | bytes 131104 | tf_op jit(solution)/shard_map/ppermute | solution.py:24
  37.4 2.5 %collective-permute-start.13 = (f32[2,32,512]{2,1,0:T(8,128)S(1)}, f32[2,32,512]{2,1,0:T(8,128)S(1)}, u32[]{:S(2)}, u32[]{:S(2)}) collective-permute-start(f32[2,32,512]{2,1,0:T(8,128)S(1)} %add.40.refs_0_), channel_id=1, source_target_pairs={{0,8},{1,3},{2,10},{3,1},{4,12},{5,7},{6,14},{7,5},{8,0},{9,11},{1... | collective-permute-start | bytes 393224 | tf_op jit(solution)/shard_map/ppermute | solution.py:24
  40.1 0.4 collective-permute-done.14
  40.5 1.9 %collective-permute-start.16 = (f32[2,32,512]{2,1,0:T(8,128)S(1)}, f32[2,32,512]{2,1,0:T(8,128)S(1)}, u32[]{:S(2)}, u32[]{:S(2)}) collective-permute-start(f32[2,32,512]{2,1,0:T(8,128)S(1)} %add.41.refs_0_), channel_id=1, source_target_pairs={{0,8},{1,3},{2,10},{3,1},{4,12},{5,7},{6,14},{7,5},{8,0},{9,11},{1... | collective-permute-start | bytes 393224 | tf_op jit(solution)/shard_map/ppermute | solution.py:24
  42.4 0.9 %collective-permute-done.13.refs_1_ = f32[2,32,512]{2,1,0:T(8,128)S(1)} collective-permute-done((f32[2,32,512]{2,1,0:T(8,128)S(1)}, f32[2,32,512]{2,1,0:T(8,128)S(1)}, u32[]{:S(2)}, u32[]{:S(2)}) %collective-permute-start.13) | collective-permute-done | bytes 131104 | tf_op jit(solution)/shard_map/ppermute | solution.py:24
  43.4 1.6 %collective-permute-start.15 = (f32[32,512]{1,0:T(8,128)S(1)}, f32[32,512]{1,0:T(8,128)S(1)}, u32[]{:S(2)}, u32[]{:S(2)}) collective-permute-start(f32[32,512]{1,0:T(8,128)S(1)} %own.4.refs_1_), channel_id=1, source_target_pairs={{0,2},{1,5},{2,0},{3,7},{4,6},{5,1},{6,4},{7,3},{8,10},{9,13},{10,... | collective-permute-start | bytes 196616 | tf_op jit(solution)/shard_map/ppermute | solution.py:24
  45.0 1.6 %collective-permute-done.16.refs_1_ = f32[2,32,512]{2,1,0:T(8,128)S(1)} collective-permute-done((f32[2,32,512]{2,1,0:T(8,128)S(1)}, f32[2,32,512]{2,1,0:T(8,128)S(1)}, u32[]{:S(2)}, u32[]{:S(2)}) %collective-permute-start.16) | collective-permute-done | bytes 131104 | tf_op jit(solution)/shard_map/ppermute | solution.py:24
  46.7 1.4 %collective-permute-start.19 = (f32[32,512]{1,0:T(8,128)S(1)}, f32[32,512]{1,0:T(8,128)S(1)}, u32[]{:S(2)}, u32[]{:S(2)}) collective-permute-start(f32[32,512]{1,0:T(8,128)S(1)} %own.5.refs_1_), channel_id=1, source_target_pairs={{0,2},{1,5},{2,0},{3,7},{4,6},{5,1},{6,4},{7,3},{8,10},{9,13},{10,... | collective-permute-start | bytes 196616 | tf_op jit(solution)/shard_map/ppermute | solution.py:24
  48.1 0.5 collective-permute-start.18
  48.6 2.4 %collective-permute-done.19.refs_2_ = f32[32,512]{1,0:T(8,128)S(1)} collective-permute-done((f32[32,512]{1,0:T(8,128)S(1)}, f32[32,512]{1,0:T(8,128)S(1)}, u32[]{:S(2)}, u32[]{:S(2)}) %collective-permute-start.19) | collective-permute-done | bytes 65568 | tf_op jit(solution)/shard_map/ppermute | solution.py:24
  51.0 1.4 %year.8 = (f32[512,512]{1,0:T(8,128)S(1)}, f32[512,512]{1,0:T(8,128)S(1)}, f32[2,2,2,32,512]{4,3,2,1,0:T(8,128)S(1)}, f32[128,512]{1,0:T(8,128)S(1)}) custom-call(s32[1]{0:T(128)} %bitcast.refs_0_.me, f32[32,512]{1,0:T(8,128)S(1)} %own.4.refs_1_, f32[32,512]{1,0:T(8,128)S(1)} %collective-permute-done.15.refs_2_, ...), custom_call_target="tpu_custom_call" | custom-call | flops 268435456 | bytes 5242880 | tf_op jit(solution)/shard_map/year/pallas_call | solution.py:457
  52.5 0.6 collective-permute-start.20
  53.1 1.6 %year.9 = (f32[512,512]{1,0:T(8,128)S(1)}, f32[512,512]{1,0:T(8,128)S(1)}, f32[2,2,2,32,512]{4,3,2,1,0:T(8,128)S(1)}, f32[128,512]{1,0:T(8,128)S(1)}) custom-call(s32[1]{0:T(128)} %bitcast.refs_0_.me, f32[32,512]{1,0:T(8,128)S(1)} %own.5.refs_1_, f32[32,512]{1,0:T(8,128)S(1)} %collective-permute-done.19.refs_2_, ...), custom_call_target="tpu_custom_call" | custom-call | flops 268435456 | bytes 5242880 | tf_op jit(solution)/shard_map/year/pallas_call | solution.py:457
  54.9 1.4 %collective-permute-start.23 = (f32[2,32,512]{2,1,0:T(8,128)S(1)}, f32[2,32,512]{2,1,0:T(8,128)S(1)}, u32[]{:S(2)}, u32[]{:S(2)}) collective-permute-start(f32[2,32,512]{2,1,0:T(8,128)S(1)} %slice_bitcast_fusion.7), channel_id=1, source_target_pairs={{0,2},{1,5},{2,0},{3,7},{4,6},{5,1},{6,4},{7,3},{8,10},{9,13},{10,... | collective-permute-start | bytes 393224 | tf_op jit(solution)/shard_map/ppermute | solution.py:24
  56.4 1.4 %collective-permute-start.26 = (f32[2,32,512]{2,1,0:T(8,128)S(1)}, f32[2,32,512]{2,1,0:T(8,128)S(1)}, u32[]{:S(2)}, u32[]{:S(2)}) collective-permute-start(f32[2,32,512]{2,1,0:T(8,128)S(1)} %slice_bitcast_fusion.4), channel_id=1, source_target_pairs={{0,2},{1,5},{2,0},{3,7},{4,6},{5,1},{6,4},{7,3},{8,10},{9,13},{10,... | collective-permute-start | bytes 393224 | tf_op jit(solution)/shard_map/ppermute | solution.py:24
  57.8 1.3 %returns.16 = (f32[128,1024]{1,0:T(8,128)S(1)}, f32[8,128]{1,0:T(8,128)}) custom-call(f32[2,136,128]{2,1,0:T(8,128)S(1)} %constant_dynamic-update-slice_fusion.refs_0_, f32[2,136,128]{2,1,0:T(8,128)S(1)} %collective-permute-done.3.refs_0_.refs_1_, f32[2,136,128]{2,1,0:T(8,128)S(1)} %collective-permute-done.2.refs_0_.refs_2_, ...), custom_call_target="tpu_custom_call" | custom-call | tf_op jit(solution)/shard_map/returns/pallas_call | solution.py:402
  59.1 0.8 collective-permute-done.23
  59.9 2.3 %collective-permute-start.25 = (f32[2,32,512]{2,1,0:T(8,128)S(1)}, f32[2,32,512]{2,1,0:T(8,128)S(1)}, u32[]{:S(2)}, u32[]{:S(2)}) collective-permute-start(f32[2,32,512]{2,1,0:T(8,128)S(1)} %fusion.1), channel_id=1, source_target_pairs={{0,4},{1,9},{2,6},{3,11},{4,0},{5,13},{6,2},{7,15},{8,12},{9,1},{1... | collective-permute-start | bytes 393224 | tf_op jit(solution)/shard_map/ppermute | solution.py:24
  62.2 1.6 %collective-permute-start.27 = (f32[2,32,512]{2,1,0:T(8,128)S(1)}, f32[2,32,512]{2,1,0:T(8,128)S(1)}, u32[]{:S(2)}, u32[]{:S(2)}) collective-permute-start(f32[2,32,512]{2,1,0:T(8,128)S(1)} %fusion), channel_id=1, source_target_pairs={{0,4},{1,9},{2,6},{3,11},{4,0},{5,13},{6,2},{7,15},{8,12},{9,1},{1... | collective-permute-start | bytes 393224 | tf_op jit(solution)/shard_map/ppermute | solution.py:24
  63.8 0.3 rates.6.refs_16_
  64.1 1.3 %returns.17 = (f32[128,1024]{1,0:T(8,128)S(1)}, f32[8,128]{1,0:T(8,128)}) custom-call(f32[8,136,128]{2,1,0:T(8,128)S(1)} %collective-permute-done.10.refs_0_, bf16[2,2,128,1024]{3,2,1,0:T(8,128)(2,1)S(1)} %get-tuple-element.199.refs_4_.refs_1_), custom_call_target="tpu_custom_call" | custom-call | tf_op jit(solution)/shard_map/returns/pallas_call | solution.py:402
  65.4 1.2 %collective-permute-done.25 = f32[2,32,512]{2,1,0:T(8,128)S(1)} collective-permute-done((f32[2,32,512]{2,1,0:T(8,128)S(1)}, f32[2,32,512]{2,1,0:T(8,128)S(1)}, u32[]{:S(2)}, u32[]{:S(2)}) %collective-permute-start.25) | collective-permute-done | bytes 131104 | tf_op jit(solution)/shard_map/ppermute | solution.py:24
  66.6 2.2 %collective-permute-start.29 = (f32[2,32,512]{2,1,0:T(8,128)S(1)}, f32[2,32,512]{2,1,0:T(8,128)S(1)}, u32[]{:S(2)}, u32[]{:S(2)}) collective-permute-start(f32[2,32,512]{2,1,0:T(8,128)S(1)} %add.46.refs_0_), channel_id=1, source_target_pairs={{0,8},{1,3},{2,10},{3,1},{4,12},{5,7},{6,14},{7,5},{8,0},{9,11},{1... | collective-permute-start | bytes 393224 | tf_op jit(solution)/shard_map/ppermute | solution.py:24
  68.9 0.3 rates.7.refs_17_
  69.4 2.3 %collective-permute-start.28 = (f32[2,32,512]{2,1,0:T(8,128)S(1)}, f32[2,32,512]{2,1,0:T(8,128)S(1)}, u32[]{:S(2)}, u32[]{:S(2)}) collective-permute-start(f32[2,32,512]{2,1,0:T(8,128)S(1)} %add.47.refs_0_), channel_id=1, source_target_pairs={{0,8},{1,3},{2,10},{3,1},{4,12},{5,7},{6,14},{7,5},{8,0},{9,11},{1... | collective-permute-start | bytes 393224 | tf_op jit(solution)/shard_map/ppermute | solution.py:24
  71.6 0.9 %collective-permute-done.29.refs_1_ = f32[2,32,512]{2,1,0:T(8,128)S(1)} collective-permute-done((f32[2,32,512]{2,1,0:T(8,128)S(1)}, f32[2,32,512]{2,1,0:T(8,128)S(1)}, u32[]{:S(2)}, u32[]{:S(2)}) %collective-permute-start.29) | collective-permute-done | bytes 131104 | tf_op jit(solution)/shard_map/ppermute | solution.py:24
  72.6 1.6 %collective-permute-start.31 = (f32[32,512]{1,0:T(8,128)S(1)}, f32[32,512]{1,0:T(8,128)S(1)}, u32[]{:S(2)}, u32[]{:S(2)}) collective-permute-start(f32[32,512]{1,0:T(8,128)S(1)} %own.6.refs_1_), channel_id=1, source_target_pairs={{0,2},{1,5},{2,0},{3,7},{4,6},{5,1},{6,4},{7,3},{8,10},{9,13},{10,... | collective-permute-start | bytes 196616 | tf_op jit(solution)/shard_map/ppermute | solution.py:24
  74.2 1.2 %collective-permute-done.28.refs_1_ = f32[2,32,512]{2,1,0:T(8,128)S(1)} collective-permute-done((f32[2,32,512]{2,1,0:T(8,128)S(1)}, f32[2,32,512]{2,1,0:T(8,128)S(1)}, u32[]{:S(2)}, u32[]{:S(2)}) %collective-permute-start.28) | collective-permute-done | bytes 131104 | tf_op jit(solution)/shard_map/ppermute | solution.py:24
  75.4 1.6 %collective-permute-start.30 = (f32[32,512]{1,0:T(8,128)S(1)}, f32[32,512]{1,0:T(8,128)S(1)}, u32[]{:S(2)}, u32[]{:S(2)}) collective-permute-start(f32[32,512]{1,0:T(8,128)S(1)} %own.7.refs_1_), channel_id=1, source_target_pairs={{0,2},{1,5},{2,0},{3,7},{4,6},{5,1},{6,4},{7,3},{8,10},{9,13},{10,... | collective-permute-start | bytes 196616 | tf_op jit(solution)/shard_map/ppermute | solution.py:24
  77.0 0.5 collective-permute-start.35
  77.5 2.3 %collective-permute-done.30.refs_2_ = f32[32,512]{1,0:T(8,128)S(1)} collective-permute-done((f32[32,512]{1,0:T(8,128)S(1)}, f32[32,512]{1,0:T(8,128)S(1)}, u32[]{:S(2)}, u32[]{:S(2)}) %collective-permute-start.30) | collective-permute-done | bytes 65568 | tf_op jit(solution)/shard_map/ppermute | solution.py:24
  79.8 1.0 %year.10 = (f32[512,512]{1,0:T(8,128)S(1)}, f32[512,512]{1,0:T(8,128)S(1)}, f32[64,128]{1,0:T(8,128)S(1)}) custom-call(s32[1]{0:T(128)} %bitcast.refs_0_.me, f32[32,512]{1,0:T(8,128)S(1)} %own.6.refs_1_, f32[32,512]{1,0:T(8,128)S(1)} %collective-permute-done.31.refs_2_, f32[32,512]{1,0:T(8,128)S(1)} %collective-permute-done.34.refs_3_, ...), custom_call_target="tpu_custom_call" | custom-call | flops 268435456 | bytes 5242880 | tf_op jit(solution)/shard_map/year/pallas_call | solution.py:457
  80.8 0.3 collective-permute-done.33.refs_4_
  81.0 2.1 %year.11 = (f32[512,1024]{1,0:T(8,128)}, f32[512,1024]{1,0:T(8,128)}, f32[3,64,128]{2,1,0:T(8,128)}) custom-call(s32[1]{0:T(128)} %bitcast.refs_0_.me, f32[32,512]{1,0:T(8,128)S(1)} %own.7.refs_1_, f32[32,512]{1,0:T(8,128)S(1)} %collective-permute-done.30.refs_2_, f32[32,512]{1,0:T(8,128)S(1)} %collective-permute-done.32.refs_3_, ...), custom_call_target="tpu_custom_call" | custom-call | flops 268435456 | bytes 5242880 | tf_op jit(solution)/shard_map/year/pallas_call | solution.py:457
  (64 shorter events, 2.0 us)
Async XLA Ops:
  2.4 8.3 %collective-permute-start = (f32[1,136,128]{2,1,0:T(8,128)}, f32[1,136,128]{2,1,0:T(8,128)S(1)}, u32[]{:S(2)}, u32[]{:S(2)}) collective-permute-start(f32[1,136,128]{2,1,0:T(8,128)} %bitcast.58), channel_id=1, source_target_pairs={{0,8},{1,9},{2,10},{3,11},{4,12},{5,13},{6,14},{7,15},{8,0},{9,1},... | collective-permute-start | bytes 208904 | tf_op jit(solution)/shard_map/ppermute | solution.py:24
  6.5 1.4 %copy-start.1 = (f32[3,128,1024]{2,1,0:T(8,128)S(1)}, f32[3,128,1024]{2,1,0:T(8,128)}, u32[]{:S(2)}) copy-start(f32[3,128,1024]{2,1,0:T(8,128)} %shocks.1) | copy-start | bytes 4718596
  7.9 0.9 %copy-start.2 = (f32[136,128]{1,0:T(8,128)S(1)}, f32[136,128]{1,0:T(8,128)}, u32[]{:S(2)}) copy-start(f32[136,128]{1,0:T(8,128)} %get-tuple-element.118.block) | copy-start | bytes 208900
  8.7 0.7 copy-start.3
  10.6 5.2 %collective-permute-start.3 = (f32[2,136,128]{2,1,0:T(8,128)S(1)}, f32[2,136,128]{2,1,0:T(8,128)S(1)}, u32[]{:S(2)}, u32[]{:S(2)}) collective-permute-start(f32[2,136,128]{2,1,0:T(8,128)S(1)} %constant_dynamic-update-slice_fusion.refs_0_), channel_id=1, source_target_pairs={{0,2},{1,3},{2,0},{3,1},{4,6},{5,7},{6,4},{7,5},{8,10},{9,11},{10,... | collective-permute-start | bytes 417800 | tf_op jit(solution)/shard_map/ppermute | solution.py:24
  12.2 6.3 %collective-permute-start.2 = (f32[2,136,128]{2,1,0:T(8,128)S(1)}, f32[2,136,128]{2,1,0:T(8,128)S(1)}, u32[]{:S(2)}, u32[]{:S(2)}) collective-permute-start(f32[2,136,128]{2,1,0:T(8,128)S(1)} %constant_dynamic-update-slice_fusion.refs_0_), channel_id=1, source_target_pairs={{0,4},{1,5},{2,6},{3,7},{4,0},{5,1},{6,2},{7,3},{8,12},{9,13},{10,... | collective-permute-start | bytes 417800 | tf_op jit(solution)/shard_map/ppermute | solution.py:24
  13.8 6.4 %collective-permute-start.1 = (f32[2,136,128]{2,1,0:T(8,128)S(1)}, f32[2,136,128]{2,1,0:T(8,128)S(1)}, u32[]{:S(2)}, u32[]{:S(2)}) collective-permute-start(f32[2,136,128]{2,1,0:T(8,128)S(1)} %constant_dynamic-update-slice_fusion.refs_0_), channel_id=1, source_target_pairs={{0,6},{1,7},{2,4},{3,5},{4,2},{5,3},{6,0},{7,1},{8,14},{9,15},{10,... | collective-permute-start | bytes 417800 | tf_op jit(solution)/shard_map/ppermute | solution.py:24
  15.8 6.5 %copy-start = (bf16[512,3,1024]{2,0,1:T(8,128)(2,1)S(1)}, bf16[512,3,1024]{2,0,1:T(8,128)(2,1)}, u32[]{:S(2)}) copy-start(bf16[512,3,1024]{2,0,1:T(8,128)(2,1)} %param.23) | copy-start | bytes 9437188
  20.7 1.6 %collective-permute-start.5 = (f32[128,512]{1,0:T(8,128)S(1)}, f32[128,512]{1,0:T(8,128)S(1)}, u32[]{:S(2)}, u32[]{:S(2)}) collective-permute-start(f32[128,512]{1,0:T(8,128)S(1)} %get-tuple-element.133.refs_3_), channel_id=1, source_target_pairs={{0,1},{1,0},{2,3},{3,2},{4,5},{5,4},{6,7},{7,6},{8,9},{9,8},{10,11... | collective-permute-start | bytes 786440 | tf_op jit(solution)/shard_map/ppermute | solution.py:24
  20.8 1.5 %collective-permute-start.4 = (f32[8,128]{1,0:T(8,128)S(1)}, f32[8,128]{1,0:T(8,128)S(1)}, u32[]{:S(2)}, u32[]{:S(2)}) collective-permute-start(f32[8,128]{1,0:T(8,128)S(1)} %get-tuple-element.138.refs_1_), channel_id=1, source_target_pairs={{0,1},{1,0},{2,3},{3,2},{4,5},{5,4},{6,7},{7,6},{8,9},{9,8},{10,11... | collective-permute-start | bytes 12296 | tf_op jit(solution)/shard_map/ppermute | solution.py:24
  21.9 2.4 %collective-permute-start.7 = (f32[128,512]{1,0:T(8,128)S(1)}, f32[128,512]{1,0:T(8,128)S(1)}, u32[]{:S(2)}, u32[]{:S(2)}) collective-permute-start(f32[128,512]{1,0:T(8,128)S(1)} %get-tuple-element.140.refs_3_), channel_id=1, source_target_pairs={{0,1},{1,0},{2,3},{3,2},{4,5},{5,4},{6,7},{7,6},{8,9},{9,8},{10,11... | collective-permute-start | bytes 786440 | tf_op jit(solution)/shard_map/ppermute | solution.py:24
  24.1 2.6 %collective-permute-start.6 = (f32[2,2,32,512]{3,2,1,0:T(8,128)S(1)}, f32[2,2,32,512]{3,2,1,0:T(8,128)S(1)}, u32[]{:S(2)}, u32[]{:S(2)}) collective-permute-start(f32[2,2,32,512]{3,2,1,0:T(8,128)S(1)} %slice_bitcast_fusion.3), channel_id=1, source_target_pairs={{0,1},{1,0},{2,3},{3,2},{4,5},{5,4},{6,7},{7,6},{8,9},{9,8},{10,11... | collective-permute-start | bytes 786440 | tf_op jit(solution)/shard_map/ppermute | solution.py:24
  26.0 2.1 %collective-permute-start.9 = (f32[2,2,32,512]{3,2,1,0:T(8,128)S(1)}, f32[2,2,32,512]{3,2,1,0:T(8,128)S(1)}, u32[]{:S(2)}, u32[]{:S(2)}) collective-permute-start(f32[2,2,32,512]{3,2,1,0:T(8,128)S(1)} %slice_bitcast_fusion.2), channel_id=1, source_target_pairs={{0,1},{1,0},{2,3},{3,2},{4,5},{5,4},{6,7},{7,6},{8,9},{9,8},{10,11... | collective-permute-start | bytes 786440 | tf_op jit(solution)/shard_map/ppermute | solution.py:24
  26.5 5.3 %collective-permute-start.10 = (f32[8,136,128]{2,1,0:T(8,128)S(1)}, f32[8,136,128]{2,1,0:T(8,128)S(1)}, u32[]{:S(2)}, u32[]{:S(2)}) collective-permute-start(f32[8,136,128]{2,1,0:T(8,128)S(1)} %pad_maximum_fusion), channel_id=1, source_target_pairs={{0,1},{1,0},{2,3},{3,2},{4,5},{5,4},{6,7},{7,6},{8,9},{9,8},{10,11... | collective-permute-start | bytes 1671176 | tf_op jit(solution)/shard_map/ppermute | solution.py:24
  26.7 5.0 %collective-permute-start.8 = (f32[2,32,512]{2,1,0:T(8,128)S(1)}, f32[2,32,512]{2,1,0:T(8,128)S(1)}, u32[]{:S(2)}, u32[]{:S(2)}) collective-permute-start(f32[2,32,512]{2,1,0:T(8,128)S(1)} %slice_bitcast_fusion.11), channel_id=1, source_target_pairs={{0,2},{1,5},{2,0},{3,7},{4,6},{5,1},{6,4},{7,3},{8,10},{9,13},{10,... | collective-permute-start | bytes 393224 | tf_op jit(solution)/shard_map/ppermute | solution.py:24
  28.2 5.1 %collective-permute-start.12 = (f32[2,32,512]{2,1,0:T(8,128)S(1)}, f32[2,32,512]{2,1,0:T(8,128)S(1)}, u32[]{:S(2)}, u32[]{:S(2)}) collective-permute-start(f32[2,32,512]{2,1,0:T(8,128)S(1)} %slice_bitcast_fusion.8), channel_id=1, source_target_pairs={{0,2},{1,5},{2,0},{3,7},{4,6},{5,1},{6,4},{7,3},{8,10},{9,13},{10,... | collective-permute-start | bytes 393224 | tf_op jit(solution)/shard_map/ppermute | solution.py:24
  31.8 5.6 %collective-permute-start.11 = (f32[2,32,512]{2,1,0:T(8,128)S(1)}, f32[2,32,512]{2,1,0:T(8,128)S(1)}, u32[]{:S(2)}, u32[]{:S(2)}) collective-permute-start(f32[2,32,512]{2,1,0:T(8,128)S(1)} %fusion.3), channel_id=1, source_target_pairs={{0,4},{1,9},{2,6},{3,11},{4,0},{5,13},{6,2},{7,15},{8,12},{9,1},{1... | collective-permute-start | bytes 393224 | tf_op jit(solution)/shard_map/ppermute | solution.py:24
  33.3 7.2 %collective-permute-start.14 = (f32[2,32,512]{2,1,0:T(8,128)S(1)}, f32[2,32,512]{2,1,0:T(8,128)S(1)}, u32[]{:S(2)}, u32[]{:S(2)}) collective-permute-start(f32[2,32,512]{2,1,0:T(8,128)S(1)} %fusion.2), channel_id=1, source_target_pairs={{0,4},{1,9},{2,6},{3,11},{4,0},{5,13},{6,2},{7,15},{8,12},{9,1},{1... | collective-permute-start | bytes 393224 | tf_op jit(solution)/shard_map/ppermute | solution.py:24
  37.4 5.9 %collective-permute-start.13 = (f32[2,32,512]{2,1,0:T(8,128)S(1)}, f32[2,32,512]{2,1,0:T(8,128)S(1)}, u32[]{:S(2)}, u32[]{:S(2)}) collective-permute-start(f32[2,32,512]{2,1,0:T(8,128)S(1)} %add.40.refs_0_), channel_id=1, source_target_pairs={{0,8},{1,3},{2,10},{3,1},{4,12},{5,7},{6,14},{7,5},{8,0},{9,11},{1... | collective-permute-start | bytes 393224 | tf_op jit(solution)/shard_map/ppermute | solution.py:24
  40.5 6.1 %collective-permute-start.16 = (f32[2,32,512]{2,1,0:T(8,128)S(1)}, f32[2,32,512]{2,1,0:T(8,128)S(1)}, u32[]{:S(2)}, u32[]{:S(2)}) collective-permute-start(f32[2,32,512]{2,1,0:T(8,128)S(1)} %add.41.refs_0_), channel_id=1, source_target_pairs={{0,8},{1,3},{2,10},{3,1},{4,12},{5,7},{6,14},{7,5},{8,0},{9,11},{1... | collective-permute-start | bytes 393224 | tf_op jit(solution)/shard_map/ppermute | solution.py:24
  43.4 4.7 %collective-permute-start.15 = (f32[32,512]{1,0:T(8,128)S(1)}, f32[32,512]{1,0:T(8,128)S(1)}, u32[]{:S(2)}, u32[]{:S(2)}) collective-permute-start(f32[32,512]{1,0:T(8,128)S(1)} %own.4.refs_1_), channel_id=1, source_target_pairs={{0,2},{1,5},{2,0},{3,7},{4,6},{5,1},{6,4},{7,3},{8,10},{9,13},{10,... | collective-permute-start | bytes 196616 | tf_op jit(solution)/shard_map/ppermute | solution.py:24
  46.7 4.3 %collective-permute-start.19 = (f32[32,512]{1,0:T(8,128)S(1)}, f32[32,512]{1,0:T(8,128)S(1)}, u32[]{:S(2)}, u32[]{:S(2)}) collective-permute-start(f32[32,512]{1,0:T(8,128)S(1)} %own.5.refs_1_), channel_id=1, source_target_pairs={{0,2},{1,5},{2,0},{3,7},{4,6},{5,1},{6,4},{7,3},{8,10},{9,13},{10,... | collective-permute-start | bytes 196616 | tf_op jit(solution)/shard_map/ppermute | solution.py:24
  48.1 2.9 %collective-permute-start.17 = (f32[32,512]{1,0:T(8,128)S(1)}, f32[32,512]{1,0:T(8,128)S(1)}, u32[]{:S(2)}, u32[]{:S(2)}) collective-permute-start(f32[32,512]{1,0:T(8,128)S(1)} %own.4.refs_1_), channel_id=1, source_target_pairs={{0,1},{1,0},{2,3},{3,2},{4,5},{5,4},{6,7},{7,6},{8,9},{9,8},{10,11... | collective-permute-start | bytes 196616 | tf_op jit(solution)/shard_map/ppermute | solution.py:24
  48.1 2.9 %collective-permute-start.18 = (f32[32,512]{1,0:T(8,128)S(1)}, f32[32,512]{1,0:T(8,128)S(1)}, u32[]{:S(2)}, u32[]{:S(2)}) collective-permute-start(f32[32,512]{1,0:T(8,128)S(1)} %collective-permute-done.15.refs_2_), channel_id=1, source_target_pairs={{0,1},{1,0},{2,3},{3,2},{4,5},{5,4},{6,7},{7,6},{8,9},{9,8},{10,11... | collective-permute-start | bytes 196616 | tf_op jit(solution)/shard_map/ppermute | solution.py:24
  48.6 3.9 %collective-permute-start.21 = (f32[32,512]{1,0:T(8,128)S(1)}, f32[32,512]{1,0:T(8,128)S(1)}, u32[]{:S(2)}, u32[]{:S(2)}) collective-permute-start(f32[32,512]{1,0:T(8,128)S(1)} %own.5.refs_1_), channel_id=1, source_target_pairs={{0,1},{1,0},{2,3},{3,2},{4,5},{5,4},{6,7},{7,6},{8,9},{9,8},{10,11... | collective-permute-start | bytes 196616 | tf_op jit(solution)/shard_map/ppermute | solution.py:24
  51.0 1.5 %collective-permute-start.22 = (f32[32,512]{1,0:T(8,128)S(1)}, f32[32,512]{1,0:T(8,128)S(1)}, u32[]{:S(2)}, u32[]{:S(2)}) collective-permute-start(f32[32,512]{1,0:T(8,128)S(1)} %collective-permute-done.19.refs_2_), channel_id=1, source_target_pairs={{0,1},{1,0},{2,3},{3,2},{4,5},{5,4},{6,7},{7,6},{8,9},{9,8},{10,11... | collective-permute-start | bytes 196616 | tf_op jit(solution)/shard_map/ppermute | solution.py:24
  52.5 2.3 %collective-permute-start.20 = (f32[2,2,32,512]{3,2,1,0:T(8,128)S(1)}, f32[2,2,32,512]{3,2,1,0:T(8,128)S(1)}, u32[]{:S(2)}, u32[]{:S(2)}) collective-permute-start(f32[2,2,32,512]{3,2,1,0:T(8,128)S(1)} %slice_bitcast_fusion.1), channel_id=1, source_target_pairs={{0,1},{1,0},{2,3},{3,2},{4,5},{5,4},{6,7},{7,6},{8,9},{9,8},{10,11... | collective-permute-start | bytes 786440 | tf_op jit(solution)/shard_map/ppermute | solution.py:24
  54.7 1.6 %collective-permute-start.24 = (f32[2,2,32,512]{3,2,1,0:T(8,128)S(1)}, f32[2,2,32,512]{3,2,1,0:T(8,128)S(1)}, u32[]{:S(2)}, u32[]{:S(2)}) collective-permute-start(f32[2,2,32,512]{3,2,1,0:T(8,128)S(1)} %slice_bitcast_fusion), channel_id=1, source_target_pairs={{0,1},{1,0},{2,3},{3,2},{4,5},{5,4},{6,7},{7,6},{8,9},{9,8},{10,11... | collective-permute-start | bytes 786440 | tf_op jit(solution)/shard_map/ppermute | solution.py:24
  54.9 5.0 %collective-permute-start.23 = (f32[2,32,512]{2,1,0:T(8,128)S(1)}, f32[2,32,512]{2,1,0:T(8,128)S(1)}, u32[]{:S(2)}, u32[]{:S(2)}) collective-permute-start(f32[2,32,512]{2,1,0:T(8,128)S(1)} %slice_bitcast_fusion.7), channel_id=1, source_target_pairs={{0,2},{1,5},{2,0},{3,7},{4,6},{5,1},{6,4},{7,3},{8,10},{9,13},{10,... | collective-permute-start | bytes 393224 | tf_op jit(solution)/shard_map/ppermute | solution.py:24
  56.4 5.8 %collective-permute-start.26 = (f32[2,32,512]{2,1,0:T(8,128)S(1)}, f32[2,32,512]{2,1,0:T(8,128)S(1)}, u32[]{:S(2)}, u32[]{:S(2)}) collective-permute-start(f32[2,32,512]{2,1,0:T(8,128)S(1)} %slice_bitcast_fusion.4), channel_id=1, source_target_pairs={{0,2},{1,5},{2,0},{3,7},{4,6},{5,1},{6,4},{7,3},{8,10},{9,13},{10,... | collective-permute-start | bytes 393224 | tf_op jit(solution)/shard_map/ppermute | solution.py:24
  59.9 6.7 %collective-permute-start.25 = (f32[2,32,512]{2,1,0:T(8,128)S(1)}, f32[2,32,512]{2,1,0:T(8,128)S(1)}, u32[]{:S(2)}, u32[]{:S(2)}) collective-permute-start(f32[2,32,512]{2,1,0:T(8,128)S(1)} %fusion.1), channel_id=1, source_target_pairs={{0,4},{1,9},{2,6},{3,11},{4,0},{5,13},{6,2},{7,15},{8,12},{9,1},{1... | collective-permute-start | bytes 393224 | tf_op jit(solution)/shard_map/ppermute | solution.py:24
  62.2 7.1 %collective-permute-start.27 = (f32[2,32,512]{2,1,0:T(8,128)S(1)}, f32[2,32,512]{2,1,0:T(8,128)S(1)}, u32[]{:S(2)}, u32[]{:S(2)}) collective-permute-start(f32[2,32,512]{2,1,0:T(8,128)S(1)} %fusion), channel_id=1, source_target_pairs={{0,4},{1,9},{2,6},{3,11},{4,0},{5,13},{6,2},{7,15},{8,12},{9,1},{1... | collective-permute-start | bytes 393224 | tf_op jit(solution)/shard_map/ppermute | solution.py:24
  66.6 5.9 %collective-permute-start.29 = (f32[2,32,512]{2,1,0:T(8,128)S(1)}, f32[2,32,512]{2,1,0:T(8,128)S(1)}, u32[]{:S(2)}, u32[]{:S(2)}) collective-permute-start(f32[2,32,512]{2,1,0:T(8,128)S(1)} %add.46.refs_0_), channel_id=1, source_target_pairs={{0,8},{1,3},{2,10},{3,1},{4,12},{5,7},{6,14},{7,5},{8,0},{9,11},{1... | collective-permute-start | bytes 393224 | tf_op jit(solution)/shard_map/ppermute | solution.py:24
  69.4 6.0 %collective-permute-start.28 = (f32[2,32,512]{2,1,0:T(8,128)S(1)}, f32[2,32,512]{2,1,0:T(8,128)S(1)}, u32[]{:S(2)}, u32[]{:S(2)}) collective-permute-start(f32[2,32,512]{2,1,0:T(8,128)S(1)} %add.47.refs_0_), channel_id=1, source_target_pairs={{0,8},{1,3},{2,10},{3,1},{4,12},{5,7},{6,14},{7,5},{8,0},{9,11},{1... | collective-permute-start | bytes 393224 | tf_op jit(solution)/shard_map/ppermute | solution.py:24
  72.6 4.4 %collective-permute-start.31 = (f32[32,512]{1,0:T(8,128)S(1)}, f32[32,512]{1,0:T(8,128)S(1)}, u32[]{:S(2)}, u32[]{:S(2)}) collective-permute-start(f32[32,512]{1,0:T(8,128)S(1)} %own.6.refs_1_), channel_id=1, source_target_pairs={{0,2},{1,5},{2,0},{3,7},{4,6},{5,1},{6,4},{7,3},{8,10},{9,13},{10,... | collective-permute-start | bytes 196616 | tf_op jit(solution)/shard_map/ppermute | solution.py:24
  75.4 4.3 %collective-permute-start.30 = (f32[32,512]{1,0:T(8,128)S(1)}, f32[32,512]{1,0:T(8,128)S(1)}, u32[]{:S(2)}, u32[]{:S(2)}) collective-permute-start(f32[32,512]{1,0:T(8,128)S(1)} %own.7.refs_1_), channel_id=1, source_target_pairs={{0,2},{1,5},{2,0},{3,7},{4,6},{5,1},{6,4},{7,3},{8,10},{9,13},{10,... | collective-permute-start | bytes 196616 | tf_op jit(solution)/shard_map/ppermute | solution.py:24
  77.0 2.8 %collective-permute-start.34 = (f32[32,512]{1,0:T(8,128)S(1)}, f32[32,512]{1,0:T(8,128)S(1)}, u32[]{:S(2)}, u32[]{:S(2)}) collective-permute-start(f32[32,512]{1,0:T(8,128)S(1)} %own.6.refs_1_), channel_id=1, source_target_pairs={{0,1},{1,0},{2,3},{3,2},{4,5},{5,4},{6,7},{7,6},{8,9},{9,8},{10,11... | collective-permute-start | bytes 196616 | tf_op jit(solution)/shard_map/ppermute | solution.py:24
  77.0 2.8 %collective-permute-start.35 = (f32[32,512]{1,0:T(8,128)S(1)}, f32[32,512]{1,0:T(8,128)S(1)}, u32[]{:S(2)}, u32[]{:S(2)}) collective-permute-start(f32[32,512]{1,0:T(8,128)S(1)} %collective-permute-done.31.refs_2_), channel_id=1, source_target_pairs={{0,1},{1,0},{2,3},{3,2},{4,5},{5,4},{6,7},{7,6},{8,9},{9,8},{10,11... | collective-permute-start | bytes 196616 | tf_op jit(solution)/shard_map/ppermute | solution.py:24
  77.5 3.3 %collective-permute-start.32 = (f32[32,512]{1,0:T(8,128)S(1)}, f32[32,512]{1,0:T(8,128)S(1)}, u32[]{:S(2)}, u32[]{:S(2)}) collective-permute-start(f32[32,512]{1,0:T(8,128)S(1)} %own.7.refs_1_), channel_id=1, source_target_pairs={{0,1},{1,0},{2,3},{3,2},{4,5},{5,4},{6,7},{7,6},{8,9},{9,8},{10,11... | collective-permute-start | bytes 196616 | tf_op jit(solution)/shard_map/ppermute | solution.py:24
  79.8 1.3 %collective-permute-start.33 = (f32[32,512]{1,0:T(8,128)S(1)}, f32[32,512]{1,0:T(8,128)S(1)}, u32[]{:S(2)}, u32[]{:S(2)}) collective-permute-start(f32[32,512]{1,0:T(8,128)S(1)} %collective-permute-done.30.refs_2_), channel_id=1, source_target_pairs={{0,1},{1,0},{2,3},{3,2},{4,5},{5,4},{6,7},{7,6},{8,9},{9,8},{10,11... | collective-permute-start | bytes 196616 | tf_op jit(solution)/shard_map/ppermute | solution.py:24
